TPU v7x, 32 devices: a whole 2x2x4 slice. The times are simulated.
32 devices in a mesh: expert: 8 (over z, x), tensor: 4 (over y, core).
Axes of the slice: x: 2, y: 2, z: 4, core: 2. Of those that a mesh axis runs over, the one named last changes fastest.
Arguments:
- tokens: bfloat16 [2048, 1024], P('expert'), may hold values from -6 to 6
- cotangent: bfloat16 [2048, 1024], P('expert'), may hold values from -6 to 6
- segments: int32 [8, 256], P('expert'), may hold values from 0 to 2, never falling along the last dimension, each value on 1 to 128 neighbouring positions
- routes: int32 [2048, 8], P('expert'), may hold values from 0 to 31, all different within a row; in each aligned block of 64 rows (0 to 63, 64 to 127, ...) at most 32 rows name the same one
- gates: float32 [2048, 8], P('expert'), may hold values from 0.06 to 0.19
- w_query: float32 [1024, 1024], P('expert', 'tensor'), may hold values from -0.1875 to 0.1875
- key_projection: float32 [1024, 512], P('expert', 'tensor'), may hold values from -0.1875 to 0.1875
- value_projection: float32 [1024, 512], P('expert', 'tensor'), may hold values from -0.1875 to 0.1875
- w_out: float32 [1024, 1024], P('tensor', 'expert'), may hold values from -0.75 to 0.75
- gain_attn: float32 [1024], P('expert'), may hold values from 0.1 to 1.9
- gain_moe: float32 [1024], P('expert'), may hold values from 0.1 to 1.9
- w_gate: float32 [32, 1024, 512], P(None, 'expert', 'tensor'), may hold values from -0.1875 to 0.1875
- w_up: float32 [32, 1024, 512], P(None, 'expert', 'tensor'), may hold values from -0.1875 to 0.1875
- w_down: float32 [32, 512, 1024], P(None, 'tensor', 'expert'), may hold values from -0.75 to 0.75
Outputs:
- output: bfloat16 [2048, 1024], P('expert')
- grad_tokens: float32 [2048, 1024], P('expert')
- grad_query: float32 [1024, 1024], P('expert', 'tensor')
- grad_key: float32 [1024, 512], P('expert', 'tensor')
- grad_value: float32 [1024, 512], P('expert', 'tensor')
- grad_out: float32 [1024, 1024], P('tensor', 'expert')
- grad_gain_attn: float32 [1024], P('expert')
- grad_gain_moe: float32 [1024], P('expert')
- grad_gate: float32 [32, 1024, 512], P(None, 'expert', 'tensor')
- grad_up: float32 [32, 1024, 512], P(None, 'expert', 'tensor')
- grad_down: float32 [32, 512, 1024], P(None, 'tensor', 'expert')
Inputs may be any that keep to these rules, and one draw needn't show every extreme that they name: Within each row of segments the document numbers never fall; each document holds 1 to 128 tokens and one holds exactly 128. `routes`: each row names 8 different experts. In each aligned block of 64 rows no expert is named by more than 32 rows, and in at least one block some expert is named by exactly 32 rows.
All inputs are finite; a program needn't handle non-finite values.
Results may differ from a plain program's by a relative error of at most 0.012.
The roundings to bfloat16 on the way count: a program that leaves them out, or rounds other values in their place, can miss the bound.
Values may be sent and summed in bfloat16 or wider, within the bound.
No kernel may reach another device: no remote copies, remote signals or barrier semaphores. Data moves between devices by JAX's collectives and lax.ppermute only.
A program may use at most 256 MiB of HBM per device.

v0:
```python
import jax
import jax.numpy as jnp
from jax import lax
from jax.sharding import PartitionSpec as P

MODEL_WIDTH = 1024
HEAD_SIZE = 64
EXPERTS = 32
TOP = 8
GROUPS = 4
GROUP_TOKENS = 64
MOST = 32


EPS = 1e-06
THETA = 10000.0
MASKED = -1e30


def positions_of(documents):
    index = jnp.arange(documents.shape[0], dtype=jnp.int32)
    begins = jnp.concatenate(
        [jnp.ones((1,), jnp.int32), (documents[1:] != documents[:-1]).astype(jnp.int32)]
    )
    first = lax.cummax(index * begins, axis=0)
    return index - first


def rope_tables(position, width):
    half = width // 2
    freqs = THETA ** (-2.0 * jnp.arange(half, dtype=jnp.float32) / width)
    angle = position.astype(jnp.float32)[:, None] * freqs[None, :]
    return (jnp.cos(angle), jnp.sin(angle))


def rotary_apply(field, cosine_table, sine_table):
    half = field.shape[-1] // 2
    first = field[..., :half]
    second = field[..., half:]
    cosine_table = cosine_table[:, None, :]
    sine_table = sine_table[:, None, :]
    return jnp.concatenate(
        [first * cosine_table - second * sine_table, second * cosine_table + first * sine_table],
        axis=-1,
    )


def rotate_back(field, cosine_table, sine_table):
    half = field.shape[-1] // 2
    first = field[..., :half]
    second = field[..., half:]
    cosine_table = cosine_table[:, None, :]
    sine_table = sine_table[:, None, :]
    return jnp.concatenate(
        [first * cosine_table + second * sine_table, second * cosine_table - first * sine_table],
        axis=-1,
    )


def rms_scale(field):
    return lax.rsqrt(jnp.mean(field * field, axis=-1, keepdims=True) + EPS)


def norm_back(grad, field, scale, gain):
    weighted = grad * gain
    inner = jnp.mean(weighted * field, axis=-1, keepdims=True)
    return scale * weighted - field * (scale * scale * scale) * inner


def block_scores(query_block, key_rows, documents, start):
    count = query_block.shape[0]
    raw = jnp.einsum(
        "qhgd,khd->hgqk", query_block, key_rows, preferred_element_type=jnp.float32
    ) * HEAD_SIZE ** (-0.5)
    row_index = start + jnp.arange(count)
    col_index = jnp.arange(key_rows.shape[0])
    allowed = (col_index[None, :] <= row_index[:, None]) & (
        documents[None, :] == documents[:, None]
    )
    return jnp.where(allowed[None, None], raw, MASKED)


def slot_tables(route_block, local_experts, replicas, slots):
    flat = route_block.reshape(-1)
    matches = (flat[:, None] == jnp.arange(EXPERTS, dtype=jnp.int32)[None, :]).astype(jnp.int32)
    rank = jnp.sum((jnp.cumsum(matches, axis=0) - matches) * matches, axis=1)
    owner = flat // local_experts * replicas + rank // slots
    place = (owner * local_experts + flat % local_experts) * slots + rank % slots
    total = EXPERTS * MOST
    source = (
        jnp.zeros((total,), jnp.int32).at[place].set(jnp.arange(flat.shape[0], dtype=jnp.int32))
    )
    filled = jnp.zeros((total,), jnp.int32).at[place].set(1)
    return (place, source, filled)


def reduce_parts(field):
    return lax.psum_scatter(field, "tensor", scatter_dimension=1, tiled=True)


def join_parts(field):
    return lax.all_gather(field, "tensor", axis=1, tiled=True)


def local(
    tokens,
    cotangent,
    segments,
    routes,
    gates,
    w_query,
    key_projection,
    value_projection,
    w_out,
    gain_attn,
    gain_moe,
    w_gate,
    w_up,
    w_down,
):
    weights = (
        lax.all_gather(w_query.astype(jnp.bfloat16), "expert", axis=0, tiled=True),
        lax.all_gather(key_projection.astype(jnp.bfloat16), "expert", axis=0, tiled=True),
        lax.all_gather(value_projection.astype(jnp.bfloat16), "expert", axis=0, tiled=True),
        lax.all_gather(w_out.astype(jnp.bfloat16), "expert", axis=1, tiled=True),
        lax.all_gather(gain_attn.astype(jnp.bfloat16), "expert", axis=0, tiled=True),
        lax.all_gather(gain_moe.astype(jnp.bfloat16), "expert", axis=0, tiled=True),
    )
    query_weight, key_matrix, value_matrix, out_weight, attn_gain, moe_gain = weights
    local_experts = EXPERTS
    replicas = 1
    owners = 1
    every = (
        lax.all_gather(w_gate.astype(jnp.bfloat16), "expert", axis=1, tiled=True),
        lax.all_gather(w_up.astype(jnp.bfloat16), "expert", axis=1, tiled=True),
        lax.all_gather(w_down.astype(jnp.bfloat16), "expert", axis=2, tiled=True),
    )
    gate_local, up_local, down_local = every
    slots = MOST // replicas
    hidden_part = gate_local.shape[2]
    inputs = tokens.astype(jnp.float32)
    first_scale = rms_scale(inputs)
    first_gain = attn_gain.astype(jnp.float32)
    first_hidden = (inputs * first_scale * first_gain).astype(jnp.bfloat16)
    documents = segments[0]
    cosine_table, sine_table = rope_tables(positions_of(documents), HEAD_SIZE)
    sequence_length = inputs.shape[0]
    heads = query_weight.shape[1] // HEAD_SIZE
    groups = key_matrix.shape[1] // HEAD_SIZE
    per_group = heads // groups
    query_rows = rotary_apply(
        jnp.dot(first_hidden, query_weight, preferred_element_type=jnp.float32).reshape(
            sequence_length, heads, HEAD_SIZE
        ),
        cosine_table,
        sine_table,
    )
    query_rows = query_rows.astype(jnp.bfloat16).reshape(
        sequence_length, groups, per_group, HEAD_SIZE
    )
    key_rows = rotary_apply(
        jnp.dot(first_hidden, key_matrix, preferred_element_type=jnp.float32).reshape(
            sequence_length, groups, HEAD_SIZE
        ),
        cosine_table,
        sine_table,
    ).astype(jnp.bfloat16)
    value_rows = (
        jnp.dot(first_hidden, value_matrix, preferred_element_type=jnp.float32)
        .astype(jnp.bfloat16)
        .reshape(sequence_length, groups, HEAD_SIZE)
    )
    block = min(512, sequence_length)
    start = 0
    scores = block_scores(query_rows, key_rows, documents, start)
    peak = jnp.max(scores, axis=-1, keepdims=True)
    raised = jnp.exp(scores - peak)
    summed = jnp.sum(raised, axis=-1, keepdims=True)
    shares = (raised / summed).astype(jnp.bfloat16)
    mixed_blocks = jnp.einsum(
        "hgqk,khd->qhgd", shares, value_rows, preferred_element_type=jnp.float32
    ).reshape(block, heads * HEAD_SIZE)
    totals = [peak + jnp.log(summed)]
    mixed = mixed_blocks.astype(jnp.bfloat16)
    branch = jnp.dot(mixed, out_weight, preferred_element_type=jnp.float32)
    attention = join_parts(reduce_parts(branch))
    middle = inputs + attention
    second_scale = rms_scale(middle)
    second_gain = moe_gain.astype(jnp.float32)
    second_hidden = (middle * second_scale * second_gain).astype(jnp.bfloat16)
    kept = []
    combined = []
    for group in range(GROUPS):
        rows = slice(group * GROUP_TOKENS, (group + 1) * GROUP_TOKENS)
        place, source, filled = slot_tables(routes[rows], local_experts, replicas, slots)
        picked = jnp.where(
            filled[:, None] > 0, second_hidden[rows][source // TOP], jnp.zeros((), jnp.bfloat16)
        )
        arrived = picked.reshape(owners, local_experts, slots, MODEL_WIDTH)
        gate_pre = jnp.einsum(
            "nlsd,ldf->nlsf", arrived, gate_local, preferred_element_type=jnp.float32
        )
        up_pre = jnp.einsum("nlsd,ldf->nlsf", arrived, up_local, preferred_element_type=jnp.float32)
        active = (jax.nn.silu(gate_pre) * up_pre).astype(jnp.bfloat16)
        produced = jnp.einsum(
            "nlsf,lfd->nlsd", active, down_local, preferred_element_type=jnp.float32
        ).astype(jnp.bfloat16)
        pair_out = (
            produced.reshape(-1, MODEL_WIDTH)[place]
            .astype(jnp.float32)
            .reshape(GROUP_TOKENS, TOP, MODEL_WIDTH)
        )
        combined.append(jnp.sum(gates[rows][:, :, None] * pair_out, axis=1))
        kept.append((place, source, filled, arrived, gate_pre, up_pre, active))
    expert_cols = jnp.concatenate(combined, axis=0)
    expert_cols = reduce_parts(expert_cols)
    expert_part = join_parts(expert_cols)
    output = (middle + expert_part).astype(jnp.bfloat16)
    grad_output = cotangent.astype(jnp.float32)
    grad_gate_w = jnp.zeros((local_experts, MODEL_WIDTH, hidden_part), jnp.float32)
    grad_up_w = jnp.zeros((local_experts, MODEL_WIDTH, hidden_part), jnp.float32)
    grad_down_w = jnp.zeros((local_experts, hidden_part, MODEL_WIDTH), jnp.float32)
    pieces = []
    for group in range(GROUPS):
        rows = slice(group * GROUP_TOKENS, (group + 1) * GROUP_TOKENS)
        place, source, filled, arrived, gate_pre, up_pre, active = kept[group]
        weight_flat = gates[rows].reshape(-1)
        scaled = (weight_flat[source][:, None] * grad_output[rows][source // TOP]).astype(
            jnp.bfloat16
        )
        picked = jnp.where(filled[:, None] > 0, scaled, jnp.zeros((), jnp.bfloat16))
        arrived_grad = picked.reshape(owners, local_experts, slots, MODEL_WIDTH)
        grad_active = jnp.einsum(
            "nlsd,lfd->nlsf", arrived_grad, down_local, preferred_element_type=jnp.float32
        )
        grad_down_w = grad_down_w + jnp.einsum(
            "nlsf,nlsd->lfd", active, arrived_grad, preferred_element_type=jnp.float32
        )
        squash = jax.nn.sigmoid(gate_pre)
        grad_gate = (grad_active * up_pre * squash * (1.0 + gate_pre * (1.0 - squash))).astype(
            jnp.bfloat16
        )
        grad_up = (grad_active * gate_pre * squash).astype(jnp.bfloat16)
        grad_gate_w = grad_gate_w + jnp.einsum(
            "nlsd,nlsf->ldf", arrived, grad_gate, preferred_element_type=jnp.float32
        )
        grad_up_w = grad_up_w + jnp.einsum(
            "nlsd,nlsf->ldf", arrived, grad_up, preferred_element_type=jnp.float32
        )
        grad_rows = jnp.einsum(
            "nlsf,ldf->nlsd", grad_gate, gate_local, preferred_element_type=jnp.float32
        )
        grad_rows = grad_rows + jnp.einsum(
            "nlsf,ldf->nlsd", grad_up, up_local, preferred_element_type=jnp.float32
        )
        grad_rows_low = grad_rows.astype(jnp.bfloat16)
        pair_grad = (
            grad_rows_low.reshape(-1, MODEL_WIDTH)[place]
            .astype(jnp.float32)
            .reshape(GROUP_TOKENS, TOP, MODEL_WIDTH)
        )
        pieces.append(jnp.sum(pair_grad, axis=1))
    grad_cols = jnp.concatenate(pieces, axis=0)
    grad_cols = reduce_parts(grad_cols)
    grad_second = join_parts(grad_cols)
    grad_moe_gain = jnp.sum(grad_second * middle * second_scale, axis=0)
    grad_middle = grad_output + norm_back(grad_second, middle, second_scale, second_gain)
    grad_branch = grad_middle.astype(jnp.bfloat16)
    grad_out_w = jnp.einsum("tk,td->kd", mixed, grad_branch, preferred_element_type=jnp.float32)
    grad_mixed = jnp.einsum(
        "td,kd->tk", grad_branch, out_weight, preferred_element_type=jnp.float32
    )
    grad_mixed = grad_mixed.astype(jnp.bfloat16).reshape(
        sequence_length, groups, per_group, HEAD_SIZE
    )
    grad_keys = jnp.zeros((sequence_length, groups, HEAD_SIZE), jnp.float32)
    grad_values = jnp.zeros((sequence_length, groups, HEAD_SIZE), jnp.float32)
    grad_query_blocks = []
    for index, start in enumerate(range(0, sequence_length, block)):
        scores = block_scores(query_rows, key_rows, documents, start)
        shares = jnp.exp(scores - totals[index])
        shares_low = shares.astype(jnp.bfloat16)
        grad_shares = jnp.einsum(
            "qhgd,khd->hgqk", grad_mixed, value_rows, preferred_element_type=jnp.float32
        )
        inner = jnp.sum(shares * grad_shares, axis=-1, keepdims=True)
        grad_scores = (shares * (grad_shares - inner)).astype(jnp.bfloat16)
        grad_query_blocks.append(
            jnp.einsum("hgqk,khd->qhgd", grad_scores, key_rows, preferred_element_type=jnp.float32)
            * HEAD_SIZE ** (-0.5)
        )
        grad_keys = jnp.einsum(
            "hgqk,qhgd->khd", grad_scores, query_rows, preferred_element_type=jnp.float32
        ) * HEAD_SIZE ** (-0.5)
        grad_values = jnp.einsum(
            "hgqk,qhgd->khd", shares_low, grad_mixed, preferred_element_type=jnp.float32
        )
    grad_query_low = rotate_back(
        grad_query_blocks[0].reshape(sequence_length, heads, HEAD_SIZE), cosine_table, sine_table
    )
    grad_query_low = grad_query_low.astype(jnp.bfloat16).reshape(sequence_length, heads * HEAD_SIZE)
    grad_key_low = (
        rotate_back(grad_keys, cosine_table, sine_table)
        .astype(jnp.bfloat16)
        .reshape(sequence_length, groups * HEAD_SIZE)
    )
    grad_value_low = grad_values.astype(jnp.bfloat16).reshape(sequence_length, groups * HEAD_SIZE)
    partial_first = jnp.einsum(
        "tk,dk->td", grad_query_low, query_weight, preferred_element_type=jnp.float32
    )
    partial_first = partial_first + jnp.einsum(
        "tk,dk->td", grad_key_low, key_matrix, preferred_element_type=jnp.float32
    )
    partial_first = partial_first + jnp.einsum(
        "tk,dk->td", grad_value_low, value_matrix, preferred_element_type=jnp.float32
    )
    grad_first = join_parts(reduce_parts(partial_first))
    grad_attn_gain = jnp.sum(grad_first * inputs * first_scale, axis=0)
    grad_input = grad_middle + norm_back(grad_first, inputs, first_scale, first_gain)
    grad_query_w = jnp.einsum(
        "td,tk->dk", first_hidden, grad_query_low, preferred_element_type=jnp.float32
    )
    grad_key_w = jnp.einsum(
        "td,tk->dk", first_hidden, grad_key_low, preferred_element_type=jnp.float32
    )
    grad_value_w = jnp.einsum(
        "td,tk->dk", first_hidden, grad_value_low, preferred_element_type=jnp.float32
    )
    shards = (
        lax.psum_scatter(grad_query_w, "expert", scatter_dimension=0, tiled=True),
        lax.psum_scatter(grad_key_w, "expert", scatter_dimension=0, tiled=True),
        lax.psum_scatter(grad_value_w, "expert", scatter_dimension=0, tiled=True),
        lax.psum_scatter(grad_out_w, "expert", scatter_dimension=1, tiled=True),
        lax.psum_scatter(grad_attn_gain, "expert", scatter_dimension=0, tiled=True),
        lax.psum_scatter(grad_moe_gain, "expert", scatter_dimension=0, tiled=True),
    )
    expert_shards = (
        lax.psum_scatter(grad_gate_w, "expert", scatter_dimension=1, tiled=True),
        lax.psum_scatter(grad_up_w, "expert", scatter_dimension=1, tiled=True),
        lax.psum_scatter(grad_down_w, "expert", scatter_dimension=2, tiled=True),
    )
    gate_shard, up_shard, down_shard = expert_shards
    return (
        output,
        grad_input,
        shards[0],
        shards[1],
        shards[2],
        shards[3],
        shards[4],
        shards[5],
        gate_shard,
        up_shard,
        down_shard,
    )


def solution(mesh):
    placed = (
        P("expert", None),
        P("expert", None),
        P("expert", None),
        P("expert", None),
        P("expert", None),
        P("expert", "tensor"),
        P("expert", "tensor"),
        P("expert", "tensor"),
        P("tensor", "expert"),
        P("expert"),
        P("expert"),
        P(None, "expert", "tensor"),
        P(None, "expert", "tensor"),
        P(None, "tensor", "expert"),
    )
    return jax.shard_map(
        local,
        mesh=mesh,
        in_specs=placed,
        out_specs=(
            P("expert", None),
            P("expert", None),
            P("expert", "tensor"),
            P("expert", "tensor"),
            P("expert", "tensor"),
            P("tensor", "expert"),
            P("expert"),
            P("expert"),
            P(None, "expert", "tensor"),
            P(None, "expert", "tensor"),
            P(None, "tensor", "expert"),
        ),
        check_vma=False,
    )
```

profile of v0, /device:TPU:1, one launch (start us, length us, event | category | flops | bytes accessed | tf_op | source)
XLA Modules:
  0.0 1983.7 jit_solution(5280754940437083585)
XLA Ops:
  8.2 25.9 %all_gather.40 = bf16[1024,128]{1,0:T(8,128)(2,1)S(1)} all-gather(bf16[128,128]{1,0:T(8,128)(2,1)S(1)} %convert_element_type.349), channel_id=1, replica_groups=mesh['expert'=8,'tensor'=4] {'expert'}, dimensions={0}, use_global_device_ids=true | all-gather | bytes 294912 | tf_op jit(solution)/shard_map/all_gather | solution.py:124
  34.7 16.5 all-gather
  54.0 25.7 %all_gather.42 = bf16[1024,256]{1,0:T(8,128)(2,1)S(1)} all-gather(bf16[128,256]{1,0:T(8,128)(2,1)S(1)} %convert_element_type.354), channel_id=1, replica_groups=mesh['expert'=8,'tensor'=4] {'expert'}, dimensions={0}, use_global_device_ids=true | all-gather | bytes 589824 | tf_op jit(solution)/shard_map/all_gather | solution.py:122
  83.6 24.8 %all_gather.41 = bf16[1024,128]{1,0:T(8,128)(2,1)S(1)} all-gather(bf16[128,128]{1,0:T(8,128)(2,1)S(1)} %convert_element_type.351), channel_id=1, replica_groups=mesh['expert'=8,'tensor'=4] {'expert'}, dimensions={0}, use_global_device_ids=true | all-gather | bytes 294912 | tf_op jit(solution)/shard_map/all_gather | solution.py:123
  109.3 23.1 %all_gather.43 = bf16[256,1024]{1,0:T(8,128)(2,1)S(1)} all-gather(bf16[256,128]{1,0:T(8,128)(2,1)S(1)} %convert_element_type.359), channel_id=1, replica_groups=mesh['expert'=8,'tensor'=4] {'expert'}, dimensions={1}, use_global_device_ids=true | all-gather | bytes 589824 | tf_op jit(solution)/shard_map/all_gather | solution.py:125
  135.5 48.0 %reduce-scatter.12.cloned.1.call-done = f32[256,256]{1,0:T(8,128)} async-done(((f32[256,1024]{1,0:T(8,128)}), f32[256,256]{1,0:T(8,128)}) %reduce-scatter.12.cloned.1.call-update) | async-done | bytes 262160 | tf_op jit(solution)/shard_map/reduce_scatter | solution.py:98
  190.6 16.6 all-gather.1
  307.3 21.6 %all-gather.12.cloned.1.call-done = bf16[32,1024,128]{2,1,0:T(8,128)(2,1)} async-done(((bf16[32,128,128]{2,1,0:T(8,128)(2,1)}), bf16[32,1024,128]{2,1,0:T(8,128)(2,1)}) %all-gather.12.cloned.1.call-update) | async-done | bytes 8388624 | tf_op jit(solution)/shard_map/all_gather | solution.py:134
  333.8 120.5 %all-gather.14.cloned.1.call-done = bf16[32,1024,128]{2,1,0:T(8,128)(2,1)} async-done(((bf16[32,128,128]{2,1,0:T(8,128)(2,1)}), bf16[32,1024,128]{2,1,0:T(8,128)(2,1)}) %all-gather.14.cloned.1.call-update) | async-done | bytes 8388624 | tf_op jit(solution)/shard_map/all_gather | solution.py:135
  460.0 120.0 %all-gather.16.cloned.1.call-done = bf16[32,128,1024]{2,1,0:T(8,128)(2,1)} async-done(((bf16[32,128,128]{2,1,0:T(8,128)(2,1)}), bf16[32,128,1024]{2,1,0:T(8,128)(2,1)}) %all-gather.16.cloned.1.call-update) | async-done | bytes 8388624 | tf_op jit(solution)/shard_map/all_gather | solution.py:136
  743.8 23.3 %reduce-scatter.14.cloned.1.call-done = f32[256,256]{1,0:T(8,128)} async-done(((f32[256,1024]{1,0:T(8,128)}), f32[256,256]{1,0:T(8,128)}) %reduce-scatter.14.cloned.1.call-update) | async-done | bytes 262160 | tf_op jit(solution)/shard_map/reduce_scatter | solution.py:98
  767.4 18.5 all-gather.20.cloned.1.call-done
  788.0 16.3 all-gather.18.cloned.1.call-done
  812.0 24.6 %reduce-scatter.18.cloned.1.call-done = f32[256,256]{1,0:T(8,128)} async-done(((f32[256,1024]{1,0:T(8,128)}), f32[256,256]{1,0:T(8,128)}) %reduce-scatter.18.cloned.1.call-update) | async-done | bytes 262160 | tf_op jit(solution)/shard_map/reduce_scatter | solution.py:98
  865.0 23.2 %add_add_fusion.2 = f32[32,1024,128]{2,1,0:T(8,128)} fusion(f32[32,1024,128]{2,1,0:T(8,128)} %fusion.20, f32[32,1024,128]{2,1,0:T(8,128)} %fusion.12, f32[32,1024,128]{2,1,0:T(8,128)} %fusion.16, bf16[32,32,1024]{2,1,0:T(8,128)(2,1)S(1)} %bitcast.433, pred[32,32]{1,0:T(8,128)(4,1)S(1)} %broadcast_in_dim.173, bf16[1,32,32,128]{3,2,1,0:T(8,128)(2,1)S(1)} %copy-done.36), kind=kOutput, calls=%fused_computation.30 | convolution fusion | flops 282066944 | bytes 69469184 | tf_op jit(solution)/shard_map/nlsd,nlsf->ldf/dot_general | solution.py:244
  907.5 17.3 add_add_fusion.1
  925.7 10.5 fusion.65
  952.6 23.1 %add_add_fusion = f32[32,128,1024]{2,1,0:T(8,128)} fusion(f32[32,128,1024]{2,1,0:T(8,128)} %fusion.65, f32[32,128,1024]{2,1,0:T(8,128)} %fusion.71, f32[32,128,1024]{2,1,0:T(8,128)} %fusion.68, f32[32,32,1024]{2,1,0:T(8,128)S(1)} %bitcast.452, f32[32,32]{1,0:T(8,128)S(1)} %copy-done.74, pred[32,32]{1,0:T(8,128)(4,1)S(1)} %broadcast_in_dim.173, ...), kind=kOutput, calls=%fused_computation.28 | convolution fusion | flops 284164096 | bytes 71570432 | tf_op jit(solution)/shard_map/nlsf,nlsd->lfd/dot_general | solution.py:236
  979.2 17.9 all-reduce.2
  1000.8 49.9 %reduce-scatter.20.cloned.1.call-done = f32[128,256]{1,0:T(8,128)} async-done(((f32[1024,256]{1,0:T(8,128)}), f32[128,256]{1,0:T(8,128)}) %reduce-scatter.20.cloned.1.call-update) | async-done | bytes 131088 | tf_op jit(solution)/shard_map/reduce_scatter | solution.py:330
  1050.7 67.0 %reduce-scatter.26.cloned.1.call-done = f32[256,128]{1,0:T(8,128)} async-done(((f32[256,1024]{1,0:T(8,128)}), f32[256,128]{1,0:T(8,128)}) %reduce-scatter.26.cloned.1.call-update) | async-done | bytes 131088 | tf_op jit(solution)/shard_map/reduce_scatter | solution.py:333
  1117.8 286.8 %reduce-scatter.28.cloned.1.call-done = f32[32,128,128]{2,1,0:T(8,128)} async-done(((f32[32,1024,128]{2,1,0:T(8,128)}), f32[32,128,128]{2,1,0:T(8,128)}) %reduce-scatter.28.cloned.1.call-update) | async-done | bytes 2097168 | tf_op jit(solution)/shard_map/reduce_scatter | solution.py:338
  1404.6 285.7 %reduce-scatter.30.cloned.1.call-done = f32[32,128,128]{2,1,0:T(8,128)} async-done(((f32[32,1024,128]{2,1,0:T(8,128)}), f32[32,128,128]{2,1,0:T(8,128)}) %reduce-scatter.30.cloned.1.call-update) | async-done | bytes 2097168 | tf_op jit(solution)/shard_map/reduce_scatter | solution.py:339
  1690.3 286.0 %reduce-scatter.32.cloned.1.call-done = f32[32,128,128]{2,1,0:T(8,128)} async-done(((f32[32,128,1024]{2,1,0:T(8,128)}), f32[32,128,128]{2,1,0:T(8,128)}) %reduce-scatter.32.cloned.1.call-update) | async-done | bytes 2097168 | tf_op jit(solution)/shard_map/reduce_scatter | solution.py:340
  (482 shorter events, 373.6 us)
Async XLA Ops:
  7.2 176.3 %reduce-scatter.12.cloned.1.call-start = ((), (), s32[]{:S(2)}) async-start(), calls=%async_computation.11 | async-start | bytes 1310720 | tf_op jit(solution)/shard_map/reduce_scatter | solution.py:98
  135.5 149.3 %all-gather.10.cloned.1.call-start = ((), (), s32[]{:S(2)}) async-start(), calls=%async_computation.12 | async-start | bytes 1310720 | tf_op jit(solution)/shard_map/all_gather | solution.py:102
  183.5 145.4 %all-gather.12.cloned.1.call-start = ((), (), s32[]{:S(2)}) async-start(), calls=%async_computation.13 | async-start | bytes 9437184 | tf_op jit(solution)/shard_map/all_gather | solution.py:134
  184.8 269.5 %all-gather.14.cloned.1.call-start = ((), (), s32[]{:S(2)}) async-start(), calls=%async_computation.14 | async-start | bytes 9437184 | tf_op jit(solution)/shard_map/all_gather | solution.py:135
  187.8 392.2 %all-gather.16.cloned.1.call-start = ((), (), s32[]{:S(2)}) async-start(), calls=%async_computation.15 | async-start | bytes 9437184 | tf_op jit(solution)/shard_map/all_gather | solution.py:136
  189.0 554.0 %reduce-scatter.16.cloned.1.call-start = ((), (), s32[]{:S(2)}) async-start(), calls=%async_computation.18 | async-start | bytes 1310720 | tf_op jit(solution)/shard_map/reduce_scatter | solution.py:98
  221.1 358.9 %copy-start.73 = (f32[32,32]{1,0:T(8,128)}, f32[32,32]{1,0:T(8,128)S(1)}, u32[]{:S(2)}) copy-start(f32[32,32]{1,0:T(8,128)S(1)} %mul.668) | copy-start | bytes 12292
  235.2 377.3 %copy-start.75 = (f32[32,32]{1,0:T(8,128)}, f32[32,32]{1,0:T(8,128)S(1)}, u32[]{:S(2)}) copy-start(f32[32,32]{1,0:T(8,128)S(1)} %mul.659) | copy-start | bytes 12292
  249.0 399.6 %copy-start.77 = (f32[32,32]{1,0:T(8,128)}, f32[32,32]{1,0:T(8,128)S(1)}, u32[]{:S(2)}) copy-start(f32[32,32]{1,0:T(8,128)S(1)} %mul.650) | copy-start | bytes 12292
  262.7 418.4 %copy-start.79 = (f32[32,32]{1,0:T(8,128)}, f32[32,32]{1,0:T(8,128)S(1)}, u32[]{:S(2)}) copy-start(f32[32,32]{1,0:T(8,128)S(1)} %mul.641) | copy-start | bytes 12292
  291.2 163.1 %copy-start.1 = (bf16[1024,1024]{1,0:T(8,128)(2,1)}, bf16[1024,1024]{1,0:T(8,128)(2,1)S(1)}, u32[]{:S(2)}) copy-start(bf16[1024,1024]{1,0:T(8,128)(2,1)S(1)} %gather_fusion.6) | copy-start | bytes 6291460
  587.5 118.4 %copy-start.26 = (bf16[1,32,32,128]{3,2,1,0:T(8,128)(2,1)}, bf16[1,32,32,128]{3,2,1,0:T(8,128)(2,1)S(1)}, u32[]{:S(2)}) copy-start(bf16[1,32,32,128]{3,2,1,0:T(8,128)(2,1)S(1)} %get-tuple-element.32) | copy-start | bytes 786436
  705.9 61.2 %reduce-scatter.14.cloned.1.call-start = ((), (), s32[]{:S(2)}) async-start(), calls=%async_computation.16 | async-start | bytes 1310720 | tf_op jit(solution)/shard_map/reduce_scatter | solution.py:98
  743.0 42.9 %all-gather.20.cloned.1.call-start = ((), (), s32[]{:S(2)}) async-start(), calls=%async_computation.19 | async-start | bytes 1310720 | tf_op jit(solution)/shard_map/all_gather | solution.py:102
  743.7 60.5 %all-gather.18.cloned.1.call-start = ((), (), s32[]{:S(2)}) async-start(), calls=%async_computation.17 | async-start | bytes 1310720 | tf_op jit(solution)/shard_map/all_gather | solution.py:102
  767.1 69.5 %reduce-scatter.18.cloned.1.call-start = ((), (), s32[]{:S(2)}) async-start(), calls=%async_computation.20 | async-start | bytes 1310720 | tf_op jit(solution)/shard_map/reduce_scatter | solution.py:98
  812.0 165.7 %all-gather.22.cloned.1.call-start = ((), (), s32[]{:S(2)}) async-start(), calls=%async_computation.21 | async-start | bytes 1310720 | tf_op jit(solution)/shard_map/all_gather | solution.py:102
  836.7 164.1 %reduce-scatter.22.cloned.1.call-start = ((), (), s32[]{:S(2)}) async-start(), calls=%async_computation.23 | async-start | bytes 589824 | tf_op jit(solution)/shard_map/reduce_scatter | solution.py:331
  838.1 162.7 %reduce-scatter.24.cloned.1.call-start = ((), (), s32[]{:S(2)}) async-start(), calls=%async_computation.24 | async-start | bytes 589824 | tf_op jit(solution)/shard_map/reduce_scatter | solution.py:332
  839.4 211.3 %reduce-scatter.20.cloned.1.call-start = ((), (), s32[]{:S(2)}) async-start(), calls=%async_computation.22 | async-start | bytes 1179648 | tf_op jit(solution)/shard_map/reduce_scatter | solution.py:330
  840.9 276.8 %reduce-scatter.26.cloned.1.call-start = ((), (), s32[]{:S(2)}) async-start(), calls=%async_computation.25 | async-start | bytes 1179648 | tf_op jit(solution)/shard_map/reduce_scatter | solution.py:333
  864.3 540.3 %reduce-scatter.28.cloned.1.call-start = ((), (), s32[]{:S(2)}) async-start(), calls=%async_computation.26 | async-start | bytes 18874368 | tf_op jit(solution)/shard_map/reduce_scatter | solution.py:338
  888.2 802.1 %reduce-scatter.30.cloned.1.call-start = ((), (), s32[]{:S(2)}) async-start(), calls=%async_computation.27 | async-start | bytes 18874368 | tf_op jit(solution)/shard_map/reduce_scatter | solution.py:339
  924.8 1051.5 %reduce-scatter.32.cloned.1.call-start = ((), (), s32[]{:S(2)}) async-start(), calls=%async_computation.28 | async-start | bytes 18874368 | tf_op jit(solution)/shard_map/reduce_scatter | solution.py:340
  (107 other events, 1841.1 us)
Sparse Core Ops, SparseCore 0:
  135.6 47.8 reduce-scatter.11
  185.2 17.1 all-gather.9
  204.7 124.1 all-gather.11
  331.2 123.0 all-gather.13
  456.4 123.5 all-gather.15
  706.0 23.5 reduce-scatter.15
  743.1 23.9 reduce-scatter.13
  768.7 17.1 all-gather.19
  787.5 16.7 all-gather.17
  812.1 24.5 reduce-scatter.17
  838.2 17.0 all-gather.21
  859.1 59.6 reduce-scatter.21
  923.1 60.8 reduce-scatter.23
  987.9 62.8 reduce-scatter.19
  1054.9 62.7 reduce-scatter.25
  1122.0 282.5 reduce-scatter.27
  1409.3 280.9 reduce-scatter.29
  1694.5 281.7 reduce-scatter.31
where the time goes:
time: 1990 us; the launch traced here: 1980 us
  waiting for transfers between devices  1370 us (69%)
  matrix products  280 us (14%)
  blocking collectives  150 us (8%)
  local copies, waits for them, and re-layouts  122 us (6%)
  other arithmetic  42.7 us (2%)
    reduce_scatter x1, waiting for transfers between devices, local(): lax.psum_scatter(grad_gate_w, 'expert', scatter_dimension=1, tiled=True)  287 us
    reduce_scatter x1, waiting for transfers between devices, local(): lax.psum_scatter(grad_down_w, 'expert', scatter_dimension=2, tiled=True)  286 us
    reduce_scatter x1, waiting for transfers between devices, local(): lax.psum_scatter(grad_up_w, 'expert', scatter_dimension=1, tiled=True)  286 us
    all_gather x1, waiting for transfers between devices, local(): lax.all_gather(w_up.astype(jnp.bfloat16), 'expert', axis=1, tiled=True)  121 us
    all_gather x1, waiting for transfers between devices, local(): lax.all_gather(w_down.astype(jnp.bfloat16), 'expert', axis=2, tiled=True)  120 us
    reduce_scatter x4, waiting for transfers between devices, reduce_parts(): return lax.psum_scatter(field, 'tensor', scatter_dimension=1, tiled=True)  95.9 us
    reduce_scatter x1, waiting for transfers between devices, local(): lax.psum_scatter(grad_out_w, 'expert', scatter_dimension=1, tiled=True)  67 us
    reduce_scatter x1, waiting for transfers between devices, local(): lax.psum_scatter(grad_query_w, 'expert', scatter_dimension=0, tiled=True)  49.9 us
  transfers between devices with their start and end apart: 18, of which 13 were waited for; matrix products, arithmetic and copies ran while one was open for 15% of the time, Pallas kernels for 0%

commit v1 on v0

v1 whole, which is shorter than its diff:
```python
import jax
import jax.numpy as jnp
from jax import lax
from jax.sharding import PartitionSpec as P

HEAD_SIZE = 64
EXPERTS = 32
TOP = 8
EPS = 1e-06
THETA = 10000.0
MASKED = -1e30

LOW = jnp.bfloat16
FULL = jnp.float32
ROWS_ON_ROWS = (((0,), (0,)), ((), ()))
COLS_ON_ROWS = (((1,), (0,)), ((), ()))
COLS_ON_COLS = (((1,), (1,)), ((), ()))


def mul(left, right, dims=COLS_ON_ROWS):
    return lax.dot_general(left, right, dims, preferred_element_type=FULL)


def swap(field, axis, mask):
    count = lax.axis_size(axis)
    return lax.ppermute(field, axis, [(i, i ^ mask) for i in range(count)])


def stages_of(count, first_bit):
    bits = [1 << b for b in range(first_bit, count.bit_length() - 1)]
    bits.reverse()
    stages = []
    if len(bits) >= 2:
        stages.append([bits[0], bits[1], bits[0] | bits[1]])
        bits = bits[2:]
    return stages + [[b] for b in bits]


def gather_stage(field, axis, masks):
    return jnp.concatenate([field] + [swap(field, axis, m) for m in masks], axis=0)


def scatter_stage(low_parts, kept, axis, masks):
    total = kept
    for part, m in zip(low_parts, masks):
        total = total + swap(part, axis, m).astype(FULL)
    return total


def reorder(field, mine, count, dim):
    size = field.shape[dim] // count
    return jnp.concatenate(
        [lax.dynamic_slice_in_dim(field, (mine ^ m) * size, size, dim) for m in range(count)],
        axis=dim,
    )


def rms_scale(field):
    return lax.rsqrt(jnp.mean(field * field, axis=-1, keepdims=True) + EPS)


def norm_back(grad, field, scale, gain):
    weighted = grad * gain
    inner = jnp.mean(weighted * field, axis=-1, keepdims=True)
    return scale * weighted - field * (scale * scale * scale) * inner


def turn(field, cosine, sine):
    half = field.shape[-1] // 2
    first, second = field[..., :half], field[..., half:]
    cosine, sine = cosine[:, None, :], sine[:, None, :]
    return jnp.concatenate(
        [first * cosine - second * sine, second * cosine + first * sine], axis=-1
    )


def local(
    tokens,
    cotangent,
    segments,
    routes,
    gates,
    w_query,
    key_projection,
    value_projection,
    w_out,
    gain_attn,
    gain_moe,
    w_gate,
    w_up,
    w_down,
):
    n_e, n_t = lax.axis_size("expert"), lax.axis_size("tensor")
    e, t = lax.axis_index("expert"), lax.axis_index("tensor")
    replicas = max(1, n_e // EXPERTS)
    own_experts = EXPERTS * replicas // n_e
    first_bit = replicas.bit_length() - 1
    length, width = tokens.shape
    part = width // n_e
    rows = length // n_t
    q_cols, k_cols = w_query.shape[1], key_projection.shape[1]
    hidden = w_gate.shape[2]
    group_masks = [m for s in stages_of(n_e, 0) for m in s]

    qkv_shard = jnp.concatenate([w_query, key_projection, value_projection], axis=1).astype(LOW)
    out_shard = w_out.astype(LOW)
    gain_shard = jnp.stack([gain_attn, gain_moe]).astype(LOW)

    def every(shard):
        held = {0: shard}
        for masks in stages_of(n_e, 0):
            fresh = {}
            for m in masks:
                for k, piece in held.items():
                    fresh[k ^ m] = swap(piece, "expert", m)
            held.update(fresh)
        return [held[m] for m in range(n_e)]

    qkv_rows = jnp.concatenate(every(qkv_shard), axis=0)
    out_cols = jnp.concatenate(every(out_shard), axis=1)
    gains = lax.all_gather(gain_shard, "expert", axis=1, tiled=True).astype(FULL)
    first_gain, second_gain = gains[0:1], gains[1:2]

    packed = jnp.concatenate(
        [
            w.astype(LOW).reshape(EXPERTS // own_experts, own_experts, w.shape[1] * w.shape[2] // 128, 128)
            for w in (w_gate, w_up, w_down)
        ],
        axis=1,
    )

    def to_owner(m):
        return lax.dynamic_index_in_dim(packed, (e ^ m) // replicas, 0, keepdims=False)

    arrived = [to_owner(0)] + [swap(to_owner(m), "expert", m) for m in range(1, n_e)]
    gate_up = jnp.zeros((n_e, part, 2 * own_experts * hidden), LOW)
    down = jnp.zeros((own_experts * hidden, width), LOW)
    for m, piece in enumerate(arrived):
        block = piece[: 2 * own_experts].reshape(2 * own_experts, part, hidden)
        block = block.transpose(1, 0, 2).reshape(1, part, 2 * own_experts * hidden)
        gate_up = lax.dynamic_update_slice(gate_up, block, (e ^ m, 0, 0))
        block = piece[2 * own_experts :].reshape(own_experts * hidden, part)
        down = lax.dynamic_update_slice(down, block, (0, (e ^ m) * part))
    gate_up = gate_up.reshape(width, 2 * own_experts * hidden)

    e_stages = [("expert", s) for s in stages_of(n_e, first_bit)]
    t_stages = [("tensor", [1 << b]) for b in reversed(range(n_t.bit_length() - 1))]
    t_last = t_stages[-1:]
    t_stages = t_stages[:-1]
    paths = [e_stages + t_stages, e_stages[:1] + t_stages + e_stages[1:]]

    def gather_tokens(block):
        half = block.shape[0] // 2
        chunks = []
        for field, path in zip((block[:half], block[half:]), paths):
            for axis, masks in path:
                field = gather_stage(field, axis, masks)
            chunks.append(field)
        field = jnp.concatenate(chunks, axis=0)
        for axis, masks in t_last:
            field = gather_stage(field, axis, masks)
        return field

    def scatter_tokens(field):
        for axis, masks in t_last:
            size = field.shape[0] // 2
            field = scatter_stage([field[size:].astype(LOW)], field[:size], axis, masks)
        half = field.shape[0] // 2
        done = []
        for chunk, path in zip((field[:half], field[half:]), paths):
            for axis, masks in reversed(path):
                size = chunk.shape[0] // (len(masks) + 1)
                sent = [
                    chunk[(i + 1) * size : (i + 2) * size].astype(LOW) for i in range(len(masks))
                ]
                chunk = scatter_stage(sent, chunk[:size], axis, masks)
            done.append(chunk)
        return jnp.concatenate(done, axis=0)

    own = t * rows
    grad_rows = lax.dynamic_slice_in_dim(cotangent, own, rows, 0)
    gate_rows = lax.dynamic_slice_in_dim(gates, own, rows, 0)
    route_rows = lax.dynamic_slice_in_dim(routes, own, rows, 0)
    gate_high = gate_rows.astype(LOW)
    gate_rest = (gate_rows - gate_high.astype(FULL)).astype(LOW)
    extra = jnp.concatenate(
        [
            route_rows.astype(LOW),
            gate_high,
            gate_rest,
            jnp.zeros((rows, 128 - 3 * TOP), LOW),
        ],
        axis=1,
    )
    grad_all = gather_tokens(jnp.concatenate([grad_rows, extra], axis=1))
    extra_all = grad_all[:, width : width + 3 * TOP].astype(FULL)
    grad_all = grad_all[:, :width]
    route_all = extra_all[:, :TOP].astype(jnp.int32)
    gate_all = extra_all[:, TOP : 2 * TOP] + extra_all[:, 2 * TOP :]
    first_expert = e // replicas * own_experts
    gate_of = jnp.concatenate(
        [
            jnp.broadcast_to(
                jnp.sum(
                    jnp.where(route_all == first_expert + j, gate_all, 0.0), axis=1, keepdims=True
                ),
                (route_all.shape[0], hidden),
            )
            for j in range(own_experts)
        ],
        axis=1,
    )

    inputs = tokens.astype(FULL)
    first_scale = rms_scale(inputs)
    first_hidden = (inputs * first_scale * first_gain).astype(LOW)
    hidden_rel = reorder(first_hidden, e, n_e, 1)
    documents = segments[0]
    index = jnp.arange(length)
    allowed = (index[None, :] <= index[:, None]) & (documents[None, :] == documents[:, None])
    position = jnp.sum(allowed.astype(FULL), axis=1) - 1.0
    freqs = THETA ** (-2.0 * jnp.arange(HEAD_SIZE // 2, dtype=FULL) / HEAD_SIZE)
    angle = position[:, None] * freqs[None, :]
    cosine, sine = jnp.cos(angle), jnp.sin(angle)
    heads, groups = q_cols // HEAD_SIZE, k_cols // HEAD_SIZE
    per_group = heads // groups
    qkv = mul(hidden_rel, qkv_rows)
    turned = turn(
        qkv[:, : q_cols + k_cols].reshape(length, heads + groups, HEAD_SIZE), cosine, sine
    ).astype(LOW)
    query = turned[:, :heads].reshape(length, groups, per_group, HEAD_SIZE)
    key = turned[:, heads:]
    value = qkv[:, q_cols + k_cols :].astype(LOW).reshape(length, groups, HEAD_SIZE)
    scores = jnp.einsum("qhgd,khd->hgqk", query, key, preferred_element_type=FULL)
    scores = jnp.where(allowed[None, None], scores * HEAD_SIZE**-0.5, MASKED)
    peak = jnp.max(scores, axis=-1, keepdims=True)
    raised = jnp.exp(scores - peak)
    shares = raised / jnp.sum(raised, axis=-1, keepdims=True)
    shares_low = shares.astype(LOW)
    mixed = jnp.einsum("hgqk,khd->qhgd", shares_low, value, preferred_element_type=FULL)
    mixed = mixed.astype(LOW).reshape(length, q_cols)
    order = [0]
    for axis, masks in reversed(t_stages + t_last):
        order = [k ^ b for b in [0] + masks for k in order] if False else order
    order = list(range(n_t))
    for_stage = [masks[0] for axis, masks in t_last + t_stages]
    order = [0]
    for b in reversed(for_stage):
        order = order + [k ^ b for k in order]
    mixed_rel = jnp.concatenate(
        [lax.dynamic_slice_in_dim(mixed, (t ^ m) * rows, rows, 0) for m in order], axis=0
    )

    def scatter_rows(field):
        for b in for_stage:
            size = field.shape[0] // 2
            field = scatter_stage([field[size:].astype(LOW)], field[:size], "tensor", [b])
        return field

    def gather_rows(field):
        for b in reversed(for_stage):
            field = gather_stage(field, "tensor", [b])
        return field

    own_inputs = lax.dynamic_slice_in_dim(tokens, own, rows, 0).astype(FULL)
    attention = reorder(scatter_rows(mul(mixed_rel, out_cols)), e, n_e, 1)
    middle = own_inputs + attention
    second_scale = rms_scale(middle)
    second_hidden = (middle * second_scale * second_gain).astype(LOW)

    hidden_all = gather_tokens(second_hidden)
    both = mul(hidden_all, gate_up)
    wide = own_experts * hidden
    gate_pre, up_pre = both[:, :wide], both[:, wide:]
    back = mul(grad_all, down, COLS_ON_COLS) * gate_of
    squash = jax.nn.sigmoid(gate_pre)
    silu = gate_pre * squash
    active = (silu * up_pre).astype(LOW).astype(FULL)
    active = (active * gate_of).astype(LOW)
    grad_gate = (back * up_pre * squash * (1.0 + gate_pre * (1.0 - squash))).astype(LOW)
    grad_up = (back * silu).astype(LOW)
    grad_both = jnp.concatenate([grad_gate, grad_up], axis=1)
    grad_second = scatter_tokens(mul(grad_both, gate_up, COLS_ON_COLS))
    expert_out = scatter_tokens(mul(active, down))
    output_rows = (middle + expert_out).astype(LOW)
    output = lax.all_gather(output_rows, "tensor", axis=0, tiled=True)

    grad_gate_up_w = mul(hidden_all, grad_both, ROWS_ON_ROWS)
    grad_down_w = mul(active, grad_all, ROWS_ON_ROWS)

    def to_holder(m):
        block = lax.dynamic_slice_in_dim(grad_gate_up_w, (e ^ m) * part, part, 0)
        block = block.reshape(part, 2 * own_experts, hidden).transpose(1, 0, 2)
        block = block.reshape(2 * own_experts, part * hidden // 128, 128)
        other = lax.dynamic_slice_in_dim(grad_down_w, (e ^ m) * part, part, 1)
        other = other.reshape(own_experts, hidden * part // 128, 128)
        return jnp.concatenate([block, other], axis=0)

    returned = [to_holder(0)] + [
        swap(to_holder(m).astype(LOW), "expert", m).astype(FULL) for m in range(1, n_e)
    ]
    shards = [jnp.zeros((EXPERTS,) + w.shape[1:], FULL) for w in (w_gate, w_up, w_down)]
    totals = {}
    for m, piece in enumerate(returned):
        root = m // replicas
        totals[root] = totals[root] + piece if root in totals else piece
    for root, piece in totals.items():
        at = (e // replicas ^ root) * own_experts
        for i, shard in enumerate(shards):
            block = piece[i * own_experts : (i + 1) * own_experts]
            shards[i] = lax.dynamic_update_slice(
                shard, block.reshape((own_experts,) + shard.shape[1:]), (at, 0, 0)
            )

    own_grad = grad_rows.astype(FULL)
    moe_gain_part = jnp.sum(grad_second * middle * second_scale, axis=0, keepdims=True)
    grad_middle = own_grad + norm_back(grad_second, middle, second_scale, second_gain)
    branch_rel = gather_rows(reorder(grad_middle.astype(LOW), e, n_e, 1))
    grad_out_w = mul(mixed_rel, branch_rel, ROWS_ON_ROWS)
    grad_mixed_rel = mul(branch_rel, out_cols, COLS_ON_COLS).astype(LOW)
    place = {m: k for k, m in enumerate(order)}

    def natural_rows(field):
        table = jnp.array([place[m] for m in range(n_t)], jnp.int32)
        return jnp.concatenate(
            [lax.dynamic_slice_in_dim(field, table[t ^ k] * rows, rows, 0) for k in range(n_t)],
            axis=0,
        )

    grad_mixed = natural_rows(grad_mixed_rel).reshape(length, groups, per_group, HEAD_SIZE)
    grad_shares = jnp.einsum("qhgd,khd->hgqk", grad_mixed, value, preferred_element_type=FULL)
    inner = jnp.sum(shares * grad_shares, axis=-1, keepdims=True)
    grad_scores = (shares * (grad_shares - inner)).astype(LOW)
    grad_query = jnp.einsum("hgqk,khd->qhgd", grad_scores, key, preferred_element_type=FULL)
    grad_key = jnp.einsum("hgqk,qhgd->khd", grad_scores, query, preferred_element_type=FULL)
    grad_value = jnp.einsum("hgqk,qhgd->khd", shares_low, grad_mixed, preferred_element_type=FULL)
    grad_turned = jnp.concatenate(
        [grad_query.reshape(length, heads, HEAD_SIZE), grad_key], axis=1
    ) * HEAD_SIZE**-0.5
    grad_qkv = jnp.concatenate(
        [
            turn(grad_turned, cosine, -sine).astype(LOW).reshape(length, q_cols + k_cols),
            grad_value.astype(LOW).reshape(length, k_cols),
        ],
        axis=1,
    )
    grad_qkv_w = mul(hidden_rel, grad_qkv, ROWS_ON_ROWS)
    grad_qkv_rel = jnp.concatenate(
        [lax.dynamic_slice_in_dim(grad_qkv, (t ^ m) * rows, rows, 0) for m in order], axis=0
    )
    grad_first = reorder(
        scatter_rows(mul(grad_qkv_rel, qkv_rows, COLS_ON_COLS)), e, n_e, 1
    )
    own_scale = lax.dynamic_slice_in_dim(first_scale, own, rows, 0)
    attn_gain_part = jnp.sum(grad_first * own_inputs * own_scale, axis=0, keepdims=True)
    grad_input = grad_middle + norm_back(grad_first, own_inputs, own_scale, first_gain)
    grad_input = lax.all_gather(grad_input.astype(LOW), "tensor", axis=0, tiled=True).astype(FULL)

    def shared(blocks):
        held = blocks
        for masks in reversed(stages_of(n_e, 0)):
            span = {0, *masks}
            bits = 0
            for m in masks:
                bits |= m
            kept = {}
            for k in held:
                if k & bits == 0:
                    total = held[k]
                    for m in masks:
                        total = total + swap(held[k ^ m].astype(LOW), "expert", m).astype(FULL)
                    kept[k] = total
            held = kept
        return held[0]

    qkv_grad = shared({m: grad_qkv_w[m * part : (m + 1) * part] for m in range(n_e)})
    out_grad = shared({m: grad_out_w[:, m * part : (m + 1) * part] for m in range(n_e)})
    gain_parts = jnp.concatenate([attn_gain_part, moe_gain_part], axis=0)
    gain_grads = lax.psum(gain_parts, ("expert", "tensor"))
    gain_grads = lax.dynamic_slice_in_dim(gain_grads, e * part, part, 1)
    return (
        output,
        grad_input,
        qkv_grad[:, :q_cols],
        qkv_grad[:, q_cols : q_cols + k_cols],
        qkv_grad[:, q_cols + k_cols :],
        out_grad,
        gain_grads[0],
        gain_grads[1],
        shards[0],
        shards[1],
        shards[2],
    )


def solution(mesh):
    by_rows = P("expert", None)
    by_both = P("expert", "tensor")
    in_experts = P(None, "expert", "tensor")
    down_specs = P(None, "tensor", "expert")
    return jax.shard_map(
        local,
        mesh=mesh,
        in_specs=(by_rows,) * 5
        + (by_both,) * 3
        + (P("tensor", "expert"), P("expert"), P("expert"), in_experts, in_experts, down_specs),
        out_specs=(by_rows, by_rows)
        + (by_both,) * 3
        + (P("tensor", "expert"), P("expert"), P("expert"), in_experts, in_experts, down_specs),
        check_vma=False,
    )
```

time: 1990 us -> 587 us (0.29)
  waiting for transfers between devices: 1370 us -> 145 us
  matrix products: 280 us -> 44.8 us
  starting transfers between devices: 1.49 us -> 147 us
  blocking collectives: 150 us -> 73.9 us
    reduce_scatter x11 -> x0, waiting for transfers between devices: 1070 us -> none  [the longest x1 287 us: local(): lax.psum_scatter(grad_gate_w, 'expert', scatter_dimension=1, tiled=True)]
    all_gather x7 -> x0, waiting for transfers between devices: 297 us -> none  [the longest x1 121 us: local(): lax.all_gather(w_up.astype(jnp.bfloat16), 'expert', axis=1, tiled=True)]
    dot_general x53 -> x16, matrix products: 280 us -> 40.9 us  [the longest x12 38 us: mul(): return lax.dot_general(left, right, dims, preferred_element_type=FULL)]
    ppermute x0 -> x92, starting transfers between devices: none -> 147 us  [swap(): return lax.ppermute(field, axis, [(i, i ^ mask) for i in range(count)])]
    ppermute x0 -> x92, waiting for transfers between devices: none -> 145 us  [swap(): return lax.ppermute(field, axis, [(i, i ^ mask) for i in range(count)])]
    all_gather x6 -> x3, blocking collectives: 133 us -> 32.4 us  [the longest x1 15.6 us: local(): lax.all_gather(gain_shard, 'expert', axis=1, tiled=True).astype(FULL)]
    gather x20 -> x0, local copies, waits for them, and re-layouts: 92.7 us -> none  [the longest x4 27.5 us: local(): weight_flat[source][:, None] * grad_output[rows][source // TOP]]
    psum x0 -> x1, blocking collectives: none -> 41.5 us  [local(): gain_grads = lax.psum(gain_parts, ('expert', 'tensor'))]
  transfers between devices with their start and end apart: 18 -> 92, of which waited for: 13 -> 42; matrix products, arithmetic and copies ran while one was open for 15% -> 25% of each run, Pallas kernels for 0% -> 0%
where the time goes in v1:
time: 587 us; the launch traced here: 581 us
  starting transfers between devices  147 us (25%)
  waiting for transfers between devices  145 us (25%)
  local copies, waits for them, and re-layouts  122 us (21%)
  blocking collectives  73.9 us (13%)
  matrix products  44.8 us (8%)
  other arithmetic  43.1 us (7%)
    ppermute x92, starting transfers between devices, swap(): return lax.ppermute(field, axis, [(i, i ^ mask) for i in range(count)])  147 us
    ppermute x92, waiting for transfers between devices, swap(): return lax.ppermute(field, axis, [(i, i ^ mask) for i in range(count)])  145 us
    psum x1, blocking collectives, local(): gain_grads = lax.psum(gain_parts, ('expert', 'tensor'))  41.5 us
    unnamed x238, local copies, waits for them, and re-layouts  41 us
    dot_general x12, matrix products, mul(): return lax.dot_general(left, right, dims, preferred_element_type=FULL)  38 us
    slice x17, local copies, waits for them, and re-layouts, local(): block = piece[2 * own_experts:].reshape(own_experts * hidden, part)  21.8 us
    all_gather x1, blocking collectives, local(): lax.all_gather(gain_shard, 'expert', axis=1, tiled=True).astype(FULL)  15.6 us
  transfers between devices with their start and end apart: 92, of which 42 were waited for; matrix products, arithmetic and copies ran while one was open for 25% of the time, Pallas kernels for 0%

profile of v1, /device:TPU:1, one launch (start us, length us, event | category | flops | bytes accessed | tf_op | source)
XLA Modules:
  0.0 581.2 jit_solution(11754964551788626318)
XLA Ops:
  19.0 15.6 %all_gather.9 = bf16[2,1024]{1,0:T(2,128)(2,1)S(1)} all-gather(bf16[2,128]{1,0:T(2,128)(2,1)S(1)} %pad_maximum_fusion.29), channel_id=1, replica_groups=mesh['expert'=8,'tensor'=4] {'expert'}, dimensions={1}, use_global_device_ids=true | all-gather | bytes 4608 | tf_op jit(solution)/shard_map/all_gather | solution.py:121
  75.2 7.4 %collective-permute-done.10 = bf16[256,128]{1,0:T(8,128)(2,1)S(1)} collective-permute-done((bf16[256,128]{1,0:T(8,128)(2,1)}, bf16[256,128]{1,0:T(8,128)(2,1)S(1)}, u32[]{:S(2)}, u32[]{:S(2)}) %collective-permute-start.10) | collective-permute-done | bytes 65568 | tf_op jit(solution)/shard_map/ppermute | solution.py:26
  82.9 4.8 collective-permute-done.12
  90.8 5.1 collective-permute-done.13
  96.0 9.1 %collective-permute-done.2 = bf16[128,512]{1,0:T(8,128)(2,1)S(1)} collective-permute-done((bf16[128,512]{1,0:T(8,128)(2,1)S(1)}, bf16[128,512]{1,0:T(8,128)(2,1)S(1)}, u32[]{:S(2)}, u32[]{:S(2)}) %collective-permute-start.2) | collective-permute-done | bytes 131104 | tf_op jit(solution)/shard_map/ppermute | solution.py:26
  115.8 5.5 collective-permute-start.14
  154.9 12.8 %collective-permute-done.29 = bf16[12,128,128]{1,2,0:T(8,128)(2,1)S(1)} collective-permute-done((bf16[12,128,128]{1,2,0:T(8,128)(2,1)S(1)}, bf16[12,128,128]{1,2,0:T(8,128)(2,1)S(1)}, u32[]{:S(2)}, u32[]{:S(2)}) %collective-permute-start.29) | collective-permute-done | bytes 393248 | tf_op jit(solution)/shard_map/ppermute | solution.py:26
  182.1 19.1 %collective-permute-done.31 = bf16[12,128,128]{1,2,0:T(8,128)(2,1)} collective-permute-done((bf16[12,128,128]{1,2,0:T(8,128)(2,1)}, bf16[12,128,128]{1,2,0:T(8,128)(2,1)}, u32[]{:S(2)}, u32[]{:S(2)}) %collective-permute-start.31) | collective-permute-done | bytes 393248 | tf_op jit(solution)/shard_map/ppermute | solution.py:26
  234.6 8.9 %collective-permute-start.21 = (bf16[32,1024]{1,0:T(8,128)(2,1)S(1)}, bf16[32,1024]{1,0:T(8,128)(2,1)S(1)}, u32[]{:S(2)}, u32[]{:S(2)}) collective-permute-start(bf16[32,1024]{1,0:T(8,128)(2,1)S(1)} %get-tuple-element.168), channel_id=1, source_target_pairs={{0,16},{4,20},{8,24},{12,28},{16,0},{20,4},{24,8},{28,12},{1,17},{... | collective-permute-start | bytes 196616 | tf_op jit(solution)/shard_map/ppermute | solution.py:26
  249.1 5.5 collective-permute-start.44
  261.9 10.4 %collective-permute-done.25 = bf16[256,1024]{1,0:T(8,128)(2,1)S(1)} collective-permute-done((bf16[256,1024]{1,0:T(8,128)(2,1)S(1)}, bf16[256,1024]{1,0:T(8,128)(2,1)S(1)}, u32[]{:S(2)}, u32[]{:S(2)}) %collective-permute-start.25) | collective-permute-done | bytes 524320 | tf_op jit(solution)/shard_map/ppermute | solution.py:26
  281.2 6.9 %fusion.103 = f32[2048,1024]{0,1:T(8,128)} fusion(bf16[2048,1024]{1,0:T(8,128)(2,1)S(1)} %constant_dynamic-update-slice_fusion.54, bf16[1024,1024]{1,0:T(8,128)(2,1)S(1)} %bitcast.185), kind=kOutput, calls=%fused_computation.428 | convolution fusion | flops 4294967296 | bytes 14680064 | tf_op jit(solution)/shard_map/dot_general | solution.py:21
  288.6 7.7 %multiply_convert_fusion.1 = (bf16[2048,512]{0,1:T(8,128)(2,1)}, bf16[2048,512]{0,1:T(8,128)(2,1)}, bf16[2048,512]{0,1:T(8,128)(2,1)S(1)}) fusion(f32[2048,1024]{0,1:T(8,128)} %fusion.103, f32[2048,128]{0,1:T(8,128)S(1)} %broadcast_in_dim.45, f32[2048,128]{0,1:T(8,128)S(1)} %broadcast_in_dim.44, f32[2048,128]{0,1:T(8,128)S(1)} %broadcast_in_dim.43, ...), kind=kOutput, calls=%fused_computation.11 | convolution fusion | flops 2170552320 | bytes 24117248 | tf_op jit(solution)/shard_map/dot_general | solution.py:21
  299.9 5.6 fusion.104
  310.0 7.0 %fusion.10 = f32[2048,1024]{1,0:T(8,128)} fusion(bf16[1024,1024]{1,0:T(8,128)(2,1)S(1)} %bitcast.186, bf16[2048,512]{0,1:T(8,128)(2,1)S(1)} %copy-done.82, bf16[2048,512]{0,1:T(8,128)(2,1)S(1)} %copy-done.81), kind=kOutput, calls=%fused_computation.21 | convolution fusion | flops 4303355904 | bytes 14680064 | tf_op jit(solution)/shard_map/dot_general | solution.py:21
  336.8 29.4 %collective-permute-start.87 = (bf16[12,128,128]{2,1,0:T(8,128)(2,1)S(1)}, bf16[12,128,128]{2,1,0:T(8,128)(2,1)}, u32[]{:S(2)}, u32[]{:S(2)}) collective-permute-start(bf16[12,128,128]{2,1,0:T(8,128)(2,1)S(1)} %pad_maximum_fusion.9), channel_id=1, source_target_pairs={{0,12},{4,8},{8,4},{12,0},{16,28},{20,24},{24,20},{28,16},{1,13},{... | collective-permute-start | bytes 1179656 | tf_op jit(solution)/shard_map/ppermute | solution.py:26
  366.2 7.5 %collective-permute-start.86 = (bf16[12,128,128]{2,1,0:T(8,128)(2,1)}, bf16[12,128,128]{2,1,0:T(8,128)(2,1)}, u32[]{:S(2)}, u32[]{:S(2)}) collective-permute-start(bf16[12,128,128]{2,1,0:T(8,128)(2,1)} %pad_maximum_fusion.8), channel_id=1, source_target_pairs={{0,8},{4,12},{8,0},{12,4},{16,24},{20,28},{24,16},{28,20},{1,9},{5... | collective-permute-start | bytes 1179656 | tf_op jit(solution)/shard_map/ppermute | solution.py:26
  373.7 9.4 %collective-permute-done.89 = bf16[12,128,128]{2,1,0:T(8,128)(2,1)} collective-permute-done((bf16[12,128,128]{2,1,0:T(8,128)(2,1)S(1)}, bf16[12,128,128]{2,1,0:T(8,128)(2,1)}, u32[]{:S(2)}, u32[]{:S(2)}) %collective-permute-start.89) | collective-permute-done | bytes 393248 | tf_op jit(solution)/shard_map/ppermute | solution.py:26
  416.5 5.2 collective-permute-done.46
  426.4 6.6 %collective-permute-done.57 = bf16[256,1024]{1,0:T(8,128)(2,1)S(1)} collective-permute-done((bf16[256,1024]{1,0:T(8,128)(2,1)S(1)}, bf16[256,1024]{1,0:T(8,128)(2,1)S(1)}, u32[]{:S(2)}, u32[]{:S(2)}) %collective-permute-start.57) | collective-permute-done | bytes 524320 | tf_op jit(solution)/shard_map/ppermute | solution.py:26
  471.4 6.8 %collective-permute-start.68 = (bf16[128,1024]{1,0:T(8,128)(2,1)S(1)}, bf16[128,1024]{1,0:T(8,128)(2,1)S(1)}, u32[]{:S(2)}, u32[]{:S(2)}) collective-permute-start(bf16[128,1024]{1,0:T(8,128)(2,1)S(1)} %pad_maximum_fusion.20), channel_id=1, source_target_pairs={{0,1},{1,0},{2,3},{3,2},{4,5},{5,4},{6,7},{7,6},{8,9},{9,8},{10,11... | collective-permute-start | bytes 786440 | tf_op jit(solution)/shard_map/ppermute | solution.py:26
  479.1 7.5 %all_gather.10 = bf16[256,1024]{1,0:T(8,128)(2,1)S(1)} all-gather(bf16[64,1024]{1,0:T(8,128)(2,1)S(1)} %get-tuple-element.134), channel_id=1, replica_groups=mesh['expert'=8,'tensor'=4] {'tensor'}, dimensions={0}, use_global_device_ids=true | all-gather | bytes 655360 | tf_op jit(solution)/shard_map/all_gather | solution.py:286
  527.6 41.5 %psum.7 = f32[2,1024]{1,0:T(2,128)S(1)} all-reduce(f32[2,1024]{1,0:T(2,128)S(1)} %pad_maximum_fusion.28), channel_id=1, replica_groups=mesh['expert'=8,'tensor'=4] {'expert','tensor'}, use_global_device_ids=true, to_apply=%region_14.15 | all-reduce | flops 2048 | bytes 16384 | tf_op jit(solution)/shard_map/psum | solution.py:379
  569.8 9.3 %all_gather.11 = bf16[256,1024]{1,0:T(8,128)(2,1)S(1)} all-gather(bf16[64,1024]{1,0:T(8,128)(2,1)S(1)} %fusion.24), channel_id=1, replica_groups=mesh['expert'=8,'tensor'=4] {'tensor'}, dimensions={0}, use_global_device_ids=true | all-gather | bytes 655360 | tf_op jit(solution)/shard_map/all_gather | solution.py:357
  (639 shorter events, 320.9 us)
Async XLA Ops:
  3.8 63.7 %collective-permute-start.34 = (bf16[32,1152]{1,0:T(8,128)(2,1)}, bf16[32,1152]{1,0:T(8,128)(2,1)}, u32[]{:S(2)}, u32[]{:S(2)}) collective-permute-start(bf16[32,1152]{1,0:T(8,128)(2,1)} %get-tuple-element.160), channel_id=1, source_target_pairs={{0,16},{4,20},{8,24},{12,28},{16,0},{20,4},{24,8},{28,12},{1,17},{... | collective-permute-start | bytes 221192 | tf_op jit(solution)/shard_map/ppermute | solution.py:26
  7.0 60.9 %collective-permute-start.35 = (bf16[32,1152]{1,0:T(8,128)(2,1)}, bf16[32,1152]{1,0:T(8,128)(2,1)}, u32[]{:S(2)}, u32[]{:S(2)}) collective-permute-start(bf16[32,1152]{1,0:T(8,128)(2,1)} %get-tuple-element.160), channel_id=1, source_target_pairs={{0,8},{4,12},{8,0},{12,4},{16,24},{20,28},{24,16},{28,20},{1,9},{5... | collective-permute-start | bytes 221192 | tf_op jit(solution)/shard_map/ppermute | solution.py:26
  8.3 62.9 %collective-permute-start.36 = (bf16[32,1152]{1,0:T(8,128)(2,1)}, bf16[32,1152]{1,0:T(8,128)(2,1)}, u32[]{:S(2)}, u32[]{:S(2)}) collective-permute-start(bf16[32,1152]{1,0:T(8,128)(2,1)} %get-tuple-element.160), channel_id=1, source_target_pairs={{0,24},{4,28},{8,16},{12,20},{16,8},{20,12},{24,0},{28,4},{1,25},{... | collective-permute-start | bytes 221192 | tf_op jit(solution)/shard_map/ppermute | solution.py:26
  9.8 55.7 %collective-permute-start.7 = (bf16[256,128]{1,0:T(8,128)(2,1)}, bf16[256,128]{1,0:T(8,128)(2,1)}, u32[]{:S(2)}, u32[]{:S(2)}) collective-permute-start(bf16[256,128]{1,0:T(8,128)(2,1)} %get-tuple-element.40), channel_id=1, source_target_pairs={{0,4},{4,0},{8,12},{12,8},{16,20},{20,16},{24,28},{28,24},{1,5},{5... | collective-permute-start | bytes 196616 | tf_op jit(solution)/shard_map/ppermute | solution.py:26
  11.0 55.6 %collective-permute-start.8 = (bf16[256,128]{1,0:T(8,128)(2,1)}, bf16[256,128]{1,0:T(8,128)(2,1)}, u32[]{:S(2)}, u32[]{:S(2)}) collective-permute-start(bf16[256,128]{1,0:T(8,128)(2,1)} %get-tuple-element.40), channel_id=1, source_target_pairs={{0,8},{4,12},{8,0},{12,4},{16,24},{20,28},{24,16},{28,20},{1,9},{5... | collective-permute-start | bytes 196616 | tf_op jit(solution)/shard_map/ppermute | solution.py:26
  66.6 22.6 %collective-permute-start.1 = (bf16[128,512]{1,0:T(8,128)(2,1)S(1)}, bf16[128,512]{1,0:T(8,128)(2,1)S(1)}, u32[]{:S(2)}, u32[]{:S(2)}) collective-permute-start(bf16[128,512]{1,0:T(8,128)(2,1)S(1)} %get-tuple-element.177), channel_id=1, source_target_pairs={{0,8},{4,12},{8,0},{12,4},{16,24},{20,28},{24,16},{28,20},{1,9},{5... | collective-permute-start | bytes 393224 | tf_op jit(solution)/shard_map/ppermute | solution.py:26
  67.9 22.9 %collective-permute-start.5 = (bf16[128,512]{1,0:T(8,128)(2,1)S(1)}, bf16[128,512]{1,0:T(8,128)(2,1)S(1)}, u32[]{:S(2)}, u32[]{:S(2)}) collective-permute-start(bf16[128,512]{1,0:T(8,128)(2,1)S(1)} %get-tuple-element.177), channel_id=1, source_target_pairs={{0,24},{4,28},{8,16},{12,20},{16,8},{20,12},{24,0},{28,4},{1,25},{... | collective-permute-start | bytes 393224 | tf_op jit(solution)/shard_map/ppermute | solution.py:26
  87.7 66.1 %collective-permute-start.27 = (bf16[12,128,128]{1,2,0:T(8,128)(2,1)}, bf16[12,128,128]{1,2,0:T(8,128)(2,1)S(1)}, u32[]{:S(2)}, u32[]{:S(2)}) collective-permute-start(bf16[12,128,128]{1,2,0:T(8,128)(2,1)} %get-tuple-element.61), channel_id=1, source_target_pairs={{0,4},{4,0},{8,12},{12,8},{16,20},{20,16},{24,28},{28,24},{1,5},{5... | collective-permute-start | bytes 1179656 | tf_op jit(solution)/shard_map/ppermute | solution.py:26
  89.2 36.6 %collective-permute-start.37 = (bf16[128,1152]{1,0:T(8,128)(2,1)S(1)}, bf16[128,1152]{1,0:T(8,128)(2,1)}, u32[]{:S(2)}, u32[]{:S(2)}) collective-permute-start(bf16[128,1152]{1,0:T(8,128)(2,1)S(1)} %pad_maximum_fusion.14), channel_id=1, source_target_pairs={{0,4},{4,0},{8,12},{12,8},{16,20},{20,16},{24,28},{28,24},{1,5},{5... | collective-permute-start | bytes 884744 | tf_op jit(solution)/shard_map/ppermute | solution.py:26
  148.6 24.6 %collective-permute-start.30 = (bf16[12,128,128]{1,2,0:T(8,128)(2,1)S(1)}, bf16[12,128,128]{1,2,0:T(8,128)(2,1)S(1)}, u32[]{:S(2)}, u32[]{:S(2)}) collective-permute-start(bf16[12,128,128]{1,2,0:T(8,128)(2,1)S(1)} %copy-done.50), channel_id=1, source_target_pairs={{0,16},{4,20},{8,24},{12,28},{16,0},{20,4},{24,8},{28,12},{1,17},{... | collective-permute-start | bytes 1179656 | tf_op jit(solution)/shard_map/ppermute | solution.py:26
  153.8 77.9 %collective-permute-start.20 = (bf16[256,1024]{1,0:T(8,128)(2,1)}, bf16[256,1024]{1,0:T(8,128)(2,1)}, u32[]{:S(2)}, u32[]{:S(2)}) collective-permute-start(bf16[256,1024]{1,0:T(8,128)(2,1)} %get-tuple-element.152), channel_id=1, source_target_pairs={{0,2},{1,3},{2,0},{3,1},{4,6},{5,7},{6,4},{7,5},{8,10},{9,11},{10,... | collective-permute-start | bytes 1572872 | tf_op jit(solution)/shard_map/ppermute | solution.py:26
  154.7 46.6 %collective-permute-start.31 = (bf16[12,128,128]{1,2,0:T(8,128)(2,1)}, bf16[12,128,128]{1,2,0:T(8,128)(2,1)}, u32[]{:S(2)}, u32[]{:S(2)}) collective-permute-start(bf16[12,128,128]{1,2,0:T(8,128)(2,1)} %get-tuple-element.57), channel_id=1, source_target_pairs={{0,20},{4,16},{8,28},{12,24},{16,4},{20,0},{24,12},{28,8},{1,21},{... | collective-permute-start | bytes 1179656 | tf_op jit(solution)/shard_map/ppermute | solution.py:26
  167.8 36.9 %collective-permute-start.32 = (bf16[12,128,128]{1,2,0:T(8,128)(2,1)}, bf16[12,128,128]{1,2,0:T(8,128)(2,1)}, u32[]{:S(2)}, u32[]{:S(2)}) collective-permute-start(bf16[12,128,128]{1,2,0:T(8,128)(2,1)} %get-tuple-element.56), channel_id=1, source_target_pairs={{0,24},{4,28},{8,16},{12,20},{16,8},{20,12},{24,0},{28,4},{1,25},{... | collective-permute-start | bytes 1179656 | tf_op jit(solution)/shard_map/ppermute | solution.py:26
  169.3 38.8 %collective-permute-start.33 = (bf16[12,128,128]{1,2,0:T(8,128)(2,1)}, bf16[12,128,128]{1,2,0:T(8,128)(2,1)}, u32[]{:S(2)}, u32[]{:S(2)}) collective-permute-start(bf16[12,128,128]{1,2,0:T(8,128)(2,1)} %get-tuple-element.55), channel_id=1, source_target_pairs={{0,28},{4,24},{8,20},{12,16},{16,12},{20,8},{24,4},{28,0},{1,29},{... | collective-permute-start | bytes 1179656 | tf_op jit(solution)/shard_map/ppermute | solution.py:26
  173.1 73.8 %collective-permute-start.43 = (bf16[256,1152]{1,0:T(8,128)(2,1)}, bf16[256,1152]{1,0:T(8,128)(2,1)}, u32[]{:S(2)}, u32[]{:S(2)}) collective-permute-start(bf16[256,1152]{1,0:T(8,128)(2,1)} %get-tuple-element.124), channel_id=1, source_target_pairs={{0,4},{4,0},{8,12},{12,8},{16,20},{20,16},{24,28},{28,24},{1,5},{5... | collective-permute-start | bytes 1769480 | tf_op jit(solution)/shard_map/ppermute | solution.py:26
  249.1 28.3 %collective-permute-start.44 = (bf16[1024,1152]{1,0:T(8,128)(2,1)}, bf16[1024,1152]{1,0:T(8,128)(2,1)S(1)}, u32[]{:S(2)}, u32[]{:S(2)}) collective-permute-start(bf16[1024,1152]{1,0:T(8,128)(2,1)} %get-tuple-element.104), channel_id=1, source_target_pairs={{0,1},{1,0},{2,3},{3,2},{4,5},{5,4},{6,7},{7,6},{8,9},{9,8},{10,11... | collective-permute-start | bytes 7077896 | tf_op jit(solution)/shard_map/ppermute | solution.py:26
  321.8 44.5 %collective-permute-start.90 = (bf16[12,128,128]{2,1,0:T(8,128)(2,1)}, bf16[12,128,128]{2,1,0:T(8,128)(2,1)}, u32[]{:S(2)}, u32[]{:S(2)}) collective-permute-start(bf16[12,128,128]{2,1,0:T(8,128)(2,1)} %pad_maximum_fusion.12), channel_id=1, source_target_pairs={{0,24},{4,28},{8,16},{12,20},{16,8},{20,12},{24,0},{28,4},{1,25},{... | collective-permute-start | bytes 1179656 | tf_op jit(solution)/shard_map/ppermute | solution.py:26
  324.3 58.8 %collective-permute-start.89 = (bf16[12,128,128]{2,1,0:T(8,128)(2,1)S(1)}, bf16[12,128,128]{2,1,0:T(8,128)(2,1)}, u32[]{:S(2)}, u32[]{:S(2)}) collective-permute-start(bf16[12,128,128]{2,1,0:T(8,128)(2,1)S(1)} %pad_maximum_fusion.11), channel_id=1, source_target_pairs={{0,20},{4,16},{8,28},{12,24},{16,4},{20,0},{24,12},{28,8},{1,21},{... | collective-permute-start | bytes 1179656 | tf_op jit(solution)/shard_map/ppermute | solution.py:26
  324.9 65.5 %collective-permute-start.88 = (bf16[12,128,128]{2,1,0:T(8,128)(2,1)S(1)}, bf16[12,128,128]{2,1,0:T(8,128)(2,1)}, u32[]{:S(2)}, u32[]{:S(2)}) collective-permute-start(bf16[12,128,128]{2,1,0:T(8,128)(2,1)S(1)} %pad_maximum_fusion.10), channel_id=1, source_target_pairs={{0,16},{4,20},{8,24},{12,28},{16,0},{20,4},{24,8},{28,12},{1,17},{... | collective-permute-start | bytes 1179656 | tf_op jit(solution)/shard_map/ppermute | solution.py:26
  332.2 74.6 %collective-permute-start.45 = (bf16[1024,1024]{1,0:T(8,128)(2,1)}, bf16[1024,1024]{1,0:T(8,128)(2,1)}, u32[]{:S(2)}, u32[]{:S(2)}) collective-permute-start(bf16[1024,1024]{1,0:T(8,128)(2,1)} %slice.820), channel_id=1, source_target_pairs={{0,1},{1,0},{2,3},{3,2},{4,5},{5,4},{6,7},{7,6},{8,9},{9,8},{10,11... | collective-permute-start | bytes 6291464 | tf_op jit(solution)/shard_map/ppermute | solution.py:26
  336.8 62.2 %collective-permute-start.87 = (bf16[12,128,128]{2,1,0:T(8,128)(2,1)S(1)}, bf16[12,128,128]{2,1,0:T(8,128)(2,1)}, u32[]{:S(2)}, u32[]{:S(2)}) collective-permute-start(bf16[12,128,128]{2,1,0:T(8,128)(2,1)S(1)} %pad_maximum_fusion.9), channel_id=1, source_target_pairs={{0,12},{4,8},{8,4},{12,0},{16,28},{20,24},{24,20},{28,16},{1,13},{... | collective-permute-start | bytes 1179656 | tf_op jit(solution)/shard_map/ppermute | solution.py:26
  366.2 33.9 %collective-permute-start.86 = (bf16[12,128,128]{2,1,0:T(8,128)(2,1)}, bf16[12,128,128]{2,1,0:T(8,128)(2,1)}, u32[]{:S(2)}, u32[]{:S(2)}) collective-permute-start(bf16[12,128,128]{2,1,0:T(8,128)(2,1)} %pad_maximum_fusion.8), channel_id=1, source_target_pairs={{0,8},{4,12},{8,0},{12,4},{16,24},{20,28},{24,16},{28,20},{1,9},{5... | collective-permute-start | bytes 1179656 | tf_op jit(solution)/shard_map/ppermute | solution.py:26
  390.4 22.0 %collective-permute-start.56 = (bf16[1024,1024]{1,0:T(8,128)(2,1)}, bf16[1024,1024]{1,0:T(8,128)(2,1)}, u32[]{:S(2)}, u32[]{:S(2)}) collective-permute-start(bf16[1024,1024]{1,0:T(8,128)(2,1)} %slice.819), channel_id=1, source_target_pairs={{0,1},{1,0},{2,3},{3,2},{4,5},{5,4},{6,7},{7,6},{8,9},{9,8},{10,11... | collective-permute-start | bytes 6291464 | tf_op jit(solution)/shard_map/ppermute | solution.py:26
  495.5 24.3 %collective-permute-start.69 = (bf16[128,1024]{1,0:T(8,128)(2,1)S(1)}, bf16[128,1024]{1,0:T(8,128)(2,1)S(1)}, u32[]{:S(2)}, u32[]{:S(2)}) collective-permute-start(bf16[128,1024]{1,0:T(8,128)(2,1)S(1)} %slice.821), channel_id=1, source_target_pairs={{0,1},{1,0},{2,3},{3,2},{4,5},{5,4},{6,7},{7,6},{8,9},{9,8},{10,11... | collective-permute-start | bytes 786440 | tf_op jit(solution)/shard_map/ppermute | solution.py:26
  (157 other events, 1787.3 us)

commit v2 on v1

v2 whole, which is shorter than its diff:
```python
import functools

import jax
import jax.numpy as jnp
from jax import lax
from jax.experimental import pallas as pl
from jax.experimental.pallas import tpu as pltpu
from jax.sharding import PartitionSpec as P

HEAD_SIZE = 64
EXPERTS = 32
TOP = 8
EPS = 1e-06
THETA = 10000.0
MASKED = -1e30
LANES = 128
LIMIT = 56 * 1024 * 1024

LOW = jnp.bfloat16
FULL = jnp.float32
ROWS_ON_ROWS = (((0,), (0,)), ((), ()))
COLS_ON_ROWS = (((1,), (0,)), ((), ()))
COLS_ON_COLS = (((1,), (1,)), ((), ()))


def mul(left, right, dims=COLS_ON_ROWS):
    return lax.dot_general(left, right, dims, preferred_element_type=FULL)


def shape(dims, dtype):
    return jax.ShapeDtypeStruct(dims, dtype)


def call(body, outs, *args, grid=None, in_specs=None, out_specs=None, scratch=(), flops=0):
    size = sum(a.size * a.dtype.itemsize for a in args)
    size += sum(o.size * jnp.dtype(o.dtype).itemsize for o in outs)
    whole = pl.BlockSpec(memory_space=pltpu.VMEM)
    if in_specs is None:
        in_specs = [whole] * (len(args) - 1)
    if out_specs is None:
        out_specs = [whole] * len(outs)
    extra = {} if grid is None else {"grid": grid}
    return pl.pallas_call(
        body,
        out_shape=list(outs),
        in_specs=[pl.BlockSpec(memory_space=pltpu.SMEM)] + list(in_specs),
        out_specs=list(out_specs),
        scratch_shapes=list(scratch),
        compiler_params=pltpu.CompilerParams(vmem_limit_bytes=LIMIT),
        cost_estimate=pl.CostEstimate(flops=flops, bytes_accessed=size, transcendentals=0),
        **extra,
    )(*args)


def swap(field, axis, mask):
    count = lax.axis_size(axis)
    return lax.ppermute(field, axis, [(i, i ^ mask) for i in range(count)])


def swap_by_parity(field, even, odd):
    n_e, n_t = lax.axis_size("expert"), lax.axis_size("tensor")
    pairs = []
    for e in range(n_e):
        for t in range(n_t):
            axis, mask = odd if t & 1 else even
            to = ((e ^ mask) * n_t + t) if axis == "expert" else (e * n_t + (t ^ mask))
            pairs.append((e * n_t + t, to))
    return lax.ppermute(field, ("expert", "tensor"), pairs)


def first_and_rest(count, first_bit):
    bits = [1 << b for b in range(first_bit, count.bit_length() - 1)]
    bits.reverse()
    if len(bits) < 2:
        return bits, []
    return [bits[0], bits[1], bits[0] | bits[1]], bits[2:]


def rotate(field, cosine, sine):
    lane = lax.broadcasted_iota(jnp.int32, (field.shape[0], LANES), 1)
    low_half = lane % HEAD_SIZE < HEAD_SIZE // 2
    turned = []
    for at in range(0, field.shape[1], LANES):
        block = field[:, at : at + LANES]
        ahead = pltpu.roll(block, LANES - HEAD_SIZE // 2, 1)
        behind = pltpu.roll(block, HEAD_SIZE // 2, 1)
        turned.append(block * cosine + jnp.where(low_half, ahead, behind) * sine)
    return jnp.concatenate(turned, axis=1)


def admitted(doc_row, doc_col):
    length = doc_row.shape[1]
    row = lax.broadcasted_iota(jnp.int32, (length, length), 0)
    col = lax.broadcasted_iota(jnp.int32, (length, length), 1)
    return (col <= row) & (doc_row == doc_col)


def softmax_of(query, key, allowed):
    scores = mul(query, key, COLS_ON_COLS) * HEAD_SIZE**-0.5
    scores = jnp.where(allowed, scores, MASKED)
    raised = jnp.exp(scores - jnp.max(scores, axis=1, keepdims=True))
    return raised / jnp.sum(raised, axis=1, keepdims=True)


def place_rows(target, sources, masks, me, part, pitch):
    for source, names in zip(sources, masks):
        for k, m in enumerate(names):
            at = pl.multiple_of((me ^ m) * part, part)
            target[pl.ds(at, part), :] = source[k * pitch : k * pitch + part, :]


def attend_body(masks, part, pitch, q_cols, k_cols, rows, order, where, *refs):
    n = len(masks)
    sources = refs[:n]
    tokens, gain, doc_row, doc_col, cosine, sine = refs[n : n + 6]
    weights, hidden, qkv_out, mixed_out = refs[n + 6 : n + 10]
    mixed = refs[n + 10]
    place_rows(weights, sources, masks, where[0], part, pitch)
    x = tokens[...].astype(FULL)
    scale = lax.rsqrt(jnp.mean(x * x, axis=1, keepdims=True) + EPS)
    first = (x * scale * gain[0:1, :]).astype(LOW)
    hidden[...] = first
    qkv = mul(first, weights[...])
    turned = rotate(qkv[:, : q_cols + k_cols], cosine[...], sine[...]).astype(LOW)
    values = qkv[:, q_cols + k_cols :].astype(LOW)
    qkv_out[:, : q_cols + k_cols] = turned
    qkv_out[:, q_cols + k_cols :] = values
    allowed = admitted(doc_row[...], doc_col[...])
    per_group = q_cols // k_cols
    for h in range(q_cols // HEAD_SIZE):
        at, g = h * HEAD_SIZE, h // per_group * HEAD_SIZE
        shares = softmax_of(
            turned[:, at : at + HEAD_SIZE],
            turned[:, q_cols + g : q_cols + g + HEAD_SIZE],
            allowed,
        ).astype(LOW)
        mixed[:, at : at + HEAD_SIZE] = mul(shares, values[:, g : g + HEAD_SIZE]).astype(LOW)
    for k, m in enumerate(order):
        at = pl.multiple_of((where[1] ^ m) * rows, rows)
        mixed_out[k * rows : (k + 1) * rows, :] = mixed[pl.ds(at, rows), :]


def branch_body(masks, part, where, *refs):
    n = len(masks)
    sources = refs[:n]
    mixed, weights, kept, sent = refs[n:]
    place_rows(weights, sources, masks, where[0], part, part)
    half = kept.shape[0]
    product = mul(mixed[...], weights[...], COLS_ON_COLS)
    kept[...] = product[:half]
    sent[...] = product[half:].astype(LOW)


def middle_body(rows, where, tokens, kept, got, gain, middle, hidden):
    at = pl.multiple_of(where[1] * rows, rows)
    m = tokens[pl.ds(at, rows), :].astype(FULL) + (kept[...] + got[...].astype(FULL))
    middle[...] = m
    scale = lax.rsqrt(jnp.mean(m * m, axis=1, keepdims=True) + EPS)
    hidden[...] = (m * scale * gain[1:2, :]).astype(LOW)


def owner_body(n_piece, n_e, part, own, hid, replicas, where, *refs):
    pieces = refs[:n_e]
    grads = refs[n_e : n_e + n_piece]
    weights, gate_out, back_out, buffer = refs[n_e + n_piece :]
    width = n_e * part
    step = pl.program_id(0)

    @pl.when(step == 0)
    def _():
        place_rows(weights, pieces, [[m] for m in range(n_e)], where[0], part, part)

    for k in range(n_piece):

        @pl.when(step == k)
        def _():
            buffer[...] = grads[k][...]

    extra = buffer[:, width:].astype(FULL)
    lane = lax.broadcasted_iota(jnp.int32, extra.shape, 1)
    gate = pltpu.roll(extra, LANES - TOP, 1) + pltpu.roll(extra, LANES - 2 * TOP, 1)
    first = where[0] // replicas * own
    back = mul(buffer[:, :width], weights[:, 2 * own * hid :])
    table = jnp.zeros(extra.shape, FULL)
    for j in range(own):
        hit = (lane < TOP) & (extra == (first + j).astype(FULL))
        column = jnp.sum(jnp.where(hit, gate, 0.0), axis=1, keepdims=True)
        table = jnp.where(lane == j, column, table)
        back_out[:, j * hid : (j + 1) * hid] = back[:, j * hid : (j + 1) * hid] * column
    gate_out[...] = table


def expert_body(n_piece, own, hid, where, *refs):
    rows = refs[:n_piece]
    weights, gate, back, grad_hidden, active_out, grad_both, buffer = refs[n_piece:]
    step = pl.program_id(0)
    for k in range(n_piece):

        @pl.when(step == k)
        def _():
            buffer[...] = rows[k][...]

    wide = own * hid
    both = mul(buffer[...], weights[:, : 2 * wide])
    for j in range(own):
        at = slice(j * hid, (j + 1) * hid)
        up_at = slice(wide + j * hid, wide + (j + 1) * hid)
        pre, up = both[:, at], both[:, up_at]
        squash = 1.0 / (1.0 + jnp.exp(-pre))
        silu = pre * squash
        active = (silu * up).astype(LOW).astype(FULL)
        active_out[:, at] = (active * gate[:, j : j + 1]).astype(LOW)
        d = back[:, at]
        grad_both[:, at] = (d * up * squash * (1.0 + pre * (1.0 - squash))).astype(LOW)
        grad_both[:, up_at] = (d * silu).astype(LOW)
    product = mul(grad_both[...], weights[:, : 2 * wide], COLS_ON_COLS)
    grad_hidden[...] = product.astype(grad_hidden.dtype)


def out_body(where, active, weights, out):
    out[...] = mul(active[...], weights[...], COLS_ON_COLS).astype(out.dtype)


def weight_grad_body(n_piece, where, *refs):
    hidden = refs[:n_piece]
    grads = refs[n_piece : 2 * n_piece]
    both = refs[2 * n_piece : 2 * n_piece + 2]
    active = refs[2 * n_piece + 2 : 2 * n_piece + 4]
    out, column = refs[2 * n_piece + 4 :]
    size = hidden[0].shape[0]
    half = n_piece // 2 * size
    wide = both[0].shape[1]
    for sources, right, cols in ((hidden, both, slice(0, wide)), (grads, active, slice(wide, None))):
        for k in range(n_piece):
            column[k * size : (k + 1) * size, :] = sources[k][...]
        total = mul(column[:half], right[0][...], ROWS_ON_ROWS)
        total = total + mul(column[half:], right[1][...], ROWS_ON_ROWS)
        out[:, cols] = total.astype(LOW)


def middle_back_body(n_got, where, *refs):
    kept, got = refs[0], refs[1 : 1 + n_got]
    middle, grad, gain, grad_middle, low, gain_part = refs[1 + n_got :]
    total = kept[...]
    for piece in got:
        total = total + piece[...].astype(FULL)
    m = middle[...]
    scale = lax.rsqrt(jnp.mean(m * m, axis=1, keepdims=True) + EPS)
    gain_part[...] = jnp.broadcast_to(
        jnp.sum(total * m * scale, axis=0, keepdims=True), gain_part.shape
    )
    weighted = total * gain[1:2, :]
    inner = jnp.mean(weighted * m, axis=1, keepdims=True)
    back = grad[...].astype(FULL) + (scale * weighted - m * (scale * scale * scale) * inner)
    grad_middle[...] = back
    low[...] = back.astype(LOW)


def attend_back_body(n_piece, q_cols, k_cols, rows, part, order, even, odd, where, *refs):
    pieces = refs[:n_piece]
    mixed, out_weights, qkv_in, doc_row, doc_col, cosine, sine, hidden, weights = refs[
        n_piece : n_piece + 9
    ]
    kept, sent, first_kept, first_sent, branch, natural, grad_qkv, grads = refs[n_piece + 9 :]
    for k in range(n_piece):
        branch[k * rows : (k + 1) * rows, :] = pieces[k][...]
    grad_mixed = mul(branch[...], out_weights[...]).astype(LOW)
    for k, m in enumerate(order):
        at = pl.multiple_of((where[1] ^ m) * rows, rows)
        natural[pl.ds(at, rows), :q_cols] = grad_mixed[k * rows : (k + 1) * rows]
    qk = q_cols + k_cols
    total = qk + k_cols
    grads[:, total:] = mul(branch[...], mixed[...], ROWS_ON_ROWS)
    allowed = admitted(doc_row[...], doc_col[...])
    per_group = q_cols // k_cols
    query_grads, key_grads, value_grads = [], [], []
    for g in range(k_cols // HEAD_SIZE):
        key = qkv_in[:, q_cols + g * HEAD_SIZE : q_cols + (g + 1) * HEAD_SIZE]
        value = qkv_in[:, qk + g * HEAD_SIZE : qk + (g + 1) * HEAD_SIZE]
        key_grad = value_grad = None
        for h in range(g * per_group, (g + 1) * per_group):
            at = slice(h * HEAD_SIZE, (h + 1) * HEAD_SIZE)
            query = qkv_in[:, at]
            shares = softmax_of(query, key, allowed)
            grad = natural[:, at]
            grad_shares = mul(grad, value, COLS_ON_COLS)
            inner = jnp.sum(shares * grad_shares, axis=1, keepdims=True)
            grad_scores = (shares * (grad_shares - inner)).astype(LOW)
            query_grads.append(mul(grad_scores, key))
            dk = mul(grad_scores, query, ROWS_ON_ROWS)
            dv = mul(shares.astype(LOW), grad, ROWS_ON_ROWS)
            key_grad = dk if key_grad is None else key_grad + dk
            value_grad = dv if value_grad is None else value_grad + dv
        key_grads.append(key_grad)
        value_grads.append(value_grad)
    turned = jnp.concatenate(query_grads + key_grads, axis=1) * HEAD_SIZE**-0.5
    grad_qkv[:, :qk] = rotate(turned, cosine[...], -sine[...]).astype(LOW)
    grad_qkv[:, qk:] = jnp.concatenate(value_grads, axis=1).astype(LOW)
    grads[:, :total] = mul(hidden[...], grad_qkv[...], ROWS_ON_ROWS)
    for names, target in ((even, kept), (odd, sent)):
        for k, m in enumerate(names):
            at = pl.multiple_of((where[0] ^ m) * part, part)
            target[k * part : (k + 1) * part, :] = grads[pl.ds(at, part), :].astype(target.dtype)
    for k, m in enumerate(order):
        at = pl.multiple_of((where[1] ^ m) * rows, rows)
        natural[k * rows : (k + 1) * rows, :total] = grad_qkv[pl.ds(at, rows), :]
    product = mul(natural[:, :total], weights[...], COLS_ON_COLS)
    half = first_kept.shape[0]
    first_kept[...] = product[:half]
    first_sent[...] = product[half:].astype(LOW)


def tokens_back_body(rows, where, tokens, kept, got, gain, grad_middle, moe_part, out):
    at = pl.multiple_of(where[1] * rows, rows)
    x = tokens[pl.ds(at, rows), :].astype(FULL)
    scale = lax.rsqrt(jnp.mean(x * x, axis=1, keepdims=True) + EPS)
    first = kept[...] + got[...].astype(FULL)
    attn_part = jnp.sum(first * x * scale, axis=0, keepdims=True)
    weighted = first * gain[0:1, :]
    inner = jnp.mean(weighted * x, axis=1, keepdims=True)
    out[:rows] = grad_middle[...] + (scale * weighted - x * (scale * scale * scale) * inner)
    line = lax.broadcasted_iota(jnp.int32, moe_part.shape, 0)
    out[rows:] = jnp.where(line == 0, attn_part, jnp.where(line == 1, moe_part[...], 0.0))


def unpack_body(n_e, own, hid, replicas, turn, where, *refs):
    pieces = refs[:n_e]
    outs = refs[n_e:]
    step = pl.program_id(0)
    for root in range(n_e // replicas):

        @pl.when(step == root)
        def _():
            total = pieces[root * replicas][...].astype(FULL)
            for r in range(1, replicas):
                total = total + pieces[root * replicas + r][...].astype(FULL)
            for i, out in enumerate(outs):
                for j in range(own):
                    at = (i * own + j) * hid
                    block = total[:, at : at + hid]
                    out[j] = block.T if turn and i == 2 else block


def local(
    tokens,
    cotangent,
    segments,
    routes,
    gates,
    w_query,
    key_projection,
    value_projection,
    w_out,
    gain_attn,
    gain_moe,
    w_gate,
    w_up,
    w_down,
):
    n_e, n_t = lax.axis_size("expert"), lax.axis_size("tensor")
    e, t = lax.axis_index("expert"), lax.axis_index("tensor")
    where = jnp.stack([e, t]).astype(jnp.int32)
    replicas = max(1, n_e // EXPERTS)
    own_experts = EXPERTS * replicas // n_e
    first_bit = replicas.bit_length() - 1
    length, width = tokens.shape
    part = width // n_e
    rows = length // n_t
    q_cols, k_cols = w_query.shape[1], key_projection.shape[1]
    qkv_cols = q_cols + 2 * k_cols
    hidden = w_gate.shape[2]
    wide = own_experts * hidden

    pad = 16
    gain_rows = jnp.stack([gain_attn, gain_moe])
    gain_rows = jnp.pad(gain_rows, ((0, pad - 2), (0, qkv_cols - part)))
    qkv_shard = jnp.concatenate(
        [
            jnp.concatenate([w_query, key_projection, value_projection], axis=1),
            gain_rows,
        ],
        axis=0,
    ).astype(LOW)
    out_shard = w_out.T.astype(LOW)

    masks_first, bits_rest = first_and_rest(n_e, 0)

    def every(shard):
        arrays = [jnp.concatenate([shard] + [swap(shard, "expert", m) for m in masks_first])]
        names = [[0] + masks_first]
        for b in bits_rest:
            arrays = arrays + [swap(a, "expert", b) for a in arrays]
            names = names + [[m ^ b for m in line] for line in names]
        return arrays, names

    qkv_arrays, names = every(qkv_shard)
    out_arrays, _ = every(out_shard)
    pitch = part + pad
    held = {}
    for array, line in zip(qkv_arrays, names):
        for k, m in enumerate(line):
            held[m] = array[k * pitch + part : k * pitch + part + 2, :part]
    gains = jnp.stack([held[m] for m in range(n_e)]).astype(FULL)
    gains = jnp.concatenate(
        [lax.dynamic_index_in_dim(gains, e ^ k, 0, keepdims=False) for k in range(n_e)], axis=1
    )

    def blocks(w):
        w = w.reshape(EXPERTS // own_experts, own_experts, part, hidden)
        return w.transpose(0, 2, 1, 3).reshape(EXPERTS // own_experts, part, wide)

    packed = jnp.concatenate(
        [blocks(w.astype(LOW)) for w in (w_gate, w_up, w_down.transpose(0, 2, 1))], axis=2
    )

    def to_owner(m):
        return lax.dynamic_index_in_dim(packed, (e ^ m) // replicas, 0, keepdims=False)

    arrived = [to_owner(0)] + [swap(to_owner(m), "expert", m) for m in range(1, n_e)]

    masks_tok, bits_tok = first_and_rest(n_e, first_bit)
    e_rest = [("expert", b) for b in bits_tok]
    t_bits = [("tensor", 1 << b) for b in reversed(range(n_t.bit_length() - 1))]
    even_path, odd_path = e_rest + t_bits[:-1], t_bits[:-1] + e_rest
    last = t_bits[-1]

    def gather_tokens(block):
        pieces = [jnp.concatenate([block] + [swap(block, "expert", m) for m in masks_tok])]
        for even, odd in zip(even_path, odd_path):
            pieces = pieces + [swap_by_parity(p, even, odd) for p in pieces]
        return pieces + [swap(p, *last) for p in pieces]

    def scatter_tokens(kept, sent):
        pieces = [a + swap(s, *last).astype(FULL) for a, s in zip(kept, sent)]
        for even, odd in zip(reversed(even_path), reversed(odd_path)):
            half = len(pieces) // 2
            pieces = [
                a + swap_by_parity(b.astype(LOW), even, odd).astype(FULL)
                for a, b in zip(pieces[:half], pieces[half:])
            ]
        (piece,) = pieces
        size = piece.shape[0] // (len(masks_tok) + 1)
        got = [
            swap(piece[(i + 1) * size : (i + 2) * size].astype(LOW), "expert", m)
            for i, m in enumerate(masks_tok)
        ]
        return piece[:size], got

    own = t * rows
    grad_rows = lax.dynamic_slice_in_dim(cotangent, own, rows, 0)
    gate_rows = lax.dynamic_slice_in_dim(gates, own, rows, 0)
    route_rows = lax.dynamic_slice_in_dim(routes, own, rows, 0)
    gate_high = gate_rows.astype(LOW)
    gate_rest = (gate_rows - gate_high.astype(FULL)).astype(LOW)
    extra = jnp.concatenate([route_rows.astype(LOW), gate_high, gate_rest], axis=1)
    extra = jnp.pad(extra, ((0, 0), (0, LANES - 3 * TOP)))
    grad_pieces = gather_tokens(jnp.concatenate([grad_rows, extra], axis=1))

    documents = segments[0]
    doc_row, doc_col = documents[None, :], documents[:, None]
    index = jnp.arange(length)
    same = (index[None, :] < index[:, None]) & (doc_row == doc_col)
    position = jnp.sum(same.astype(FULL), axis=1, keepdims=True)
    lane = jnp.arange(LANES)
    freqs = THETA ** (-2.0 * (lane % (HEAD_SIZE // 2)).astype(FULL) / HEAD_SIZE)
    angle = position * freqs[None, :]
    cosine = jnp.cos(angle)
    sine = jnp.sin(angle) * jnp.where(lane % HEAD_SIZE < HEAD_SIZE // 2, -1.0, 1.0)[None, :]
    t_masks = [b for _, b in reversed(t_bits)]
    order = [0]
    for b in reversed(t_masks):
        order = order + [k ^ b for k in order]
    weights, first_hidden, qkv, mixed = call(
        functools.partial(attend_body, names, part, pitch, q_cols, k_cols, rows, order),
        [
            shape((width, qkv_cols), LOW),
            shape((length, width), LOW),
            shape((length, qkv_cols), LOW),
            shape((length, q_cols), LOW),
        ],
        where, *qkv_arrays, tokens, gains, doc_row, doc_col, cosine, sine,
        scratch=[pltpu.VMEM((length, q_cols), LOW)],
        flops=2 * length * (width * qkv_cols + 2 * length * q_cols),
    )
    out_weights, kept, sent = call(
        functools.partial(branch_body, names, part),
        [
            shape((width, q_cols), LOW),
            shape((length // 2, width), FULL),
            shape((length // 2, width), LOW),
        ],
        where, *out_arrays, mixed,
        flops=2 * length * width * q_cols,
    )

    def scatter_rows(kept, sent):
        for b in t_masks[:-1]:
            total = kept + swap(sent, "tensor", b).astype(FULL)
            half = total.shape[0] // 2
            kept, sent = total[:half], total[half:].astype(LOW)
        return kept, swap(sent, "tensor", t_masks[-1])

    kept, got = scatter_rows(kept, sent)
    middle, second_hidden = call(
        functools.partial(middle_body, rows),
        [shape((rows, width), FULL), shape((rows, width), LOW)],
        where, tokens, kept, got, gains,
    )

    n_piece = len(grad_pieces)
    size = grad_pieces[0].shape[0]
    total_rows = n_piece * size
    whole = lambda a: pl.BlockSpec(a.shape, lambda i: (0,) * a.ndim)
    tile = lambda cols: pl.BlockSpec((size, cols), lambda i: (i, 0))
    expert_weights, gate_table, back = call(
        functools.partial(owner_body, n_piece, n_e, part, own_experts, hidden, replicas),
        [
            shape((width, 3 * wide), LOW),
            shape((total_rows, LANES), FULL),
            shape((total_rows, wide), FULL),
        ],
        where, *arrived, *grad_pieces,
        grid=(n_piece,),
        in_specs=[whole(a) for a in arrived] + [whole(a) for a in grad_pieces],
        out_specs=[
            pl.BlockSpec((width, 3 * wide), lambda i: (0, 0)),
            tile(LANES),
            tile(wide),
        ],
        scratch=[pltpu.VMEM((size, width + LANES), LOW)],
        flops=2 * total_rows * width * wide,
    )
    hidden_pieces = gather_tokens(second_hidden)
    half = n_piece // 2

    def experts(first, out_type):
        chosen = hidden_pieces[first : first + half]
        later = lambda cols: pl.BlockSpec((size, cols), lambda i: (i + first, 0))
        return call(
            functools.partial(expert_body, half, own_experts, hidden),
            [
                shape((half * size, width), out_type),
                shape((half * size, wide), LOW),
                shape((half * size, 2 * wide), LOW),
            ],
            where, *chosen, expert_weights, gate_table, back,
            grid=(half,),
            in_specs=[whole(a) for a in chosen]
            + [whole(expert_weights), later(LANES), later(wide)],
            out_specs=[tile(width), tile(wide), tile(2 * wide)],
            scratch=[pltpu.VMEM((size, width), LOW)],
            flops=2 * half * size * width * 4 * wide,
        )

    def pieces_of(field):
        return [field[k * size : (k + 1) * size] for k in range(half)]

    sent_hidden, sent_active, sent_both = experts(half, LOW)
    kept_hidden, kept_active, kept_both = experts(0, FULL)
    grad_kept, grad_got = scatter_tokens(pieces_of(kept_hidden), pieces_of(sent_hidden))

    def down(active, out_type):
        return call(
            out_body,
            [shape((half * size, width), out_type)],
            where, active, expert_weights,
            grid=(half,),
            in_specs=[tile(wide), pl.BlockSpec((width, wide), lambda i: (0, 2))],
            out_specs=[tile(width)],
            flops=2 * half * size * width * wide,
        )[0]

    sent_out, kept_out = down(sent_active, LOW), down(kept_active, FULL)
    out_kept, out_got = scatter_tokens(pieces_of(kept_out), pieces_of(sent_out))
    expert_out = out_kept
    for piece in out_got:
        expert_out = expert_out + piece.astype(FULL)
    output_rows = (middle + expert_out).astype(LOW)
    output = lax.all_gather(output_rows, "tensor", axis=0, tiled=True)

    block = 256
    column = pl.BlockSpec((size, block), lambda i: (0, i))
    (weight_grads,) = call(
        functools.partial(weight_grad_body, n_piece),
        [shape((width, 3 * wide), LOW)],
        where, *hidden_pieces, *grad_pieces, kept_both, sent_both, kept_active, sent_active,
        grid=(width // block,),
        in_specs=[column] * (2 * n_piece)
        + [whole(kept_both), whole(sent_both), whole(kept_active), whole(sent_active)],
        out_specs=[pl.BlockSpec((block, 3 * wide), lambda i: (i, 0))],
        scratch=[pltpu.VMEM((total_rows, block), LOW)],
        flops=2 * total_rows * width * 3 * wide,
    )

    def to_holder(m):
        return lax.dynamic_slice_in_dim(weight_grads, (e ^ m) * part, part, 0)

    returned = [to_holder(0)] + [swap(to_holder(m), "expert", m) for m in range(1, n_e)]
    turn = part % LANES == 0
    at_root = lambda dims: pl.BlockSpec(
        (own_experts,) + dims, lambda i, where: ((where[0] // replicas) ^ i, 0, 0)
    )
    out_dims = [(part, hidden), (part, hidden), (hidden, part) if turn else (part, hidden)]
    shards = pl.pallas_call(
        functools.partial(unpack_body, n_e, own_experts, hidden, replicas, turn),
        out_shape=[shape((EXPERTS,) + d, FULL) for d in out_dims],
        grid_spec=pltpu.PrefetchScalarGridSpec(
            num_scalar_prefetch=1,
            grid=(n_e // replicas,),
            in_specs=[pl.BlockSpec(a.shape, lambda i, where: (0, 0)) for a in returned],
            out_specs=[at_root(d) for d in out_dims],
        ),
        compiler_params=pltpu.CompilerParams(vmem_limit_bytes=LIMIT),
        cost_estimate=pl.CostEstimate(
            flops=0, bytes_accessed=6 * EXPERTS * part * hidden * 3, transcendentals=0
        ),
    )(where, *returned)
    gate_shard, up_shard, down_shard = shards
    if not turn:
        down_shard = down_shard.transpose(0, 2, 1)

    grad_middle, branch_grad, moe_part = call(
        functools.partial(middle_back_body, len(grad_got)),
        [shape((rows, width), FULL), shape((rows, width), LOW), shape((16, width), FULL)],
        where, grad_kept, *grad_got, middle, grad_rows, gains,
    )
    branch_pieces = [branch_grad]
    for b in reversed(t_masks):
        branch_pieces = branch_pieces + [swap(p, "tensor", b) for p in branch_pieces]
    low_bit = bits_rest[-1:] or [0]
    odd = [m for m in range(n_e) if low_bit[0] and m & low_bit[0]]
    even = [m for m in range(n_e) if m not in odd]
    all_cols = qkv_cols + q_cols
    kept_w, sent_w, first_kept, first_sent = call(
        functools.partial(
            attend_back_body, len(branch_pieces), q_cols, k_cols, rows, part, order, even,
            [m ^ low_bit[0] for m in even],
        ),
        [
            shape((len(even) * part, all_cols), FULL),
            shape((len(even) * part, all_cols), LOW),
            shape((length // 2, width), FULL),
            shape((length // 2, width), LOW),
        ],
        where, *branch_pieces, mixed, out_weights, qkv, doc_row, doc_col, cosine, sine,
        first_hidden, weights,
        scratch=[
            pltpu.VMEM((length, width), LOW),
            pltpu.VMEM((length, max(q_cols, qkv_cols)), LOW),
            pltpu.VMEM((length, qkv_cols), LOW),
            pltpu.VMEM((width, all_cols), FULL),
        ],
        flops=2 * length * width * (2 * q_cols + 2 * qkv_cols),
    )
    total = kept_w + swap(sent_w, "expert", low_bit[0]).astype(FULL)
    names_left = even
    for b in reversed(bits_rest[:-1]):
        keep = [k for k, m in enumerate(names_left) if not m & b]
        give = [names_left.index(names_left[k] ^ b) for k in keep]
        pick = lambda ks: jnp.concatenate([total[k * part : (k + 1) * part] for k in ks])
        total = pick(keep) + swap(pick(give).astype(LOW), "expert", b).astype(FULL)
        names_left = [names_left[k] for k in keep]
    attn_grad = total[:part]
    for m in masks_first:
        k = names_left.index(m)
        attn_grad = attn_grad + swap(
            total[k * part : (k + 1) * part].astype(LOW), "expert", m
        ).astype(FULL)

    kept, got = scatter_rows(first_kept, first_sent)
    (token_rows,) = call(
        functools.partial(tokens_back_body, rows),
        [shape((rows + 16, width), FULL)],
        where, tokens, kept, got, gains, grad_middle, moe_part,
    )
    gathered = lax.all_gather(token_rows.astype(LOW), "tensor", axis=0, tiled=True)
    gathered = gathered.reshape(n_t, rows + 16, width).astype(FULL)
    grad_input = gathered[:, :rows].reshape(length, width)
    gain_sum = jnp.sum(gathered[:, rows : rows + 2], axis=0)

    def gain_block(m):
        return lax.dynamic_slice_in_dim(gain_sum, (e ^ m) * part, part, 1)

    held = {m: gain_block(m) for m in range(n_e)}
    for b in reversed(bits_rest):
        keep = [m for m in held if not m & b]
        sent = jnp.concatenate([held[m ^ b] for m in keep], axis=0)
        got = swap(sent, "expert", b)
        held = {m: held[m] + got[2 * k : 2 * k + 2] for k, m in enumerate(keep)}
    gain_grads = held[0]
    for m in masks_first:
        gain_grads = gain_grads + swap(held[m], "expert", m)
    return (
        output,
        grad_input,
        attn_grad[:, :q_cols],
        attn_grad[:, q_cols : q_cols + k_cols],
        attn_grad[:, q_cols + k_cols : qkv_cols],
        attn_grad[:, qkv_cols:].T,
        gain_grads[0],
        gain_grads[1],
        gate_shard,
        up_shard,
        down_shard,
    )


def solution(mesh):
    by_rows = P("expert", None)
    by_both = P("expert", "tensor")
    in_experts = P(None, "expert", "tensor")
    down_specs = P(None, "tensor", "expert")
    return jax.shard_map(
        local,
        mesh=mesh,
        in_specs=(by_rows,) * 5
        + (by_both,) * 3
        + (P("tensor", "expert"), P("expert"), P("expert"), in_experts, in_experts, down_specs),
        out_specs=(by_rows, by_rows)
        + (by_both,) * 3
        + (P("tensor", "expert"), P("expert"), P("expert"), in_experts, in_experts, down_specs),
        check_vma=False,
    )
```

time: 587 us -> 426 us (0.73)
  local copies, waits for them, and re-layouts: 122 us -> 30.5 us
  Pallas kernels: 0 us -> 79.1 us
  blocking collectives: 73.9 us -> 17.8 us
  matrix products: 44.8 us -> 0 us
  starting transfers between devices: 147 us -> 128 us
  other arithmetic: 43.1 us -> 24.2 us
    pallas_call x0 -> x13, Pallas kernels: none -> 79.1 us  [the longest x12 72.3 us: call(): pl.pallas_call(body, out_shape=list(outs), in_specs=[pl.BlockSpec(memory_...]
    dot_general x17 -> x0, matrix products: 43.3 us -> none  [the longest x12 38 us: mul(): return lax.dot_general(left, right, dims, preferred_element_type=FULL)]
    psum x1 -> x0, blocking collectives: 41.5 us -> none  [local(): gain_grads = lax.psum(gain_parts, ('expert', 'tensor'))]
    slice x54 -> x12, local copies, waits for them, and re-layouts: 41.9 us -> 9.35 us  [the longest x2 5.33 us: pieces_of(): return [field[k * size:(k + 1) * size] for k in range(half)]]
    unnamed x238 -> x121, local copies, waits for them, and re-layouts: 41 us -> 11.3 us
    ppermute x92 -> x65, starting transfers between devices: 147 us -> 118 us  [swap(): return lax.ppermute(field, axis, [(i, i ^ mask) for i in range(count)])]
    ppermute x92 -> x65, waiting for transfers between devices: 145 us -> 122 us  [swap(): return lax.ppermute(field, axis, [(i, i ^ mask) for i in range(count)])]
    ppermute x0 -> x12, waiting for transfers between devices: none -> 19 us  [swap_by_parity(): return lax.ppermute(field, ('expert', 'tensor'), pairs)]
  transfers between devices with their start and end apart: 92 -> 77, of which waited for: 42 -> 19; matrix products, arithmetic and copies ran while one was open for 25% -> 10% of each run, Pallas kernels for 0% -> 16%
where the time goes in v2:
time: 426 us; the launch traced here: 422 us
  waiting for transfers between devices  141 us (33%)
  starting transfers between devices  128 us (30%)
  Pallas kernels  79.1 us (19%)
  local copies, waits for them, and re-layouts  30.5 us (7%)
  other arithmetic  24.2 us (6%)
  blocking collectives  17.8 us (4%)
    ppermute x65, waiting for transfers between devices, swap(): return lax.ppermute(field, axis, [(i, i ^ mask) for i in range(count)])  122 us
    ppermute x65, starting transfers between devices, swap(): return lax.ppermute(field, axis, [(i, i ^ mask) for i in range(count)])  118 us
    pallas_call x12, Pallas kernels, call(): pl.pallas_call(body, out_shape=list(outs), in_specs=[pl.BlockSpec(memory_...  72.3 us
    ppermute x12, waiting for transfers between devices, swap_by_parity(): return lax.ppermute(field, ('expert', 'tensor'), pairs)  19 us
    unnamed x121, local copies, waits for them, and re-layouts  11.3 us
    ppermute x12, starting transfers between devices, swap_by_parity(): return lax.ppermute(field, ('expert', 'tensor'), pairs)  9.45 us
    all_gather x1, blocking collectives, local(): output = lax.all_gather(output_rows, 'tensor', axis=0, tiled=True)  9.32 us
  transfers between devices with their start and end apart: 77, of which 19 were waited for; matrix products, arithmetic and copies ran while one was open for 10% of the time, Pallas kernels for 16%

profile of v2, /device:TPU:1, one launch (start us, length us, event | category | flops | bytes accessed | tf_op | source)
XLA Modules:
  0.0 422.3 jit_solution(3529370979635213338)
XLA Ops:
  31.3 8.3 %collective-permute-start.24 = (bf16[64,1152]{1,0:T(8,128)(2,1)}, bf16[64,1152]{1,0:T(8,128)(2,1)S(1)}, u32[]{:S(2)}, u32[]{:S(2)}) collective-permute-start(bf16[64,1152]{1,0:T(8,128)(2,1)} %pad_maximum_fusion.4), channel_id=1, source_target_pairs={{0,8},{4,12},{8,0},{12,4},{16,24},{20,28},{24,16},{28,20},{1,9},{5... | collective-permute-start | bytes 442376 | tf_op jit(solution)/shard_map/ppermute | solution.py:57
  74.1 14.2 %collective-permute-done.17.refs_2_ = bf16[128,1536]{1,0:T(8,128)(2,1)S(1)} collective-permute-done((bf16[128,1536]{1,0:T(8,128)(2,1)S(1)}, bf16[128,1536]{1,0:T(8,128)(2,1)S(1)}, u32[]{:S(2)}, u32[]{:S(2)}) %collective-permute-start.17) | collective-permute-done | bytes 393248 | tf_op jit(solution)/shard_map/ppermute | solution.py:57
  88.4 7.2 %collective-permute-done.18.refs_3_ = bf16[128,1536]{1,0:T(8,128)(2,1)S(1)} collective-permute-done((bf16[128,1536]{1,0:T(8,128)(2,1)S(1)}, bf16[128,1536]{1,0:T(8,128)(2,1)S(1)}, u32[]{:S(2)}, u32[]{:S(2)}) %collective-permute-start.18) | collective-permute-done | bytes 393248 | tf_op jit(solution)/shard_map/ppermute | solution.py:57
  102.5 13.5 %collective-permute-done.12 = bf16[64,1024]{1,0:T(8,128)(2,1)S(1)} collective-permute-done((bf16[64,1024]{1,0:T(8,128)(2,1)}, bf16[64,1024]{1,0:T(8,128)(2,1)S(1)}, u32[]{:S(2)}, u32[]{:S(2)}) %collective-permute-start.12) | collective-permute-done | bytes 131104 | tf_op jit(solution)/shard_map/ppermute | solution.py:57
  123.0 7.0 %collective-permute-done.22.refs_7_ = bf16[128,1536]{1,0:T(8,128)(2,1)S(1)} collective-permute-done((bf16[128,1536]{1,0:T(8,128)(2,1)S(1)}, bf16[128,1536]{1,0:T(8,128)(2,1)S(1)}, u32[]{:S(2)}, u32[]{:S(2)}) %collective-permute-start.22) | collective-permute-done | bytes 393248 | tf_op jit(solution)/shard_map/ppermute | solution.py:57
  135.3 9.1 %collective-permute-done.28.refs_11_ = bf16[256,1152]{1,0:T(8,128)(2,1)S(1)} collective-permute-done((bf16[256,1152]{1,0:T(8,128)(2,1)S(1)}, bf16[256,1152]{1,0:T(8,128)(2,1)S(1)}, u32[]{:S(2)}, u32[]{:S(2)}) %collective-permute-start.28) | collective-permute-done | bytes 589856 | tf_op jit(solution)/shard_map/ppermute | solution.py:68
  150.4 5.3 %collective-permute-done.15.refs_3_ = bf16[256,1024]{1,0:T(8,128)(2,1)} collective-permute-done((bf16[256,1024]{1,0:T(8,128)(2,1)S(1)}, bf16[256,1024]{1,0:T(8,128)(2,1)}, u32[]{:S(2)}, u32[]{:S(2)}) %collective-permute-start.15) | collective-permute-done | bytes 524320 | tf_op jit(solution)/shard_map/ppermute | solution.py:68
  155.9 10.1 %shard_map.224 = (bf16[1024,1536]{1,0:T(8,128)(2,1)}, f32[2048,128]{1,0:T(8,128)}, f32[2048,512]{1,0:T(8,128)}) custom-call(s32[2]{0:T(128)} %pad_add_fusion.where, bf16[128,1536]{1,0:T(8,128)(2,1)} %get-tuple-element.140.refs_0_, bf16[128,1536]{1,0:T(8,128)(2,1)} %copy-done.43, bf16[128,1536]{1,0:T(8,128)(2,1)} %copy-done.44, bf16[128,1536]{1,0:T(8,128)(2,1)} %copy-done.45, ...), custom_call_target="tpu_custom_call" | custom-call | flops 2147483648 | bytes 16252936 | tf_op jit(solution)/shard_map/pallas_call | solution.py:43
  166.1 10.0 %shard_map.227 = (bf16[1024,1024]{1,0:T(8,128)(2,1)}, bf16[1024,512]{1,0:T(8,128)(2,1)}, bf16[1024,1024]{1,0:T(8,128)(2,1)}) custom-call(s32[2]{0:T(128)} %pad_add_fusion.where, bf16[256,1024]{1,0:T(8,128)(2,1)} %collective-permute-done.33.refs_0_.refs_4_, bf16[256,1024]{1,0:T(8,128)(2,1)} %collective-permute-done.34.refs_1_.refs_5_, ...), custom_call_target="tpu_custom_call" | custom-call | flops 4294967296 | bytes 15728648 | tf_op jit(solution)/shard_map/pallas_call | solution.py:43
  179.1 10.1 %shard_map.225 = (f32[1024,1024]{1,0:T(8,128)}, bf16[1024,512]{1,0:T(8,128)(2,1)}, bf16[1024,1024]{1,0:T(8,128)(2,1)}) custom-call(s32[2]{0:T(128)} %pad_add_fusion.where, bf16[256,1024]{1,0:T(8,128)(2,1)} %copy-done.32, bf16[256,1024]{1,0:T(8,128)(2,1)} %copy-done.42, bf16[256,1024]{1,0:T(8,128)(2,1)} %collective-permute-done.14.refs_2_, ...), custom_call_target="tpu_custom_call" | custom-call | flops 4294967296 | bytes 17825800 | tf_op jit(solution)/shard_map/pallas_call | solution.py:43
  200.8 12.3 %shard_map.232 = bf16[1024,1536]{1,0:T(8,128)(2,1)} custom-call(s32[2]{0:T(128)} %pad_add_fusion.where, bf16[256,1024]{1,0:T(8,128)(2,1)} %copy-done.32, bf16[256,1024]{1,0:T(8,128)(2,1)} %copy-done.42, bf16[256,1024]{1,0:T(8,128)(2,1)} %collective-permute-done.14.refs_2_, bf16[256,1024]{1,0:T(8,128)(2,1)} %collective-permute-done.15.refs_3_, ...), custom_call_target="tpu_custom_call" | custom-call | flops 6442450944 | bytes 18350088 | tf_op jit(solution)/shard_map/pallas_call | solution.py:43
  219.1 18.4 %collective-permute-start.71 = (bf16[128,1536]{1,0:T(8,128)(2,1)S(1)}, bf16[128,1536]{1,0:T(8,128)(2,1)S(1)}, u32[]{:S(2)}, u32[]{:S(2)}) collective-permute-start(bf16[128,1536]{1,0:T(8,128)(2,1)S(1)} %get-tuple-element.130), channel_id=1, source_target_pairs={{0,8},{4,12},{8,0},{12,4},{16,24},{20,28},{24,16},{28,20},{1,9},{5... | collective-permute-start | bytes 1179656 | tf_op jit(solution)/shard_map/ppermute | solution.py:57
  237.5 5.2 %shard_map.226 = f32[1024,1024]{1,0:T(8,128)} custom-call(s32[2]{0:T(128)} %pad_add_fusion.where, bf16[1024,512]{1,0:T(8,128)(2,1)} %get-tuple-element.47.active.refs_18_, bf16[1024,1536]{1,0:T(8,128)(2,1)} %get-tuple-element.44.refs_4_.weights), custom_call_target="tpu_custom_call" | custom-call | flops 1073741824 | bytes 8388616 | tf_op jit(solution)/shard_map/pallas_call | solution.py:43
  245.0 6.1 %collective-permute-start.72 = (bf16[128,1536]{1,0:T(8,128)(2,1)}, bf16[128,1536]{1,0:T(8,128)(2,1)S(1)}, u32[]{:S(2)}, u32[]{:S(2)}) collective-permute-start(bf16[128,1536]{1,0:T(8,128)(2,1)} %get-tuple-element.129), channel_id=1, source_target_pairs={{0,12},{4,8},{8,4},{12,0},{16,28},{20,24},{24,20},{28,16},{1,13},{... | collective-permute-start | bytes 1179656 | tf_op jit(solution)/shard_map/ppermute | solution.py:57
  265.2 7.5 %collective-permute-start.76 = (bf16[128,1536]{1,0:T(8,128)(2,1)}, bf16[128,1536]{1,0:T(8,128)(2,1)}, u32[]{:S(2)}, u32[]{:S(2)}) collective-permute-start(bf16[128,1536]{1,0:T(8,128)(2,1)} %get-tuple-element.125), channel_id=1, source_target_pairs={{0,28},{4,24},{8,20},{12,16},{16,12},{20,8},{24,4},{28,0},{1,29},{... | collective-permute-start | bytes 1179656 | tf_op jit(solution)/shard_map/ppermute | solution.py:57
  272.7 27.6 %collective-permute-done.74.refs_5_ = bf16[128,1536]{1,0:T(8,128)(2,1)S(1)} collective-permute-done((bf16[128,1536]{1,0:T(8,128)(2,1)}, bf16[128,1536]{1,0:T(8,128)(2,1)S(1)}, u32[]{:S(2)}, u32[]{:S(2)}) %collective-permute-start.74) | collective-permute-done | bytes 393248 | tf_op jit(solution)/shard_map/ppermute | solution.py:57
  304.1 22.5 %collective-permute-done.54.refs_1_ = bf16[64,1024]{1,0:T(8,128)(2,1)S(1)} collective-permute-done((bf16[64,1024]{1,0:T(8,128)(2,1)S(1)}, bf16[64,1024]{1,0:T(8,128)(2,1)S(1)}, u32[]{:S(2)}, u32[]{:S(2)}) %collective-permute-start.54) | collective-permute-done | bytes 131104 | tf_op jit(solution)/shard_map/ppermute | solution.py:57
  326.6 6.0 %collective-permute-start.37 = (bf16[256,1024]{1,0:T(8,128)(2,1)S(1)}, bf16[256,1024]{1,0:T(8,128)(2,1)S(1)}, u32[]{:S(2)}, u32[]{:S(2)}) collective-permute-start(bf16[256,1024]{1,0:T(8,128)(2,1)S(1)} %get-tuple-element.145), channel_id=1, source_target_pairs={{0,1},{1,0},{2,3},{3,2},{4,5},{5,4},{6,7},{7,6},{8,9},{9,8},{10,11... | collective-permute-start | bytes 1572872 | tf_op jit(solution)/shard_map/ppermute | solution.py:57
  341.6 9.3 %collective-permute-done.57.refs_1_ = bf16[64,1024]{1,0:T(8,128)(2,1)S(1)} collective-permute-done((bf16[64,1024]{1,0:T(8,128)(2,1)}, bf16[64,1024]{1,0:T(8,128)(2,1)S(1)}, u32[]{:S(2)}, u32[]{:S(2)}) %collective-permute-start.57) | collective-permute-done | bytes 131104 | tf_op jit(solution)/shard_map/ppermute | solution.py:57
  350.9 6.8 %shard_map.233 = (f32[32,128,128]{2,1,0:T(8,128)}, f32[32,128,128]{2,1,0:T(8,128)}, f32[32,128,128]{2,1,0:T(8,128)}) custom-call(s32[2]{0:T(128)} %pad_add_fusion.where, bf16[128,1536]{1,0:T(8,128)(2,1)} %get-tuple-element.132.refs_0_, bf16[128,1536]{1,0:T(8,128)(2,1)} %copy-done.15, bf16[128,1536]{1,0:T(8,128)(2,1)} %copy-done.16, ...), custom_call_target="tpu_custom_call" | custom-call | bytes 9437184 | tf_op jit(solution)/shard_map/pallas_call | solution.py:604
  357.7 7.0 %shard_map.230 = (f32[512,768]{1,0:T(8,128)}, bf16[512,768]{1,0:T(8,128)(2,1)}, f32[128,1024]{1,0:T(8,128)}, bf16[128,1024]{1,0:T(8,128)(2,1)}) custom-call(s32[2]{0:T(128)} %pad_add_fusion.where, bf16[64,1024]{1,0:T(8,128)(2,1)} %get-tuple-element.51.refs_0_, bf16[64,1024]{1,0:T(8,128)(2,1)} %copy-done.31, ...), custom_call_target="tpu_custom_call" | custom-call | flops 805306368 | bytes 6424584 | tf_op jit(solution)/shard_map/pallas_call | solution.py:43
  377.8 8.5 %all_gather.7 = bf16[320,1024]{1,0:T(8,128)(2,1)S(1)} all-gather(bf16[80,1024]{1,0:T(8,128)(2,1)S(1)} %convert_element_type.197), channel_id=1, replica_groups=mesh['expert'=8,'tensor'=4] {'tensor'}, dimensions={0}, use_global_device_ids=true | all-gather | bytes 819200 | tf_op jit(solution)/shard_map/all_gather | solution.py:676
  393.2 9.3 %all_gather.6 = bf16[256,1024]{1,0:T(8,128)(2,1)S(1)} all-gather(bf16[64,1024]{1,0:T(8,128)(2,1)S(1)} %fusion.11), channel_id=1, replica_groups=mesh['expert'=8,'tensor'=4] {'tensor'}, dimensions={0}, use_global_device_ids=true | all-gather | bytes 655360 | tf_op jit(solution)/shard_map/all_gather | solution.py:579
  408.0 7.6 %collective-permute-done.63 = bf16[128,768]{1,0:T(8,128)(2,1)S(1)} collective-permute-done((bf16[128,768]{1,0:T(8,128)(2,1)S(1)}, bf16[128,768]{1,0:T(8,128)(2,1)S(1)}, u32[]{:S(2)}, u32[]{:S(2)}) %collective-permute-start.63) | collective-permute-done | bytes 196640 | tf_op jit(solution)/shard_map/ppermute | solution.py:57
  (333 shorter events, 171.7 us)
Async XLA Ops:
  19.6 42.6 %collective-permute-start.23 = (bf16[64,1152]{1,0:T(8,128)(2,1)}, bf16[64,1152]{1,0:T(8,128)(2,1)}, u32[]{:S(2)}, u32[]{:S(2)}) collective-permute-start(bf16[64,1152]{1,0:T(8,128)(2,1)} %pad_maximum_fusion.4), channel_id=1, source_target_pairs={{0,16},{4,20},{8,24},{12,28},{16,0},{20,4},{24,8},{28,12},{1,17},{... | collective-permute-start | bytes 442376 | tf_op jit(solution)/shard_map/ppermute | solution.py:57
  31.3 30.9 %collective-permute-start.24 = (bf16[64,1152]{1,0:T(8,128)(2,1)}, bf16[64,1152]{1,0:T(8,128)(2,1)S(1)}, u32[]{:S(2)}, u32[]{:S(2)}) collective-permute-start(bf16[64,1152]{1,0:T(8,128)(2,1)} %pad_maximum_fusion.4), channel_id=1, source_target_pairs={{0,8},{4,12},{8,0},{12,4},{16,24},{20,28},{24,16},{28,20},{1,9},{5... | collective-permute-start | bytes 442376 | tf_op jit(solution)/shard_map/ppermute | solution.py:57
  39.6 28.7 %collective-permute-start.25 = (bf16[64,1152]{1,0:T(8,128)(2,1)}, bf16[64,1152]{1,0:T(8,128)(2,1)S(1)}, u32[]{:S(2)}, u32[]{:S(2)}) collective-permute-start(bf16[64,1152]{1,0:T(8,128)(2,1)} %pad_maximum_fusion.4), channel_id=1, source_target_pairs={{0,24},{4,28},{8,16},{12,20},{16,8},{20,12},{24,0},{28,4},{1,25},{... | collective-permute-start | bytes 442376 | tf_op jit(solution)/shard_map/ppermute | solution.py:57
  62.3 33.4 %collective-permute-start.18 = (bf16[128,1536]{1,0:T(8,128)(2,1)S(1)}, bf16[128,1536]{1,0:T(8,128)(2,1)S(1)}, u32[]{:S(2)}, u32[]{:S(2)}) collective-permute-start(bf16[128,1536]{1,0:T(8,128)(2,1)S(1)} %get-tuple-element.137), channel_id=1, source_target_pairs={{0,12},{4,8},{8,4},{12,0},{16,28},{20,24},{24,20},{28,16},{1,13},{... | collective-permute-start | bytes 1179656 | tf_op jit(solution)/shard_map/ppermute | solution.py:57
  63.7 33.4 %collective-permute-start.19 = (bf16[128,1536]{1,0:T(8,128)(2,1)S(1)}, bf16[128,1536]{1,0:T(8,128)(2,1)S(1)}, u32[]{:S(2)}, u32[]{:S(2)}) collective-permute-start(bf16[128,1536]{1,0:T(8,128)(2,1)S(1)} %get-tuple-element.136), channel_id=1, source_target_pairs={{0,16},{4,20},{8,24},{12,28},{16,0},{20,4},{24,8},{28,12},{1,17},{... | collective-permute-start | bytes 1179656 | tf_op jit(solution)/shard_map/ppermute | solution.py:57
  68.4 29.0 %collective-permute-start.10 = (bf16[64,1024]{1,0:T(8,128)(2,1)}, bf16[64,1024]{1,0:T(8,128)(2,1)S(1)}, u32[]{:S(2)}, u32[]{:S(2)}) collective-permute-start(bf16[64,1024]{1,0:T(8,128)(2,1)} %get-tuple-element.43), channel_id=1, source_target_pairs={{0,16},{4,20},{8,24},{12,28},{16,0},{20,4},{24,8},{28,12},{1,17},{... | collective-permute-start | bytes 393224 | tf_op jit(solution)/shard_map/ppermute | solution.py:57
  71.1 46.9 %collective-permute-start.20 = (bf16[128,1536]{1,0:T(8,128)(2,1)S(1)}, bf16[128,1536]{1,0:T(8,128)(2,1)S(1)}, u32[]{:S(2)}, u32[]{:S(2)}) collective-permute-start(bf16[128,1536]{1,0:T(8,128)(2,1)S(1)} %get-tuple-element.135), channel_id=1, source_target_pairs={{0,20},{4,16},{8,28},{12,24},{16,4},{20,0},{24,12},{28,8},{1,21},{... | collective-permute-start | bytes 1179656 | tf_op jit(solution)/shard_map/ppermute | solution.py:57
  88.4 34.6 %collective-permute-start.26 = (bf16[256,1152]{1,0:T(8,128)(2,1)S(1)}, bf16[256,1152]{1,0:T(8,128)(2,1)S(1)}, u32[]{:S(2)}, u32[]{:S(2)}) collective-permute-start(bf16[256,1152]{1,0:T(8,128)(2,1)S(1)} %pad_maximum_fusion.1.refs_8_), channel_id=1, source_target_pairs={{0,4},{1,3},{2,6},{3,1},{4,0},{5,7},{6,2},{7,5},{8,12},{9,11},{10,... | collective-permute-start | bytes 1769480 | tf_op jit(solution)/shard_map/ppermute | solution.py:68
  101.2 32.0 %collective-permute-start.27 = (bf16[256,1152]{1,0:T(8,128)(2,1)S(1)}, bf16[256,1152]{1,0:T(8,128)(2,1)S(1)}, u32[]{:S(2)}, u32[]{:S(2)}) collective-permute-start(bf16[256,1152]{1,0:T(8,128)(2,1)S(1)} %pad_maximum_fusion.1.refs_8_), channel_id=1, source_target_pairs={{0,2},{1,5},{2,0},{3,7},{4,6},{5,1},{6,4},{7,3},{8,10},{9,13},{10,... | collective-permute-start | bytes 1769480 | tf_op jit(solution)/shard_map/ppermute | solution.py:68
  189.7 63.3 %collective-permute-start.47 = (bf16[256,1024]{1,0:T(8,128)(2,1)S(1)}, bf16[256,1024]{1,0:T(8,128)(2,1)S(1)}, u32[]{:S(2)}, u32[]{:S(2)}) collective-permute-start(bf16[256,1024]{1,0:T(8,128)(2,1)S(1)} %get-tuple-element.141), channel_id=1, source_target_pairs={{0,1},{1,0},{2,3},{3,2},{4,5},{5,4},{6,7},{7,6},{8,9},{9,8},{10,11... | collective-permute-start | bytes 1572872 | tf_op jit(solution)/shard_map/ppermute | solution.py:57
  213.1 42.3 %collective-permute-start.49 = (bf16[256,1024]{1,0:T(8,128)(2,1)}, bf16[256,1024]{1,0:T(8,128)(2,1)}, u32[]{:S(2)}, u32[]{:S(2)}) collective-permute-start(bf16[256,1024]{1,0:T(8,128)(2,1)} %get-tuple-element.121), channel_id=1, source_target_pairs={{0,2},{1,5},{2,0},{3,7},{4,6},{5,1},{6,4},{7,3},{8,10},{9,13},{10,... | collective-permute-start | bytes 1572872 | tf_op jit(solution)/shard_map/ppermute | solution.py:68
  214.5 43.9 %collective-permute-start.53 = (bf16[256,1024]{1,0:T(8,128)(2,1)S(1)}, bf16[256,1024]{1,0:T(8,128)(2,1)S(1)}, u32[]{:S(2)}, u32[]{:S(2)}) collective-permute-start(bf16[256,1024]{1,0:T(8,128)(2,1)S(1)} %add_convert_fusion), channel_id=1, source_target_pairs={{0,4},{1,3},{2,6},{3,1},{4,0},{5,7},{6,2},{7,5},{8,12},{9,11},{10,... | collective-permute-start | bytes 1572872 | tf_op jit(solution)/shard_map/ppermute | solution.py:68
  219.1 32.0 %collective-permute-start.71 = (bf16[128,1536]{1,0:T(8,128)(2,1)S(1)}, bf16[128,1536]{1,0:T(8,128)(2,1)S(1)}, u32[]{:S(2)}, u32[]{:S(2)}) collective-permute-start(bf16[128,1536]{1,0:T(8,128)(2,1)S(1)} %get-tuple-element.130), channel_id=1, source_target_pairs={{0,8},{4,12},{8,0},{12,4},{16,24},{20,28},{24,16},{28,20},{1,9},{5... | collective-permute-start | bytes 1179656 | tf_op jit(solution)/shard_map/ppermute | solution.py:57
  252.9 47.3 %collective-permute-start.74 = (bf16[128,1536]{1,0:T(8,128)(2,1)}, bf16[128,1536]{1,0:T(8,128)(2,1)S(1)}, u32[]{:S(2)}, u32[]{:S(2)}) collective-permute-start(bf16[128,1536]{1,0:T(8,128)(2,1)} %get-tuple-element.127), channel_id=1, source_target_pairs={{0,20},{4,16},{8,28},{12,24},{16,4},{20,0},{24,12},{28,8},{1,21},{... | collective-permute-start | bytes 1179656 | tf_op jit(solution)/shard_map/ppermute | solution.py:57
  255.4 44.9 %collective-permute-start.40 = (bf16[256,1024]{1,0:T(8,128)(2,1)S(1)}, bf16[256,1024]{1,0:T(8,128)(2,1)S(1)}, u32[]{:S(2)}, u32[]{:S(2)}) collective-permute-start(bf16[256,1024]{1,0:T(8,128)(2,1)S(1)} %get-tuple-element.147), channel_id=1, source_target_pairs={{0,1},{1,0},{2,3},{3,2},{4,5},{5,4},{6,7},{7,6},{8,9},{9,8},{10,11... | collective-permute-start | bytes 1572872 | tf_op jit(solution)/shard_map/ppermute | solution.py:57
  259.3 43.2 %collective-permute-start.42 = (bf16[256,1024]{1,0:T(8,128)(2,1)S(1)}, bf16[256,1024]{1,0:T(8,128)(2,1)S(1)}, u32[]{:S(2)}, u32[]{:S(2)}) collective-permute-start(bf16[256,1024]{1,0:T(8,128)(2,1)S(1)} %get-tuple-element.124), channel_id=1, source_target_pairs={{0,2},{1,5},{2,0},{3,7},{4,6},{5,1},{6,4},{7,3},{8,10},{9,13},{10,... | collective-permute-start | bytes 1572872 | tf_op jit(solution)/shard_map/ppermute | solution.py:68
  263.4 76.2 %collective-permute-start.75 = (bf16[128,1536]{1,0:T(8,128)(2,1)}, bf16[128,1536]{1,0:T(8,128)(2,1)S(1)}, u32[]{:S(2)}, u32[]{:S(2)}) collective-permute-start(bf16[128,1536]{1,0:T(8,128)(2,1)} %get-tuple-element.126), channel_id=1, source_target_pairs={{0,24},{4,28},{8,16},{12,20},{16,8},{20,12},{24,0},{28,4},{1,25},{... | collective-permute-start | bytes 1179656 | tf_op jit(solution)/shard_map/ppermute | solution.py:57
  265.2 74.9 %collective-permute-start.76 = (bf16[128,1536]{1,0:T(8,128)(2,1)}, bf16[128,1536]{1,0:T(8,128)(2,1)}, u32[]{:S(2)}, u32[]{:S(2)}) collective-permute-start(bf16[128,1536]{1,0:T(8,128)(2,1)} %get-tuple-element.125), channel_id=1, source_target_pairs={{0,28},{4,24},{8,20},{12,16},{16,12},{20,8},{24,4},{28,0},{1,29},{... | collective-permute-start | bytes 1179656 | tf_op jit(solution)/shard_map/ppermute | solution.py:57
  300.3 32.3 %collective-permute-start.55 = (bf16[64,1024]{1,0:T(8,128)(2,1)S(1)}, bf16[64,1024]{1,0:T(8,128)(2,1)S(1)}, u32[]{:S(2)}, u32[]{:S(2)}) collective-permute-start(bf16[64,1024]{1,0:T(8,128)(2,1)S(1)} %get-tuple-element.153), channel_id=1, source_target_pairs={{0,8},{4,12},{8,0},{12,4},{16,24},{20,28},{24,16},{28,20},{1,9},{5... | collective-permute-start | bytes 393224 | tf_op jit(solution)/shard_map/ppermute | solution.py:57
  302.4 33.1 %collective-permute-start.56 = (bf16[64,1024]{1,0:T(8,128)(2,1)S(1)}, bf16[64,1024]{1,0:T(8,128)(2,1)S(1)}, u32[]{:S(2)}, u32[]{:S(2)}) collective-permute-start(bf16[64,1024]{1,0:T(8,128)(2,1)S(1)} %get-tuple-element.152), channel_id=1, source_target_pairs={{0,24},{4,28},{8,16},{12,20},{16,8},{20,12},{24,0},{28,4},{1,25},{... | collective-permute-start | bytes 393224 | tf_op jit(solution)/shard_map/ppermute | solution.py:57
  326.6 38.6 %collective-permute-start.37 = (bf16[256,1024]{1,0:T(8,128)(2,1)S(1)}, bf16[256,1024]{1,0:T(8,128)(2,1)S(1)}, u32[]{:S(2)}, u32[]{:S(2)}) collective-permute-start(bf16[256,1024]{1,0:T(8,128)(2,1)S(1)} %get-tuple-element.145), channel_id=1, source_target_pairs={{0,1},{1,0},{2,3},{3,2},{4,5},{5,4},{6,7},{7,6},{8,9},{9,8},{10,11... | collective-permute-start | bytes 1572872 | tf_op jit(solution)/shard_map/ppermute | solution.py:57
  333.3 31.9 %collective-permute-start.39 = (bf16[256,1024]{1,0:T(8,128)(2,1)S(1)}, bf16[256,1024]{1,0:T(8,128)(2,1)S(1)}, u32[]{:S(2)}, u32[]{:S(2)}) collective-permute-start(bf16[256,1024]{1,0:T(8,128)(2,1)S(1)} %get-tuple-element.123), channel_id=1, source_target_pairs={{0,2},{1,5},{2,0},{3,7},{4,6},{5,1},{6,4},{7,3},{8,10},{9,13},{10,... | collective-permute-start | bytes 1572872 | tf_op jit(solution)/shard_map/ppermute | solution.py:68
  335.5 29.7 %collective-permute-start.43 = (bf16[256,1024]{1,0:T(8,128)(2,1)S(1)}, bf16[256,1024]{1,0:T(8,128)(2,1)S(1)}, u32[]{:S(2)}, u32[]{:S(2)}) collective-permute-start(bf16[256,1024]{1,0:T(8,128)(2,1)S(1)} %fusion.2), channel_id=1, source_target_pairs={{0,4},{1,3},{2,6},{3,1},{4,0},{5,7},{6,2},{7,5},{8,12},{9,11},{10,... | collective-permute-start | bytes 1572872 | tf_op jit(solution)/shard_map/ppermute | solution.py:68
  371.5 32.2 %collective-permute-start.62 = (bf16[512,768]{1,0:T(8,128)(2,1)S(1)}, bf16[512,768]{1,0:T(8,128)(2,1)S(1)}, u32[]{:S(2)}, u32[]{:S(2)}) collective-permute-start(bf16[512,768]{1,0:T(8,128)(2,1)S(1)} %copy-done.35), channel_id=1, source_target_pairs={{0,4},{4,0},{8,12},{12,8},{16,20},{20,16},{24,28},{28,24},{1,5},{5... | collective-permute-start | bytes 2359304 | tf_op jit(solution)/shard_map/ppermute | solution.py:57
  (103 other events, 1963.9 us)

commit v3 on v2

v3 whole, which is shorter than its diff:
```python
import functools

import jax
import jax.numpy as jnp
from jax import lax
from jax.experimental import pallas as pl
from jax.experimental.pallas import tpu as pltpu
from jax.sharding import PartitionSpec as P

HEAD_SIZE = 64
EXPERTS = 32
TOP = 8
EPS = 1e-06
THETA = 10000.0
MASKED = -1e30
LANES = 128
LIMIT = 56 * 1024 * 1024

LOW = jnp.bfloat16
FULL = jnp.float32
ROWS_ON_ROWS = (((0,), (0,)), ((), ()))
COLS_ON_ROWS = (((1,), (0,)), ((), ()))
COLS_ON_COLS = (((1,), (1,)), ((), ()))


def mul(left, right, dims=COLS_ON_ROWS):
    return lax.dot_general(left, right, dims, preferred_element_type=FULL)


def shape(dims, dtype):
    return jax.ShapeDtypeStruct(dims, dtype)


def call(body, outs, *args, grid=None, in_specs=None, out_specs=None, scratch=(), flops=0):
    size = sum(a.size * a.dtype.itemsize for a in args)
    size += sum(o.size * jnp.dtype(o.dtype).itemsize for o in outs)
    whole = pl.BlockSpec(memory_space=pltpu.VMEM)
    if in_specs is None:
        in_specs = [whole] * (len(args) - 1)
    if out_specs is None:
        out_specs = [whole] * len(outs)
    extra = {} if grid is None else {"grid": grid}
    return pl.pallas_call(
        body,
        out_shape=list(outs),
        in_specs=[pl.BlockSpec(memory_space=pltpu.SMEM)] + list(in_specs),
        out_specs=list(out_specs),
        scratch_shapes=list(scratch),
        compiler_params=pltpu.CompilerParams(vmem_limit_bytes=LIMIT),
        cost_estimate=pl.CostEstimate(flops=flops, bytes_accessed=size, transcendentals=0),
        **extra,
    )(*args)


def swap(field, axis, mask):
    count = lax.axis_size(axis)
    return lax.ppermute(field, axis, [(i, i ^ mask) for i in range(count)])


def after(field, *earlier):
    return lax.optimization_barrier((field, *earlier))[0]


def swap_by_parity(field, even, odd):
    n_e, n_t = lax.axis_size("expert"), lax.axis_size("tensor")
    pairs = []
    for e in range(n_e):
        for t in range(n_t):
            axis, mask = odd if t & 1 else even
            to = ((e ^ mask) * n_t + t) if axis == "expert" else (e * n_t + (t ^ mask))
            pairs.append((e * n_t + t, to))
    return lax.ppermute(field, ("expert", "tensor"), pairs)


def bits_of(count, first_bit=0):
    return [1 << b for b in reversed(range(first_bit, count.bit_length() - 1))]


def position_in(mask, bits):
    return sum(jnp.where(mask & b != 0, 1 << i, 0) for i, b in enumerate(bits))


def order_of(bits):
    order = [0]
    for b in bits:
        order = order + [k ^ b for k in order]
    return order


def rotate(field, cosine, sine):
    lane = lax.broadcasted_iota(jnp.int32, (field.shape[0], LANES), 1)
    low_half = lane % HEAD_SIZE < HEAD_SIZE // 2
    turned = []
    for at in range(0, field.shape[1], LANES):
        block = field[:, at : at + LANES]
        ahead = pltpu.roll(block, LANES - HEAD_SIZE // 2, 1)
        behind = pltpu.roll(block, HEAD_SIZE // 2, 1)
        turned.append(block * cosine + jnp.where(low_half, ahead, behind) * sine)
    return jnp.concatenate(turned, axis=1)


def admitted(doc_row, doc_col):
    length = doc_row.shape[1]
    row = lax.broadcasted_iota(jnp.int32, (length, length), 0)
    col = lax.broadcasted_iota(jnp.int32, (length, length), 1)
    return (col <= row) & (doc_row == doc_col)


def softmax_of(query, key, allowed):
    scores = mul(query, key, COLS_ON_COLS) * HEAD_SIZE**-0.5
    scores = jnp.where(allowed, scores, MASKED)
    raised = jnp.exp(scores - jnp.max(scores, axis=1, keepdims=True))
    return raised / jnp.sum(raised, axis=1, keepdims=True)


def place_rows(target, sources, orders, where, part, pitch):
    count = len(orders[0]) // len(sources)
    for p, (even, odd) in enumerate(zip(*orders)):
        at = pl.multiple_of((where[0] ^ jnp.where(where[1] & 1 == 0, even, odd)) * part, part)
        k = p % count * pitch
        target[pl.ds(at, part), :] = sources[p // count][k : k + part, :]


def pack_body(own, hid, replicas, turn, where, gate, up, down, down_out, *sided):
    side = where[0] & 1
    for j in range(own):
        at = slice(j * hid, (j + 1) * hid)
        for k in range(2):
            block = down[(k * own if replicas == 1 else 0) + j]
            down_out[0, k, :, at] = (block.T if turn else block).astype(LOW)
            place = ((side ^ k) * own if replicas == 1 else 0) + j
            for source, out in ((gate, sided[k]), (up, sided[2 + k])):
                out[0, :, at] = source[place].astype(LOW)


def attend_body(orders, n, part, pitch, q_cols, k_cols, rows, order, where, *refs):
    sources = refs[:n]
    tokens, gain_in, doc_row, doc_col, cosine, sine = refs[n : n + 6]
    weights, hidden, qkv_out, mixed_out, gain = refs[n + 6 : n + 11]
    mixed = refs[n + 11]
    place_rows(weights, sources, orders, where, part, pitch)
    if part % LANES == 0:
        count = len(orders[0]) // n
        for p, (even, odd) in enumerate(zip(*orders)):
            at = pl.multiple_of((where[0] ^ jnp.where(where[1] & 1 == 0, even, odd)) * part, part)
            k = p % count * pitch + part
            gain[:, pl.ds(at, part)] = sources[p // count][k : k + gain.shape[0], :part].astype(FULL)
    else:
        gain[...] = gain_in[...]
    x = tokens[...].astype(FULL)
    scale = lax.rsqrt(jnp.mean(x * x, axis=1, keepdims=True) + EPS)
    first = (x * scale * gain[0:1, :]).astype(LOW)
    hidden[...] = first
    qkv = mul(first, weights[...])
    turned = rotate(qkv[:, : q_cols + k_cols], cosine[...], sine[...]).astype(LOW)
    values = qkv[:, q_cols + k_cols :].astype(LOW)
    qkv_out[:, : q_cols + k_cols] = turned
    qkv_out[:, q_cols + k_cols :] = values
    allowed = admitted(doc_row[...], doc_col[...])
    per_group = q_cols // k_cols
    for h in range(q_cols // HEAD_SIZE):
        at, g = h * HEAD_SIZE, h // per_group * HEAD_SIZE
        shares = softmax_of(
            turned[:, at : at + HEAD_SIZE],
            turned[:, q_cols + g : q_cols + g + HEAD_SIZE],
            allowed,
        ).astype(LOW)
        mixed[:, at : at + HEAD_SIZE] = mul(shares, values[:, g : g + HEAD_SIZE]).astype(LOW)
    for k, m in enumerate(order):
        at = pl.multiple_of((where[1] ^ m) * rows, rows)
        mixed_out[k * rows : (k + 1) * rows, :] = mixed[pl.ds(at, rows), :]


def branch_body(orders, n, part, where, *refs):
    sources = refs[:n]
    mixed, weights, kept, sent = refs[n:]
    place_rows(weights, sources, orders, where, part, part)
    half = kept.shape[0]
    product = mul(mixed[...], weights[...], COLS_ON_COLS)
    kept[...] = product[:half]
    sent[...] = product[half:].astype(LOW)


def middle_body(rows, where, tokens, kept, got, gain, middle, hidden):
    at = pl.multiple_of(where[1] * rows, rows)
    m = tokens[pl.ds(at, rows), :].astype(FULL) + (kept[...] + got[...].astype(FULL))
    middle[...] = m
    scale = lax.rsqrt(jnp.mean(m * m, axis=1, keepdims=True) + EPS)
    hidden[...] = (m * scale * gain[1:2, :]).astype(LOW)


def pick_tile(buffer, sources, tiles, step):
    for k, source in enumerate(sources):

        @pl.when(step // tiles == k)
        def _():
            buffer[...] = source[...]


def owner_body(n_piece, tiles, part, own, hid, replicas, where, *refs):
    grads = refs[:n_piece]
    this, other, gate_out, back_out, weights, buffer = refs[n_piece:]
    width = weights.shape[0]
    step = pl.program_id(0)

    @pl.when(step == 0)
    def _():
        for z in range(this.shape[0]):
            for k, source in enumerate((this, other)):
                at = pl.multiple_of((2 * z + ((where[0] & 1) ^ k)) * part, part)
                weights[pl.ds(at, part), :] = source[z]

    pick_tile(buffer, grads, tiles, step)
    extra = buffer[:, width:].astype(FULL)
    lane = lax.broadcasted_iota(jnp.int32, extra.shape, 1)
    gate = pltpu.roll(extra, LANES - TOP, 1) + pltpu.roll(extra, LANES - 2 * TOP, 1)
    first = where[0] // replicas * own
    back = mul(buffer[:, :width], weights[...])
    table = jnp.zeros(extra.shape, FULL)
    for j in range(own):
        hit = (lane < TOP) & (extra == (first + j).astype(FULL))
        column = jnp.sum(jnp.where(hit, gate, 0.0), axis=1, keepdims=True)
        table = jnp.where(lane == j, column, table)
        back_out[:, j * hid : (j + 1) * hid] = back[:, j * hid : (j + 1) * hid] * column
    gate_out[...] = table


def expert_body(n_piece, tiles, own, hid, where, *refs):
    rows = refs[:n_piece]
    gate_rows, up_rows, gate, back, grad_hidden, active_out, grad_gate, grad_up, buffer = refs[
        n_piece:
    ]
    pick_tile(buffer, rows, tiles, pl.program_id(0))
    gate_pre = mul(buffer[...], gate_rows[...])
    up_pre = mul(buffer[...], up_rows[...])
    for j in range(own):
        at = slice(j * hid, (j + 1) * hid)
        pre, up = gate_pre[:, at], up_pre[:, at]
        squash = 1.0 / (1.0 + jnp.exp(-pre))
        silu = pre * squash
        active = (silu * up).astype(LOW).astype(FULL)
        active_out[:, at] = (active * gate[:, j : j + 1]).astype(LOW)
        d = back[:, at]
        grad_gate[:, at] = (d * up * squash * (1.0 + pre * (1.0 - squash))).astype(LOW)
        grad_up[:, at] = (d * silu).astype(LOW)
    product = mul(grad_gate[...], gate_rows[...], COLS_ON_COLS)
    product = product + mul(grad_up[...], up_rows[...], COLS_ON_COLS)
    grad_hidden[...] = product.astype(grad_hidden.dtype)


def out_body(where, active, weights, out):
    out[...] = mul(active[...], weights[...], COLS_ON_COLS).astype(out.dtype)


def weight_grad_body(n_source, where, *refs):
    sources = refs[:n_source]
    column = refs[-1]
    count = (len(refs) - 1 - n_source) // 3
    rights, outs = refs[n_source : n_source + 2 * count], refs[n_source + 2 * count : -1]
    size = sources[0].shape[0]
    for k, source in enumerate(sources):
        column[k * size : (k + 1) * size, :] = source[...]
    half = column.shape[0] // 2
    for k, out in enumerate(outs):
        total = mul(column[:half], rights[2 * k][...], ROWS_ON_ROWS)
        out[...] = (total + mul(column[half:], rights[2 * k + 1][...], ROWS_ON_ROWS)).astype(LOW)


def middle_back_body(where, *refs):
    kept, got, middle, grad, gain, grad_middle, low, gain_part = refs
    total = kept[...] + got[...].astype(FULL)
    m = middle[...]
    scale = lax.rsqrt(jnp.mean(m * m, axis=1, keepdims=True) + EPS)
    gain_part[...] = jnp.broadcast_to(
        jnp.sum(total * m * scale, axis=0, keepdims=True), gain_part.shape
    )
    weighted = total * gain[1:2, :]
    inner = jnp.mean(weighted * m, axis=1, keepdims=True)
    back = grad[...].astype(FULL) + (scale * weighted - m * (scale * scale * scale) * inner)
    grad_middle[...] = back
    low[...] = back.astype(LOW)


def attend_back_body(n_piece, q_cols, k_cols, rows, part, order, orders, where, *refs):
    pieces = refs[:n_piece]
    mixed, out_weights, qkv_in, doc_row, doc_col, cosine, sine, hidden, weights = refs[
        n_piece : n_piece + 9
    ]
    kept, sent, first_kept, first_sent, branch, natural, grad_qkv, grads = refs[n_piece + 9 :]
    for k in range(n_piece):
        branch[k * rows : (k + 1) * rows, :] = pieces[k][...]
    grad_mixed = mul(branch[...], out_weights[...]).astype(LOW)
    for k, m in enumerate(order):
        at = pl.multiple_of((where[1] ^ m) * rows, rows)
        natural[pl.ds(at, rows), :q_cols] = grad_mixed[k * rows : (k + 1) * rows]
    qk = q_cols + k_cols
    total = qk + k_cols
    grads[:, total:] = mul(branch[...], mixed[...], ROWS_ON_ROWS)
    allowed = admitted(doc_row[...], doc_col[...])
    per_group = q_cols // k_cols
    query_grads, key_grads, value_grads = [], [], []
    for g in range(k_cols // HEAD_SIZE):
        key = qkv_in[:, q_cols + g * HEAD_SIZE : q_cols + (g + 1) * HEAD_SIZE]
        value = qkv_in[:, qk + g * HEAD_SIZE : qk + (g + 1) * HEAD_SIZE]
        key_grad = value_grad = None
        for h in range(g * per_group, (g + 1) * per_group):
            at = slice(h * HEAD_SIZE, (h + 1) * HEAD_SIZE)
            query = qkv_in[:, at]
            shares = softmax_of(query, key, allowed)
            grad = natural[:, at]
            grad_shares = mul(grad, value, COLS_ON_COLS)
            inner = jnp.sum(shares * grad_shares, axis=1, keepdims=True)
            grad_scores = (shares * (grad_shares - inner)).astype(LOW)
            query_grads.append(mul(grad_scores, key))
            dk = mul(grad_scores, query, ROWS_ON_ROWS)
            dv = mul(shares.astype(LOW), grad, ROWS_ON_ROWS)
            key_grad = dk if key_grad is None else key_grad + dk
            value_grad = dv if value_grad is None else value_grad + dv
        key_grads.append(key_grad)
        value_grads.append(value_grad)
    turned = jnp.concatenate(query_grads + key_grads, axis=1) * HEAD_SIZE**-0.5
    grad_qkv[:, :qk] = rotate(turned, cosine[...], -sine[...]).astype(LOW)
    grad_qkv[:, qk:] = jnp.concatenate(value_grads, axis=1).astype(LOW)
    grads[:, :total] = mul(hidden[...], grad_qkv[...], ROWS_ON_ROWS)
    for p, (even, odd) in enumerate(zip(*orders)):
        at = pl.multiple_of((where[0] ^ jnp.where(where[1] & 1 == 0, even, odd)) * part, part)
        target = kept if p < len(orders[0]) // 2 else sent
        k = p % (len(orders[0]) // 2)
        target[k * part : (k + 1) * part, :] = grads[pl.ds(at, part), :].astype(target.dtype)
    for k, m in enumerate(order):
        at = pl.multiple_of((where[1] ^ m) * rows, rows)
        natural[k * rows : (k + 1) * rows, :total] = grad_qkv[pl.ds(at, rows), :]
    product = mul(natural[:, :total], weights[...], COLS_ON_COLS)
    half = first_kept.shape[0]
    first_kept[...] = product[:half]
    first_sent[...] = product[half:].astype(LOW)


def tokens_back_body(rows, where, tokens, kept, got, gain, grad_middle, moe_part, out):
    at = pl.multiple_of(where[1] * rows, rows)
    x = tokens[pl.ds(at, rows), :].astype(FULL)
    scale = lax.rsqrt(jnp.mean(x * x, axis=1, keepdims=True) + EPS)
    first = kept[...] + got[...].astype(FULL)
    attn_part = jnp.sum(first * x * scale, axis=0, keepdims=True)
    weighted = first * gain[0:1, :]
    inner = jnp.mean(weighted * x, axis=1, keepdims=True)
    out[:rows] = grad_middle[...] + (scale * weighted - x * (scale * scale * scale) * inner)
    line = lax.broadcasted_iota(jnp.int32, moe_part.shape, 0)
    out[rows:] = jnp.where(line == 0, attn_part, jnp.where(line == 1, moe_part[...], 0.0))


def unpack_body(own, hid, replicas, turn, where, this, other, out):
    side = where[0] & 1
    for j in range(own):
        pieces = [source[0, :, j * hid : (j + 1) * hid].astype(FULL) for source in (this, other)]
        pieces = [piece.T for piece in pieces] if turn else pieces
        if replicas == 1:
            out[side * own + j] = pieces[0]
            out[(1 - side) * own + j] = pieces[1]
        else:
            first = 2 * pl.program_id(0) % replicas == 0
            out[j] = pieces[0] + pieces[1] + jnp.where(first, 0.0, out[j])


def local(
    tokens,
    cotangent,
    segments,
    routes,
    gates,
    w_query,
    key_projection,
    value_projection,
    w_out,
    gain_attn,
    gain_moe,
    w_gate,
    w_up,
    w_down,
):
    n_e, n_t = lax.axis_size("expert"), lax.axis_size("tensor")
    e, t = lax.axis_index("expert"), lax.axis_index("tensor")
    where = jnp.stack([e, t]).astype(jnp.int32)
    replicas = max(1, n_e // EXPERTS)
    own_experts = EXPERTS * replicas // n_e
    first_bit = replicas.bit_length() - 1
    length, width = tokens.shape
    part = width // n_e
    rows = length // n_t
    q_cols, k_cols = w_query.shape[1], key_projection.shape[1]
    qkv_cols = q_cols + 2 * k_cols
    hidden = w_gate.shape[2]
    wide = own_experts * hidden

    pad = 16
    gain_rows = jnp.stack([gain_attn, gain_moe])
    gain_rows = jnp.pad(gain_rows, ((0, pad - 2), (0, qkv_cols - part)))
    qkv_shard = jnp.concatenate(
        [
            jnp.concatenate([w_query, key_projection, value_projection], axis=1),
            gain_rows,
        ],
        axis=0,
    ).astype(LOW)
    out_shard = w_out.T.astype(LOW)

    e_bits, t_bits = bits_of(n_e), bits_of(n_t)
    even_bits, odd_bits = e_bits, e_bits[-1:] + e_bits[:-1]
    orders = order_of(even_bits), order_of(odd_bits)
    by_parity = [(("expert", a), ("expert", b)) for a, b in zip(even_bits, odd_bits)]

    def every(shard, before_last):
        came = []
        for even, odd in by_parity[:-1]:
            came.append(swap_by_parity(shard, even, odd))
            shard = jnp.concatenate([shard, came[-1]])
        shard, *before_last = lax.optimization_barrier((shard, *before_last))
        came.append(swap_by_parity(shard, *by_parity[-1]))
        return [shard, came[-1]], came, before_last

    pairs = n_e // 2
    turn = part % LANES == 0
    pair_experts = 2 * own_experts // replicas or 1
    at_pair = lambda dims: pl.BlockSpec(
        (pair_experts,) + dims, lambda z: (2 * z // max(2, replicas), 0, 0)
    )
    sources = [w_gate, w_up, w_down if turn else w_down.transpose(0, 2, 1)]
    sided = pl.BlockSpec((1, part, wide), lambda z: (z, 0, 0))
    packed = call(
        functools.partial(pack_body, own_experts, hidden, replicas, turn),
        [shape((pairs, 2, part, wide), LOW)] + [shape((pairs, part, wide), LOW)] * 4,
        where, *sources,
        grid=(pairs,),
        in_specs=[at_pair(w.shape[1:]) for w in sources],
        out_specs=[pl.BlockSpec((1, 2, part, wide), lambda z: (z, 0, 0, 0))] + [sided] * 4,
    )
    side = e & 1
    lines = [[z * 2 + k for z in range(n_e // 2)] for k in range(2)]

    def along(blocks):
        return lax.all_to_all(
            blocks, "expert", 0, 0, tiled=True, axis_index_groups=lines
        )

    def sides(blocks):
        this = lax.dynamic_index_in_dim(blocks, side, 1, keepdims=False)
        return this, lax.dynamic_index_in_dim(blocks, 1 - side, 1, keepdims=False)

    def to_neighbour(this, other, *earlier):
        got = swap(after(other, *earlier), "expert", 1)
        return jnp.where(
            side == 0, jnp.concatenate([this, got], axis=1), jnp.concatenate([got, this], axis=1)
        )

    def from_neighbour(blocks, *earlier):
        blocks = along(after(blocks.reshape(n_e // 2, 2 * part, wide), *earlier))
        this, other = sides(blocks.reshape(n_e // 2, 2, part, wide))
        return this, swap(other, "expert", 1)

    qkv_arrays, qkv_came, packed = every(qkv_shard, packed)
    out_arrays, _, _ = every(after(out_shard, qkv_came[0]), ())
    down_this, down_other = from_neighbour(packed[0], qkv_came[-1])
    near = [to_neighbour(*packed[k : k + 2], qkv_came[-1]) for k in (1, 3)]
    pitch = part + pad
    gains = jnp.zeros((pad, LANES), FULL)
    if part % LANES:
        held = jnp.concatenate(
            [a.reshape(-1, pitch, qkv_cols)[:, part:, :part] for a in qkv_arrays]
        ).astype(FULL)
        on_even = [position_in(e ^ k, even_bits) for k in range(n_e)]
        on_odd = [position_in(e ^ k, odd_bits) for k in range(n_e)]
        gains = jnp.concatenate(
            [
                lax.dynamic_index_in_dim(held, jnp.where(t & 1 == 0, a, b), 0, keepdims=False)
                for a, b in zip(on_even, on_odd)
            ],
            axis=1,
        )

    e_path = [("expert", b) for b in bits_of(n_e, first_bit)]
    t_path = [("tensor", b) for b in t_bits]
    even_path, odd_path = e_path + t_path[:-1], e_path[:-1] + t_path[:-1] + e_path[-1:]
    path = list(zip(even_path, odd_path))
    last = t_path[-1]

    def gather_tokens(field, ties=()):
        came = []
        for even, odd in path:
            if len(came) == 2 and ties:
                field = after(field, *ties)
            came.append(swap_by_parity(field, even, odd))
            pieces = [field, came[-1]]
            field = jnp.concatenate(pieces)
        return pieces + [swap(p, *last) for p in pieces], came

    def scatter_tokens(kept, sent, ties):
        total = kept + swap(sent, *last).astype(FULL)
        came = []
        for even, odd in reversed(path):
            half = total.shape[0] // 2
            kept, sent = total[:half], total[half:].astype(LOW)
            if len(came) < len(ties) and ties[len(came)]:
                sent = after(sent, *ties[len(came)])
            came.append(swap_by_parity(sent, even, odd))
            total = kept + came[-1].astype(FULL)
        return kept, came

    own = t * rows
    grad_rows = lax.dynamic_slice_in_dim(cotangent, own, rows, 0)
    gate_rows = lax.dynamic_slice_in_dim(gates, own, rows, 0)
    route_rows = lax.dynamic_slice_in_dim(routes, own, rows, 0)
    gate_high = gate_rows.astype(LOW)
    gate_rest = (gate_rows - gate_high.astype(FULL)).astype(LOW)
    extra = jnp.concatenate([route_rows.astype(LOW), gate_high, gate_rest], axis=1)
    extra = jnp.pad(extra, ((0, 0), (0, LANES - 3 * TOP)))
    grad_pieces, _ = gather_tokens(after(jnp.concatenate([grad_rows, extra], axis=1), out_arrays[-1]))

    documents = segments[0]
    doc_row, doc_col = documents[None, :], documents[:, None]
    index = jnp.arange(length)
    same = (index[None, :] < index[:, None]) & (doc_row == doc_col)
    position = jnp.sum(same.astype(FULL), axis=1, keepdims=True)
    lane = jnp.arange(LANES)
    freqs = THETA ** (-2.0 * (lane % (HEAD_SIZE // 2)).astype(FULL) / HEAD_SIZE)
    angle = position * freqs[None, :]
    cosine = jnp.cos(angle)
    sine = jnp.sin(angle) * jnp.where(lane % HEAD_SIZE < HEAD_SIZE // 2, -1.0, 1.0)[None, :]
    t_masks = t_bits[::-1]
    order = order_of(t_bits)
    weights, first_hidden, qkv, mixed, gains = call(
        functools.partial(attend_body, orders, 2, part, pitch, q_cols, k_cols, rows, order),
        [
            shape((width, qkv_cols), LOW),
            shape((length, width), LOW),
            shape((length, qkv_cols), LOW),
            shape((length, q_cols), LOW),
            shape((pad, width), FULL),
        ],
        where, *qkv_arrays, tokens, gains, doc_row, doc_col, cosine, sine,
        scratch=[pltpu.VMEM((length, q_cols), LOW)],
        flops=2 * length * (width * qkv_cols + 2 * length * q_cols),
    )
    out_weights, kept, sent = call(
        functools.partial(branch_body, orders, 2, part),
        [
            shape((width, q_cols), LOW),
            shape((length // 2, width), FULL),
            shape((length // 2, width), LOW),
        ],
        where, *out_arrays, mixed,
        flops=2 * length * width * q_cols,
    )

    def all_rows(field):
        size = field.shape[0]
        for b in t_bits:
            field = jnp.concatenate([field, swap(field, "tensor", b)])
        at = [position_in(t ^ k, t_bits) * size for k in range(n_t)]
        return jnp.concatenate([lax.dynamic_slice_in_dim(field, a, size, 0) for a in at])

    def scatter_rows(kept, sent):
        for b in t_masks[:-1]:
            total = kept + swap(sent, "tensor", b).astype(FULL)
            half = total.shape[0] // 2
            kept, sent = total[:half], total[half:].astype(LOW)
        return kept, swap(sent, "tensor", t_masks[-1])

    kept, got = scatter_rows(kept, sent)
    middle, second_hidden = call(
        functools.partial(middle_body, rows),
        [shape((rows, width), FULL), shape((rows, width), LOW)],
        where, tokens, kept, got, gains,
    )

    size = 256
    total_rows = sum(p.shape[0] for p in grad_pieces)
    steps = total_rows // size
    whole = lambda a: pl.BlockSpec(a.shape, lambda i: (0,) * a.ndim)
    tile = lambda cols: pl.BlockSpec((size, cols), lambda i: (i, 0))

    def tiles_of(pieces):
        count = pieces[0].shape[0] // size
        return count, [
            pl.BlockSpec((size, p.shape[1]), lambda i, k=k: (jnp.clip(i - k * count, 0, count - 1), 0))
            for k, p in enumerate(pieces)
        ]

    tiles, specs = tiles_of(grad_pieces)
    gate_table, back, down_rows = call(
        functools.partial(owner_body, len(grad_pieces), tiles, part, own_experts, hidden, replicas),
        [
            shape((total_rows, LANES), FULL),
            shape((total_rows, wide), FULL),
            shape((width, wide), LOW),
        ],
        where, *grad_pieces, down_this, down_other,
        grid=(steps,),
        in_specs=specs + [whole(down_this), whole(down_other)],
        out_specs=[tile(LANES), tile(wide), pl.BlockSpec((width, wide), lambda i: (0, 0))],
        scratch=[pltpu.VMEM((size, width + LANES), LOW)],
        flops=2 * total_rows * width * wide,
    )
    hidden_pieces, hidden_came = gather_tokens(second_hidden, [down_other, *near])
    gate_rows, up_rows = (
        along(after(p, hidden_came[1])).reshape(width, wide) for p in near
    )
    half = steps // 2

    def experts(chosen, first, out_type):
        later = lambda cols: pl.BlockSpec((size, cols), lambda i: (i + first, 0))
        tiles, specs = tiles_of(chosen)
        return call(
            functools.partial(expert_body, len(chosen), tiles, own_experts, hidden),
            [
                shape((half * size, width), out_type),
                shape((half * size, wide), LOW),
                shape((half * size, wide), LOW),
                shape((half * size, wide), LOW),
            ],
            where, *chosen, gate_rows, up_rows, gate_table, back,
            grid=(half,),
            in_specs=specs
            + [whole(gate_rows), whole(up_rows), later(LANES), later(wide)],
            out_specs=[tile(width), tile(wide), tile(wide), tile(wide)],
            scratch=[pltpu.VMEM((size, width), LOW)],
            flops=2 * half * size * width * 4 * wide,
        )

    sent_hidden, *sent_right = experts(hidden_pieces[2:], half, LOW)
    kept_hidden, *kept_right = experts(hidden_pieces[:2], 0, FULL)

    block = 256
    column = lambda a: pl.BlockSpec((a.shape[0], block), lambda i: (0, i))

    def weight_grad(sources, chosen):
        rights = [side[k] for k in chosen for side in (kept_right, sent_right)]
        return call(
            functools.partial(weight_grad_body, len(sources)),
            [shape((width, wide), LOW)] * len(chosen),
            where, *sources, *rights,
            grid=(width // block,),
            in_specs=[column(a) for a in sources] + [whole(a) for a in rights],
            out_specs=[pl.BlockSpec((block, wide), lambda i: (i, 0))] * len(chosen),
            scratch=[pltpu.VMEM((total_rows, block), LOW)],
            flops=2 * total_rows * width * wide * len(chosen),
        )

    (down_grad,) = weight_grad(grad_pieces, [0])
    gate_grad, up_grad = weight_grad(hidden_pieces, [1, 2])
    down_back = from_neighbour(down_grad)
    def down(active, out_type):
        return call(
            out_body,
            [shape((half * size, width), out_type)],
            where, active, down_rows,
            grid=(half,),
            in_specs=[tile(wide), whole(down_rows)],
            out_specs=[tile(width)],
            flops=2 * half * size * width * wide,
        )[0]

    sent_out = down(after(sent_right[0], up_grad), LOW)
    kept_out = down(after(kept_right[0], up_grad), FULL)
    grad_kept, grad_came = scatter_tokens(
        kept_hidden, sent_hidden, [(), (down_grad,), (down_back[0], gate_grad, kept_out, sent_out)]
    )
    grad_got = grad_came[-1]
    out_kept, out_came = scatter_tokens(kept_out, sent_out, [(grad_came[1],)])
    out_got = out_came[-1]
    output_rows = (middle + (out_kept + out_got.astype(FULL))).astype(LOW)
    output = all_rows(output_rows)

    grad_middle, branch_grad, moe_part = call(
        middle_back_body,
        [shape((rows, width), FULL), shape((rows, width), LOW), shape((16, width), FULL)],
        where, after(grad_kept, out_came[0]), grad_got, middle, grad_rows, gains,
    )
    branch_pieces = [branch_grad]
    for b in reversed(t_masks):
        branch_pieces = branch_pieces + [swap(p, "tensor", b) for p in branch_pieces]
    all_cols = qkv_cols + q_cols
    kept_w, sent_w, first_kept, first_sent = call(
        functools.partial(
            attend_back_body, len(branch_pieces), q_cols, k_cols, rows, part, order, orders
        ),
        [
            shape((width // 2, all_cols), FULL),
            shape((width // 2, all_cols), LOW),
            shape((length // 2, width), FULL),
            shape((length // 2, width), LOW),
        ],
        where, *branch_pieces[:-1], after(branch_pieces[-1], out_came[1]), mixed, out_weights, qkv, doc_row, doc_col, cosine, sine,
        first_hidden, weights,
        scratch=[
            pltpu.VMEM((length, width), LOW),
            pltpu.VMEM((length, max(q_cols, qkv_cols)), LOW),
            pltpu.VMEM((length, qkv_cols), LOW),
            pltpu.VMEM((width, all_cols), FULL),
        ],
        flops=2 * length * width * (2 * q_cols + 2 * qkv_cols),
    )
    attn_came = []
    for even, odd in reversed(by_parity):
        attn_came.append(swap_by_parity(sent_w, even, odd))
        attn_grad = kept_w + attn_came[-1].astype(FULL)
        half_rows = attn_grad.shape[0] // 2
        kept_w, sent_w = attn_grad[:half_rows], attn_grad[half_rows:].astype(LOW)

    gate_back = from_neighbour(gate_grad, grad_got)
    returned = [
        gate_back,
        from_neighbour(up_grad, gate_back[0]),
        down_back,
    ]

    out_dims = [(part, hidden), (part, hidden), (hidden, part) if turn else (part, hidden)]

    def unpack(pair, dims, turned):
        source = pl.BlockSpec((1, part, wide), lambda z: (z, 0, 0))
        return call(
            functools.partial(unpack_body, own_experts, hidden, replicas, turned),
            [shape((EXPERTS,) + dims, FULL)],
            where, *pair,
            grid=(n_e // 2,),
            in_specs=[source, source],
            out_specs=[at_pair(dims)],
        )[0]

    shards = [unpack(p, d, turn and i == 2) for i, (p, d) in enumerate(zip(returned, out_dims))]
    gate_shard, up_shard, down_shard = shards
    if not turn:
        down_shard = down_shard.transpose(0, 2, 1)

    kept, got = scatter_rows(first_kept, first_sent)
    (token_rows,) = call(
        functools.partial(tokens_back_body, rows),
        [shape((rows + 16, width), FULL)],
        where, tokens, kept, after(got, attn_came[0], gate_back[0]), gains, grad_middle, moe_part,
    )
    gathered = all_rows(token_rows.astype(LOW))
    gathered = gathered.reshape(n_t, rows + 16, width).astype(FULL)
    grad_input = gathered[:, :rows].reshape(length, width)
    gain_sum = jnp.sum(gathered[:, rows : rows + 2], axis=0)

    def gain_block(m):
        return lax.dynamic_slice_in_dim(gain_sum, (e ^ m) * part, part, 1)

    lines = jnp.stack([gain_block(m) for m in order_of(e_bits)])
    for b in reversed(e_bits):
        half_rows = lines.shape[0] // 2
        lines = lines[:half_rows] + swap(lines[half_rows:], "expert", b)
    gain_grads = lines[0]
    return (
        output,
        grad_input,
        attn_grad[:, :q_cols],
        attn_grad[:, q_cols : q_cols + k_cols],
        attn_grad[:, q_cols + k_cols : qkv_cols],
        attn_grad[:, qkv_cols:].T,
        gain_grads[0],
        gain_grads[1],
        gate_shard,
        up_shard,
        down_shard,
    )


def solution(mesh):
    by_rows = P("expert", None)
    by_both = P("expert", "tensor")
    in_experts = P(None, "expert", "tensor")
    down_specs = P(None, "tensor", "expert")
    return jax.shard_map(
        local,
        mesh=mesh,
        in_specs=(by_rows,) * 5
        + (by_both,) * 3
        + (P("tensor", "expert"), P("expert"), P("expert"), in_experts, in_experts, down_specs),
        out_specs=(by_rows, by_rows)
        + (by_both,) * 3
        + (P("tensor", "expert"), P("expert"), P("expert"), in_experts, in_experts, down_specs),
        check_vma=False,
    )
```

time: 426 us -> 365 us (0.86)
  waiting for transfers between devices: 141 us -> 110 us
  starting transfers between devices: 128 us -> 106 us
  blocking collectives: 17.8 us -> 0 us
  Pallas kernels: 79.1 us -> 88.4 us
    ppermute x65 -> x26, waiting for transfers between devices: 122 us -> 16.7 us  [swap(): return lax.ppermute(field, axis, [(i, i ^ mask) for i in range(count)])]
    ppermute x65 -> x26, starting transfers between devices: 118 us -> 46 us  [swap(): return lax.ppermute(field, axis, [(i, i ^ mask) for i in range(count)])]
    ppermute x12 -> x25, waiting for transfers between devices: 19 us -> 77.5 us  [swap_by_parity(): return lax.ppermute(field, ('expert', 'tensor'), pairs)]
    all_to_all x0 -> x6, starting transfers between devices: none -> 25.9 us  [along(): lax.all_to_all(blocks, 'expert', 0, 0, tiled=True, axis_index_groups=lines)]
    ppermute x12 -> x25, starting transfers between devices: 9.45 us -> 34.2 us  [swap_by_parity(): return lax.ppermute(field, ('expert', 'tensor'), pairs)]
    all_gather x2 -> x0, blocking collectives: 17.8 us -> none  [the longest x1 9.32 us: local(): output = lax.all_gather(output_rows, 'tensor', axis=0, tiled=True)]
    pallas_call x12 -> x17, Pallas kernels: 72.3 us -> 88.4 us  [call(): pl.pallas_call(body, out_shape=list(outs), in_specs=[pl.BlockSpec(memory_...]
    all_to_all x0 -> x6, waiting for transfers between devices: none -> 15.3 us  [along(): lax.all_to_all(blocks, 'expert', 0, 0, tiled=True, axis_index_groups=lines)]
  transfers between devices with their start and end apart: 77 -> 57, of which waited for: 19 -> 24; matrix products, arithmetic and copies ran while one was open for 10% -> 12% of each run, Pallas kernels for 16% -> 21%
where the time goes in v3:
time: 365 us; the launch traced here: 364 us
  waiting for transfers between devices  110 us (30%)
  starting transfers between devices  106 us (29%)
  Pallas kernels  88.4 us (24%)
  local copies, waits for them, and re-layouts  33 us (9%)
  other arithmetic  25.4 us (7%)
    pallas_call x17, Pallas kernels, call(): pl.pallas_call(body, out_shape=list(outs), in_specs=[pl.BlockSpec(memory_...  88.4 us
    ppermute x25, waiting for transfers between devices, swap_by_parity(): return lax.ppermute(field, ('expert', 'tensor'), pairs)  77.5 us
    ppermute x26, starting transfers between devices, swap(): return lax.ppermute(field, axis, [(i, i ^ mask) for i in range(count)])  46 us
    ppermute x25, starting transfers between devices, swap_by_parity(): return lax.ppermute(field, ('expert', 'tensor'), pairs)  34.2 us
    all_to_all x6, starting transfers between devices, along(): lax.all_to_all(blocks, 'expert', 0, 0, tiled=True, axis_index_groups=lines)  25.9 us
    ppermute x26, waiting for transfers between devices, swap(): return lax.ppermute(field, axis, [(i, i ^ mask) for i in range(count)])  16.7 us
    unnamed x80, local copies, waits for them, and re-layouts  15.6 us
    all_to_all x6, waiting for transfers between devices, along(): lax.all_to_all(blocks, 'expert', 0, 0, tiled=True, axis_index_groups=lines)  15.3 us
  transfers between devices with their start and end apart: 57, of which 24 were waited for; matrix products, arithmetic and copies ran while one was open for 12% of the time, Pallas kernels for 21%

profile of v3, /device:TPU:1, one launch (start us, length us, event | category | flops | bytes accessed | tf_op | source)
XLA Modules:
  0.0 363.8 jit_solution(10892435272808275045)
XLA Ops:
  7.8 4.9 %shard_map.221 = (bf16[4,2,128,512]{3,2,1,0:T(8,128)(2,1)}, bf16[4,128,512]{2,1,0:T(8,128)(2,1)}, bf16[4,128,512]{2,1,0:T(8,128)(2,1)}, bf16[4,128,512]{2,1,0:T(8,128)(2,1)}, bf16[4,128,512]{2,1,0:T(8,128)(2,1)}) custom-call(s32[2]{0:T(128)} %pad_add_fusion.where, f32[32,128,128]{2,1,0:T(8,128)} %gate.1, f32[32,128,128]{2,1,0:T(8,128)} %up.1, ...), custom_call_target="tpu_custom_call" | custom-call | bytes 9437192 | tf_op jit(solution)/shard_map/pallas_call | solution.py:43
  16.8 5.6 %collective-permute-done.4 = bf16[288,512]{1,0:T(8,128)(2,1)S(1)} collective-permute-done((bf16[288,512]{1,0:T(8,128)(2,1)S(1)}, bf16[288,512]{1,0:T(8,128)(2,1)S(1)}, u32[]{:S(2)}, u32[]{:S(2)}) %collective-permute-start.4) | collective-permute-done | bytes 294944 | tf_op jit(solution)/shard_map/ppermute | solution.py:72
  27.9 6.6 %collective-permute-done.2 = bf16[256,256]{1,0:T(8,128)(2,1)S(1)} collective-permute-done((bf16[256,256]{1,0:T(8,128)(2,1)S(1)}, bf16[256,256]{1,0:T(8,128)(2,1)S(1)}, u32[]{:S(2)}, u32[]{:S(2)}) %collective-permute-start.2) | collective-permute-done | bytes 131104 | tf_op jit(solution)/shard_map/ppermute | solution.py:72
  52.4 19.3 %collective-permute-done.15 = bf16[64,1152]{1,0:T(8,128)(2,1)S(1)} collective-permute-done((bf16[64,1152]{1,0:T(8,128)(2,1)S(1)}, bf16[64,1152]{1,0:T(8,128)(2,1)S(1)}, u32[]{:S(2)}, u32[]{:S(2)}) %collective-permute-start.15) | collective-permute-done | bytes 147488 | tf_op jit(solution)/shard_map/ppermute | solution.py:72
  85.1 5.8 %collective-permute-done.8 = bf16[64,1024]{1,0:T(8,128)(2,1)S(1)} collective-permute-done((bf16[64,1024]{1,0:T(8,128)(2,1)}, bf16[64,1024]{1,0:T(8,128)(2,1)S(1)}, u32[]{:S(2)}, u32[]{:S(2)}) %collective-permute-start.8) | collective-permute-done | bytes 131104 | tf_op jit(solution)/shard_map/ppermute | solution.py:72
  118.6 9.5 %all-to-all-done.2 = bf16[4,256,512]{2,1,0:T(8,128)(2,1)S(1)} async-done(((bf16[4,256,512]{2,1,0:T(8,128)(2,1)}), bf16[4,256,512]{2,1,0:T(8,128)(2,1)S(1)}, u32[]{:S(2)}, u32[]{:S(2)}) %all-to-all-start.2) | async-done | bytes 1048608 | tf_op jit(solution)/shard_map/all_to_all | solution.py:441
  131.8 6.9 %collective-permute-start.19 = (bf16[512,1152]{1,0:T(8,128)(2,1)}, bf16[512,1152]{1,0:T(8,128)(2,1)S(1)}, u32[]{:S(2)}, u32[]{:S(2)}) collective-permute-start(bf16[512,1152]{1,0:T(8,128)(2,1)} %constant_dynamic-update-slice_fusion.2.refs_0_), channel_id=1, source_target_pairs={{0,1},{1,0},{2,3},{3,2},{4,5},{5,4},{6,7},{7,6},{8,9},{9,8},{10,11... | collective-permute-start | bytes 3538952 | tf_op jit(solution)/shard_map/ppermute | solution.py:57
  139.2 5.3 %collective-permute-done.14.refs_1_ = bf16[512,1024]{1,0:T(8,128)(2,1)} collective-permute-done((bf16[512,1024]{1,0:T(8,128)(2,1)}, bf16[512,1024]{1,0:T(8,128)(2,1)}, u32[]{:S(2)}, u32[]{:S(2)}) %collective-permute-start.14) | collective-permute-done | bytes 1048608 | tf_op jit(solution)/shard_map/ppermute | solution.py:72
  149.5 9.3 %shard_map.225 = (f32[2048,128]{1,0:T(8,128)}, f32[2048,512]{1,0:T(8,128)}, bf16[1024,512]{1,0:T(8,128)(2,1)}) custom-call(s32[2]{0:T(128)} %pad_add_fusion.where, bf16[512,1152]{1,0:T(8,128)(2,1)} %constant_dynamic-update-slice_fusion.2.refs_0_, bf16[512,1152]{1,0:T(8,128)(2,1)} %collective-permute-done.18.refs_1_, bf16[512,1152]{1,0:T(8,128)(2,1)} %copy-done.35, ...), custom_call_target="tpu_custom_call" | custom-call | flops 2147483648 | bytes 12058632 | tf_op jit(solution)/shard_map/pallas_call | solution.py:43
  159.8 9.0 %shard_map.227 = (bf16[1024,1024]{1,0:T(8,128)(2,1)}, bf16[1024,512]{1,0:T(8,128)(2,1)}, bf16[1024,512]{1,0:T(8,128)(2,1)}, bf16[1024,512]{1,0:T(8,128)(2,1)}) custom-call(s32[2]{0:T(128)} %pad_add_fusion.where, bf16[512,1024]{1,0:T(8,128)(2,1)} %collective-permute-done.21.refs_0_.refs_2_, bf16[512,1024]{1,0:T(8,128)(2,1)} %collective-permute-done.22.refs_1_.refs_3_, ...), custom_call_target="tpu_custom_call" | custom-call | flops 4294967296 | bytes 14680072 | tf_op jit(solution)/shard_map/pallas_call | solution.py:43
  168.9 9.2 %shard_map.226 = (f32[1024,1024]{1,0:T(8,128)}, bf16[1024,512]{1,0:T(8,128)(2,1)}, bf16[1024,512]{1,0:T(8,128)(2,1)}, bf16[1024,512]{1,0:T(8,128)(2,1)}) custom-call(s32[2]{0:T(128)} %pad_add_fusion.where, bf16[512,1024]{1,0:T(8,128)(2,1)} %constant_dynamic-update-slice_fusion.refs_0_, bf16[512,1024]{1,0:T(8,128)(2,1)} %collective-permute-done.14.refs_1_, ...), custom_call_target="tpu_custom_call" | custom-call | flops 4294967296 | bytes 16777224 | tf_op jit(solution)/shard_map/pallas_call | solution.py:43
  178.1 8.6 %shard_map.228 = (bf16[1024,512]{1,0:T(8,128)(2,1)}, bf16[1024,512]{1,0:T(8,128)(2,1)}) custom-call(s32[2]{0:T(128)} %pad_add_fusion.where, bf16[512,1024]{1,0:T(8,128)(2,1)} %constant_dynamic-update-slice_fusion.refs_0_, bf16[512,1024]{1,0:T(8,128)(2,1)} %collective-permute-done.14.refs_1_, bf16[512,1024]{1,0:T(8,128)(2,1)} %collective-permute-done.21.refs_0_.refs_2_, ...), custom_call_target="tpu_custom_call" | custom-call | flops 4294967296 | bytes 10485768 | tf_op jit(solution)/shard_map/pallas_call | solution.py:43
  186.7 5.0 %shard_map.230 = bf16[1024,1024]{1,0:T(8,128)(2,1)} custom-call(s32[2]{0:T(128)} %pad_add_fusion.where, bf16[1024,512]{1,0:T(8,128)(2,1)} %get-tuple-element.106.active.refs_5_, bf16[1024,512]{1,0:T(8,128)(2,1)} %get-tuple-element.104.weights), custom_call_target="tpu_custom_call" | custom-call | flops 1073741824 | bytes 4194312 | tf_op jit(solution)/shard_map/pallas_call | solution.py:43
  196.4 6.3 %shard_map.231 = bf16[1024,512]{1,0:T(8,128)(2,1)} custom-call(s32[2]{0:T(128)} %pad_add_fusion.where, bf16[512,1152]{1,0:T(8,128)(2,1)} %constant_dynamic-update-slice_fusion.2.refs_0_, bf16[512,1152]{1,0:T(8,128)(2,1)} %collective-permute-done.18.refs_1_, bf16[512,1152]{1,0:T(8,128)(2,1)} %copy-done.35, bf16[512,1152]{1,0:T(8,128)(2,1)} %copy-done.36, ...), custom_call_target="tpu_custom_call" | custom-call | flops 2147483648 | bytes 7864328 | tf_op jit(solution)/shard_map/pallas_call | solution.py:43
  213.2 5.2 %shard_map.229 = f32[1024,1024]{1,0:T(8,128)} custom-call(s32[2]{0:T(128)} %pad_add_fusion.where, bf16[1024,512]{1,0:T(8,128)(2,1)} %get-tuple-element.103.active.refs_4_, bf16[1024,512]{1,0:T(8,128)(2,1)} %get-tuple-element.104.weights), custom_call_target="tpu_custom_call" | custom-call | flops 1073741824 | bytes 6291464 | tf_op jit(solution)/shard_map/pallas_call | solution.py:43
  226.4 5.8 %all-to-all-done.3 = bf16[4,256,512]{2,1,0:T(8,128)(2,1)} async-done(((bf16[4,256,512]{2,1,0:T(8,128)(2,1)}), bf16[4,256,512]{2,1,0:T(8,128)(2,1)}, u32[]{:S(2)}, u32[]{:S(2)}) %all-to-all-start.3) | async-done | bytes 1048608 | tf_op jit(solution)/shard_map/all_to_all | solution.py:441
  234.9 4.5 %collective-permute-done.27 = bf16[512,1024]{1,0:T(8,128)(2,1)} collective-permute-done((bf16[512,1024]{1,0:T(8,128)(2,1)}, bf16[512,1024]{1,0:T(8,128)(2,1)}, u32[]{:S(2)}, u32[]{:S(2)}) %collective-permute-start.27) | collective-permute-done | bytes 1048608 | tf_op jit(solution)/shard_map/ppermute | solution.py:72
  242.2 4.5 %collective-permute-done.34.refs_1_ = bf16[64,1024]{1,0:T(8,128)(2,1)S(1)} collective-permute-done((bf16[64,1024]{1,0:T(8,128)(2,1)S(1)}, bf16[64,1024]{1,0:T(8,128)(2,1)S(1)}, u32[]{:S(2)}, u32[]{:S(2)}) %collective-permute-start.34) | collective-permute-done | bytes 131104 | tf_op jit(solution)/shard_map/ppermute | solution.py:72
  246.7 5.7 %all-to-all-start.4 = ((bf16[4,256,512]{2,1,0:T(8,128)(2,1)}), bf16[4,256,512]{2,1,0:T(8,128)(2,1)}, u32[]{:S(2)}, u32[]{:S(2)}) async-start(bf16[4,256,512]{2,1,0:T(8,128)(2,1)} %bitcast.67), calls=%async_computation.4 | async-start | bytes 2097152 | tf_op jit(solution)/shard_map/all_to_all | solution.py:441
  255.3 5.9 %collective-permute-start.35 = (bf16[64,1024]{1,0:T(8,128)(2,1)}, bf16[64,1024]{1,0:T(8,128)(2,1)S(1)}, u32[]{:S(2)}, u32[]{:S(2)}) collective-permute-start(bf16[64,1024]{1,0:T(8,128)(2,1)} %get-tuple-element.114.refs_0_), channel_id=1, source_target_pairs={{0,2},{1,3},{2,0},{3,1},{4,6},{5,7},{6,4},{7,5},{8,10},{9,11},{10,... | collective-permute-start | bytes 393224 | tf_op jit(solution)/shard_map/ppermute | solution.py:57
  267.9 7.1 %shard_map.233 = (f32[512,768]{1,0:T(8,128)}, bf16[512,768]{1,0:T(8,128)(2,1)}, f32[128,1024]{1,0:T(8,128)}, bf16[128,1024]{1,0:T(8,128)(2,1)}) custom-call(s32[2]{0:T(128)} %pad_add_fusion.where, bf16[64,1024]{1,0:T(8,128)(2,1)} %get-tuple-element.114.refs_0_, bf16[64,1024]{1,0:T(8,128)(2,1)} %copy-done.29, bf16[64,1024]{1,0:T(8,128)(2,1)} %copy-done.31, ...), custom_call_target="tpu_custom_call" | custom-call | flops 805306368 | bytes 6424584 | tf_op jit(solution)/shard_map/pallas_call | solution.py:43
  279.5 6.1 %collective-permute-start.39 = (bf16[64,1024]{1,0:T(8,128)(2,1)S(1)}, bf16[64,1024]{1,0:T(8,128)(2,1)S(1)}, u32[]{:S(2)}, u32[]{:S(2)}) collective-permute-start(bf16[64,1024]{1,0:T(8,128)(2,1)S(1)} %slice.235), channel_id=1, source_target_pairs={{0,2},{1,3},{2,0},{3,1},{4,6},{5,7},{6,4},{7,5},{8,10},{9,11},{10,... | collective-permute-start | bytes 393224 | tf_op jit(solution)/shard_map/ppermute | solution.py:57
  303.7 5.2 %all-to-all-start.5 = ((bf16[4,256,512]{2,1,0:T(8,128)(2,1)}), bf16[4,256,512]{2,1,0:T(8,128)(2,1)S(1)}, u32[]{:S(2)}, u32[]{:S(2)}) async-start(bf16[4,256,512]{2,1,0:T(8,128)(2,1)} %bitcast.66), calls=%async_computation.5 | async-start | bytes 2097152 | tf_op jit(solution)/shard_map/all_to_all | solution.py:441
  335.3 10.7 %collective-permute-done.43 = bf16[256,768]{1,0:T(8,128)(2,1)S(1)} collective-permute-done((bf16[256,768]{1,0:T(8,128)(2,1)S(1)}, bf16[256,768]{1,0:T(8,128)(2,1)S(1)}, u32[]{:S(2)}, u32[]{:S(2)}) %collective-permute-start.43) | collective-permute-done | bytes 393248 | tf_op jit(solution)/shard_map/ppermute | solution.py:72
  (272 shorter events, 190.5 us)
Async XLA Ops:
  22.5 16.3 %collective-permute-start.5 = (bf16[576,512]{1,0:T(8,128)(2,1)S(1)}, bf16[576,512]{1,0:T(8,128)(2,1)S(1)}, u32[]{:S(2)}, u32[]{:S(2)}) collective-permute-start(bf16[576,512]{1,0:T(8,128)(2,1)S(1)} %pad_maximum_fusion.2.refs_0_), channel_id=1, source_target_pairs={{0,4},{1,9},{2,6},{3,11},{4,0},{5,13},{6,2},{7,15},{8,12},{9,1},{1... | collective-permute-start | bytes 1769480 | tf_op jit(solution)/shard_map/ppermute | solution.py:72
  38.7 53.8 %all-to-all-start = ((bf16[4,256,512]{2,1,0:T(8,128)(2,1)}), bf16[4,256,512]{2,1,0:T(8,128)(2,1)S(1)}, u32[]{:S(2)}, u32[]{:S(2)}) async-start(bf16[4,256,512]{2,1,0:T(8,128)(2,1)} %bitcast.7), calls=%async_computation | async-start | bytes 2097152 | tf_op jit(solution)/shard_map/all_to_all | solution.py:441
  42.4 29.3 %collective-permute-start.15 = (bf16[64,1152]{1,0:T(8,128)(2,1)S(1)}, bf16[64,1152]{1,0:T(8,128)(2,1)S(1)}, u32[]{:S(2)}, u32[]{:S(2)}) collective-permute-start(bf16[64,1152]{1,0:T(8,128)(2,1)S(1)} %fusion.4), channel_id=1, source_target_pairs={{0,16},{1,17},{2,18},{3,19},{4,20},{5,21},{6,22},{7,23},{8,24},{9,... | collective-permute-start | bytes 442376 | tf_op jit(solution)/shard_map/ppermute | solution.py:72
  51.7 21.5 %collective-permute-start.6 = (bf16[128,1024]{1,0:T(8,128)(2,1)}, bf16[128,1024]{1,0:T(8,128)(2,1)S(1)}, u32[]{:S(2)}, u32[]{:S(2)}) collective-permute-start(bf16[128,1024]{1,0:T(8,128)(2,1)} %get-tuple-element.79), channel_id=1, source_target_pairs={{0,1},{1,0},{2,3},{3,2},{4,5},{5,4},{6,7},{7,6},{8,9},{9,8},{10,11... | collective-permute-start | bytes 786440 | tf_op jit(solution)/shard_map/ppermute | solution.py:57
  71.8 22.0 %collective-permute-start.12 = (bf16[4,128,512]{2,1,0:T(8,128)(2,1)}, bf16[4,128,512]{2,1,0:T(8,128)(2,1)}, u32[]{:S(2)}, u32[]{:S(2)}) collective-permute-start(bf16[4,128,512]{2,1,0:T(8,128)(2,1)} %get-tuple-element.90), channel_id=1, source_target_pairs={{0,4},{4,0},{8,12},{12,8},{16,20},{20,16},{24,28},{28,24},{1,5},{5... | collective-permute-start | bytes 1572872 | tf_op jit(solution)/shard_map/ppermute | solution.py:57
  76.3 27.3 %collective-permute-start.11 = (bf16[4,128,512]{2,1,0:T(8,128)(2,1)}, bf16[4,128,512]{2,1,0:T(8,128)(2,1)}, u32[]{:S(2)}, u32[]{:S(2)}) collective-permute-start(bf16[4,128,512]{2,1,0:T(8,128)(2,1)} %get-tuple-element.87), channel_id=1, source_target_pairs={{0,4},{4,0},{8,12},{12,8},{16,20},{20,16},{24,28},{28,24},{1,5},{5... | collective-permute-start | bytes 1572872 | tf_op jit(solution)/shard_map/ppermute | solution.py:57
  83.8 25.8 %collective-permute-start.17 = (bf16[256,1152]{1,0:T(8,128)(2,1)S(1)}, bf16[256,1152]{1,0:T(8,128)(2,1)S(1)}, u32[]{:S(2)}, u32[]{:S(2)}) collective-permute-start(bf16[256,1152]{1,0:T(8,128)(2,1)S(1)} %pad_maximum_fusion.3), channel_id=1, source_target_pairs={{0,4},{1,3},{2,6},{3,1},{4,0},{5,7},{6,2},{7,5},{8,12},{9,11},{10,... | collective-permute-start | bytes 1769480 | tf_op jit(solution)/shard_map/ppermute | solution.py:72
  99.3 28.7 %all-to-all-start.2 = ((bf16[4,256,512]{2,1,0:T(8,128)(2,1)}), bf16[4,256,512]{2,1,0:T(8,128)(2,1)S(1)}, u32[]{:S(2)}, u32[]{:S(2)}) async-start(bf16[4,256,512]{2,1,0:T(8,128)(2,1)} %maximum_select_fusion.1), calls=%async_computation.2 | async-start | bytes 2097152 | tf_op jit(solution)/shard_map/all_to_all | solution.py:441
  110.5 28.1 %collective-permute-start.18 = (bf16[512,1152]{1,0:T(8,128)(2,1)}, bf16[512,1152]{1,0:T(8,128)(2,1)}, u32[]{:S(2)}, u32[]{:S(2)}) collective-permute-start(bf16[512,1152]{1,0:T(8,128)(2,1)} %constant_dynamic-update-slice_fusion.2.refs_0_), channel_id=1, source_target_pairs={{0,2},{1,5},{2,0},{3,7},{4,6},{5,1},{6,4},{7,3},{8,10},{9,13},{10,... | collective-permute-start | bytes 3538952 | tf_op jit(solution)/shard_map/ppermute | solution.py:72
  117.6 26.8 %collective-permute-start.14 = (bf16[512,1024]{1,0:T(8,128)(2,1)}, bf16[512,1024]{1,0:T(8,128)(2,1)}, u32[]{:S(2)}, u32[]{:S(2)}) collective-permute-start(bf16[512,1024]{1,0:T(8,128)(2,1)} %constant_dynamic-update-slice_fusion.refs_0_), channel_id=1, source_target_pairs={{0,2},{1,5},{2,0},{3,7},{4,6},{5,1},{6,4},{7,3},{8,10},{9,13},{10,... | collective-permute-start | bytes 3145736 | tf_op jit(solution)/shard_map/ppermute | solution.py:72
  128.1 30.8 %all-to-all-start.1 = ((bf16[4,256,512]{2,1,0:T(8,128)(2,1)}), bf16[4,256,512]{2,1,0:T(8,128)(2,1)S(1)}, u32[]{:S(2)}, u32[]{:S(2)}) async-start(bf16[4,256,512]{2,1,0:T(8,128)(2,1)} %maximum_select_fusion), calls=%async_computation.1 | async-start | bytes 2097152 | tf_op jit(solution)/shard_map/all_to_all | solution.py:441
  131.8 16.2 %collective-permute-start.19 = (bf16[512,1152]{1,0:T(8,128)(2,1)}, bf16[512,1152]{1,0:T(8,128)(2,1)S(1)}, u32[]{:S(2)}, u32[]{:S(2)}) collective-permute-start(bf16[512,1152]{1,0:T(8,128)(2,1)} %constant_dynamic-update-slice_fusion.2.refs_0_), channel_id=1, source_target_pairs={{0,1},{1,0},{2,3},{3,2},{4,5},{5,4},{6,7},{7,6},{8,9},{9,8},{10,11... | collective-permute-start | bytes 3538952 | tf_op jit(solution)/shard_map/ppermute | solution.py:57
  138.7 20.1 %collective-permute-start.21 = (bf16[512,1024]{1,0:T(8,128)(2,1)}, bf16[512,1024]{1,0:T(8,128)(2,1)}, u32[]{:S(2)}, u32[]{:S(2)}) collective-permute-start(bf16[512,1024]{1,0:T(8,128)(2,1)} %constant_dynamic-update-slice_fusion.refs_0_), channel_id=1, source_target_pairs={{0,1},{1,0},{2,3},{3,2},{4,5},{5,4},{6,7},{7,6},{8,9},{9,8},{10,11... | collective-permute-start | bytes 3145736 | tf_op jit(solution)/shard_map/ppermute | solution.py:57
  168.8 23.4 %collective-permute-start.24 = (bf16[1024,1024]{1,0:T(8,128)(2,1)}, bf16[1024,1024]{1,0:T(8,128)(2,1)S(1)}, u32[]{:S(2)}, u32[]{:S(2)}) collective-permute-start(bf16[1024,1024]{1,0:T(8,128)(2,1)} %get-tuple-element.108), channel_id=1, source_target_pairs={{0,1},{1,0},{2,3},{3,2},{4,5},{5,4},{6,7},{7,6},{8,9},{9,8},{10,11... | collective-permute-start | bytes 6291464 | tf_op jit(solution)/shard_map/ppermute | solution.py:57
  191.7 26.7 %collective-permute-start.23 = (bf16[1024,1024]{1,0:T(8,128)(2,1)}, bf16[1024,1024]{1,0:T(8,128)(2,1)}, u32[]{:S(2)}, u32[]{:S(2)}) collective-permute-start(bf16[1024,1024]{1,0:T(8,128)(2,1)} %shard_map.230), channel_id=1, source_target_pairs={{0,1},{1,0},{2,3},{3,2},{4,5},{5,4},{6,7},{7,6},{8,9},{9,8},{10,11... | collective-permute-start | bytes 6291464 | tf_op jit(solution)/shard_map/ppermute | solution.py:57
  202.7 29.6 %all-to-all-start.3 = ((bf16[4,256,512]{2,1,0:T(8,128)(2,1)}), bf16[4,256,512]{2,1,0:T(8,128)(2,1)}, u32[]{:S(2)}, u32[]{:S(2)}) async-start(bf16[4,256,512]{2,1,0:T(8,128)(2,1)} %bitcast.73), calls=%async_computation.3 | async-start | bytes 2097152 | tf_op jit(solution)/shard_map/all_to_all | solution.py:441
  241.8 19.4 %collective-permute-start.28 = (bf16[256,1024]{1,0:T(8,128)(2,1)}, bf16[256,1024]{1,0:T(8,128)(2,1)S(1)}, u32[]{:S(2)}, u32[]{:S(2)}) collective-permute-start(bf16[256,1024]{1,0:T(8,128)(2,1)} %slice.229), channel_id=1, source_target_pairs={{0,4},{1,3},{2,6},{3,1},{4,0},{5,7},{6,2},{7,5},{8,12},{9,11},{10,... | collective-permute-start | bytes 1572872 | tf_op jit(solution)/shard_map/ppermute | solution.py:72
  246.7 46.1 %all-to-all-start.4 = ((bf16[4,256,512]{2,1,0:T(8,128)(2,1)}), bf16[4,256,512]{2,1,0:T(8,128)(2,1)}, u32[]{:S(2)}, u32[]{:S(2)}) async-start(bf16[4,256,512]{2,1,0:T(8,128)(2,1)} %bitcast.67), calls=%async_computation.4 | async-start | bytes 2097152 | tf_op jit(solution)/shard_map/all_to_all | solution.py:441
  275.2 23.9 %collective-permute-start.50 = (bf16[4,128,512]{2,1,0:T(8,128)(2,1)S(1)}, bf16[4,128,512]{2,1,0:T(8,128)(2,1)S(1)}, u32[]{:S(2)}, u32[]{:S(2)}) collective-permute-start(bf16[4,128,512]{2,1,0:T(8,128)(2,1)S(1)} %copy-done.19), channel_id=1, source_target_pairs={{0,4},{4,0},{8,12},{12,8},{16,20},{20,16},{24,28},{28,24},{1,5},{5... | collective-permute-start | bytes 1572872 | tf_op jit(solution)/shard_map/ppermute | solution.py:57
  275.2 19.9 %collective-permute-start.40 = (bf16[512,768]{1,0:T(8,128)(2,1)}, bf16[512,768]{1,0:T(8,128)(2,1)S(1)}, u32[]{:S(2)}, u32[]{:S(2)}) collective-permute-start(bf16[512,768]{1,0:T(8,128)(2,1)} %get-tuple-element.122), channel_id=1, source_target_pairs={{0,4},{1,9},{2,6},{3,11},{4,0},{5,13},{6,2},{7,15},{8,12},{9,1},{1... | collective-permute-start | bytes 2359304 | tf_op jit(solution)/shard_map/ppermute | solution.py:72
  288.5 20.5 %collective-permute-start.31 = (bf16[64,1024]{1,0:T(8,128)(2,1)S(1)}, bf16[64,1024]{1,0:T(8,128)(2,1)S(1)}, u32[]{:S(2)}, u32[]{:S(2)}) collective-permute-start(bf16[64,1024]{1,0:T(8,128)(2,1)S(1)} %fusion.2), channel_id=1, source_target_pairs={{0,2},{1,3},{2,0},{3,1},{4,6},{5,7},{6,4},{7,5},{8,10},{9,11},{10,... | collective-permute-start | bytes 393224 | tf_op jit(solution)/shard_map/ppermute | solution.py:57
  303.7 44.1 %all-to-all-start.5 = ((bf16[4,256,512]{2,1,0:T(8,128)(2,1)}), bf16[4,256,512]{2,1,0:T(8,128)(2,1)S(1)}, u32[]{:S(2)}, u32[]{:S(2)}) async-start(bf16[4,256,512]{2,1,0:T(8,128)(2,1)} %bitcast.66), calls=%async_computation.5 | async-start | bytes 2097152 | tf_op jit(solution)/shard_map/all_to_all | solution.py:441
  313.2 32.8 %collective-permute-start.43 = (bf16[256,768]{1,0:T(8,128)(2,1)S(1)}, bf16[256,768]{1,0:T(8,128)(2,1)S(1)}, u32[]{:S(2)}, u32[]{:S(2)}) collective-permute-start(bf16[256,768]{1,0:T(8,128)(2,1)S(1)} %slice.231), channel_id=1, source_target_pairs={{0,8},{1,17},{2,10},{3,19},{4,12},{5,21},{6,14},{7,23},{8,0},{9,25... | collective-permute-start | bytes 1179656 | tf_op jit(solution)/shard_map/ppermute | solution.py:72
  331.2 16.1 %collective-permute-start.47 = (f32[1,2,128]{2,1,0:T(2,128)S(1)}, f32[1,2,128]{2,1,0:T(2,128)S(1)}, u32[]{:S(2)}, u32[]{:S(2)}) collective-permute-start(f32[1,2,128]{2,1,0:T(2,128)S(1)} %slice.195), channel_id=1, source_target_pairs={{0,16},{4,20},{8,24},{12,28},{16,0},{20,4},{24,8},{28,12},{1,17},{... | collective-permute-start | bytes 3080 | tf_op jit(solution)/shard_map/ppermute | solution.py:57
  (70 other events, 579.5 us)

commit v4 on v3

--- a/solution.py
+++ b/solution.py
@@ -14,7 +14,8 @@
 THETA = 10000.0
 MASKED = -1e30
 LANES = 128
-LIMIT = 56 * 1024 * 1024
+LIMIT = 24 * 1024 * 1024
+LARGE = 56 * 1024 * 1024
 
 LOW = jnp.bfloat16
 FULL = jnp.float32
@@ -31,7 +32,7 @@
     return jax.ShapeDtypeStruct(dims, dtype)
 
 
-def call(body, outs, *args, grid=None, in_specs=None, out_specs=None, scratch=(), flops=0):
+def call(body, outs, *args, grid=None, in_specs=None, out_specs=None, scratch=(), flops=0, limit=LIMIT):
     size = sum(a.size * a.dtype.itemsize for a in args)
     size += sum(o.size * jnp.dtype(o.dtype).itemsize for o in outs)
     whole = pl.BlockSpec(memory_space=pltpu.VMEM)
@@ -46,7 +47,7 @@
         in_specs=[pl.BlockSpec(memory_space=pltpu.SMEM)] + list(in_specs),
         out_specs=list(out_specs),
         scratch_shapes=list(scratch),
-        compiler_params=pltpu.CompilerParams(vmem_limit_bytes=LIMIT),
+        compiler_params=pltpu.CompilerParams(vmem_limit_bytes=limit),
         cost_estimate=pl.CostEstimate(flops=flops, bytes_accessed=size, transcendentals=0),
         **extra,
     )(*args)
@@ -129,15 +130,15 @@
             block = down[(k * own if replicas == 1 else 0) + j]
             down_out[0, k, :, at] = (block.T if turn else block).astype(LOW)
             place = ((side ^ k) * own if replicas == 1 else 0) + j
-            for source, out in ((gate, sided[k]), (up, sided[2 + k])):
-                out[0, :, at] = source[place].astype(LOW)
+            sided[k][0, :, at] = gate[place].astype(LOW)
+            up_at = slice((own + j) * hid, (own + j + 1) * hid)
+            sided[k][0, :, up_at] = up[place].astype(LOW)
 
 
 def attend_body(orders, n, part, pitch, q_cols, k_cols, rows, order, where, *refs):
     sources = refs[:n]
     tokens, gain_in, doc_row, doc_col, cosine, sine = refs[n : n + 6]
-    weights, hidden, qkv_out, mixed_out, gain = refs[n + 6 : n + 11]
-    mixed = refs[n + 11]
+    weights, hidden, qkv_out, mixed_out, gain, kept, sent, mixed = refs[n + 6 :]
     place_rows(weights, sources, orders, where, part, pitch)
     if part % LANES == 0:
         count = len(orders[0]) // n
@@ -151,7 +152,7 @@
     scale = lax.rsqrt(jnp.mean(x * x, axis=1, keepdims=True) + EPS)
     first = (x * scale * gain[0:1, :]).astype(LOW)
     hidden[...] = first
-    qkv = mul(first, weights[...])
+    qkv = mul(first, weights[:, : q_cols + 2 * k_cols])
     turned = rotate(qkv[:, : q_cols + k_cols], cosine[...], sine[...]).astype(LOW)
     values = qkv[:, q_cols + k_cols :].astype(LOW)
     qkv_out[:, : q_cols + k_cols] = turned
@@ -169,14 +170,8 @@
     for k, m in enumerate(order):
         at = pl.multiple_of((where[1] ^ m) * rows, rows)
         mixed_out[k * rows : (k + 1) * rows, :] = mixed[pl.ds(at, rows), :]
-
-
-def branch_body(orders, n, part, where, *refs):
-    sources = refs[:n]
-    mixed, weights, kept, sent = refs[n:]
-    place_rows(weights, sources, orders, where, part, part)
+    product = mul(mixed_out[...], weights[:, q_cols + 2 * k_cols :], COLS_ON_COLS)
     half = kept.shape[0]
-    product = mul(mixed[...], weights[...], COLS_ON_COLS)
     kept[...] = product[:half]
     sent[...] = product[half:].astype(LOW)
 
@@ -227,24 +222,22 @@
 
 def expert_body(n_piece, tiles, own, hid, where, *refs):
     rows = refs[:n_piece]
-    gate_rows, up_rows, gate, back, grad_hidden, active_out, grad_gate, grad_up, buffer = refs[
-        n_piece:
-    ]
+    weights, gate, back, grad_hidden, active_out, grad_both, buffer = refs[n_piece:]
     pick_tile(buffer, rows, tiles, pl.program_id(0))
-    gate_pre = mul(buffer[...], gate_rows[...])
-    up_pre = mul(buffer[...], up_rows[...])
+    wide = own * hid
+    both = mul(buffer[...], weights[...])
     for j in range(own):
         at = slice(j * hid, (j + 1) * hid)
-        pre, up = gate_pre[:, at], up_pre[:, at]
+        up_at = slice(wide + j * hid, wide + (j + 1) * hid)
+        pre, up = both[:, at], both[:, up_at]
         squash = 1.0 / (1.0 + jnp.exp(-pre))
         silu = pre * squash
         active = (silu * up).astype(LOW).astype(FULL)
         active_out[:, at] = (active * gate[:, j : j + 1]).astype(LOW)
         d = back[:, at]
-        grad_gate[:, at] = (d * up * squash * (1.0 + pre * (1.0 - squash))).astype(LOW)
-        grad_up[:, at] = (d * silu).astype(LOW)
-    product = mul(grad_gate[...], gate_rows[...], COLS_ON_COLS)
-    product = product + mul(grad_up[...], up_rows[...], COLS_ON_COLS)
+        grad_both[:, at] = (d * up * squash * (1.0 + pre * (1.0 - squash))).astype(LOW)
+        grad_both[:, up_at] = (d * silu).astype(LOW)
+    product = mul(grad_both[...], weights[...], COLS_ON_COLS)
     grad_hidden[...] = product.astype(grad_hidden.dtype)
 
 
@@ -252,18 +245,22 @@
     out[...] = mul(active[...], weights[...], COLS_ON_COLS).astype(out.dtype)
 
 
-def weight_grad_body(n_source, where, *refs):
+def weight_grad_body(n_source, part, where, *refs):
     sources = refs[:n_source]
-    column = refs[-1]
-    count = (len(refs) - 1 - n_source) // 3
-    rights, outs = refs[n_source : n_source + 2 * count], refs[n_source + 2 * count : -1]
-    size = sources[0].shape[0]
+    kept, sent, *outs, column, total = refs[n_source:]
+    half, size = kept.shape[0], sources[0].shape[0]
     for k, source in enumerate(sources):
         column[k * size : (k + 1) * size, :] = source[...]
-    half = column.shape[0] // 2
-    for k, out in enumerate(outs):
-        total = mul(column[:half], rights[2 * k][...], ROWS_ON_ROWS)
-        out[...] = (total + mul(column[half:], rights[2 * k + 1][...], ROWS_ON_ROWS)).astype(LOW)
+    product = mul(column[:half], kept[...], ROWS_ON_ROWS)
+    total[...] = (product + mul(column[half:], sent[...], ROWS_ON_ROWS)).astype(LOW)
+    for z in range(total.shape[0] // (2 * part)):
+        for k in range(2):
+            if len(outs) == 2:
+                at = pl.multiple_of((2 * z + ((where[0] & 1) ^ k)) * part, part)
+                outs[k][z] = total[pl.ds(at, part), :]
+            else:
+                at = (2 * z + k) * part
+                outs[0][z, k] = total[at : at + part, :]
 
 
 def middle_back_body(where, *refs):
@@ -283,13 +280,11 @@
 
 def attend_back_body(n_piece, q_cols, k_cols, rows, part, order, orders, where, *refs):
     pieces = refs[:n_piece]
-    mixed, out_weights, qkv_in, doc_row, doc_col, cosine, sine, hidden, weights = refs[
-        n_piece : n_piece + 9
-    ]
-    kept, sent, first_kept, first_sent, branch, natural, grad_qkv, grads = refs[n_piece + 9 :]
+    mixed, qkv_in, doc_row, doc_col, cosine, sine, hidden, weights = refs[n_piece : n_piece + 8]
+    kept, sent, first_kept, first_sent, branch, natural, grad_qkv, grads = refs[n_piece + 8 :]
     for k in range(n_piece):
         branch[k * rows : (k + 1) * rows, :] = pieces[k][...]
-    grad_mixed = mul(branch[...], out_weights[...]).astype(LOW)
+    grad_mixed = mul(branch[...], weights[:, q_cols + 2 * k_cols :]).astype(LOW)
     for k, m in enumerate(order):
         at = pl.multiple_of((where[1] ^ m) * rows, rows)
         natural[pl.ds(at, rows), :q_cols] = grad_mixed[k * rows : (k + 1) * rows]
@@ -330,7 +325,7 @@
     for k, m in enumerate(order):
         at = pl.multiple_of((where[1] ^ m) * rows, rows)
         natural[k * rows : (k + 1) * rows, :total] = grad_qkv[pl.ds(at, rows), :]
-    product = mul(natural[:, :total], weights[...], COLS_ON_COLS)
+    product = mul(natural[:, :total], weights[:, :total], COLS_ON_COLS)
     half = first_kept.shape[0]
     first_kept[...] = product[:half]
     first_sent[...] = product[half:].astype(LOW)
@@ -349,14 +344,16 @@
     out[rows:] = jnp.where(line == 0, attn_part, jnp.where(line == 1, moe_part[...], 0.0))
 
 
-def unpack_body(own, hid, replicas, turn, where, this, other, out):
-    side = where[0] & 1
-    for j in range(own):
-        pieces = [source[0, :, j * hid : (j + 1) * hid].astype(FULL) for source in (this, other)]
+def unpack_body(own, hid, replicas, turn, where, source, *outs):
+    part = source.shape[0] // 2
+    for k in range(own * len(outs)):
+        out, j = outs[k // own], k % own
+        cols = slice(k * hid, (k + 1) * hid)
+        pieces = [source[i * part : (i + 1) * part, cols].astype(FULL) for i in range(2)]
         pieces = [piece.T for piece in pieces] if turn else pieces
         if replicas == 1:
-            out[side * own + j] = pieces[0]
-            out[(1 - side) * own + j] = pieces[1]
+            out[j] = pieces[0]
+            out[own + j] = pieces[1]
         else:
             first = 2 * pl.program_id(0) % replicas == 0
             out[j] = pieces[0] + pieces[1] + jnp.where(first, 0.0, out[j])
@@ -393,30 +390,27 @@
     wide = own_experts * hidden
 
     pad = 16
-    gain_rows = jnp.stack([gain_attn, gain_moe])
-    gain_rows = jnp.pad(gain_rows, ((0, pad - 2), (0, qkv_cols - part)))
-    qkv_shard = jnp.concatenate(
-        [
-            jnp.concatenate([w_query, key_projection, value_projection], axis=1),
-            gain_rows,
-        ],
-        axis=0,
-    ).astype(LOW)
-    out_shard = w_out.T.astype(LOW)
+    all_cols = qkv_cols + q_cols
+    gain_rows = jnp.pad(jnp.stack([gain_attn, gain_moe]), ((0, pad - 2), (0, all_cols - part)))
+    shard = jnp.concatenate([w_query, key_projection, value_projection, w_out.T], axis=1)
+    shard = jnp.concatenate([shard, gain_rows]).astype(LOW)
 
     e_bits, t_bits = bits_of(n_e), bits_of(n_t)
     even_bits, odd_bits = e_bits, e_bits[-1:] + e_bits[:-1]
     orders = order_of(even_bits), order_of(odd_bits)
     by_parity = [(("expert", a), ("expert", b)) for a, b in zip(even_bits, odd_bits)]
 
-    def every(shard, before_last):
-        came = []
-        for even, odd in by_parity[:-1]:
+    def every(shard, ready, later):
+        came, sends = [], []
+        for k, (even, odd) in enumerate(by_parity):
+            if k == 1:
+                shard, *ready = lax.optimization_barrier((shard, *ready))
+            if k == 2:
+                shard = after(shard, later)
+            sends.append(shard)
             came.append(swap_by_parity(shard, even, odd))
             shard = jnp.concatenate([shard, came[-1]])
-        shard, *before_last = lax.optimization_barrier((shard, *before_last))
-        came.append(swap_by_parity(shard, *by_parity[-1]))
-        return [shard, came[-1]], came, before_last
+        return [sends[-1], came[-1]], came, sends, ready
 
     pairs = n_e // 2
     turn = part % LANES == 0
@@ -425,14 +419,14 @@
         (pair_experts,) + dims, lambda z: (2 * z // max(2, replicas), 0, 0)
     )
     sources = [w_gate, w_up, w_down if turn else w_down.transpose(0, 2, 1)]
-    sided = pl.BlockSpec((1, part, wide), lambda z: (z, 0, 0))
+    sided = pl.BlockSpec((1, part, 2 * wide), lambda z: (z, 0, 0))
     packed = call(
         functools.partial(pack_body, own_experts, hidden, replicas, turn),
-        [shape((pairs, 2, part, wide), LOW)] + [shape((pairs, part, wide), LOW)] * 4,
+        [shape((pairs, 2, part, wide), LOW)] + [shape((pairs, part, 2 * wide), LOW)] * 2,
         where, *sources,
         grid=(pairs,),
         in_specs=[at_pair(w.shape[1:]) for w in sources],
-        out_specs=[pl.BlockSpec((1, 2, part, wide), lambda z: (z, 0, 0, 0))] + [sided] * 4,
+        out_specs=[pl.BlockSpec((1, 2, part, wide), lambda z: (z, 0, 0, 0))] + [sided] * 2,
     )
     side = e & 1
     lines = [[z * 2 + k for z in range(n_e // 2)] for k in range(2)]
@@ -442,9 +436,13 @@
             blocks, "expert", 0, 0, tiled=True, axis_index_groups=lines
         )
 
-    def sides(blocks):
+    def from_neighbour(blocks, *earlier):
+        cols = blocks.shape[-1]
+        blocks = along(after(blocks.reshape(pairs, 2 * part, cols), *earlier))
+        blocks = blocks.reshape(pairs, 2, part, cols)
         this = lax.dynamic_index_in_dim(blocks, side, 1, keepdims=False)
-        return this, lax.dynamic_index_in_dim(blocks, 1 - side, 1, keepdims=False)
+        other = lax.dynamic_index_in_dim(blocks, 1 - side, 1, keepdims=False)
+        return this, swap(other, "expert", 1)
 
     def to_neighbour(this, other, *earlier):
         got = swap(after(other, *earlier), "expert", 1)
@@ -452,20 +450,33 @@
             side == 0, jnp.concatenate([this, got], axis=1), jnp.concatenate([got, this], axis=1)
         )
 
-    def from_neighbour(blocks, *earlier):
-        blocks = along(after(blocks.reshape(n_e // 2, 2 * part, wide), *earlier))
-        this, other = sides(blocks.reshape(n_e // 2, 2, part, wide))
-        return this, swap(other, "expert", 1)
-
-    qkv_arrays, qkv_came, packed = every(qkv_shard, packed)
-    out_arrays, _, _ = every(after(out_shard, qkv_came[0]), ())
-    down_this, down_other = from_neighbour(packed[0], qkv_came[-1])
-    near = [to_neighbour(*packed[k : k + 2], qkv_came[-1]) for k in (1, 3)]
+    e_path = [("expert", b) for b in bits_of(n_e, first_bit)]
+    t_path = [("tensor", b) for b in t_bits]
+    even_path, odd_path = e_path + t_path[:-1], e_path[:-1] + t_path[:-1] + e_path[-1:]
+    path = list(zip(even_path, odd_path))
+    last = t_path[-1]
+
+    own = t * rows
+    grad_rows = lax.dynamic_slice_in_dim(cotangent, own, rows, 0)
+    gate_rows = lax.dynamic_slice_in_dim(gates, own, rows, 0)
+    route_rows = lax.dynamic_slice_in_dim(routes, own, rows, 0)
+    gate_high = gate_rows.astype(LOW)
+    gate_rest = (gate_rows - gate_high.astype(FULL)).astype(LOW)
+    extra = jnp.concatenate([route_rows.astype(LOW), gate_high, gate_rest], axis=1)
+    extra = jnp.pad(extra, ((0, 0), (0, LANES - 3 * TOP)))
+    grad_steps = [jnp.concatenate([grad_rows, extra], axis=1)]
+    grad_first = swap_by_parity(grad_steps[0], *path[0])
+    attn_arrays, attn_came, attn_sends, packed = every(shard, packed, grad_first)
+    grad_steps.append(jnp.concatenate([grad_steps[0], grad_first]))
+    grad_second = swap_by_parity(after(grad_steps[1], attn_sends[-1]), *path[1])
+    grad_steps.append(jnp.concatenate([grad_steps[1], grad_second]))
+    down_this, down_other = from_neighbour(packed[0], attn_came[-1])
+    near = to_neighbour(*packed[1:], attn_came[-1])
     pitch = part + pad
     gains = jnp.zeros((pad, LANES), FULL)
     if part % LANES:
         held = jnp.concatenate(
-            [a.reshape(-1, pitch, qkv_cols)[:, part:, :part] for a in qkv_arrays]
+            [a.reshape(-1, pitch, all_cols)[:, part:, :part] for a in attn_arrays]
         ).astype(FULL)
         on_even = [position_in(e ^ k, even_bits) for k in range(n_e)]
         on_odd = [position_in(e ^ k, odd_bits) for k in range(n_e)]
@@ -477,43 +488,15 @@
             axis=1,
         )
 
-    e_path = [("expert", b) for b in bits_of(n_e, first_bit)]
-    t_path = [("tensor", b) for b in t_bits]
-    even_path, odd_path = e_path + t_path[:-1], e_path[:-1] + t_path[:-1] + e_path[-1:]
-    path = list(zip(even_path, odd_path))
-    last = t_path[-1]
-
-    def gather_tokens(field, ties=()):
-        came = []
-        for even, odd in path:
-            if len(came) == 2 and ties:
-                field = after(field, *ties)
-            came.append(swap_by_parity(field, even, odd))
-            pieces = [field, came[-1]]
-            field = jnp.concatenate(pieces)
-        return pieces + [swap(p, *last) for p in pieces], came
-
-    def scatter_tokens(kept, sent, ties):
-        total = kept + swap(sent, *last).astype(FULL)
-        came = []
-        for even, odd in reversed(path):
-            half = total.shape[0] // 2
-            kept, sent = total[:half], total[half:].astype(LOW)
-            if len(came) < len(ties) and ties[len(came)]:
-                sent = after(sent, *ties[len(came)])
-            came.append(swap_by_parity(sent, even, odd))
-            total = kept + came[-1].astype(FULL)
-        return kept, came
-
-    own = t * rows
-    grad_rows = lax.dynamic_slice_in_dim(cotangent, own, rows, 0)
-    gate_rows = lax.dynamic_slice_in_dim(gates, own, rows, 0)
-    route_rows = lax.dynamic_slice_in_dim(routes, own, rows, 0)
-    gate_high = gate_rows.astype(LOW)
-    gate_rest = (gate_rows - gate_high.astype(FULL)).astype(LOW)
-    extra = jnp.concatenate([route_rows.astype(LOW), gate_high, gate_rest], axis=1)
-    extra = jnp.pad(extra, ((0, 0), (0, LANES - 3 * TOP)))
-    grad_pieces, _ = gather_tokens(after(jnp.concatenate([grad_rows, extra], axis=1), out_arrays[-1]))
+    def add_halves(kept, got):
+        half = got.shape[0] // 2
+        return kept[:half] + got[:half].astype(FULL), (
+            kept[half:] + got[half:].astype(FULL)
+        ).astype(LOW)
+
+    def scatter_stage(kept, sent, k):
+        got = swap_by_parity(sent, *path[-1 - k])
+        return (kept, got) if k == len(path) - 1 else add_halves(kept, got)
 
     documents = segments[0]
     doc_row, doc_col = documents[None, :], documents[:, None]
@@ -527,30 +510,21 @@
     sine = jnp.sin(angle) * jnp.where(lane % HEAD_SIZE < HEAD_SIZE // 2, -1.0, 1.0)[None, :]
     t_masks = t_bits[::-1]
     order = order_of(t_bits)
-    weights, first_hidden, qkv, mixed, gains = call(
+    weights, first_hidden, qkv, mixed, gains, kept, sent = call(
         functools.partial(attend_body, orders, 2, part, pitch, q_cols, k_cols, rows, order),
         [
-            shape((width, qkv_cols), LOW),
+            shape((width, all_cols), LOW),
             shape((length, width), LOW),
             shape((length, qkv_cols), LOW),
             shape((length, q_cols), LOW),
             shape((pad, width), FULL),
-        ],
-        where, *qkv_arrays, tokens, gains, doc_row, doc_col, cosine, sine,
-        scratch=[pltpu.VMEM((length, q_cols), LOW)],
-        flops=2 * length * (width * qkv_cols + 2 * length * q_cols),
-    )
-    out_weights, kept, sent = call(
-        functools.partial(branch_body, orders, 2, part),
-        [
-            shape((width, q_cols), LOW),
             shape((length // 2, width), FULL),
             shape((length // 2, width), LOW),
         ],
-        where, *out_arrays, mixed,
-        flops=2 * length * width * q_cols,
-    )
-
+        where, *attn_arrays[:-1], after(attn_arrays[-1], grad_second), tokens, gains, doc_row, doc_col, cosine, sine,
+        scratch=[pltpu.VMEM((length, q_cols), LOW)],
+        flops=2 * length * (width * qkv_cols + 2 * length * q_cols),
+    )
     def all_rows(field):
         size = field.shape[0]
         for b in t_bits:
@@ -565,13 +539,33 @@
             kept, sent = total[:half], total[half:].astype(LOW)
         return kept, swap(sent, "tensor", t_masks[-1])
 
+    grad_third = swap_by_parity(after(grad_steps[-1], attn_arrays[-1]), *path[2])
     kept, got = scatter_rows(kept, sent)
     middle, second_hidden = call(
         functools.partial(middle_body, rows),
         [shape((rows, width), FULL), shape((rows, width), LOW)],
-        where, tokens, kept, got, gains,
-    )
-
+        where, tokens, kept, after(got, grad_third, down_this), gains,
+    )
+
+    hidden_field = second_hidden
+    for k, (even, odd) in enumerate(path):
+        if k == 1:
+            hidden_field = after(hidden_field, near, *([grad_got] if len(path) > 3 else []))
+        if k == 2:
+            hidden_field = after(hidden_field, down_other)
+        hidden_got = swap_by_parity(hidden_field, even, odd)
+        if k == 1:
+            gate_up_rows = along(after(near, hidden_got)).reshape(width, 2 * wide)
+        hidden_pieces = [hidden_field, hidden_got]
+        hidden_field = jnp.concatenate(hidden_pieces)
+        if k == 0:
+            grad_field, grad_got = grad_steps[-1], grad_third
+            for k in range(3, len(path)):
+                grad_field = jnp.concatenate([grad_field, grad_got])
+                grad_got = swap_by_parity(after(grad_field, second_hidden), *path[k])
+            grad_pieces = [grad_field, grad_got]
+    hidden_pieces = hidden_pieces + [swap(p, *last) for p in hidden_pieces]
+    grad_pieces = grad_pieces + [swap(p, *last) for p in grad_pieces]
     size = 256
     total_rows = sum(p.shape[0] for p in grad_pieces)
     steps = total_rows // size
@@ -599,10 +593,7 @@
         out_specs=[tile(LANES), tile(wide), pl.BlockSpec((width, wide), lambda i: (0, 0))],
         scratch=[pltpu.VMEM((size, width + LANES), LOW)],
         flops=2 * total_rows * width * wide,
-    )
-    hidden_pieces, hidden_came = gather_tokens(second_hidden, [down_other, *near])
-    gate_rows, up_rows = (
-        along(after(p, hidden_came[1])).reshape(width, wide) for p in near
+        limit=LARGE,
     )
     half = steps // 2
 
@@ -614,40 +605,41 @@
             [
                 shape((half * size, width), out_type),
                 shape((half * size, wide), LOW),
-                shape((half * size, wide), LOW),
-                shape((half * size, wide), LOW),
+                shape((half * size, 2 * wide), LOW),
             ],
-            where, *chosen, gate_rows, up_rows, gate_table, back,
+            where, *chosen, gate_up_rows, gate_table, back,
             grid=(half,),
             in_specs=specs
-            + [whole(gate_rows), whole(up_rows), later(LANES), later(wide)],
-            out_specs=[tile(width), tile(wide), tile(wide), tile(wide)],
+            + [whole(gate_up_rows), later(LANES), later(wide)],
+            out_specs=[tile(width), tile(wide), tile(2 * wide)],
             scratch=[pltpu.VMEM((size, width), LOW)],
             flops=2 * half * size * width * 4 * wide,
+            limit=LARGE,
         )
 
-    sent_hidden, *sent_right = experts(hidden_pieces[2:], half, LOW)
-    kept_hidden, *kept_right = experts(hidden_pieces[:2], 0, FULL)
+    sent_hidden, sent_active, sent_both = experts(hidden_pieces[2:], half, LOW)
+    kept_hidden, kept_active, kept_both = experts(hidden_pieces[:2], 0, FULL)
 
     block = 256
     column = lambda a: pl.BlockSpec((a.shape[0], block), lambda i: (0, i))
 
-    def weight_grad(sources, chosen):
-        rights = [side[k] for k in chosen for side in (kept_right, sent_right)]
+    def weight_grad(sources, kept, sent, sided):
+        cols = kept.shape[1]
+        dims = [(part, cols)] * 2 if sided else [(2, part, cols)]
+        count = block // (2 * part)
         return call(
-            functools.partial(weight_grad_body, len(sources)),
-            [shape((width, wide), LOW)] * len(chosen),
-            where, *sources, *rights,
+            functools.partial(weight_grad_body, len(sources), part),
+            [shape((pairs,) + d, LOW) for d in dims],
+            where, *sources, kept, sent,
             grid=(width // block,),
-            in_specs=[column(a) for a in sources] + [whole(a) for a in rights],
-            out_specs=[pl.BlockSpec((block, wide), lambda i: (i, 0))] * len(chosen),
-            scratch=[pltpu.VMEM((total_rows, block), LOW)],
-            flops=2 * total_rows * width * wide * len(chosen),
+            in_specs=[column(a) for a in sources] + [whole(kept), whole(sent)],
+            out_specs=[pl.BlockSpec((count,) + d, lambda i, n=len(d): (i,) + (0,) * n) for d in dims],
+            scratch=[pltpu.VMEM((total_rows, block), LOW), pltpu.VMEM((block, cols), LOW)],
+            flops=2 * total_rows * width * cols,
+            limit=LARGE,
         )
 
-    (down_grad,) = weight_grad(grad_pieces, [0])
-    gate_grad, up_grad = weight_grad(hidden_pieces, [1, 2])
-    down_back = from_neighbour(down_grad)
+    hidden_kept, hidden_sent = add_halves(kept_hidden, swap(sent_hidden, *last))
     def down(active, out_type):
         return call(
             out_body,
@@ -657,31 +649,41 @@
             in_specs=[tile(wide), whole(down_rows)],
             out_specs=[tile(width)],
             flops=2 * half * size * width * wide,
+            limit=LARGE,
         )[0]
 
-    sent_out = down(after(sent_right[0], up_grad), LOW)
-    kept_out = down(after(kept_right[0], up_grad), FULL)
-    grad_kept, grad_came = scatter_tokens(
-        kept_hidden, sent_hidden, [(), (down_grad,), (down_back[0], gate_grad, kept_out, sent_out)]
-    )
-    grad_got = grad_came[-1]
-    out_kept, out_came = scatter_tokens(kept_out, sent_out, [(grad_came[1],)])
-    out_got = out_came[-1]
-    output_rows = (middle + (out_kept + out_got.astype(FULL))).astype(LOW)
-    output = all_rows(output_rows)
+    steps_back = len(path)
+    kept, sent = scatter_stage(hidden_kept, hidden_sent, 0)
+    (down_grad,) = weight_grad(grad_pieces, kept_active, after(sent_active, hidden_sent), False)
+    sent_out = down(after(sent_active, down_grad), LOW)
+    kept_out = down(after(kept_active, down_grad), FULL)
+    kept, sent = scatter_stage(kept, after(sent, down_grad), 1)
+    out_kept, out_sent = add_halves(kept_out, swap(sent_out, *last))
+    both_this, both_other = weight_grad(hidden_pieces, kept_both, after(sent_both, sent_out), True)
+    grad_near = to_neighbour(both_this, both_other)
+    down_back = from_neighbour(down_grad)
+    sent = after(sent, down_back[0], both_other, kept_out)
+    for k in range(2, steps_back - 1):
+        kept, sent = scatter_stage(kept, sent, k)
+    grad_kept, grad_got = scatter_stage(kept, after(sent, out_sent), steps_back - 1)
+    out_kept, out_sent = scatter_stage(out_kept, out_sent, 0)
+    out_first = out_sent
+    out_kept, out_sent = scatter_stage(out_kept, out_sent, 1)
+    out_second = out_sent
+    both_back = along(after(grad_near, grad_got)).reshape(width, 2 * wide)
 
     grad_middle, branch_grad, moe_part = call(
         middle_back_body,
         [shape((rows, width), FULL), shape((rows, width), LOW), shape((16, width), FULL)],
-        where, after(grad_kept, out_came[0]), grad_got, middle, grad_rows, gains,
+        where, grad_kept, grad_got, middle, grad_rows, gains,
     )
     branch_pieces = [branch_grad]
     for b in reversed(t_masks):
         branch_pieces = branch_pieces + [swap(p, "tensor", b) for p in branch_pieces]
-    all_cols = qkv_cols + q_cols
+    sum_orders = orders[0], orders[0]
     kept_w, sent_w, first_kept, first_sent = call(
         functools.partial(
-            attend_back_body, len(branch_pieces), q_cols, k_cols, rows, part, order, orders
+            attend_back_body, len(branch_pieces), q_cols, k_cols, rows, part, order, sum_orders
         ),
         [
             shape((width // 2, all_cols), FULL),
@@ -689,7 +691,7 @@
             shape((length // 2, width), FULL),
             shape((length // 2, width), LOW),
         ],
-        where, *branch_pieces[:-1], after(branch_pieces[-1], out_came[1]), mixed, out_weights, qkv, doc_row, doc_col, cosine, sine,
+        where, *branch_pieces[:-1], after(branch_pieces[-1], out_first), mixed, qkv, doc_row, doc_col, cosine, sine,
         first_hidden, weights,
         scratch=[
             pltpu.VMEM((length, width), LOW),
@@ -699,57 +701,60 @@
         ],
         flops=2 * length * width * (2 * q_cols + 2 * qkv_cols),
     )
-    attn_came = []
-    for even, odd in reversed(by_parity):
-        attn_came.append(swap_by_parity(sent_w, even, odd))
-        attn_grad = kept_w + attn_came[-1].astype(FULL)
-        half_rows = attn_grad.shape[0] // 2
-        kept_w, sent_w = attn_grad[:half_rows], attn_grad[half_rows:].astype(LOW)
-
-    gate_back = from_neighbour(gate_grad, grad_got)
-    returned = [
-        gate_back,
-        from_neighbour(up_grad, gate_back[0]),
-        down_back,
-    ]
-
-    out_dims = [(part, hidden), (part, hidden), (hidden, part) if turn else (part, hidden)]
-
-    def unpack(pair, dims, turned):
-        source = pl.BlockSpec((1, part, wide), lambda z: (z, 0, 0))
-        return call(
-            functools.partial(unpack_body, own_experts, hidden, replicas, turned),
-            [shape((EXPERTS,) + dims, FULL)],
-            where, *pair,
-            grid=(n_e // 2,),
-            in_specs=[source, source],
-            out_specs=[at_pair(dims)],
-        )[0]
-
-    shards = [unpack(p, d, turn and i == 2) for i, (p, d) in enumerate(zip(returned, out_dims))]
-    gate_shard, up_shard, down_shard = shards
-    if not turn:
-        down_shard = down_shard.transpose(0, 2, 1)
-
+    got_w = swap(sent_w, "expert", e_bits[-1])
+    attn_grad = kept_w + got_w.astype(FULL)
     kept, got = scatter_rows(first_kept, first_sent)
     (token_rows,) = call(
         functools.partial(tokens_back_body, rows),
         [shape((rows + 16, width), FULL)],
-        where, tokens, kept, after(got, attn_came[0], gate_back[0]), gains, grad_middle, moe_part,
+        where, tokens, kept, after(got, got_w, out_second), gains, grad_middle, moe_part,
     )
     gathered = all_rows(token_rows.astype(LOW))
     gathered = gathered.reshape(n_t, rows + 16, width).astype(FULL)
     grad_input = gathered[:, :rows].reshape(length, width)
     gain_sum = jnp.sum(gathered[:, rows : rows + 2], axis=0)
 
-    def gain_block(m):
-        return lax.dynamic_slice_in_dim(gain_sum, (e ^ m) * part, part, 1)
-
-    lines = jnp.stack([gain_block(m) for m in order_of(e_bits)])
-    for b in reversed(e_bits):
-        half_rows = lines.shape[0] // 2
-        lines = lines[:half_rows] + swap(lines[half_rows:], "expert", b)
-    gain_grads = lines[0]
+    blocks = gain_sum.reshape(2, n_e, part).transpose(1, 0, 2)
+
+    half_rows = attn_grad.shape[0] // 2
+    kept_w, sent_w = attn_grad[:half_rows], attn_grad[half_rows:].astype(LOW)
+    blocks = after(blocks, sent_w)
+    gain_grads = jnp.sum(lax.all_to_all(blocks, "expert", 0, 0, tiled=True), axis=0)
+    out_sent = after(out_sent, both_back)
+    for k, b in enumerate(reversed(e_bits[:-1])):
+        attn_grad = kept_w + swap(sent_w, "expert", b).astype(FULL)
+        half_rows = attn_grad.shape[0] // 2
+        kept_w, sent_w = attn_grad[:half_rows], attn_grad[half_rows:].astype(LOW)
+        if k == 0:
+            out_kept, out_sent = scatter_stage(out_kept, out_sent, 2)
+            out_sent = after(out_sent, sent_w)
+    for k in range(3, steps_back):
+        out_kept, out_sent = scatter_stage(out_kept, out_sent, k)
+    output_rows = (middle + (out_kept + out_sent.astype(FULL))).astype(LOW)
+    output = all_rows(output_rows)
+
+    out_dims = [(part, hidden), (part, hidden), (hidden, part) if turn else (part, hidden)]
+
+    def unpack(source, dims, turned):
+        cols = source.shape[1]
+        return call(
+            functools.partial(unpack_body, own_experts, hidden, replicas, turned),
+            [shape((EXPERTS,) + dims, FULL)] * (cols // wide),
+            where, source,
+            grid=(pairs,),
+            in_specs=[pl.BlockSpec((2 * part, cols), lambda z: (z, 0))],
+            out_specs=[at_pair(dims)] * (cols // wide),
+        )
+
+    sides_of = lambda this, other: jnp.where(
+        side == 0, jnp.stack([this, other], axis=1), jnp.stack([other, this], axis=1)
+    )
+    down_back = sides_of(*down_back).reshape(width, wide)
+    shards = unpack(both_back, out_dims[0], False) + unpack(down_back, out_dims[2], turn)
+    gate_shard, up_shard, down_shard = shards
+    if not turn:
+        down_shard = down_shard.transpose(0, 2, 1)
+
     return (
         output,
         grad_input,

time: 365 us -> 342 us (0.937)
  starting transfers between devices: 106 us -> 70.4 us
  waiting for transfers between devices: 110 us -> 128 us
  Pallas kernels: 88.4 us -> 71 us
  other arithmetic: 25.4 us -> 39.9 us
    ppermute x26 -> x24, waiting for transfers between devices: 16.7 us -> 36.5 us  [swap(): return lax.ppermute(field, axis, [(i, i ^ mask) for i in range(count)])]
    ppermute x26 -> x24, starting transfers between devices: 46 us -> 26.7 us  [swap(): return lax.ppermute(field, axis, [(i, i ^ mask) for i in range(count)])]
    pallas_call x17 -> x15, Pallas kernels: 88.4 us -> 71 us  [call(): pl.pallas_call(body, out_shape=list(outs), in_specs=[pl.BlockSpec(memory_...]
    ppermute x25 -> x19, starting transfers between devices: 34.2 us -> 20.3 us  [swap_by_parity(): return lax.ppermute(field, ('expert', 'tensor'), pairs)]
    convert_element_type x1 -> x7, other arithmetic: 0.05 us -> 10.4 us  [the longest x6 10.4 us: add_halves(): return (kept[:half] + got[:half].astype(FULL), (kept[half:] + got[half:]....]
    all_to_all x6 -> x4, waiting for transfers between devices: 15.3 us -> 5.65 us  [along(): lax.all_to_all(blocks, 'expert', 0, 0, tiled=True, axis_index_groups=lines)]
    ppermute x25 -> x19, waiting for transfers between devices: 77.5 us -> 86.1 us  [swap_by_parity(): return lax.ppermute(field, ('expert', 'tensor'), pairs)]
    all_to_all x6 -> x4, starting transfers between devices: 25.9 us -> 18.7 us  [along(): lax.all_to_all(blocks, 'expert', 0, 0, tiled=True, axis_index_groups=lines)]
  transfers between devices with their start and end apart: 57 -> 48, of which waited for: 24 -> 22; matrix products, arithmetic and copies ran while one was open for 12% -> 12% of each run, Pallas kernels for 21% -> 18%
where the time goes in v4:
time: 342 us; the launch traced here: 341 us
  waiting for transfers between devices  128 us (37%)
  Pallas kernels  71 us (21%)
  starting transfers between devices  70.4 us (21%)
  other arithmetic  39.9 us (12%)
  local copies, waits for them, and re-layouts  29.8 us (9%)
    ppermute x19, waiting for transfers between devices, swap_by_parity(): return lax.ppermute(field, ('expert', 'tensor'), pairs)  86.1 us
    pallas_call x15, Pallas kernels, call(): pl.pallas_call(body, out_shape=list(outs), in_specs=[pl.BlockSpec(memory_...  71 us
    ppermute x24, waiting for transfers between devices, swap(): return lax.ppermute(field, axis, [(i, i ^ mask) for i in range(count)])  36.5 us
    ppermute x24, starting transfers between devices, swap(): return lax.ppermute(field, axis, [(i, i ^ mask) for i in range(count)])  26.7 us
    unnamed x93, local copies, waits for them, and re-layouts  21.2 us
    ppermute x19, starting transfers between devices, swap_by_parity(): return lax.ppermute(field, ('expert', 'tensor'), pairs)  20.3 us
    all_to_all x4, starting transfers between devices, along(): lax.all_to_all(blocks, 'expert', 0, 0, tiled=True, axis_index_groups=lines)  18.7 us
    convert_element_type x6, other arithmetic, add_halves(): return (kept[:half] + got[:half].astype(FULL), (kept[half:] + got[half:]....  10.4 us
  transfers between devices with their start and end apart: 48, of which 22 were waited for; matrix products, arithmetic and copies ran while one was open for 12% of the time, Pallas kernels for 18%

profile of v4, /device:TPU:1, one launch (start us, length us, event | category | flops | bytes accessed | tf_op | source)
XLA Modules:
  0.0 340.8 jit_solution(13016202483690524118)
XLA Ops:
  18.6 15.0 %collective-permute-done.1 = bf16[288,768]{1,0:T(8,128)(2,1)} collective-permute-done((bf16[288,768]{1,0:T(8,128)(2,1)S(1)}, bf16[288,768]{1,0:T(8,128)(2,1)}, u32[]{:S(2)}, u32[]{:S(2)}) %collective-permute-start.1) | collective-permute-done | bytes 442400 | tf_op jit(solution)/shard_map/ppermute | solution.py:73
  37.3 12.9 %collective-permute-done.3.refs_1_ = bf16[576,768]{1,0:T(8,128)(2,1)S(1)} collective-permute-done((bf16[576,768]{1,0:T(8,128)(2,1)S(1)}, bf16[576,768]{1,0:T(8,128)(2,1)S(1)}, u32[]{:S(2)}, u32[]{:S(2)}) %collective-permute-start.3) | collective-permute-done | bytes 884768 | tf_op jit(solution)/shard_map/ppermute | solution.py:73
  51.0 4.2 %all-to-all-start = ((bf16[4,256,512]{2,1,0:T(8,128)(2,1)}), bf16[4,256,512]{2,1,0:T(8,128)(2,1)}, u32[]{:S(2)}, u32[]{:S(2)}) async-start(bf16[4,256,512]{2,1,0:T(8,128)(2,1)} %bitcast.39), calls=%async_computation | async-start | bytes 2097152 | tf_op jit(solution)/shard_map/all_to_all | solution.py:435
  72.8 5.6 %all-to-all-done = bf16[4,256,512]{2,1,0:T(8,128)(2,1)} async-done(((bf16[4,256,512]{2,1,0:T(8,128)(2,1)}), bf16[4,256,512]{2,1,0:T(8,128)(2,1)}, u32[]{:S(2)}, u32[]{:S(2)}) %all-to-all-start) | async-done | bytes 1048608 | tf_op jit(solution)/shard_map/all_to_all | solution.py:435
  81.5 9.7 %collective-permute-done.9 = bf16[4,128,1024]{2,1,0:T(8,128)(2,1)} collective-permute-done((bf16[4,128,1024]{2,1,0:T(8,128)(2,1)}, bf16[4,128,1024]{2,1,0:T(8,128)(2,1)}, u32[]{:S(2)}, u32[]{:S(2)}) %collective-permute-start.9) | collective-permute-done | bytes 1048608 | tf_op jit(solution)/shard_map/ppermute | solution.py:58
  95.2 11.8 %collective-permute-done.10.refs_1_ = bf16[512,1152]{1,0:T(8,128)(2,1)} collective-permute-done((bf16[512,1152]{1,0:T(8,128)(2,1)}, bf16[512,1152]{1,0:T(8,128)(2,1)}, u32[]{:S(2)}, u32[]{:S(2)}) %collective-permute-start.10) | collective-permute-done | bytes 1179680 | tf_op jit(solution)/shard_map/ppermute | solution.py:73
  109.9 5.7 %collective-permute-done.11 = bf16[128,1024]{1,0:T(8,128)(2,1)S(1)} collective-permute-done((bf16[128,1024]{1,0:T(8,128)(2,1)S(1)}, bf16[128,1024]{1,0:T(8,128)(2,1)S(1)}, u32[]{:S(2)}, u32[]{:S(2)}) %collective-permute-start.11) | collective-permute-done | bytes 262176 | tf_op jit(solution)/shard_map/ppermute | solution.py:73
  116.3 4.4 %all-to-all-start.1 = ((bf16[4,256,1024]{2,1,0:T(8,128)(2,1)}), bf16[4,256,1024]{2,1,0:T(8,128)(2,1)S(1)}, u32[]{:S(2)}, u32[]{:S(2)}) async-start(bf16[4,256,1024]{2,1,0:T(8,128)(2,1)} %maximum_select_fusion), calls=%async_computation.1 | async-start | bytes 4194304 | tf_op jit(solution)/shard_map/all_to_all | solution.py:435
  122.6 11.0 %collective-permute-done.13 = bf16[256,1024]{1,0:T(8,128)(2,1)S(1)} collective-permute-done((bf16[256,1024]{1,0:T(8,128)(2,1)S(1)}, bf16[256,1024]{1,0:T(8,128)(2,1)S(1)}, u32[]{:S(2)}, u32[]{:S(2)}) %collective-permute-start.13) | collective-permute-done | bytes 524320 | tf_op jit(solution)/shard_map/ppermute | solution.py:73
  134.6 13.1 %collective-permute-done.14.refs_1_ = bf16[512,1024]{1,0:T(8,128)(2,1)S(1)} collective-permute-done((bf16[512,1024]{1,0:T(8,128)(2,1)S(1)}, bf16[512,1024]{1,0:T(8,128)(2,1)S(1)}, u32[]{:S(2)}, u32[]{:S(2)}) %collective-permute-start.14) | collective-permute-done | bytes 1048608 | tf_op jit(solution)/shard_map/ppermute | solution.py:73
  149.7 9.4 %shard_map.224 = (f32[2048,128]{1,0:T(8,128)}, f32[2048,512]{1,0:T(8,128)}, bf16[1024,512]{1,0:T(8,128)(2,1)}) custom-call(s32[2]{0:T(128)} %copy-done.23, bf16[512,1152]{1,0:T(8,128)(2,1)} %pad_maximum_fusion.refs_0_, bf16[512,1152]{1,0:T(8,128)(2,1)} %collective-permute-done.10.refs_1_, bf16[512,1152]{1,0:T(8,128)(2,1)} %copy-done.42, ...), custom_call_target="tpu_custom_call" | custom-call | flops 2147483648 | bytes 12058632 | tf_op jit(solution)/shard_map/pallas_call | solution.py:44
  160.6 9.6 %shard_map.226 = (bf16[1024,1024]{1,0:T(8,128)(2,1)}, bf16[1024,512]{1,0:T(8,128)(2,1)}, bf16[1024,1024]{1,0:T(8,128)(2,1)}) custom-call(s32[2]{0:T(128)} %copy-done.23, bf16[512,1024]{1,0:T(8,128)(2,1)} %collective-permute-done.17.refs_0_.refs_2_, bf16[512,1024]{1,0:T(8,128)(2,1)} %collective-permute-done.18.refs_1_.refs_3_, bf16[1024,1024]{1,0:T(8,128)(2,1)} %bitcast.44, ...), custom_call_target="tpu_custom_call" | custom-call | flops 4294967296 | bytes 14680072 | tf_op jit(solution)/shard_map/pallas_call | solution.py:44
  170.7 9.8 %shard_map.225 = (f32[1024,1024]{1,0:T(8,128)}, bf16[1024,512]{1,0:T(8,128)(2,1)}, bf16[1024,1024]{1,0:T(8,128)(2,1)}) custom-call(s32[2]{0:T(128)} %copy-done.23, bf16[512,1024]{1,0:T(8,128)(2,1)} %copy-done.38, bf16[512,1024]{1,0:T(8,128)(2,1)} %copy-done.44, bf16[1024,1024]{1,0:T(8,128)(2,1)} %bitcast.45, f32[2048,128]{1,0:T(8,128)} %get-tuple-element.94.refs_3_, ...), custom_call_target="tpu_custom_call" | custom-call | flops 4294967296 | bytes 16777224 | tf_op jit(solution)/shard_map/pallas_call | solution.py:44
  184.8 6.3 %shard_map.227 = bf16[4,2,128,512]{3,2,1,0:T(8,128)(2,1)} custom-call(s32[2]{0:T(128)} %copy-done.23, bf16[512,1152]{1,0:T(8,128)(2,1)} %pad_maximum_fusion.refs_0_, bf16[512,1152]{1,0:T(8,128)(2,1)} %collective-permute-done.10.refs_1_, bf16[512,1152]{1,0:T(8,128)(2,1)} %copy-done.42, bf16[512,1152]{1,0:T(8,128)(2,1)} %copy-done.43, ...), custom_call_target="tpu_custom_call" | custom-call | flops 2147483648 | bytes 7864328 | tf_op jit(solution)/shard_map/pallas_call | solution.py:44
  191.1 4.8 %shard_map.229 = bf16[1024,1024]{1,0:T(8,128)(2,1)} custom-call(s32[2]{0:T(128)} %copy-done.23, bf16[1024,512]{1,0:T(8,128)(2,1)} %get-tuple-element.103.refs_5_.active, bf16[1024,512]{1,0:T(8,128)(2,1)} %get-tuple-element.102.weights), custom_call_target="tpu_custom_call" | custom-call | flops 1073741824 | bytes 4194312 | tf_op jit(solution)/shard_map/pallas_call | solution.py:44
  196.2 5.2 %all-to-all-start.4 = ((bf16[4,256,512]{2,1,0:T(8,128)(2,1)}), bf16[4,256,512]{2,1,0:T(8,128)(2,1)}, u32[]{:S(2)}, u32[]{:S(2)}) async-start(bf16[4,256,512]{2,1,0:T(8,128)(2,1)} %bitcast.47), calls=%async_computation.4 | async-start | bytes 2097152 | tf_op jit(solution)/shard_map/all_to_all | solution.py:435
  204.3 8.9 %shard_map.230 = (bf16[4,128,1024]{2,1,0:T(8,128)(2,1)}, bf16[4,128,1024]{2,1,0:T(8,128)(2,1)}) custom-call(s32[2]{0:T(128)} %copy-done.23, bf16[512,1024]{1,0:T(8,128)(2,1)} %copy-done.38, bf16[512,1024]{1,0:T(8,128)(2,1)} %copy-done.44, bf16[512,1024]{1,0:T(8,128)(2,1)} %collective-permute-done.17.refs_0_.refs_2_, ...), custom_call_target="tpu_custom_call" | custom-call | flops 4294967296 | bytes 10485768 | tf_op jit(solution)/shard_map/pallas_call | solution.py:44
  213.5 5.2 %shard_map.228 = f32[1024,1024]{1,0:T(8,128)} custom-call(s32[2]{0:T(128)} %copy-done.23, bf16[1024,512]{1,0:T(8,128)(2,1)} %get-tuple-element.101.refs_4_.active, bf16[1024,512]{1,0:T(8,128)(2,1)} %get-tuple-element.102.weights), custom_call_target="tpu_custom_call" | custom-call | flops 1073741824 | bytes 6291464 | tf_op jit(solution)/shard_map/pallas_call | solution.py:44
  220.4 5.3 %fusion = (bf16[512,1024]{1,0:T(8,128)(2,1)}, f32[512,1024]{1,0:T(8,128)}) fusion(f32[1024,1024]{1,0:T(8,128)} %shard_map.228, bf16[1024,1024]{1,0:T(8,128)(2,1)} %collective-permute-done.20), kind=kLoop, calls=%fused_computation.1 | loop fusion | flops 2621440 | bytes 9437184 | tf_op jit(solution)/shard_map/convert_element_type | solution.py:495
  240.4 4.8 %all-to-all-start.2 = ((bf16[4,256,1024]{2,1,0:T(8,128)(2,1)}), bf16[4,256,1024]{2,1,0:T(8,128)(2,1)S(1)}, u32[]{:S(2)}, u32[]{:S(2)}) async-start(bf16[4,256,1024]{2,1,0:T(8,128)(2,1)} %maximum_select_fusion.1), calls=%async_computation.2 | async-start | bytes 4194304 | tf_op jit(solution)/shard_map/all_to_all | solution.py:435
  272.3 10.2 %collective-permute-done.32 = bf16[512,768]{1,0:T(8,128)(2,1)S(1)} collective-permute-done((bf16[512,768]{1,0:T(8,128)(2,1)S(1)}, bf16[512,768]{1,0:T(8,128)(2,1)S(1)}, u32[]{:S(2)}, u32[]{:S(2)}) %collective-permute-start.32) | collective-permute-done | bytes 786464 | tf_op jit(solution)/shard_map/ppermute | solution.py:58
  288.0 4.2 %collective-permute-start.40 = (bf16[160,1024]{1,0:T(8,128)(2,1)S(1)}, bf16[160,1024]{1,0:T(8,128)(2,1)S(1)}, u32[]{:S(2)}, u32[]{:S(2)}) collective-permute-start(bf16[160,1024]{1,0:T(8,128)(2,1)S(1)} %pad_maximum_fusion.9), channel_id=1, source_target_pairs={{0,1},{1,0},{2,3},{3,2},{4,5},{5,4},{6,7},{7,6},{8,9},{9,8},{10,11... | collective-permute-start | bytes 983048 | tf_op jit(solution)/shard_map/ppermute | solution.py:58
  301.3 4.7 %all-to-all-start.3 = ((f32[8,2,128]{2,1,0:T(2,128)}), f32[8,2,128]{2,1,0:T(2,128)S(1)}, u32[]{:S(2)}, u32[]{:S(2)}) async-start(f32[8,2,128]{2,1,0:T(2,128)} %bitcast.18), calls=%async_computation.3 | async-start | bytes 16384 | tf_op jit(solution)/shard_map/all_to_all | solution.py:722
  318.5 9.4 %collective-permute-done.34 = bf16[64,1024]{1,0:T(8,128)(2,1)S(1)} collective-permute-done((bf16[64,1024]{1,0:T(8,128)(2,1)S(1)}, bf16[64,1024]{1,0:T(8,128)(2,1)S(1)}, u32[]{:S(2)}, u32[]{:S(2)}) %collective-permute-start.34) | collective-permute-done | bytes 131104 | tf_op jit(solution)/shard_map/ppermute | solution.py:73
  (248 shorter events, 148.0 us)
Async XLA Ops:
  15.9 17.7 %collective-permute-start.1 = (bf16[288,768]{1,0:T(8,128)(2,1)S(1)}, bf16[288,768]{1,0:T(8,128)(2,1)}, u32[]{:S(2)}, u32[]{:S(2)}) collective-permute-start(bf16[288,768]{1,0:T(8,128)(2,1)S(1)} %pad_maximum_fusion.8), channel_id=1, source_target_pairs={{0,8},{1,17},{2,10},{3,19},{4,12},{5,21},{6,14},{7,23},{8,0},{9,25... | collective-permute-start | bytes 1327112 | tf_op jit(solution)/shard_map/ppermute | solution.py:73
  18.5 16.6 %collective-permute-start.2 = (bf16[64,1152]{1,0:T(8,128)(2,1)S(1)}, bf16[64,1152]{1,0:T(8,128)(2,1)S(1)}, u32[]{:S(2)}, u32[]{:S(2)}) collective-permute-start(bf16[64,1152]{1,0:T(8,128)(2,1)S(1)} %pad_maximum_fusion.14), channel_id=1, source_target_pairs={{0,16},{1,17},{2,18},{3,19},{4,20},{5,21},{6,22},{7,23},{8,24},{9,... | collective-permute-start | bytes 442376 | tf_op jit(solution)/shard_map/ppermute | solution.py:73
  35.1 15.1 %collective-permute-start.3 = (bf16[576,768]{1,0:T(8,128)(2,1)S(1)}, bf16[576,768]{1,0:T(8,128)(2,1)S(1)}, u32[]{:S(2)}, u32[]{:S(2)}) collective-permute-start(bf16[576,768]{1,0:T(8,128)(2,1)S(1)} %pad_maximum_fusion.1.refs_0_), channel_id=1, source_target_pairs={{0,4},{1,9},{2,6},{3,11},{4,0},{5,13},{6,2},{7,15},{8,12},{9,1},{1... | collective-permute-start | bytes 2654216 | tf_op jit(solution)/shard_map/ppermute | solution.py:73
  36.5 19.0 %collective-permute-start.4 = (bf16[128,1152]{1,0:T(8,128)(2,1)}, bf16[128,1152]{1,0:T(8,128)(2,1)}, u32[]{:S(2)}, u32[]{:S(2)}) collective-permute-start(bf16[128,1152]{1,0:T(8,128)(2,1)} %pad_maximum_fusion.10), channel_id=1, source_target_pairs={{0,8},{1,9},{2,10},{3,11},{4,12},{5,13},{6,14},{7,15},{8,0},{9,1},... | collective-permute-start | bytes 884744 | tf_op jit(solution)/shard_map/ppermute | solution.py:73
  51.0 27.4 %all-to-all-start = ((bf16[4,256,512]{2,1,0:T(8,128)(2,1)}), bf16[4,256,512]{2,1,0:T(8,128)(2,1)}, u32[]{:S(2)}, u32[]{:S(2)}) async-start(bf16[4,256,512]{2,1,0:T(8,128)(2,1)} %bitcast.39), calls=%async_computation | async-start | bytes 2097152 | tf_op jit(solution)/shard_map/all_to_all | solution.py:435
  57.3 13.2 %collective-permute-start.7 = (bf16[256,1152]{1,0:T(8,128)(2,1)}, bf16[256,1152]{1,0:T(8,128)(2,1)}, u32[]{:S(2)}, u32[]{:S(2)}) collective-permute-start(bf16[256,1152]{1,0:T(8,128)(2,1)} %pad_maximum_fusion.4), channel_id=1, source_target_pairs={{0,4},{1,3},{2,6},{3,1},{4,0},{5,7},{6,2},{7,5},{8,12},{9,11},{10,... | collective-permute-start | bytes 1769480 | tf_op jit(solution)/shard_map/ppermute | solution.py:73
  66.7 24.5 %collective-permute-start.9 = (bf16[4,128,1024]{2,1,0:T(8,128)(2,1)}, bf16[4,128,1024]{2,1,0:T(8,128)(2,1)}, u32[]{:S(2)}, u32[]{:S(2)}) collective-permute-start(bf16[4,128,1024]{2,1,0:T(8,128)(2,1)} %copy-done.26), channel_id=1, source_target_pairs={{0,4},{4,0},{8,12},{12,8},{16,20},{20,16},{24,28},{28,24},{1,5},{5... | collective-permute-start | bytes 3145736 | tf_op jit(solution)/shard_map/ppermute | solution.py:58
  81.4 25.5 %collective-permute-start.10 = (bf16[512,1152]{1,0:T(8,128)(2,1)}, bf16[512,1152]{1,0:T(8,128)(2,1)}, u32[]{:S(2)}, u32[]{:S(2)}) collective-permute-start(bf16[512,1152]{1,0:T(8,128)(2,1)} %pad_maximum_fusion.refs_0_), channel_id=1, source_target_pairs={{0,2},{1,5},{2,0},{3,7},{4,6},{5,1},{6,4},{7,3},{8,10},{9,13},{10,... | collective-permute-start | bytes 3538952 | tf_op jit(solution)/shard_map/ppermute | solution.py:73
  81.5 13.7 %collective-permute-start.8 = (bf16[64,1024]{1,0:T(8,128)(2,1)S(1)}, bf16[64,1024]{1,0:T(8,128)(2,1)S(1)}, u32[]{:S(2)}, u32[]{:S(2)}) collective-permute-start(bf16[64,1024]{1,0:T(8,128)(2,1)S(1)} %get-tuple-element.86), channel_id=1, source_target_pairs={{0,16},{1,17},{2,18},{3,19},{4,20},{5,21},{6,22},{7,23},{8,24},{9,... | collective-permute-start | bytes 393224 | tf_op jit(solution)/shard_map/ppermute | solution.py:73
  116.3 42.9 %all-to-all-start.1 = ((bf16[4,256,1024]{2,1,0:T(8,128)(2,1)}), bf16[4,256,1024]{2,1,0:T(8,128)(2,1)S(1)}, u32[]{:S(2)}, u32[]{:S(2)}) async-start(bf16[4,256,1024]{2,1,0:T(8,128)(2,1)} %maximum_select_fusion), calls=%async_computation.1 | async-start | bytes 4194304 | tf_op jit(solution)/shard_map/all_to_all | solution.py:435
  133.7 14.0 %collective-permute-start.14 = (bf16[512,1024]{1,0:T(8,128)(2,1)S(1)}, bf16[512,1024]{1,0:T(8,128)(2,1)S(1)}, u32[]{:S(2)}, u32[]{:S(2)}) collective-permute-start(bf16[512,1024]{1,0:T(8,128)(2,1)S(1)} %constant_dynamic-update-slice_fusion.refs_0_), channel_id=1, source_target_pairs={{0,2},{1,5},{2,0},{3,7},{4,6},{5,1},{6,4},{7,3},{8,10},{9,13},{10,... | collective-permute-start | bytes 3145736 | tf_op jit(solution)/shard_map/ppermute | solution.py:73
  134.1 13.6 %collective-permute-start.15 = (bf16[512,1152]{1,0:T(8,128)(2,1)}, bf16[512,1152]{1,0:T(8,128)(2,1)S(1)}, u32[]{:S(2)}, u32[]{:S(2)}) collective-permute-start(bf16[512,1152]{1,0:T(8,128)(2,1)} %pad_maximum_fusion.refs_0_), channel_id=1, source_target_pairs={{0,1},{1,0},{2,3},{3,2},{4,5},{5,4},{6,7},{7,6},{8,9},{9,8},{10,11... | collective-permute-start | bytes 3538952 | tf_op jit(solution)/shard_map/ppermute | solution.py:58
  134.1 13.6 %collective-permute-start.16 = (bf16[512,1152]{1,0:T(8,128)(2,1)}, bf16[512,1152]{1,0:T(8,128)(2,1)S(1)}, u32[]{:S(2)}, u32[]{:S(2)}) collective-permute-start(bf16[512,1152]{1,0:T(8,128)(2,1)} %collective-permute-done.10.refs_1_), channel_id=1, source_target_pairs={{0,1},{1,0},{2,3},{3,2},{4,5},{5,4},{6,7},{7,6},{8,9},{9,8},{10,11... | collective-permute-start | bytes 3538952 | tf_op jit(solution)/shard_map/ppermute | solution.py:58
  134.6 24.6 %collective-permute-start.17 = (bf16[512,1024]{1,0:T(8,128)(2,1)S(1)}, bf16[512,1024]{1,0:T(8,128)(2,1)}, u32[]{:S(2)}, u32[]{:S(2)}) collective-permute-start(bf16[512,1024]{1,0:T(8,128)(2,1)S(1)} %constant_dynamic-update-slice_fusion.refs_0_), channel_id=1, source_target_pairs={{0,1},{1,0},{2,3},{3,2},{4,5},{5,4},{6,7},{7,6},{8,9},{9,8},{10,11... | collective-permute-start | bytes 3145736 | tf_op jit(solution)/shard_map/ppermute | solution.py:58
  184.4 17.0 %collective-permute-start.24 = (bf16[512,1024]{1,0:T(8,128)(2,1)}, bf16[512,1024]{1,0:T(8,128)(2,1)}, u32[]{:S(2)}, u32[]{:S(2)}) collective-permute-start(bf16[512,1024]{1,0:T(8,128)(2,1)} %get-tuple-element.178), channel_id=1, source_target_pairs={{0,2},{1,5},{2,0},{3,7},{4,6},{5,1},{6,4},{7,3},{8,10},{9,13},{10,... | collective-permute-start | bytes 3145736 | tf_op jit(solution)/shard_map/ppermute | solution.py:73
  195.9 24.4 %collective-permute-start.20 = (bf16[1024,1024]{1,0:T(8,128)(2,1)}, bf16[1024,1024]{1,0:T(8,128)(2,1)}, u32[]{:S(2)}, u32[]{:S(2)}) collective-permute-start(bf16[1024,1024]{1,0:T(8,128)(2,1)} %shard_map.229), channel_id=1, source_target_pairs={{0,1},{1,0},{2,3},{3,2},{4,5},{5,4},{6,7},{7,6},{8,9},{9,8},{10,11... | collective-permute-start | bytes 6291464 | tf_op jit(solution)/shard_map/ppermute | solution.py:58
  196.2 44.2 %all-to-all-start.4 = ((bf16[4,256,512]{2,1,0:T(8,128)(2,1)}), bf16[4,256,512]{2,1,0:T(8,128)(2,1)}, u32[]{:S(2)}, u32[]{:S(2)}) async-start(bf16[4,256,512]{2,1,0:T(8,128)(2,1)} %bitcast.47), calls=%async_computation.4 | async-start | bytes 2097152 | tf_op jit(solution)/shard_map/all_to_all | solution.py:435
  203.0 15.7 %collective-permute-start.25 = (bf16[256,1024]{1,0:T(8,128)(2,1)S(1)}, bf16[256,1024]{1,0:T(8,128)(2,1)S(1)}, u32[]{:S(2)}, u32[]{:S(2)}) collective-permute-start(bf16[256,1024]{1,0:T(8,128)(2,1)S(1)} %get-tuple-element.109), channel_id=1, source_target_pairs={{0,4},{1,3},{2,6},{3,1},{4,0},{5,7},{6,2},{7,5},{8,12},{9,11},{10,... | collective-permute-start | bytes 1572872 | tf_op jit(solution)/shard_map/ppermute | solution.py:73
  213.2 24.2 %collective-permute-start.23 = (bf16[4,128,1024]{2,1,0:T(8,128)(2,1)}, bf16[4,128,1024]{2,1,0:T(8,128)(2,1)S(1)}, u32[]{:S(2)}, u32[]{:S(2)}) collective-permute-start(bf16[4,128,1024]{2,1,0:T(8,128)(2,1)} %get-tuple-element.108), channel_id=1, source_target_pairs={{0,4},{4,0},{8,12},{12,8},{16,20},{20,16},{24,28},{28,24},{1,5},{5... | collective-permute-start | bytes 3145736 | tf_op jit(solution)/shard_map/ppermute | solution.py:58
  225.7 30.2 %collective-permute-start.21 = (bf16[512,1024]{1,0:T(8,128)(2,1)}, bf16[512,1024]{1,0:T(8,128)(2,1)}, u32[]{:S(2)}, u32[]{:S(2)}) collective-permute-start(bf16[512,1024]{1,0:T(8,128)(2,1)} %get-tuple-element.179), channel_id=1, source_target_pairs={{0,2},{1,5},{2,0},{3,7},{4,6},{5,1},{6,4},{7,3},{8,10},{9,13},{10,... | collective-permute-start | bytes 3145736 | tf_op jit(solution)/shard_map/ppermute | solution.py:73
  240.4 60.9 %all-to-all-start.2 = ((bf16[4,256,1024]{2,1,0:T(8,128)(2,1)}), bf16[4,256,1024]{2,1,0:T(8,128)(2,1)S(1)}, u32[]{:S(2)}, u32[]{:S(2)}) async-start(bf16[4,256,1024]{2,1,0:T(8,128)(2,1)} %maximum_select_fusion.1), calls=%async_computation.2 | async-start | bytes 4194304 | tf_op jit(solution)/shard_map/all_to_all | solution.py:435
  262.8 19.7 %collective-permute-start.32 = (bf16[512,768]{1,0:T(8,128)(2,1)S(1)}, bf16[512,768]{1,0:T(8,128)(2,1)S(1)}, u32[]{:S(2)}, u32[]{:S(2)}) collective-permute-start(bf16[512,768]{1,0:T(8,128)(2,1)S(1)} %get-tuple-element.121), channel_id=1, source_target_pairs={{0,4},{4,0},{8,12},{12,8},{16,20},{20,16},{24,28},{28,24},{1,5},{5... | collective-permute-start | bytes 2359304 | tf_op jit(solution)/shard_map/ppermute | solution.py:58
  267.0 26.9 %collective-permute-start.42 = (bf16[4,128,512]{2,1,0:T(8,128)(2,1)}, bf16[4,128,512]{2,1,0:T(8,128)(2,1)}, u32[]{:S(2)}, u32[]{:S(2)}) collective-permute-start(bf16[4,128,512]{2,1,0:T(8,128)(2,1)} %get-tuple-element.190), channel_id=1, source_target_pairs={{0,4},{4,0},{8,12},{12,8},{16,20},{20,16},{24,28},{28,24},{1,5},{5... | collective-permute-start | bytes 1572872 | tf_op jit(solution)/shard_map/ppermute | solution.py:58
  310.2 18.6 %collective-permute-start.41 = (bf16[128,768]{1,0:T(8,128)(2,1)S(1)}, bf16[128,768]{1,0:T(8,128)(2,1)}, u32[]{:S(2)}, u32[]{:S(2)}) collective-permute-start(bf16[128,768]{1,0:T(8,128)(2,1)S(1)} %slice.303), channel_id=1, source_target_pairs={{0,16},{4,20},{8,24},{12,28},{16,0},{20,4},{24,8},{28,12},{1,17},{... | collective-permute-start | bytes 589832 | tf_op jit(solution)/shard_map/ppermute | solution.py:58
  (69 other events, 550.9 us)

commit v5 on v4

--- a/solution.py
+++ b/solution.py
@@ -133,6 +133,12 @@
             sided[k][0, :, at] = gate[place].astype(LOW)
             up_at = slice((own + j) * hid, (own + j + 1) * hid)
             sided[k][0, :, up_at] = up[place].astype(LOW)
+
+
+def interleave_body(part, where, this, other, out):
+    for k, source in enumerate((this, other)):
+        at = pl.multiple_of(((where[0] & 1) ^ k) * part, part)
+        out[0, pl.ds(at, part), :] = source[0]
 
 
 def attend_body(orders, n, part, pitch, q_cols, k_cols, rows, order, where, *refs):
@@ -436,19 +442,31 @@
             blocks, "expert", 0, 0, tiled=True, axis_index_groups=lines
         )
 
+    def split_sides(blocks):
+        blocks = blocks.reshape(pairs, 2, part, blocks.shape[-1])
+        this = lax.dynamic_index_in_dim(blocks, side, 1, keepdims=False)
+        return this, lax.dynamic_index_in_dim(blocks, 1 - side, 1, keepdims=False)
+
     def from_neighbour(blocks, *earlier):
         cols = blocks.shape[-1]
         blocks = along(after(blocks.reshape(pairs, 2 * part, cols), *earlier))
-        blocks = blocks.reshape(pairs, 2, part, cols)
-        this = lax.dynamic_index_in_dim(blocks, side, 1, keepdims=False)
-        other = lax.dynamic_index_in_dim(blocks, 1 - side, 1, keepdims=False)
+        this, other = split_sides(blocks)
         return this, swap(other, "expert", 1)
 
+    def interleave(this, other):
+        cols = this.shape[-1]
+        block = pl.BlockSpec((1, part, cols), lambda z: (z, 0, 0))
+        return call(
+            functools.partial(interleave_body, part),
+            [shape((pairs, 2 * part, cols), LOW)],
+            where, this, other,
+            grid=(pairs,),
+            in_specs=[block, block],
+            out_specs=[pl.BlockSpec((1, 2 * part, cols), lambda z: (z, 0, 0))],
+        )[0]
+
     def to_neighbour(this, other, *earlier):
-        got = swap(after(other, *earlier), "expert", 1)
-        return jnp.where(
-            side == 0, jnp.concatenate([this, got], axis=1), jnp.concatenate([got, this], axis=1)
-        )
+        return interleave(this, swap(after(other, *earlier), "expert", 1))
 
     e_path = [("expert", b) for b in bits_of(n_e, first_bit)]
     t_path = [("tensor", b) for b in t_bits]
@@ -550,9 +568,9 @@
     hidden_field = second_hidden
     for k, (even, odd) in enumerate(path):
         if k == 1:
-            hidden_field = after(hidden_field, near, *([grad_got] if len(path) > 3 else []))
+            hidden_field = after(hidden_field, near)
         if k == 2:
-            hidden_field = after(hidden_field, down_other)
+            hidden_field = after(hidden_field, down_other, grad_got)
         hidden_got = swap_by_parity(hidden_field, even, odd)
         if k == 1:
             gate_up_rows = along(after(near, hidden_got)).reshape(width, 2 * wide)
@@ -566,7 +584,7 @@
             grad_pieces = [grad_field, grad_got]
     hidden_pieces = hidden_pieces + [swap(p, *last) for p in hidden_pieces]
     grad_pieces = grad_pieces + [swap(p, *last) for p in grad_pieces]
-    size = 256
+    size = 512
     total_rows = sum(p.shape[0] for p in grad_pieces)
     steps = total_rows // size
     whole = lambda a: pl.BlockSpec(a.shape, lambda i: (0,) * a.ndim)
@@ -661,8 +679,8 @@
     out_kept, out_sent = add_halves(kept_out, swap(sent_out, *last))
     both_this, both_other = weight_grad(hidden_pieces, kept_both, after(sent_both, sent_out), True)
     grad_near = to_neighbour(both_this, both_other)
-    down_back = from_neighbour(down_grad)
-    sent = after(sent, down_back[0], both_other, kept_out)
+    down_line = along(down_grad.reshape(pairs, 2 * part, wide))
+    sent = after(sent, down_line, both_other, kept_out)
     for k in range(2, steps_back - 1):
         kept, sent = scatter_stage(kept, sent, k)
     grad_kept, grad_got = scatter_stage(kept, after(sent, out_sent), steps_back - 1)
@@ -749,7 +767,8 @@
     sides_of = lambda this, other: jnp.where(
         side == 0, jnp.stack([this, other], axis=1), jnp.stack([other, this], axis=1)
     )
-    down_back = sides_of(*down_back).reshape(width, wide)
+    down_this, down_other = split_sides(after(down_line, got_w))
+    down_back = sides_of(down_this, swap(down_other, "expert", 1)).reshape(width, wide)
     shards = unpack(both_back, out_dims[0], False) + unpack(down_back, out_dims[2], turn)
     gate_shard, up_shard, down_shard = shards
     if not turn:

time: 342 us -> 328 us (0.959)
  starting transfers between devices: 70.4 us -> 62 us
  other arithmetic: 39.9 us -> 34.4 us
    ppermute x19, waiting for transfers between devices: 86.1 us -> 64.2 us  [swap_by_parity(): return lax.ppermute(field, ('expert', 'tensor'), pairs)]
    all_to_all x4, waiting for transfers between devices: 5.65 us -> 20.3 us  [along(): lax.all_to_all(blocks, 'expert', 0, 0, tiled=True, axis_index_groups=lines)]
    select_n x2 -> x0, other arithmetic: 6.19 us -> none  [to_neighbour(): jnp.where(side == 0, jnp.concatenate([this, got], axis=1), jnp.concatenat...]
    ppermute x24, waiting for transfers between devices: 36.5 us -> 40.9 us  [swap(): return lax.ppermute(field, axis, [(i, i ^ mask) for i in range(count)])]
    unnamed x93 -> x103, local copies, waits for them, and re-layouts: 21.2 us -> 22.8 us
    pallas_call x15 -> x17, Pallas kernels: 71 us -> 70.4 us  [call(): pl.pallas_call(body, out_shape=list(outs), in_specs=[pl.BlockSpec(memory_...]
  transfers between devices with their start and end apart: 48 -> 48, of which waited for: 22 -> 24; matrix products, arithmetic and copies ran while one was open for 12% -> 11% of each run, Pallas kernels for 18% -> 19%
where the time goes in v5:
time: 328 us; the launch traced here: 326 us
  waiting for transfers between devices  126 us (38%)
  Pallas kernels  70.4 us (21%)
  starting transfers between devices  62 us (19%)
  other arithmetic  34.4 us (10%)
  local copies, waits for them, and re-layouts  32.1 us (10%)
    pallas_call x17, Pallas kernels, call(): pl.pallas_call(body, out_shape=list(outs), in_specs=[pl.BlockSpec(memory_...  70.4 us
    ppermute x19, waiting for transfers between devices, swap_by_parity(): return lax.ppermute(field, ('expert', 'tensor'), pairs)  64.2 us
    ppermute x24, waiting for transfers between devices, swap(): return lax.ppermute(field, axis, [(i, i ^ mask) for i in range(count)])  40.9 us
    ppermute x24, starting transfers between devices, swap(): return lax.ppermute(field, axis, [(i, i ^ mask) for i in range(count)])  23.5 us
    unnamed x103, local copies, waits for them, and re-layouts  22.8 us
    all_to_all x4, waiting for transfers between devices, along(): lax.all_to_all(blocks, 'expert', 0, 0, tiled=True, axis_index_groups=lines)  20.3 us
    ppermute x19, starting transfers between devices, swap_by_parity(): return lax.ppermute(field, ('expert', 'tensor'), pairs)  17.7 us
    all_to_all x4, starting transfers between devices, along(): lax.all_to_all(blocks, 'expert', 0, 0, tiled=True, axis_index_groups=lines)  16.2 us
  transfers between devices with their start and end apart: 48, of which 24 were waited for; matrix products, arithmetic and copies ran while one was open for 11% of the time, Pallas kernels for 19%

profile of v5, /device:TPU:1, one launch (start us, length us, event | category | flops | bytes accessed | tf_op | source)
XLA Modules:
  0.0 326.3 jit_solution(7499319616619933799)
XLA Ops:
  19.6 14.9 %collective-permute-done.1 = bf16[288,768]{1,0:T(8,128)(2,1)S(1)} collective-permute-done((bf16[288,768]{1,0:T(8,128)(2,1)S(1)}, bf16[288,768]{1,0:T(8,128)(2,1)S(1)}, u32[]{:S(2)}, u32[]{:S(2)}) %collective-permute-start.1) | collective-permute-done | bytes 442400 | tf_op jit(solution)/shard_map/ppermute | solution.py:73
  38.3 12.9 %collective-permute-done.3.refs_1_ = bf16[576,768]{1,0:T(8,128)(2,1)S(1)} collective-permute-done((bf16[576,768]{1,0:T(8,128)(2,1)S(1)}, bf16[576,768]{1,0:T(8,128)(2,1)S(1)}, u32[]{:S(2)}, u32[]{:S(2)}) %collective-permute-start.3) | collective-permute-done | bytes 884768 | tf_op jit(solution)/shard_map/ppermute | solution.py:73
  51.1 4.3 %all-to-all-start = ((bf16[4,256,512]{2,1,0:T(8,128)(2,1)}), bf16[4,256,512]{2,1,0:T(8,128)(2,1)}, u32[]{:S(2)}, u32[]{:S(2)}) async-start(bf16[4,256,512]{2,1,0:T(8,128)(2,1)} %bitcast.7), calls=%async_computation | async-start | bytes 2097152 | tf_op jit(solution)/shard_map/all_to_all | solution.py:441
  71.9 6.6 %all-to-all-done = bf16[4,256,512]{2,1,0:T(8,128)(2,1)} async-done(((bf16[4,256,512]{2,1,0:T(8,128)(2,1)}), bf16[4,256,512]{2,1,0:T(8,128)(2,1)}, u32[]{:S(2)}, u32[]{:S(2)}) %all-to-all-start) | async-done | bytes 1048608 | tf_op jit(solution)/shard_map/all_to_all | solution.py:441
  83.0 5.5 %collective-permute-done.9.other = bf16[4,128,1024]{2,1,0:T(8,128)(2,1)S(1)} collective-permute-done((bf16[4,128,1024]{2,1,0:T(8,128)(2,1)}, bf16[4,128,1024]{2,1,0:T(8,128)(2,1)S(1)}, u32[]{:S(2)}, u32[]{:S(2)}) %collective-permute-start.9) | collective-permute-done | bytes 1048608 | tf_op jit(solution)/shard_map/ppermute | solution.py:58
  93.5 4.4 %collective-permute-done.10 = bf16[128,1024]{1,0:T(8,128)(2,1)S(1)} collective-permute-done((bf16[128,1024]{1,0:T(8,128)(2,1)S(1)}, bf16[128,1024]{1,0:T(8,128)(2,1)S(1)}, u32[]{:S(2)}, u32[]{:S(2)}) %collective-permute-start.10) | collective-permute-done | bytes 262176 | tf_op jit(solution)/shard_map/ppermute | solution.py:73
  103.5 9.6 %collective-permute-done.11.refs_5_ = bf16[4,128,512]{2,1,0:T(8,128)(2,1)} collective-permute-done((bf16[4,128,512]{2,1,0:T(8,128)(2,1)}, bf16[4,128,512]{2,1,0:T(8,128)(2,1)}, u32[]{:S(2)}, u32[]{:S(2)}) %collective-permute-start.11) | collective-permute-done | bytes 524320 | tf_op jit(solution)/shard_map/ppermute | solution.py:58
  114.3 7.2 %collective-permute-done.13 = bf16[256,1024]{1,0:T(8,128)(2,1)S(1)} collective-permute-done((bf16[256,1024]{1,0:T(8,128)(2,1)S(1)}, bf16[256,1024]{1,0:T(8,128)(2,1)S(1)}, u32[]{:S(2)}, u32[]{:S(2)}) %collective-permute-start.13) | collective-permute-done | bytes 524320 | tf_op jit(solution)/shard_map/ppermute | solution.py:73
  123.2 12.1 %collective-permute-done.14.refs_1_ = bf16[512,1024]{1,0:T(8,128)(2,1)} collective-permute-done((bf16[512,1024]{1,0:T(8,128)(2,1)S(1)}, bf16[512,1024]{1,0:T(8,128)(2,1)}, u32[]{:S(2)}, u32[]{:S(2)}) %collective-permute-start.14) | collective-permute-done | bytes 1048608 | tf_op jit(solution)/shard_map/ppermute | solution.py:73
  137.4 7.2 %shard_map.225 = (f32[2048,128]{1,0:T(8,128)}, f32[2048,512]{1,0:T(8,128)}, bf16[1024,512]{1,0:T(8,128)(2,1)}) custom-call(s32[2]{0:T(128)} %copy-done.24, bf16[512,1152]{1,0:T(8,128)(2,1)} %pad_maximum_fusion.refs_0_, bf16[512,1152]{1,0:T(8,128)(2,1)} %collective-permute-done.12.refs_1_, bf16[512,1152]{1,0:T(8,128)(2,1)} %copy-done.48, ...), custom_call_target="tpu_custom_call" | custom-call | flops 2147483648 | bytes 12058632 | tf_op jit(solution)/shard_map/pallas_call | solution.py:44
  144.6 5.2 %all-to-all-done.1 = bf16[4,256,1024]{2,1,0:T(8,128)(2,1)S(1)} async-done(((bf16[4,256,1024]{2,1,0:T(8,128)(2,1)}), bf16[4,256,1024]{2,1,0:T(8,128)(2,1)S(1)}, u32[]{:S(2)}, u32[]{:S(2)}) %all-to-all-start.1) | async-done | bytes 2097184 | tf_op jit(solution)/shard_map/all_to_all | solution.py:441
  151.1 9.4 %shard_map.227 = (bf16[1024,1024]{1,0:T(8,128)(2,1)}, bf16[1024,512]{1,0:T(8,128)(2,1)}, bf16[1024,1024]{1,0:T(8,128)(2,1)}) custom-call(s32[2]{0:T(128)} %copy-done.24, bf16[512,1024]{1,0:T(8,128)(2,1)} %collective-permute-done.17.refs_0_.refs_2_, bf16[512,1024]{1,0:T(8,128)(2,1)} %collective-permute-done.18.refs_1_.refs_3_, bf16[1024,1024]{1,0:T(8,128)(2,1)} %bitcast.43, ...), custom_call_target="tpu_custom_call" | custom-call | flops 4294967296 | bytes 14680072 | tf_op jit(solution)/shard_map/pallas_call | solution.py:44
  162.0 9.8 %shard_map.226 = (f32[1024,1024]{1,0:T(8,128)}, bf16[1024,512]{1,0:T(8,128)(2,1)}, bf16[1024,1024]{1,0:T(8,128)(2,1)}) custom-call(s32[2]{0:T(128)} %copy-done.24, bf16[512,1024]{1,0:T(8,128)(2,1)} %copy-done.44, bf16[512,1024]{1,0:T(8,128)(2,1)} %collective-permute-done.14.refs_1_, bf16[1024,1024]{1,0:T(8,128)(2,1)} %bitcast.44, ...), custom_call_target="tpu_custom_call" | custom-call | flops 4294967296 | bytes 16777224 | tf_op jit(solution)/shard_map/pallas_call | solution.py:44
  176.6 6.3 %shard_map.228 = bf16[4,2,128,512]{3,2,1,0:T(8,128)(2,1)} custom-call(s32[2]{0:T(128)} %copy-done.24, bf16[512,1152]{1,0:T(8,128)(2,1)} %pad_maximum_fusion.refs_0_, bf16[512,1152]{1,0:T(8,128)(2,1)} %collective-permute-done.12.refs_1_, bf16[512,1152]{1,0:T(8,128)(2,1)} %copy-done.48, bf16[512,1152]{1,0:T(8,128)(2,1)} %copy-done.49, ...), custom_call_target="tpu_custom_call" | custom-call | flops 2147483648 | bytes 7864328 | tf_op jit(solution)/shard_map/pallas_call | solution.py:44
  187.0 4.3 %all-to-all-start.2 = ((bf16[4,256,512]{2,1,0:T(8,128)(2,1)}), bf16[4,256,512]{2,1,0:T(8,128)(2,1)}, u32[]{:S(2)}, u32[]{:S(2)}) async-start(bf16[4,256,512]{2,1,0:T(8,128)(2,1)} %bitcast.46), calls=%async_computation.2 | async-start | bytes 2097152 | tf_op jit(solution)/shard_map/all_to_all | solution.py:441
  193.6 8.9 %shard_map.231 = (bf16[4,128,1024]{2,1,0:T(8,128)(2,1)}, bf16[4,128,1024]{2,1,0:T(8,128)(2,1)}) custom-call(s32[2]{0:T(128)} %copy-done.24, bf16[512,1024]{1,0:T(8,128)(2,1)} %copy-done.44, bf16[512,1024]{1,0:T(8,128)(2,1)} %collective-permute-done.14.refs_1_, bf16[512,1024]{1,0:T(8,128)(2,1)} %collective-permute-done.17.refs_0_.refs_2_, ...), custom_call_target="tpu_custom_call" | custom-call | flops 4294967296 | bytes 10485768 | tf_op jit(solution)/shard_map/pallas_call | solution.py:44
  203.4 4.3 %shard_map.229 = f32[1024,1024]{1,0:T(8,128)} custom-call(s32[2]{0:T(128)} %copy-done.24, bf16[1024,512]{1,0:T(8,128)(2,1)} %get-tuple-element.102.refs_4_.active, bf16[1024,512]{1,0:T(8,128)(2,1)} %get-tuple-element.103.weights), custom_call_target="tpu_custom_call" | custom-call | flops 1073741824 | bytes 6291464 | tf_op jit(solution)/shard_map/pallas_call | solution.py:44
  208.7 8.4 %all-to-all-done.2 = bf16[4,256,512]{2,1,0:T(8,128)(2,1)} async-done(((bf16[4,256,512]{2,1,0:T(8,128)(2,1)}), bf16[4,256,512]{2,1,0:T(8,128)(2,1)}, u32[]{:S(2)}, u32[]{:S(2)}) %all-to-all-start.2) | async-done | bytes 1048608 | tf_op jit(solution)/shard_map/all_to_all | solution.py:441
  217.1 5.4 %fusion = (bf16[512,1024]{1,0:T(8,128)(2,1)}, f32[512,1024]{1,0:T(8,128)}) fusion(f32[1024,1024]{1,0:T(8,128)} %shard_map.229, bf16[1024,1024]{1,0:T(8,128)(2,1)} %collective-permute-done.20), kind=kLoop, calls=%fused_computation.1 | loop fusion | flops 2621440 | bytes 9437184 | tf_op jit(solution)/shard_map/convert_element_type | solution.py:513
  250.2 4.2 %shard_map.234 = (f32[512,768]{1,0:T(8,128)S(1)}, bf16[512,768]{1,0:T(8,128)(2,1)S(1)}, f32[128,1024]{1,0:T(8,128)S(1)}, bf16[128,1024]{1,0:T(8,128)(2,1)S(1)}) custom-call(s32[2]{0:T(128)S(1)} %copy-done.25, bf16[64,1024]{1,0:T(8,128)(2,1)S(1)} %get-tuple-element.115.refs_0_, bf16[64,1024]{1,0:T(8,128)(2,1)S(1)} %collective-permute-done.29.refs_1_, ...), custom_call_target="tpu_custom_call" | custom-call | flops 805306368 | bytes 6424584 | tf_op jit(solution)/shard_map/pallas_call | solution.py:44
  261.4 12.6 %collective-permute-done.32 = bf16[512,768]{1,0:T(8,128)(2,1)S(1)} collective-permute-done((bf16[512,768]{1,0:T(8,128)(2,1)S(1)}, bf16[512,768]{1,0:T(8,128)(2,1)S(1)}, u32[]{:S(2)}, u32[]{:S(2)}) %collective-permute-start.32) | collective-permute-done | bytes 786464 | tf_op jit(solution)/shard_map/ppermute | solution.py:58
  275.3 4.3 %collective-permute-done.39 = bf16[80,1024]{1,0:T(8,128)(2,1)S(1)} collective-permute-done((bf16[80,1024]{1,0:T(8,128)(2,1)S(1)}, bf16[80,1024]{1,0:T(8,128)(2,1)S(1)}, u32[]{:S(2)}, u32[]{:S(2)}) %collective-permute-start.39) | collective-permute-done | bytes 163872 | tf_op jit(solution)/shard_map/ppermute | solution.py:58
  288.6 4.6 %all-to-all-start.4 = ((f32[8,2,128]{2,1,0:T(2,128)}), f32[8,2,128]{2,1,0:T(2,128)S(1)}, u32[]{:S(2)}, u32[]{:S(2)}) async-start(f32[8,2,128]{2,1,0:T(2,128)} %bitcast.19), calls=%async_computation.4 | async-start | bytes 16384 | tf_op jit(solution)/shard_map/all_to_all | solution.py:740
  308.2 5.6 %collective-permute-done.34 = bf16[64,1024]{1,0:T(8,128)(2,1)S(1)} collective-permute-done((bf16[64,1024]{1,0:T(8,128)(2,1)S(1)}, bf16[64,1024]{1,0:T(8,128)(2,1)S(1)}, u32[]{:S(2)}, u32[]{:S(2)}) %collective-permute-start.34) | collective-permute-done | bytes 131104 | tf_op jit(solution)/shard_map/ppermute | solution.py:73
  (258 shorter events, 147.1 us)
Async XLA Ops:
  16.9 17.6 %collective-permute-start.1 = (bf16[288,768]{1,0:T(8,128)(2,1)S(1)}, bf16[288,768]{1,0:T(8,128)(2,1)S(1)}, u32[]{:S(2)}, u32[]{:S(2)}) collective-permute-start(bf16[288,768]{1,0:T(8,128)(2,1)S(1)} %pad_maximum_fusion.8), channel_id=1, source_target_pairs={{0,8},{1,17},{2,10},{3,19},{4,12},{5,21},{6,14},{7,23},{8,0},{9,25... | collective-permute-start | bytes 1327112 | tf_op jit(solution)/shard_map/ppermute | solution.py:73
  19.4 16.6 %collective-permute-start.2 = (bf16[64,1152]{1,0:T(8,128)(2,1)S(1)}, bf16[64,1152]{1,0:T(8,128)(2,1)S(1)}, u32[]{:S(2)}, u32[]{:S(2)}) collective-permute-start(bf16[64,1152]{1,0:T(8,128)(2,1)S(1)} %pad_maximum_fusion.14), channel_id=1, source_target_pairs={{0,16},{1,17},{2,18},{3,19},{4,20},{5,21},{6,22},{7,23},{8,24},{9,... | collective-permute-start | bytes 442376 | tf_op jit(solution)/shard_map/ppermute | solution.py:73
  36.1 15.1 %collective-permute-start.3 = (bf16[576,768]{1,0:T(8,128)(2,1)S(1)}, bf16[576,768]{1,0:T(8,128)(2,1)S(1)}, u32[]{:S(2)}, u32[]{:S(2)}) collective-permute-start(bf16[576,768]{1,0:T(8,128)(2,1)S(1)} %pad_maximum_fusion.1.refs_0_), channel_id=1, source_target_pairs={{0,4},{1,9},{2,6},{3,11},{4,0},{5,13},{6,2},{7,15},{8,12},{9,1},{1... | collective-permute-start | bytes 2654216 | tf_op jit(solution)/shard_map/ppermute | solution.py:73
  37.5 18.1 %collective-permute-start.4 = (bf16[128,1152]{1,0:T(8,128)(2,1)}, bf16[128,1152]{1,0:T(8,128)(2,1)S(1)}, u32[]{:S(2)}, u32[]{:S(2)}) collective-permute-start(bf16[128,1152]{1,0:T(8,128)(2,1)} %pad_maximum_fusion.10), channel_id=1, source_target_pairs={{0,8},{1,9},{2,10},{3,11},{4,12},{5,13},{6,14},{7,15},{8,0},{9,1},... | collective-permute-start | bytes 884744 | tf_op jit(solution)/shard_map/ppermute | solution.py:73
  51.1 27.4 %all-to-all-start = ((bf16[4,256,512]{2,1,0:T(8,128)(2,1)}), bf16[4,256,512]{2,1,0:T(8,128)(2,1)}, u32[]{:S(2)}, u32[]{:S(2)}) async-start(bf16[4,256,512]{2,1,0:T(8,128)(2,1)} %bitcast.7), calls=%async_computation | async-start | bytes 2097152 | tf_op jit(solution)/shard_map/all_to_all | solution.py:441
  56.5 13.2 %collective-permute-start.7 = (bf16[256,1152]{1,0:T(8,128)(2,1)}, bf16[256,1152]{1,0:T(8,128)(2,1)}, u32[]{:S(2)}, u32[]{:S(2)}) collective-permute-start(bf16[256,1152]{1,0:T(8,128)(2,1)} %pad_maximum_fusion.4), channel_id=1, source_target_pairs={{0,4},{1,3},{2,6},{3,1},{4,0},{5,7},{6,2},{7,5},{8,12},{9,11},{10,... | collective-permute-start | bytes 1769480 | tf_op jit(solution)/shard_map/ppermute | solution.py:73
  63.8 24.7 %collective-permute-start.9 = (bf16[4,128,1024]{2,1,0:T(8,128)(2,1)}, bf16[4,128,1024]{2,1,0:T(8,128)(2,1)S(1)}, u32[]{:S(2)}, u32[]{:S(2)}) collective-permute-start(bf16[4,128,1024]{2,1,0:T(8,128)(2,1)} %copy-done.27), channel_id=1, source_target_pairs={{0,4},{4,0},{8,12},{12,8},{16,20},{20,16},{24,28},{28,24},{1,5},{5... | collective-permute-start | bytes 3145736 | tf_op jit(solution)/shard_map/ppermute | solution.py:58
  82.8 30.3 %collective-permute-start.12 = (bf16[512,1152]{1,0:T(8,128)(2,1)}, bf16[512,1152]{1,0:T(8,128)(2,1)}, u32[]{:S(2)}, u32[]{:S(2)}) collective-permute-start(bf16[512,1152]{1,0:T(8,128)(2,1)} %pad_maximum_fusion.refs_0_), channel_id=1, source_target_pairs={{0,2},{1,5},{2,0},{3,7},{4,6},{5,1},{6,4},{7,3},{8,10},{9,13},{10,... | collective-permute-start | bytes 3538952 | tf_op jit(solution)/shard_map/ppermute | solution.py:73
  93.2 20.0 %collective-permute-start.11 = (bf16[4,128,512]{2,1,0:T(8,128)(2,1)}, bf16[4,128,512]{2,1,0:T(8,128)(2,1)}, u32[]{:S(2)}, u32[]{:S(2)}) collective-permute-start(bf16[4,128,512]{2,1,0:T(8,128)(2,1)} %get-tuple-element.193), channel_id=1, source_target_pairs={{0,4},{4,0},{8,12},{12,8},{16,20},{20,16},{24,28},{28,24},{1,5},{5... | collective-permute-start | bytes 1572872 | tf_op jit(solution)/shard_map/ppermute | solution.py:58
  98.6 51.3 %all-to-all-start.1 = ((bf16[4,256,1024]{2,1,0:T(8,128)(2,1)}), bf16[4,256,1024]{2,1,0:T(8,128)(2,1)S(1)}, u32[]{:S(2)}, u32[]{:S(2)}) async-start(bf16[4,256,1024]{2,1,0:T(8,128)(2,1)} %shard_map.224), calls=%async_computation.1 | async-start | bytes 4194304 | tf_op jit(solution)/shard_map/all_to_all | solution.py:441
  121.5 13.8 %collective-permute-start.14 = (bf16[512,1024]{1,0:T(8,128)(2,1)S(1)}, bf16[512,1024]{1,0:T(8,128)(2,1)}, u32[]{:S(2)}, u32[]{:S(2)}) collective-permute-start(bf16[512,1024]{1,0:T(8,128)(2,1)S(1)} %constant_dynamic-update-slice_fusion.refs_0_), channel_id=1, source_target_pairs={{0,2},{1,5},{2,0},{3,7},{4,6},{5,1},{6,4},{7,3},{8,10},{9,13},{10,... | collective-permute-start | bytes 3145736 | tf_op jit(solution)/shard_map/ppermute | solution.py:73
  122.7 12.7 %collective-permute-start.16 = (bf16[512,1152]{1,0:T(8,128)(2,1)}, bf16[512,1152]{1,0:T(8,128)(2,1)S(1)}, u32[]{:S(2)}, u32[]{:S(2)}) collective-permute-start(bf16[512,1152]{1,0:T(8,128)(2,1)} %collective-permute-done.12.refs_1_), channel_id=1, source_target_pairs={{0,1},{1,0},{2,3},{3,2},{4,5},{5,4},{6,7},{7,6},{8,9},{9,8},{10,11... | collective-permute-start | bytes 3538952 | tf_op jit(solution)/shard_map/ppermute | solution.py:58
  123.2 21.4 %collective-permute-start.17 = (bf16[512,1024]{1,0:T(8,128)(2,1)S(1)}, bf16[512,1024]{1,0:T(8,128)(2,1)}, u32[]{:S(2)}, u32[]{:S(2)}) collective-permute-start(bf16[512,1024]{1,0:T(8,128)(2,1)S(1)} %constant_dynamic-update-slice_fusion.refs_0_), channel_id=1, source_target_pairs={{0,1},{1,0},{2,3},{3,2},{4,5},{5,4},{6,7},{7,6},{8,9},{9,8},{10,11... | collective-permute-start | bytes 3145736 | tf_op jit(solution)/shard_map/ppermute | solution.py:58
  135.3 14.5 %collective-permute-start.18 = (bf16[512,1024]{1,0:T(8,128)(2,1)}, bf16[512,1024]{1,0:T(8,128)(2,1)}, u32[]{:S(2)}, u32[]{:S(2)}) collective-permute-start(bf16[512,1024]{1,0:T(8,128)(2,1)} %collective-permute-done.14.refs_1_), channel_id=1, source_target_pairs={{0,1},{1,0},{2,3},{3,2},{4,5},{5,4},{6,7},{7,6},{8,9},{9,8},{10,11... | collective-permute-start | bytes 3145736 | tf_op jit(solution)/shard_map/ppermute | solution.py:58
  175.7 15.6 %collective-permute-start.24 = (bf16[512,1024]{1,0:T(8,128)(2,1)}, bf16[512,1024]{1,0:T(8,128)(2,1)}, u32[]{:S(2)}, u32[]{:S(2)}) collective-permute-start(bf16[512,1024]{1,0:T(8,128)(2,1)} %get-tuple-element.180), channel_id=1, source_target_pairs={{0,2},{1,5},{2,0},{3,7},{4,6},{5,1},{6,4},{7,3},{8,10},{9,13},{10,... | collective-permute-start | bytes 3145736 | tf_op jit(solution)/shard_map/ppermute | solution.py:73
  186.7 30.3 %collective-permute-start.20 = (bf16[1024,1024]{1,0:T(8,128)(2,1)}, bf16[1024,1024]{1,0:T(8,128)(2,1)}, u32[]{:S(2)}, u32[]{:S(2)}) collective-permute-start(bf16[1024,1024]{1,0:T(8,128)(2,1)} %shard_map.230), channel_id=1, source_target_pairs={{0,1},{1,0},{2,3},{3,2},{4,5},{5,4},{6,7},{7,6},{8,9},{9,8},{10,11... | collective-permute-start | bytes 6291464 | tf_op jit(solution)/shard_map/ppermute | solution.py:58
  187.0 30.0 %all-to-all-start.2 = ((bf16[4,256,512]{2,1,0:T(8,128)(2,1)}), bf16[4,256,512]{2,1,0:T(8,128)(2,1)}, u32[]{:S(2)}, u32[]{:S(2)}) async-start(bf16[4,256,512]{2,1,0:T(8,128)(2,1)} %bitcast.46), calls=%async_computation.2 | async-start | bytes 2097152 | tf_op jit(solution)/shard_map/all_to_all | solution.py:441
  192.9 14.7 %collective-permute-start.25 = (bf16[256,1024]{1,0:T(8,128)(2,1)S(1)}, bf16[256,1024]{1,0:T(8,128)(2,1)S(1)}, u32[]{:S(2)}, u32[]{:S(2)}) collective-permute-start(bf16[256,1024]{1,0:T(8,128)(2,1)S(1)} %get-tuple-element.110), channel_id=1, source_target_pairs={{0,4},{1,3},{2,6},{3,1},{4,0},{5,7},{6,2},{7,5},{8,12},{9,11},{10,... | collective-permute-start | bytes 1572872 | tf_op jit(solution)/shard_map/ppermute | solution.py:73
  202.4 24.5 %collective-permute-start.23 = (bf16[4,128,1024]{2,1,0:T(8,128)(2,1)}, bf16[4,128,1024]{2,1,0:T(8,128)(2,1)S(1)}, u32[]{:S(2)}, u32[]{:S(2)}) collective-permute-start(bf16[4,128,1024]{2,1,0:T(8,128)(2,1)} %get-tuple-element.109), channel_id=1, source_target_pairs={{0,4},{4,0},{8,12},{12,8},{16,20},{20,16},{24,28},{28,24},{1,5},{5... | collective-permute-start | bytes 3145736 | tf_op jit(solution)/shard_map/ppermute | solution.py:58
  222.5 24.0 %collective-permute-start.21 = (bf16[512,1024]{1,0:T(8,128)(2,1)}, bf16[512,1024]{1,0:T(8,128)(2,1)}, u32[]{:S(2)}, u32[]{:S(2)}) collective-permute-start(bf16[512,1024]{1,0:T(8,128)(2,1)} %get-tuple-element.181), channel_id=1, source_target_pairs={{0,2},{1,5},{2,0},{3,7},{4,6},{5,1},{6,4},{7,3},{8,10},{9,13},{10,... | collective-permute-start | bytes 3145736 | tf_op jit(solution)/shard_map/ppermute | solution.py:73
  233.8 54.8 %all-to-all-start.3 = ((bf16[4,256,1024]{2,1,0:T(8,128)(2,1)}), bf16[4,256,1024]{2,1,0:T(8,128)(2,1)S(1)}, u32[]{:S(2)}, u32[]{:S(2)}) async-start(bf16[4,256,1024]{2,1,0:T(8,128)(2,1)} %copy-done.2), calls=%async_computation.3 | async-start | bytes 4194304 | tf_op jit(solution)/shard_map/all_to_all | solution.py:441
  254.4 19.7 %collective-permute-start.32 = (bf16[512,768]{1,0:T(8,128)(2,1)S(1)}, bf16[512,768]{1,0:T(8,128)(2,1)S(1)}, u32[]{:S(2)}, u32[]{:S(2)}) collective-permute-start(bf16[512,768]{1,0:T(8,128)(2,1)S(1)} %get-tuple-element.122), channel_id=1, source_target_pairs={{0,4},{4,0},{8,12},{12,8},{16,20},{20,16},{24,28},{28,24},{1,5},{5... | collective-permute-start | bytes 2359304 | tf_op jit(solution)/shard_map/ppermute | solution.py:58
  287.5 16.4 %collective-permute-start.42 = (bf16[4,128,512]{2,1,0:T(8,128)(2,1)}, bf16[4,128,512]{2,1,0:T(8,128)(2,1)}, u32[]{:S(2)}, u32[]{:S(2)}) collective-permute-start(bf16[4,128,512]{2,1,0:T(8,128)(2,1)} %get-tuple-element.192), channel_id=1, source_target_pairs={{0,4},{4,0},{8,12},{12,8},{16,20},{20,16},{24,28},{28,24},{1,5},{5... | collective-permute-start | bytes 1572872 | tf_op jit(solution)/shard_map/ppermute | solution.py:58
  297.0 18.5 %collective-permute-start.41 = (bf16[128,768]{1,0:T(8,128)(2,1)S(1)}, bf16[128,768]{1,0:T(8,128)(2,1)}, u32[]{:S(2)}, u32[]{:S(2)}) collective-permute-start(bf16[128,768]{1,0:T(8,128)(2,1)S(1)} %slice.303), channel_id=1, source_target_pairs={{0,16},{4,20},{8,24},{12,28},{16,0},{20,4},{24,8},{28,12},{1,17},{... | collective-permute-start | bytes 589832 | tf_op jit(solution)/shard_map/ppermute | solution.py:58
  (74 other events, 568.8 us)

commit v6 on v5

--- a/solution.py
+++ b/solution.py
@@ -557,7 +557,7 @@
             kept, sent = total[:half], total[half:].astype(LOW)
         return kept, swap(sent, "tensor", t_masks[-1])
 
-    grad_third = swap_by_parity(after(grad_steps[-1], attn_arrays[-1]), *path[2])
+    grad_third = swap_by_parity(grad_steps[-1], *path[2])
     kept, got = scatter_rows(kept, sent)
     middle, second_hidden = call(
         functools.partial(middle_body, rows),
@@ -580,7 +580,7 @@
             grad_field, grad_got = grad_steps[-1], grad_third
             for k in range(3, len(path)):
                 grad_field = jnp.concatenate([grad_field, grad_got])
-                grad_got = swap_by_parity(after(grad_field, second_hidden), *path[k])
+                grad_got = swap_by_parity(grad_field, *path[k])
             grad_pieces = [grad_field, grad_got]
     hidden_pieces = hidden_pieces + [swap(p, *last) for p in hidden_pieces]
     grad_pieces = grad_pieces + [swap(p, *last) for p in grad_pieces]
@@ -680,7 +680,7 @@
     both_this, both_other = weight_grad(hidden_pieces, kept_both, after(sent_both, sent_out), True)
     grad_near = to_neighbour(both_this, both_other)
     down_line = along(down_grad.reshape(pairs, 2 * part, wide))
-    sent = after(sent, down_line, both_other, kept_out)
+    sent = after(sent, down_line, both_other)
     for k in range(2, steps_back - 1):
         kept, sent = scatter_stage(kept, sent, k)
     grad_kept, grad_got = scatter_stage(kept, after(sent, out_sent), steps_back - 1)

time: 328 us -> 325 us (level)
  starting transfers between devices: 62 us -> 72.2 us
  waiting for transfers between devices: 126 us -> 119 us
  local copies, waits for them, and re-layouts: 32.1 us -> 25.6 us
    ppermute x24, starting transfers between devices: 23.5 us -> 35.8 us  [swap(): return lax.ppermute(field, axis, [(i, i ^ mask) for i in range(count)])]
    unnamed x103 -> x89, local copies, waits for them, and re-layouts: 22.8 us -> 17.6 us
    all_to_all x4, waiting for transfers between devices: 20.3 us -> 15.8 us  [along(): lax.all_to_all(blocks, 'expert', 0, 0, tiled=True, axis_index_groups=lines)]
    ppermute x24, waiting for transfers between devices: 40.9 us -> 36.8 us  [swap(): return lax.ppermute(field, axis, [(i, i ^ mask) for i in range(count)])]
where the time goes in v6:
time: 325 us; the launch traced here: 323 us
  waiting for transfers between devices  119 us (37%)
  starting transfers between devices  72.2 us (22%)
  Pallas kernels  71.3 us (22%)
  other arithmetic  34.2 us (11%)
  local copies, waits for them, and re-layouts  25.6 us (8%)
    pallas_call x17, Pallas kernels, call(): pl.pallas_call(body, out_shape=list(outs), in_specs=[pl.BlockSpec(memory_...  71.3 us
    ppermute x19, waiting for transfers between devices, swap_by_parity(): return lax.ppermute(field, ('expert', 'tensor'), pairs)  65.3 us
    ppermute x24, waiting for transfers between devices, swap(): return lax.ppermute(field, axis, [(i, i ^ mask) for i in range(count)])  36.8 us
    ppermute x24, starting transfers between devices, swap(): return lax.ppermute(field, axis, [(i, i ^ mask) for i in range(count)])  35.8 us
    unnamed x89, local copies, waits for them, and re-layouts  17.6 us
    ppermute x19, starting transfers between devices, swap_by_parity(): return lax.ppermute(field, ('expert', 'tensor'), pairs)  16.5 us
    all_to_all x4, starting transfers between devices, along(): lax.all_to_all(blocks, 'expert', 0, 0, tiled=True, axis_index_groups=lines)  16.2 us
    all_to_all x4, waiting for transfers between devices, along(): lax.all_to_all(blocks, 'expert', 0, 0, tiled=True, axis_index_groups=lines)  15.8 us
  transfers between devices with their start and end apart: 48, of which 24 were waited for; matrix products, arithmetic and copies ran while one was open for 11% of the time, Pallas kernels for 19%

profile of v6, /device:TPU:1, one launch (start us, length us, event | category | flops | bytes accessed | tf_op | source)
XLA Modules:
  0.0 323.3 jit_solution(13428078975171769831)
XLA Ops:
  19.5 14.9 %collective-permute-done.1 = bf16[288,768]{1,0:T(8,128)(2,1)S(1)} collective-permute-done((bf16[288,768]{1,0:T(8,128)(2,1)S(1)}, bf16[288,768]{1,0:T(8,128)(2,1)S(1)}, u32[]{:S(2)}, u32[]{:S(2)}) %collective-permute-start.1) | collective-permute-done | bytes 442400 | tf_op jit(solution)/shard_map/ppermute | solution.py:73
  38.3 12.9 %collective-permute-done.3.refs_1_ = bf16[576,768]{1,0:T(8,128)(2,1)S(1)} collective-permute-done((bf16[576,768]{1,0:T(8,128)(2,1)S(1)}, bf16[576,768]{1,0:T(8,128)(2,1)S(1)}, u32[]{:S(2)}, u32[]{:S(2)}) %collective-permute-start.3) | collective-permute-done | bytes 884768 | tf_op jit(solution)/shard_map/ppermute | solution.py:73
  51.1 4.3 %all-to-all-start = ((bf16[4,256,512]{2,1,0:T(8,128)(2,1)}), bf16[4,256,512]{2,1,0:T(8,128)(2,1)}, u32[]{:S(2)}, u32[]{:S(2)}) async-start(bf16[4,256,512]{2,1,0:T(8,128)(2,1)} %bitcast.7), calls=%async_computation | async-start | bytes 2097152 | tf_op jit(solution)/shard_map/all_to_all | solution.py:441
  70.5 8.0 %all-to-all-done = bf16[4,256,512]{2,1,0:T(8,128)(2,1)} async-done(((bf16[4,256,512]{2,1,0:T(8,128)(2,1)}), bf16[4,256,512]{2,1,0:T(8,128)(2,1)}, u32[]{:S(2)}, u32[]{:S(2)}) %all-to-all-start) | async-done | bytes 1048608 | tf_op jit(solution)/shard_map/all_to_all | solution.py:441
  89.8 5.1 %collective-permute-done.10 = bf16[128,1024]{1,0:T(8,128)(2,1)S(1)} collective-permute-done((bf16[128,1024]{1,0:T(8,128)(2,1)S(1)}, bf16[128,1024]{1,0:T(8,128)(2,1)S(1)}, u32[]{:S(2)}, u32[]{:S(2)}) %collective-permute-start.10) | collective-permute-done | bytes 262176 | tf_op jit(solution)/shard_map/ppermute | solution.py:73
  100.4 7.3 %collective-permute-done.11.refs_5_ = bf16[4,128,512]{2,1,0:T(8,128)(2,1)} collective-permute-done((bf16[4,128,512]{2,1,0:T(8,128)(2,1)}, bf16[4,128,512]{2,1,0:T(8,128)(2,1)}, u32[]{:S(2)}, u32[]{:S(2)}) %collective-permute-start.11) | collective-permute-done | bytes 524320 | tf_op jit(solution)/shard_map/ppermute | solution.py:58
  107.8 8.3 %collective-permute-done.13 = bf16[256,1024]{1,0:T(8,128)(2,1)S(1)} collective-permute-done((bf16[256,1024]{1,0:T(8,128)(2,1)S(1)}, bf16[256,1024]{1,0:T(8,128)(2,1)S(1)}, u32[]{:S(2)}, u32[]{:S(2)}) %collective-permute-start.13) | collective-permute-done | bytes 524320 | tf_op jit(solution)/shard_map/ppermute | solution.py:73
  120.5 10.0 %collective-permute-done.14.refs_1_ = bf16[512,1024]{1,0:T(8,128)(2,1)S(1)} collective-permute-done((bf16[512,1024]{1,0:T(8,128)(2,1)S(1)}, bf16[512,1024]{1,0:T(8,128)(2,1)S(1)}, u32[]{:S(2)}, u32[]{:S(2)}) %collective-permute-start.14) | collective-permute-done | bytes 1048608 | tf_op jit(solution)/shard_map/ppermute | solution.py:73
  130.4 4.3 %collective-permute-start.18 = (bf16[512,1024]{1,0:T(8,128)(2,1)S(1)}, bf16[512,1024]{1,0:T(8,128)(2,1)}, u32[]{:S(2)}, u32[]{:S(2)}) collective-permute-start(bf16[512,1024]{1,0:T(8,128)(2,1)S(1)} %collective-permute-done.14.refs_1_), channel_id=1, source_target_pairs={{0,1},{1,0},{2,3},{3,2},{4,5},{5,4},{6,7},{7,6},{8,9},{9,8},{10,11... | collective-permute-start | bytes 3145736 | tf_op jit(solution)/shard_map/ppermute | solution.py:58
  136.7 7.2 %shard_map.225 = (f32[2048,128]{1,0:T(8,128)}, f32[2048,512]{1,0:T(8,128)}, bf16[1024,512]{1,0:T(8,128)(2,1)}) custom-call(s32[2]{0:T(128)} %copy-done.22, bf16[512,1152]{1,0:T(8,128)(2,1)} %pad_maximum_fusion.refs_0_, bf16[512,1152]{1,0:T(8,128)(2,1)} %collective-permute-done.12.refs_1_, bf16[512,1152]{1,0:T(8,128)(2,1)} %copy-done.40, ...), custom_call_target="tpu_custom_call" | custom-call | flops 2147483648 | bytes 12058632 | tf_op jit(solution)/shard_map/pallas_call | solution.py:44
  145.3 9.4 %shard_map.227 = (bf16[1024,1024]{1,0:T(8,128)(2,1)}, bf16[1024,512]{1,0:T(8,128)(2,1)}, bf16[1024,1024]{1,0:T(8,128)(2,1)}) custom-call(s32[2]{0:T(128)} %copy-done.22, bf16[512,1024]{1,0:T(8,128)(2,1)} %collective-permute-done.17.refs_0_.refs_2_, bf16[512,1024]{1,0:T(8,128)(2,1)} %collective-permute-done.18.refs_1_.refs_3_, bf16[1024,1024]{1,0:T(8,128)(2,1)} %bitcast.43, ...), custom_call_target="tpu_custom_call" | custom-call | flops 4294967296 | bytes 14680072 | tf_op jit(solution)/shard_map/pallas_call | solution.py:44
  154.7 4.4 %collective-permute-start.19 = (bf16[1024,1024]{1,0:T(8,128)(2,1)}, bf16[1024,1024]{1,0:T(8,128)(2,1)S(1)}, u32[]{:S(2)}, u32[]{:S(2)}) collective-permute-start(bf16[1024,1024]{1,0:T(8,128)(2,1)} %get-tuple-element.96), channel_id=1, source_target_pairs={{0,1},{1,0},{2,3},{3,2},{4,5},{5,4},{6,7},{7,6},{8,9},{9,8},{10,11... | collective-permute-start | bytes 6291464 | tf_op jit(solution)/shard_map/ppermute | solution.py:58
  159.0 9.8 %shard_map.226 = (f32[1024,1024]{1,0:T(8,128)}, bf16[1024,512]{1,0:T(8,128)(2,1)}, bf16[1024,1024]{1,0:T(8,128)(2,1)}) custom-call(s32[2]{0:T(128)} %copy-done.22, bf16[512,1024]{1,0:T(8,128)(2,1)} %copy-done.36, bf16[512,1024]{1,0:T(8,128)(2,1)} %copy-done.42, bf16[1024,1024]{1,0:T(8,128)(2,1)} %bitcast.44, f32[2048,128]{1,0:T(8,128)} %get-tuple-element.91.refs_3_, ...), custom_call_target="tpu_custom_call" | custom-call | flops 4294967296 | bytes 16777224 | tf_op jit(solution)/shard_map/pallas_call | solution.py:44
  173.7 6.3 %shard_map.228 = bf16[4,2,128,512]{3,2,1,0:T(8,128)(2,1)} custom-call(s32[2]{0:T(128)} %copy-done.22, bf16[512,1152]{1,0:T(8,128)(2,1)} %pad_maximum_fusion.refs_0_, bf16[512,1152]{1,0:T(8,128)(2,1)} %collective-permute-done.12.refs_1_, bf16[512,1152]{1,0:T(8,128)(2,1)} %copy-done.40, bf16[512,1152]{1,0:T(8,128)(2,1)} %copy-done.41, ...), custom_call_target="tpu_custom_call" | custom-call | flops 2147483648 | bytes 7864328 | tf_op jit(solution)/shard_map/pallas_call | solution.py:44
  183.9 4.3 %all-to-all-start.2 = ((bf16[4,256,512]{2,1,0:T(8,128)(2,1)}), bf16[4,256,512]{2,1,0:T(8,128)(2,1)}, u32[]{:S(2)}, u32[]{:S(2)}) async-start(bf16[4,256,512]{2,1,0:T(8,128)(2,1)} %bitcast.46), calls=%async_computation.2 | async-start | bytes 2097152 | tf_op jit(solution)/shard_map/all_to_all | solution.py:441
  190.6 8.9 %shard_map.231 = (bf16[4,128,1024]{2,1,0:T(8,128)(2,1)}, bf16[4,128,1024]{2,1,0:T(8,128)(2,1)}) custom-call(s32[2]{0:T(128)} %copy-done.22, bf16[512,1024]{1,0:T(8,128)(2,1)} %copy-done.36, bf16[512,1024]{1,0:T(8,128)(2,1)} %copy-done.42, bf16[512,1024]{1,0:T(8,128)(2,1)} %collective-permute-done.17.refs_0_.refs_2_, ...), custom_call_target="tpu_custom_call" | custom-call | flops 4294967296 | bytes 10485768 | tf_op jit(solution)/shard_map/pallas_call | solution.py:44
  200.5 4.3 %shard_map.229 = f32[1024,1024]{1,0:T(8,128)} custom-call(s32[2]{0:T(128)} %copy-done.22, bf16[1024,512]{1,0:T(8,128)(2,1)} %get-tuple-element.98.refs_4_.active, bf16[1024,512]{1,0:T(8,128)(2,1)} %get-tuple-element.99.weights), custom_call_target="tpu_custom_call" | custom-call | flops 1073741824 | bytes 6291464 | tf_op jit(solution)/shard_map/pallas_call | solution.py:44
  205.8 7.8 %all-to-all-done.2 = bf16[4,256,512]{2,1,0:T(8,128)(2,1)} async-done(((bf16[4,256,512]{2,1,0:T(8,128)(2,1)}), bf16[4,256,512]{2,1,0:T(8,128)(2,1)}, u32[]{:S(2)}, u32[]{:S(2)}) %all-to-all-start.2) | async-done | bytes 1048608 | tf_op jit(solution)/shard_map/all_to_all | solution.py:441
  213.6 5.4 %fusion = (bf16[512,1024]{1,0:T(8,128)(2,1)}, f32[512,1024]{1,0:T(8,128)}) fusion(f32[1024,1024]{1,0:T(8,128)} %shard_map.229, bf16[1024,1024]{1,0:T(8,128)(2,1)} %collective-permute-done.20), kind=kLoop, calls=%fused_computation.1 | loop fusion | flops 2621440 | bytes 9437184 | tf_op jit(solution)/shard_map/convert_element_type | solution.py:513
  234.5 4.3 %collective-permute-start.29 = (bf16[64,1024]{1,0:T(8,128)(2,1)S(1)}, bf16[64,1024]{1,0:T(8,128)(2,1)S(1)}, u32[]{:S(2)}, u32[]{:S(2)}) collective-permute-start(bf16[64,1024]{1,0:T(8,128)(2,1)S(1)} %get-tuple-element.111.refs_0_), channel_id=1, source_target_pairs={{0,2},{1,3},{2,0},{3,1},{4,6},{5,7},{6,4},{7,5},{8,10},{9,11},{10,... | collective-permute-start | bytes 393224 | tf_op jit(solution)/shard_map/ppermute | solution.py:58
  247.2 4.2 %shard_map.234 = (f32[512,768]{1,0:T(8,128)S(1)}, bf16[512,768]{1,0:T(8,128)(2,1)S(1)}, f32[128,1024]{1,0:T(8,128)S(1)}, bf16[128,1024]{1,0:T(8,128)(2,1)S(1)}) custom-call(s32[2]{0:T(128)S(1)} %copy-done.23, bf16[64,1024]{1,0:T(8,128)(2,1)S(1)} %get-tuple-element.111.refs_0_, bf16[64,1024]{1,0:T(8,128)(2,1)S(1)} %collective-permute-done.29.refs_1_, ...), custom_call_target="tpu_custom_call" | custom-call | flops 805306368 | bytes 6424584 | tf_op jit(solution)/shard_map/pallas_call | solution.py:44
  259.2 12.0 %collective-permute-done.32 = bf16[512,768]{1,0:T(8,128)(2,1)S(1)} collective-permute-done((bf16[512,768]{1,0:T(8,128)(2,1)S(1)}, bf16[512,768]{1,0:T(8,128)(2,1)S(1)}, u32[]{:S(2)}, u32[]{:S(2)}) %collective-permute-start.32) | collective-permute-done | bytes 786464 | tf_op jit(solution)/shard_map/ppermute | solution.py:58
  272.0 5.0 %collective-permute-done.39 = bf16[80,1024]{1,0:T(8,128)(2,1)S(1)} collective-permute-done((bf16[80,1024]{1,0:T(8,128)(2,1)S(1)}, bf16[80,1024]{1,0:T(8,128)(2,1)S(1)}, u32[]{:S(2)}, u32[]{:S(2)}) %collective-permute-start.39) | collective-permute-done | bytes 163872 | tf_op jit(solution)/shard_map/ppermute | solution.py:58
  305.3 5.6 %collective-permute-done.34 = bf16[64,1024]{1,0:T(8,128)(2,1)S(1)} collective-permute-done((bf16[64,1024]{1,0:T(8,128)(2,1)S(1)}, bf16[64,1024]{1,0:T(8,128)(2,1)S(1)}, u32[]{:S(2)}, u32[]{:S(2)}) %collective-permute-start.34) | collective-permute-done | bytes 131104 | tf_op jit(solution)/shard_map/ppermute | solution.py:73
  (244 shorter events, 148.3 us)
Async XLA Ops:
  16.9 17.6 %collective-permute-start.1 = (bf16[288,768]{1,0:T(8,128)(2,1)S(1)}, bf16[288,768]{1,0:T(8,128)(2,1)S(1)}, u32[]{:S(2)}, u32[]{:S(2)}) collective-permute-start(bf16[288,768]{1,0:T(8,128)(2,1)S(1)} %pad_maximum_fusion.8), channel_id=1, source_target_pairs={{0,8},{1,17},{2,10},{3,19},{4,12},{5,21},{6,14},{7,23},{8,0},{9,25... | collective-permute-start | bytes 1327112 | tf_op jit(solution)/shard_map/ppermute | solution.py:73
  19.4 16.6 %collective-permute-start.2 = (bf16[64,1152]{1,0:T(8,128)(2,1)S(1)}, bf16[64,1152]{1,0:T(8,128)(2,1)S(1)}, u32[]{:S(2)}, u32[]{:S(2)}) collective-permute-start(bf16[64,1152]{1,0:T(8,128)(2,1)S(1)} %pad_maximum_fusion.14), channel_id=1, source_target_pairs={{0,16},{1,17},{2,18},{3,19},{4,20},{5,21},{6,22},{7,23},{8,24},{9,... | collective-permute-start | bytes 442376 | tf_op jit(solution)/shard_map/ppermute | solution.py:73
  36.1 15.1 %collective-permute-start.3 = (bf16[576,768]{1,0:T(8,128)(2,1)S(1)}, bf16[576,768]{1,0:T(8,128)(2,1)S(1)}, u32[]{:S(2)}, u32[]{:S(2)}) collective-permute-start(bf16[576,768]{1,0:T(8,128)(2,1)S(1)} %pad_maximum_fusion.1.refs_0_), channel_id=1, source_target_pairs={{0,4},{1,9},{2,6},{3,11},{4,0},{5,13},{6,2},{7,15},{8,12},{9,1},{1... | collective-permute-start | bytes 2654216 | tf_op jit(solution)/shard_map/ppermute | solution.py:73
  37.5 17.9 %collective-permute-start.4 = (bf16[128,1152]{1,0:T(8,128)(2,1)}, bf16[128,1152]{1,0:T(8,128)(2,1)}, u32[]{:S(2)}, u32[]{:S(2)}) collective-permute-start(bf16[128,1152]{1,0:T(8,128)(2,1)} %pad_maximum_fusion.10), channel_id=1, source_target_pairs={{0,8},{1,9},{2,10},{3,11},{4,12},{5,13},{6,14},{7,15},{8,0},{9,1},... | collective-permute-start | bytes 884744 | tf_op jit(solution)/shard_map/ppermute | solution.py:73
  51.1 27.4 %all-to-all-start = ((bf16[4,256,512]{2,1,0:T(8,128)(2,1)}), bf16[4,256,512]{2,1,0:T(8,128)(2,1)}, u32[]{:S(2)}, u32[]{:S(2)}) async-start(bf16[4,256,512]{2,1,0:T(8,128)(2,1)} %bitcast.7), calls=%async_computation | async-start | bytes 2097152 | tf_op jit(solution)/shard_map/all_to_all | solution.py:441
  58.2 25.6 %collective-permute-start.9 = (bf16[4,128,1024]{2,1,0:T(8,128)(2,1)}, bf16[4,128,1024]{2,1,0:T(8,128)(2,1)}, u32[]{:S(2)}, u32[]{:S(2)}) collective-permute-start(bf16[4,128,1024]{2,1,0:T(8,128)(2,1)} %copy-done.25), channel_id=1, source_target_pairs={{0,4},{4,0},{8,12},{12,8},{16,20},{20,16},{24,28},{28,24},{1,5},{5... | collective-permute-start | bytes 3145736 | tf_op jit(solution)/shard_map/ppermute | solution.py:58
  68.8 31.6 %collective-permute-start.12 = (bf16[512,1152]{1,0:T(8,128)(2,1)}, bf16[512,1152]{1,0:T(8,128)(2,1)}, u32[]{:S(2)}, u32[]{:S(2)}) collective-permute-start(bf16[512,1152]{1,0:T(8,128)(2,1)} %pad_maximum_fusion.refs_0_), channel_id=1, source_target_pairs={{0,2},{1,5},{2,0},{3,7},{4,6},{5,1},{6,4},{7,3},{8,10},{9,13},{10,... | collective-permute-start | bytes 3538952 | tf_op jit(solution)/shard_map/ppermute | solution.py:73
  89.7 18.1 %collective-permute-start.11 = (bf16[4,128,512]{2,1,0:T(8,128)(2,1)}, bf16[4,128,512]{2,1,0:T(8,128)(2,1)}, u32[]{:S(2)}, u32[]{:S(2)}) collective-permute-start(bf16[4,128,512]{2,1,0:T(8,128)(2,1)} %get-tuple-element.189), channel_id=1, source_target_pairs={{0,4},{4,0},{8,12},{12,8},{16,20},{20,16},{24,28},{28,24},{1,5},{5... | collective-permute-start | bytes 1572872 | tf_op jit(solution)/shard_map/ppermute | solution.py:58
  95.6 48.4 %all-to-all-start.1 = ((bf16[4,256,1024]{2,1,0:T(8,128)(2,1)}), bf16[4,256,1024]{2,1,0:T(8,128)(2,1)S(1)}, u32[]{:S(2)}, u32[]{:S(2)}) async-start(bf16[4,256,1024]{2,1,0:T(8,128)(2,1)} %shard_map.224), calls=%async_computation.1 | async-start | bytes 4194304 | tf_op jit(solution)/shard_map/all_to_all | solution.py:441
  116.2 14.3 %collective-permute-start.14 = (bf16[512,1024]{1,0:T(8,128)(2,1)S(1)}, bf16[512,1024]{1,0:T(8,128)(2,1)S(1)}, u32[]{:S(2)}, u32[]{:S(2)}) collective-permute-start(bf16[512,1024]{1,0:T(8,128)(2,1)S(1)} %constant_dynamic-update-slice_fusion.refs_0_), channel_id=1, source_target_pairs={{0,2},{1,5},{2,0},{3,7},{4,6},{5,1},{6,4},{7,3},{8,10},{9,13},{10,... | collective-permute-start | bytes 3145736 | tf_op jit(solution)/shard_map/ppermute | solution.py:73
  116.2 18.4 %collective-permute-start.15 = (bf16[512,1152]{1,0:T(8,128)(2,1)}, bf16[512,1152]{1,0:T(8,128)(2,1)S(1)}, u32[]{:S(2)}, u32[]{:S(2)}) collective-permute-start(bf16[512,1152]{1,0:T(8,128)(2,1)} %pad_maximum_fusion.refs_0_), channel_id=1, source_target_pairs={{0,1},{1,0},{2,3},{3,2},{4,5},{5,4},{6,7},{7,6},{8,9},{9,8},{10,11... | collective-permute-start | bytes 3538952 | tf_op jit(solution)/shard_map/ppermute | solution.py:58
  120.0 14.7 %collective-permute-start.16 = (bf16[512,1152]{1,0:T(8,128)(2,1)}, bf16[512,1152]{1,0:T(8,128)(2,1)S(1)}, u32[]{:S(2)}, u32[]{:S(2)}) collective-permute-start(bf16[512,1152]{1,0:T(8,128)(2,1)} %collective-permute-done.12.refs_1_), channel_id=1, source_target_pairs={{0,1},{1,0},{2,3},{3,2},{4,5},{5,4},{6,7},{7,6},{8,9},{9,8},{10,11... | collective-permute-start | bytes 3538952 | tf_op jit(solution)/shard_map/ppermute | solution.py:58
  120.0 23.9 %collective-permute-start.17 = (bf16[512,1024]{1,0:T(8,128)(2,1)S(1)}, bf16[512,1024]{1,0:T(8,128)(2,1)}, u32[]{:S(2)}, u32[]{:S(2)}) collective-permute-start(bf16[512,1024]{1,0:T(8,128)(2,1)S(1)} %constant_dynamic-update-slice_fusion.refs_0_), channel_id=1, source_target_pairs={{0,1},{1,0},{2,3},{3,2},{4,5},{5,4},{6,7},{7,6},{8,9},{9,8},{10,11... | collective-permute-start | bytes 3145736 | tf_op jit(solution)/shard_map/ppermute | solution.py:58
  154.7 14.2 %collective-permute-start.19 = (bf16[1024,1024]{1,0:T(8,128)(2,1)}, bf16[1024,1024]{1,0:T(8,128)(2,1)S(1)}, u32[]{:S(2)}, u32[]{:S(2)}) collective-permute-start(bf16[1024,1024]{1,0:T(8,128)(2,1)} %get-tuple-element.96), channel_id=1, source_target_pairs={{0,1},{1,0},{2,3},{3,2},{4,5},{5,4},{6,7},{7,6},{8,9},{9,8},{10,11... | collective-permute-start | bytes 6291464 | tf_op jit(solution)/shard_map/ppermute | solution.py:58
  172.7 15.5 %collective-permute-start.24 = (bf16[512,1024]{1,0:T(8,128)(2,1)}, bf16[512,1024]{1,0:T(8,128)(2,1)}, u32[]{:S(2)}, u32[]{:S(2)}) collective-permute-start(bf16[512,1024]{1,0:T(8,128)(2,1)} %get-tuple-element.176), channel_id=1, source_target_pairs={{0,2},{1,5},{2,0},{3,7},{4,6},{5,1},{6,4},{7,3},{8,10},{9,13},{10,... | collective-permute-start | bytes 3145736 | tf_op jit(solution)/shard_map/ppermute | solution.py:73
  183.9 29.7 %collective-permute-start.20 = (bf16[1024,1024]{1,0:T(8,128)(2,1)}, bf16[1024,1024]{1,0:T(8,128)(2,1)}, u32[]{:S(2)}, u32[]{:S(2)}) collective-permute-start(bf16[1024,1024]{1,0:T(8,128)(2,1)} %shard_map.230), channel_id=1, source_target_pairs={{0,1},{1,0},{2,3},{3,2},{4,5},{5,4},{6,7},{7,6},{8,9},{9,8},{10,11... | collective-permute-start | bytes 6291464 | tf_op jit(solution)/shard_map/ppermute | solution.py:58
  183.9 29.7 %all-to-all-start.2 = ((bf16[4,256,512]{2,1,0:T(8,128)(2,1)}), bf16[4,256,512]{2,1,0:T(8,128)(2,1)}, u32[]{:S(2)}, u32[]{:S(2)}) async-start(bf16[4,256,512]{2,1,0:T(8,128)(2,1)} %bitcast.46), calls=%async_computation.2 | async-start | bytes 2097152 | tf_op jit(solution)/shard_map/all_to_all | solution.py:441
  189.8 15.0 %collective-permute-start.25 = (bf16[256,1024]{1,0:T(8,128)(2,1)S(1)}, bf16[256,1024]{1,0:T(8,128)(2,1)S(1)}, u32[]{:S(2)}, u32[]{:S(2)}) collective-permute-start(bf16[256,1024]{1,0:T(8,128)(2,1)S(1)} %get-tuple-element.106), channel_id=1, source_target_pairs={{0,4},{1,3},{2,6},{3,1},{4,0},{5,7},{6,2},{7,5},{8,12},{9,11},{10,... | collective-permute-start | bytes 1572872 | tf_op jit(solution)/shard_map/ppermute | solution.py:73
  199.5 24.6 %collective-permute-start.23 = (bf16[4,128,1024]{2,1,0:T(8,128)(2,1)}, bf16[4,128,1024]{2,1,0:T(8,128)(2,1)S(1)}, u32[]{:S(2)}, u32[]{:S(2)}) collective-permute-start(bf16[4,128,1024]{2,1,0:T(8,128)(2,1)} %get-tuple-element.105), channel_id=1, source_target_pairs={{0,4},{4,0},{8,12},{12,8},{16,20},{20,16},{24,28},{28,24},{1,5},{5... | collective-permute-start | bytes 3145736 | tf_op jit(solution)/shard_map/ppermute | solution.py:58
  219.1 24.2 %collective-permute-start.21 = (bf16[512,1024]{1,0:T(8,128)(2,1)}, bf16[512,1024]{1,0:T(8,128)(2,1)}, u32[]{:S(2)}, u32[]{:S(2)}) collective-permute-start(bf16[512,1024]{1,0:T(8,128)(2,1)} %get-tuple-element.177), channel_id=1, source_target_pairs={{0,2},{1,5},{2,0},{3,7},{4,6},{5,1},{6,4},{7,3},{8,10},{9,13},{10,... | collective-permute-start | bytes 3145736 | tf_op jit(solution)/shard_map/ppermute | solution.py:73
  228.1 58.4 %all-to-all-start.3 = ((bf16[4,256,1024]{2,1,0:T(8,128)(2,1)}), bf16[4,256,1024]{2,1,0:T(8,128)(2,1)S(1)}, u32[]{:S(2)}, u32[]{:S(2)}) async-start(bf16[4,256,1024]{2,1,0:T(8,128)(2,1)} %copy-done.2), calls=%async_computation.3 | async-start | bytes 4194304 | tf_op jit(solution)/shard_map/all_to_all | solution.py:441
  251.4 19.7 %collective-permute-start.32 = (bf16[512,768]{1,0:T(8,128)(2,1)S(1)}, bf16[512,768]{1,0:T(8,128)(2,1)S(1)}, u32[]{:S(2)}, u32[]{:S(2)}) collective-permute-start(bf16[512,768]{1,0:T(8,128)(2,1)S(1)} %get-tuple-element.118), channel_id=1, source_target_pairs={{0,4},{4,0},{8,12},{12,8},{16,20},{20,16},{24,28},{28,24},{1,5},{5... | collective-permute-start | bytes 2359304 | tf_op jit(solution)/shard_map/ppermute | solution.py:58
  284.5 16.4 %collective-permute-start.42 = (bf16[4,128,512]{2,1,0:T(8,128)(2,1)}, bf16[4,128,512]{2,1,0:T(8,128)(2,1)}, u32[]{:S(2)}, u32[]{:S(2)}) collective-permute-start(bf16[4,128,512]{2,1,0:T(8,128)(2,1)} %get-tuple-element.188), channel_id=1, source_target_pairs={{0,4},{4,0},{8,12},{12,8},{16,20},{20,16},{24,28},{28,24},{1,5},{5... | collective-permute-start | bytes 1572872 | tf_op jit(solution)/shard_map/ppermute | solution.py:58
  294.0 18.6 %collective-permute-start.41 = (bf16[128,768]{1,0:T(8,128)(2,1)S(1)}, bf16[128,768]{1,0:T(8,128)(2,1)}, u32[]{:S(2)}, u32[]{:S(2)}) collective-permute-start(bf16[128,768]{1,0:T(8,128)(2,1)S(1)} %slice.303), channel_id=1, source_target_pairs={{0,16},{4,20},{8,24},{12,28},{16,0},{20,4},{24,8},{28,12},{1,17},{... | collective-permute-start | bytes 589832 | tf_op jit(solution)/shard_map/ppermute | solution.py:58
  (67 other events, 536.0 us)

commit v7 on v6

--- a/solution.py
+++ b/solution.py
@@ -654,7 +654,6 @@
             out_specs=[pl.BlockSpec((count,) + d, lambda i, n=len(d): (i,) + (0,) * n) for d in dims],
             scratch=[pltpu.VMEM((total_rows, block), LOW), pltpu.VMEM((block, cols), LOW)],
             flops=2 * total_rows * width * cols,
-            limit=LARGE,
         )
 
     hidden_kept, hidden_sent = add_halves(kept_hidden, swap(sent_hidden, *last))
@@ -667,7 +666,6 @@
             in_specs=[tile(wide), whole(down_rows)],
             out_specs=[tile(width)],
             flops=2 * half * size * width * wide,
-            limit=LARGE,
         )[0]
 
     steps_back = len(path)

time: 325 us -> 323 us (level)
  waiting for transfers between devices: 119 us -> 126 us
  starting transfers between devices: 72.2 us -> 65.7 us
  Pallas kernels: 71.3 us -> 65 us
  local copies, waits for them, and re-layouts: 25.6 us -> 29.2 us
    ppermute x24, starting transfers between devices: 35.8 us -> 29.4 us  [swap(): return lax.ppermute(field, axis, [(i, i ^ mask) for i in range(count)])]
    pallas_call x17, Pallas kernels: 71.3 us -> 65 us  [call(): pl.pallas_call(body, out_shape=list(outs), in_specs=[pl.BlockSpec(memory_...]
    all_to_all x4, waiting for transfers between devices: 15.8 us -> 19.8 us  [along(): lax.all_to_all(blocks, 'expert', 0, 0, tiled=True, axis_index_groups=lines)]
    unnamed x89 -> x115, local copies, waits for them, and re-layouts: 17.6 us -> 21.2 us
    ppermute x19, waiting for transfers between devices: 65.3 us -> 68.8 us  [swap_by_parity(): return lax.ppermute(field, ('expert', 'tensor'), pairs)]
  transfers between devices with their start and end apart: 48 -> 48, of which waited for: 24 -> 26; matrix products, arithmetic and copies ran while one was open for 11% -> 11% of each run, Pallas kernels for 19% -> 17%
where the time goes in v7:
time: 323 us; the launch traced here: 322 us
  waiting for transfers between devices  126 us (39%)
  starting transfers between devices  65.7 us (20%)
  Pallas kernels  65 us (20%)
  other arithmetic  34.9 us (11%)
  local copies, waits for them, and re-layouts  29.2 us (9%)
    ppermute x19, waiting for transfers between devices, swap_by_parity(): return lax.ppermute(field, ('expert', 'tensor'), pairs)  68.8 us
    pallas_call x17, Pallas kernels, call(): pl.pallas_call(body, out_shape=list(outs), in_specs=[pl.BlockSpec(memory_...  65 us
    ppermute x24, waiting for transfers between devices, swap(): return lax.ppermute(field, axis, [(i, i ^ mask) for i in range(count)])  36.2 us
    ppermute x24, starting transfers between devices, swap(): return lax.ppermute(field, axis, [(i, i ^ mask) for i in range(count)])  29.4 us
    unnamed x115, local copies, waits for them, and re-layouts  21.2 us
    all_to_all x4, waiting for transfers between devices, along(): lax.all_to_all(blocks, 'expert', 0, 0, tiled=True, axis_index_groups=lines)  19.8 us
    all_to_all x4, starting transfers between devices, along(): lax.all_to_all(blocks, 'expert', 0, 0, tiled=True, axis_index_groups=lines)  17.1 us
    ppermute x19, starting transfers between devices, swap_by_parity(): return lax.ppermute(field, ('expert', 'tensor'), pairs)  15 us
  transfers between devices with their start and end apart: 48, of which 26 were waited for; matrix products, arithmetic and copies ran while one was open for 11% of the time, Pallas kernels for 17%

profile of v7, /device:TPU:1, one launch (start us, length us, event | category | flops | bytes accessed | tf_op | source)
XLA Modules:
  0.0 321.9 jit_solution(12870098231196056349)
XLA Ops:
  19.5 14.9 %collective-permute-done.1 = bf16[288,768]{1,0:T(8,128)(2,1)S(1)} collective-permute-done((bf16[288,768]{1,0:T(8,128)(2,1)S(1)}, bf16[288,768]{1,0:T(8,128)(2,1)S(1)}, u32[]{:S(2)}, u32[]{:S(2)}) %collective-permute-start.1) | collective-permute-done | bytes 442400 | tf_op jit(solution)/shard_map/ppermute | solution.py:73
  38.3 12.9 %collective-permute-done.3.refs_1_ = bf16[576,768]{1,0:T(8,128)(2,1)S(1)} collective-permute-done((bf16[576,768]{1,0:T(8,128)(2,1)S(1)}, bf16[576,768]{1,0:T(8,128)(2,1)S(1)}, u32[]{:S(2)}, u32[]{:S(2)}) %collective-permute-start.3) | collective-permute-done | bytes 884768 | tf_op jit(solution)/shard_map/ppermute | solution.py:73
  51.1 4.3 %all-to-all-start = ((bf16[4,256,512]{2,1,0:T(8,128)(2,1)}), bf16[4,256,512]{2,1,0:T(8,128)(2,1)}, u32[]{:S(2)}, u32[]{:S(2)}) async-start(bf16[4,256,512]{2,1,0:T(8,128)(2,1)} %bitcast.7), calls=%async_computation | async-start | bytes 2097152 | tf_op jit(solution)/shard_map/all_to_all | solution.py:441
  69.6 9.0 %all-to-all-done = bf16[4,256,512]{2,1,0:T(8,128)(2,1)} async-done(((bf16[4,256,512]{2,1,0:T(8,128)(2,1)}), bf16[4,256,512]{2,1,0:T(8,128)(2,1)}, u32[]{:S(2)}, u32[]{:S(2)}) %all-to-all-start) | async-done | bytes 1048608 | tf_op jit(solution)/shard_map/all_to_all | solution.py:441
  91.0 4.5 %collective-permute-done.10 = bf16[128,1024]{1,0:T(8,128)(2,1)S(1)} collective-permute-done((bf16[128,1024]{1,0:T(8,128)(2,1)S(1)}, bf16[128,1024]{1,0:T(8,128)(2,1)S(1)}, u32[]{:S(2)}, u32[]{:S(2)}) %collective-permute-start.10) | collective-permute-done | bytes 262176 | tf_op jit(solution)/shard_map/ppermute | solution.py:73
  96.2 4.7 %all-to-all-start.1 = ((bf16[4,256,1024]{2,1,0:T(8,128)(2,1)}), bf16[4,256,1024]{2,1,0:T(8,128)(2,1)}, u32[]{:S(2)}, u32[]{:S(2)}) async-start(bf16[4,256,1024]{2,1,0:T(8,128)(2,1)} %shard_map.224), calls=%async_computation.1 | async-start | bytes 4194304 | tf_op jit(solution)/shard_map/all_to_all | solution.py:441
  101.9 6.8 %collective-permute-done.11.refs_5_ = bf16[4,128,512]{2,1,0:T(8,128)(2,1)} collective-permute-done((bf16[4,128,512]{2,1,0:T(8,128)(2,1)}, bf16[4,128,512]{2,1,0:T(8,128)(2,1)}, u32[]{:S(2)}, u32[]{:S(2)}) %collective-permute-start.11) | collective-permute-done | bytes 524320 | tf_op jit(solution)/shard_map/ppermute | solution.py:58
  108.7 8.4 %collective-permute-done.13 = bf16[256,1024]{1,0:T(8,128)(2,1)S(1)} collective-permute-done((bf16[256,1024]{1,0:T(8,128)(2,1)S(1)}, bf16[256,1024]{1,0:T(8,128)(2,1)S(1)}, u32[]{:S(2)}, u32[]{:S(2)}) %collective-permute-start.13) | collective-permute-done | bytes 524320 | tf_op jit(solution)/shard_map/ppermute | solution.py:73
  120.3 10.8 %collective-permute-done.14.refs_1_ = bf16[512,1024]{1,0:T(8,128)(2,1)S(1)} collective-permute-done((bf16[512,1024]{1,0:T(8,128)(2,1)S(1)}, bf16[512,1024]{1,0:T(8,128)(2,1)S(1)}, u32[]{:S(2)}, u32[]{:S(2)}) %collective-permute-start.14) | collective-permute-done | bytes 1048608 | tf_op jit(solution)/shard_map/ppermute | solution.py:73
  136.6 7.2 %shard_map.225 = (f32[2048,128]{1,0:T(8,128)}, f32[2048,512]{1,0:T(8,128)}, bf16[1024,512]{1,0:T(8,128)(2,1)}) custom-call(s32[2]{0:T(128)} %copy-done.33, bf16[512,1152]{1,0:T(8,128)(2,1)} %copy-done.12, bf16[512,1152]{1,0:T(8,128)(2,1)} %collective-permute-done.12.refs_1_, bf16[512,1152]{1,0:T(8,128)(2,1)} %copy-done.36, bf16[512,1152]{1,0:T(8,128)(2,1)} %copy-done.38, ...), custom_call_target="tpu_custom_call" | custom-call | flops 2147483648 | bytes 12058632 | tf_op jit(solution)/shard_map/pallas_call | solution.py:44
  143.9 4.5 %all-to-all-done.1 = bf16[4,256,1024]{2,1,0:T(8,128)(2,1)} async-done(((bf16[4,256,1024]{2,1,0:T(8,128)(2,1)}), bf16[4,256,1024]{2,1,0:T(8,128)(2,1)}, u32[]{:S(2)}, u32[]{:S(2)}) %all-to-all-start.1) | async-done | bytes 2097184 | tf_op jit(solution)/shard_map/all_to_all | solution.py:441
  148.4 9.4 %shard_map.227 = (bf16[1024,1024]{1,0:T(8,128)(2,1)}, bf16[1024,512]{1,0:T(8,128)(2,1)}, bf16[1024,1024]{1,0:T(8,128)(2,1)}) custom-call(s32[2]{0:T(128)} %copy-done.33, bf16[512,1024]{1,0:T(8,128)(2,1)} %collective-permute-done.17.refs_0_.refs_2_, bf16[512,1024]{1,0:T(8,128)(2,1)} %collective-permute-done.18.refs_1_.refs_3_, ...), custom_call_target="tpu_custom_call" | custom-call | flops 4294967296 | bytes 14680072 | tf_op jit(solution)/shard_map/pallas_call | solution.py:44
  159.3 9.8 %shard_map.226 = (f32[1024,1024]{1,0:T(8,128)}, bf16[1024,512]{1,0:T(8,128)(2,1)}, bf16[1024,1024]{1,0:T(8,128)(2,1)}) custom-call(s32[2]{0:T(128)} %copy-done.33, bf16[512,1024]{1,0:T(8,128)(2,1)} %copy-done.25, bf16[512,1024]{1,0:T(8,128)(2,1)} %copy-done.41, bf16[1024,1024]{1,0:T(8,128)(2,1)} %bitcast.11.refs_2_, f32[2048,128]{1,0:T(8,128)} %get-tuple-element.91.refs_3_, ...), custom_call_target="tpu_custom_call" | custom-call | flops 4294967296 | bytes 16777224 | tf_op jit(solution)/shard_map/pallas_call | solution.py:44
  169.2 5.0 %convert_add_fusion = (f32[512,1024]{1,0:T(8,128)}, bf16[512,1024]{1,0:T(8,128)(2,1)}) fusion(f32[1024,1024]{1,0:T(8,128)} %get-tuple-element.95, bf16[1024,1024]{1,0:T(8,128)(2,1)S(1)} %collective-permute-done.19), kind=kLoop, calls=%fused_computation.3 | loop fusion | flops 2621440 | bytes 9437184 | tf_op jit(solution)/shard_map/add | solution.py:511
  174.9 4.5 %shard_map.228 = bf16[4,2,128,512]{3,2,1,0:T(8,128)(2,1)S(1)} custom-call(s32[2]{0:T(128)S(1)} %copy-done.34, bf16[512,1152]{1,0:T(8,128)(2,1)S(1)} %copy-done.13, bf16[512,1152]{1,0:T(8,128)(2,1)} %collective-permute-done.12.refs_1_, bf16[512,1152]{1,0:T(8,128)(2,1)S(1)} %copy-done.37, bf16[512,1152]{1,0:T(8,128)(2,1)S(1)} %copy-done.39, ...), custom_call_target="tpu_custom_call" | custom-call | flops 2147483648 | bytes 7864328 | tf_op jit(solution)/shard_map/pallas_call | solution.py:44
  182.8 4.5 %all-to-all-start.2 = ((bf16[4,256,512]{2,1,0:T(8,128)(2,1)}), bf16[4,256,512]{2,1,0:T(8,128)(2,1)}, u32[]{:S(2)}, u32[]{:S(2)}) async-start(bf16[4,256,512]{2,1,0:T(8,128)(2,1)} %bitcast.39), calls=%async_computation.2 | async-start | bytes 2097152 | tf_op jit(solution)/shard_map/all_to_all | solution.py:441
  193.2 7.4 %shard_map.231 = (bf16[4,128,1024]{2,1,0:T(8,128)(2,1)S(1)}, bf16[4,128,1024]{2,1,0:T(8,128)(2,1)}) custom-call(s32[2]{0:T(128)S(1)} %copy-done.34, bf16[512,1024]{1,0:T(8,128)(2,1)S(1)} %copy-done.26, bf16[512,1024]{1,0:T(8,128)(2,1)S(1)} %copy-done.42, bf16[512,1024]{1,0:T(8,128)(2,1)} %collective-permute-done.17.refs_0_.refs_2_, ...), custom_call_target="tpu_custom_call" | custom-call | flops 4294967296 | bytes 10485768 | tf_op jit(solution)/shard_map/pallas_call | solution.py:44
  206.5 6.4 %all-to-all-done.2 = bf16[4,256,512]{2,1,0:T(8,128)(2,1)} async-done(((bf16[4,256,512]{2,1,0:T(8,128)(2,1)}), bf16[4,256,512]{2,1,0:T(8,128)(2,1)}, u32[]{:S(2)}, u32[]{:S(2)}) %all-to-all-start.2) | async-done | bytes 1048608 | tf_op jit(solution)/shard_map/all_to_all | solution.py:441
  212.9 5.5 %fusion = (bf16[512,1024]{1,0:T(8,128)(2,1)}, f32[512,1024]{1,0:T(8,128)}) fusion(f32[1024,1024]{1,0:T(8,128)} %copy-done.2, bf16[1024,1024]{1,0:T(8,128)(2,1)} %collective-permute-done.20), kind=kLoop, calls=%fused_computation.1 | loop fusion | flops 2621440 | bytes 9437184 | tf_op jit(solution)/shard_map/convert_element_type | solution.py:513
  245.8 4.2 %shard_map.234 = (f32[512,768]{1,0:T(8,128)S(1)}, bf16[512,768]{1,0:T(8,128)(2,1)S(1)}, f32[128,1024]{1,0:T(8,128)S(1)}, bf16[128,1024]{1,0:T(8,128)(2,1)S(1)}) custom-call(s32[2]{0:T(128)S(1)} %copy-done.34, bf16[64,1024]{1,0:T(8,128)(2,1)S(1)} %get-tuple-element.111.refs_0_, bf16[64,1024]{1,0:T(8,128)(2,1)S(1)} %collective-permute-done.29.refs_1_, ...), custom_call_target="tpu_custom_call" | custom-call | flops 805306368 | bytes 6424584 | tf_op jit(solution)/shard_map/pallas_call | solution.py:44
  257.1 12.7 %collective-permute-done.32 = bf16[512,768]{1,0:T(8,128)(2,1)S(1)} collective-permute-done((bf16[512,768]{1,0:T(8,128)(2,1)S(1)}, bf16[512,768]{1,0:T(8,128)(2,1)S(1)}, u32[]{:S(2)}, u32[]{:S(2)}) %collective-permute-start.32) | collective-permute-done | bytes 786464 | tf_op jit(solution)/shard_map/ppermute | solution.py:58
  270.9 4.4 %collective-permute-done.39 = bf16[80,1024]{1,0:T(8,128)(2,1)S(1)} collective-permute-done((bf16[80,1024]{1,0:T(8,128)(2,1)S(1)}, bf16[80,1024]{1,0:T(8,128)(2,1)S(1)}, u32[]{:S(2)}, u32[]{:S(2)}) %collective-permute-start.39) | collective-permute-done | bytes 163872 | tf_op jit(solution)/shard_map/ppermute | solution.py:58
  284.6 4.3 %all-to-all-start.4 = ((f32[8,2,128]{2,1,0:T(2,128)}), f32[8,2,128]{2,1,0:T(2,128)S(1)}, u32[]{:S(2)}, u32[]{:S(2)}) async-start(f32[8,2,128]{2,1,0:T(2,128)} %bitcast.19), calls=%async_computation.4 | async-start | bytes 16384 | tf_op jit(solution)/shard_map/all_to_all | solution.py:738
  303.8 5.7 %collective-permute-done.34 = bf16[64,1024]{1,0:T(8,128)(2,1)S(1)} collective-permute-done((bf16[64,1024]{1,0:T(8,128)(2,1)S(1)}, bf16[64,1024]{1,0:T(8,128)(2,1)S(1)}, u32[]{:S(2)}, u32[]{:S(2)}) %collective-permute-start.34) | collective-permute-done | bytes 131104 | tf_op jit(solution)/shard_map/ppermute | solution.py:73
  (270 shorter events, 149.0 us)
Async XLA Ops:
  16.9 17.6 %collective-permute-start.1 = (bf16[288,768]{1,0:T(8,128)(2,1)S(1)}, bf16[288,768]{1,0:T(8,128)(2,1)S(1)}, u32[]{:S(2)}, u32[]{:S(2)}) collective-permute-start(bf16[288,768]{1,0:T(8,128)(2,1)S(1)} %pad_maximum_fusion.8), channel_id=1, source_target_pairs={{0,8},{1,17},{2,10},{3,19},{4,12},{5,21},{6,14},{7,23},{8,0},{9,25... | collective-permute-start | bytes 1327112 | tf_op jit(solution)/shard_map/ppermute | solution.py:73
  19.4 16.6 %collective-permute-start.2 = (bf16[64,1152]{1,0:T(8,128)(2,1)S(1)}, bf16[64,1152]{1,0:T(8,128)(2,1)S(1)}, u32[]{:S(2)}, u32[]{:S(2)}) collective-permute-start(bf16[64,1152]{1,0:T(8,128)(2,1)S(1)} %pad_maximum_fusion.14), channel_id=1, source_target_pairs={{0,16},{1,17},{2,18},{3,19},{4,20},{5,21},{6,22},{7,23},{8,24},{9,... | collective-permute-start | bytes 442376 | tf_op jit(solution)/shard_map/ppermute | solution.py:73
  36.1 15.1 %collective-permute-start.3 = (bf16[576,768]{1,0:T(8,128)(2,1)S(1)}, bf16[576,768]{1,0:T(8,128)(2,1)S(1)}, u32[]{:S(2)}, u32[]{:S(2)}) collective-permute-start(bf16[576,768]{1,0:T(8,128)(2,1)S(1)} %pad_maximum_fusion.1.refs_0_), channel_id=1, source_target_pairs={{0,4},{1,9},{2,6},{3,11},{4,0},{5,13},{6,2},{7,15},{8,12},{9,1},{1... | collective-permute-start | bytes 2654216 | tf_op jit(solution)/shard_map/ppermute | solution.py:73
  37.5 17.9 %collective-permute-start.4 = (bf16[128,1152]{1,0:T(8,128)(2,1)}, bf16[128,1152]{1,0:T(8,128)(2,1)}, u32[]{:S(2)}, u32[]{:S(2)}) collective-permute-start(bf16[128,1152]{1,0:T(8,128)(2,1)} %pad_maximum_fusion.10), channel_id=1, source_target_pairs={{0,8},{1,9},{2,10},{3,11},{4,12},{5,13},{6,14},{7,15},{8,0},{9,1},... | collective-permute-start | bytes 884744 | tf_op jit(solution)/shard_map/ppermute | solution.py:73
  51.1 27.4 %all-to-all-start = ((bf16[4,256,512]{2,1,0:T(8,128)(2,1)}), bf16[4,256,512]{2,1,0:T(8,128)(2,1)}, u32[]{:S(2)}, u32[]{:S(2)}) async-start(bf16[4,256,512]{2,1,0:T(8,128)(2,1)} %bitcast.7), calls=%async_computation | async-start | bytes 2097152 | tf_op jit(solution)/shard_map/all_to_all | solution.py:441
  58.2 25.6 %collective-permute-start.9 = (bf16[4,128,1024]{2,1,0:T(8,128)(2,1)}, bf16[4,128,1024]{2,1,0:T(8,128)(2,1)}, u32[]{:S(2)}, u32[]{:S(2)}) collective-permute-start(bf16[4,128,1024]{2,1,0:T(8,128)(2,1)} %copy-done.40), channel_id=1, source_target_pairs={{0,4},{4,0},{8,12},{12,8},{16,20},{20,16},{24,28},{28,24},{1,5},{5... | collective-permute-start | bytes 3145736 | tf_op jit(solution)/shard_map/ppermute | solution.py:58
  67.8 34.1 %collective-permute-start.12 = (bf16[512,1152]{1,0:T(8,128)(2,1)S(1)}, bf16[512,1152]{1,0:T(8,128)(2,1)}, u32[]{:S(2)}, u32[]{:S(2)}) collective-permute-start(bf16[512,1152]{1,0:T(8,128)(2,1)S(1)} %pad_maximum_fusion.refs_0_), channel_id=1, source_target_pairs={{0,2},{1,5},{2,0},{3,7},{4,6},{5,1},{6,4},{7,3},{8,10},{9,13},{10,... | collective-permute-start | bytes 3538952 | tf_op jit(solution)/shard_map/ppermute | solution.py:73
  90.9 17.8 %collective-permute-start.11 = (bf16[4,128,512]{2,1,0:T(8,128)(2,1)}, bf16[4,128,512]{2,1,0:T(8,128)(2,1)}, u32[]{:S(2)}, u32[]{:S(2)}) collective-permute-start(bf16[4,128,512]{2,1,0:T(8,128)(2,1)} %get-tuple-element.189), channel_id=1, source_target_pairs={{0,4},{4,0},{8,12},{12,8},{16,20},{20,16},{24,28},{28,24},{1,5},{5... | collective-permute-start | bytes 1572872 | tf_op jit(solution)/shard_map/ppermute | solution.py:58
  96.2 52.2 %all-to-all-start.1 = ((bf16[4,256,1024]{2,1,0:T(8,128)(2,1)}), bf16[4,256,1024]{2,1,0:T(8,128)(2,1)}, u32[]{:S(2)}, u32[]{:S(2)}) async-start(bf16[4,256,1024]{2,1,0:T(8,128)(2,1)} %shard_map.224), calls=%async_computation.1 | async-start | bytes 4194304 | tf_op jit(solution)/shard_map/all_to_all | solution.py:441
  117.2 14.0 %collective-permute-start.14 = (bf16[512,1024]{1,0:T(8,128)(2,1)S(1)}, bf16[512,1024]{1,0:T(8,128)(2,1)S(1)}, u32[]{:S(2)}, u32[]{:S(2)}) collective-permute-start(bf16[512,1024]{1,0:T(8,128)(2,1)S(1)} %constant_dynamic-update-slice_fusion.refs_0_), channel_id=1, source_target_pairs={{0,2},{1,5},{2,0},{3,7},{4,6},{5,1},{6,4},{7,3},{8,10},{9,13},{10,... | collective-permute-start | bytes 3145736 | tf_op jit(solution)/shard_map/ppermute | solution.py:73
  117.2 17.3 %collective-permute-start.15 = (bf16[512,1152]{1,0:T(8,128)(2,1)S(1)}, bf16[512,1152]{1,0:T(8,128)(2,1)S(1)}, u32[]{:S(2)}, u32[]{:S(2)}) collective-permute-start(bf16[512,1152]{1,0:T(8,128)(2,1)S(1)} %pad_maximum_fusion.refs_0_), channel_id=1, source_target_pairs={{0,1},{1,0},{2,3},{3,2},{4,5},{5,4},{6,7},{7,6},{8,9},{9,8},{10,11... | collective-permute-start | bytes 3538952 | tf_op jit(solution)/shard_map/ppermute | solution.py:58
  119.8 14.7 %collective-permute-start.16 = (bf16[512,1152]{1,0:T(8,128)(2,1)}, bf16[512,1152]{1,0:T(8,128)(2,1)S(1)}, u32[]{:S(2)}, u32[]{:S(2)}) collective-permute-start(bf16[512,1152]{1,0:T(8,128)(2,1)} %collective-permute-done.12.refs_1_), channel_id=1, source_target_pairs={{0,1},{1,0},{2,3},{3,2},{4,5},{5,4},{6,7},{7,6},{8,9},{9,8},{10,11... | collective-permute-start | bytes 3538952 | tf_op jit(solution)/shard_map/ppermute | solution.py:58
  119.9 24.0 %collective-permute-start.17 = (bf16[512,1024]{1,0:T(8,128)(2,1)S(1)}, bf16[512,1024]{1,0:T(8,128)(2,1)}, u32[]{:S(2)}, u32[]{:S(2)}) collective-permute-start(bf16[512,1024]{1,0:T(8,128)(2,1)S(1)} %constant_dynamic-update-slice_fusion.refs_0_), channel_id=1, source_target_pairs={{0,1},{1,0},{2,3},{3,2},{4,5},{5,4},{6,7},{7,6},{8,9},{9,8},{10,11... | collective-permute-start | bytes 3145736 | tf_op jit(solution)/shard_map/ppermute | solution.py:58
  131.2 12.7 %collective-permute-start.18 = (bf16[512,1024]{1,0:T(8,128)(2,1)S(1)}, bf16[512,1024]{1,0:T(8,128)(2,1)}, u32[]{:S(2)}, u32[]{:S(2)}) collective-permute-start(bf16[512,1024]{1,0:T(8,128)(2,1)S(1)} %collective-permute-done.14.refs_1_), channel_id=1, source_target_pairs={{0,1},{1,0},{2,3},{3,2},{4,5},{5,4},{6,7},{7,6},{8,9},{9,8},{10,11... | collective-permute-start | bytes 3145736 | tf_op jit(solution)/shard_map/ppermute | solution.py:58
  174.2 14.3 %collective-permute-start.24 = (bf16[512,1024]{1,0:T(8,128)(2,1)}, bf16[512,1024]{1,0:T(8,128)(2,1)}, u32[]{:S(2)}, u32[]{:S(2)}) collective-permute-start(bf16[512,1024]{1,0:T(8,128)(2,1)} %get-tuple-element.176), channel_id=1, source_target_pairs={{0,2},{1,5},{2,0},{3,7},{4,6},{5,1},{6,4},{7,3},{8,10},{9,13},{10,... | collective-permute-start | bytes 3145736 | tf_op jit(solution)/shard_map/ppermute | solution.py:73
  182.5 30.4 %collective-permute-start.20 = (bf16[1024,1024]{1,0:T(8,128)(2,1)}, bf16[1024,1024]{1,0:T(8,128)(2,1)}, u32[]{:S(2)}, u32[]{:S(2)}) collective-permute-start(bf16[1024,1024]{1,0:T(8,128)(2,1)} %shard_map.230), channel_id=1, source_target_pairs={{0,1},{1,0},{2,3},{3,2},{4,5},{5,4},{6,7},{7,6},{8,9},{9,8},{10,11... | collective-permute-start | bytes 6291464 | tf_op jit(solution)/shard_map/ppermute | solution.py:58
  182.8 30.1 %all-to-all-start.2 = ((bf16[4,256,512]{2,1,0:T(8,128)(2,1)}), bf16[4,256,512]{2,1,0:T(8,128)(2,1)}, u32[]{:S(2)}, u32[]{:S(2)}) async-start(bf16[4,256,512]{2,1,0:T(8,128)(2,1)} %bitcast.39), calls=%async_computation.2 | async-start | bytes 2097152 | tf_op jit(solution)/shard_map/all_to_all | solution.py:441
  190.8 14.7 %collective-permute-start.25 = (bf16[256,1024]{1,0:T(8,128)(2,1)S(1)}, bf16[256,1024]{1,0:T(8,128)(2,1)S(1)}, u32[]{:S(2)}, u32[]{:S(2)}) collective-permute-start(bf16[256,1024]{1,0:T(8,128)(2,1)S(1)} %get-tuple-element.106), channel_id=1, source_target_pairs={{0,4},{1,3},{2,6},{3,1},{4,0},{5,7},{6,2},{7,5},{8,12},{9,11},{10,... | collective-permute-start | bytes 1572872 | tf_op jit(solution)/shard_map/ppermute | solution.py:73
  200.7 23.8 %collective-permute-start.23 = (bf16[4,128,1024]{2,1,0:T(8,128)(2,1)}, bf16[4,128,1024]{2,1,0:T(8,128)(2,1)S(1)}, u32[]{:S(2)}, u32[]{:S(2)}) collective-permute-start(bf16[4,128,1024]{2,1,0:T(8,128)(2,1)} %get-tuple-element.105), channel_id=1, source_target_pairs={{0,4},{4,0},{8,12},{12,8},{16,20},{20,16},{24,28},{28,24},{1,5},{5... | collective-permute-start | bytes 3145736 | tf_op jit(solution)/shard_map/ppermute | solution.py:58
  218.3 23.9 %collective-permute-start.21 = (bf16[512,1024]{1,0:T(8,128)(2,1)}, bf16[512,1024]{1,0:T(8,128)(2,1)}, u32[]{:S(2)}, u32[]{:S(2)}) collective-permute-start(bf16[512,1024]{1,0:T(8,128)(2,1)} %get-tuple-element.177), channel_id=1, source_target_pairs={{0,2},{1,5},{2,0},{3,7},{4,6},{5,1},{6,4},{7,3},{8,10},{9,13},{10,... | collective-permute-start | bytes 3145736 | tf_op jit(solution)/shard_map/ppermute | solution.py:73
  229.6 54.9 %all-to-all-start.3 = ((bf16[4,256,1024]{2,1,0:T(8,128)(2,1)}), bf16[4,256,1024]{2,1,0:T(8,128)(2,1)S(1)}, u32[]{:S(2)}, u32[]{:S(2)}) async-start(bf16[4,256,1024]{2,1,0:T(8,128)(2,1)} %copy-done.3), calls=%async_computation.3 | async-start | bytes 4194304 | tf_op jit(solution)/shard_map/all_to_all | solution.py:441
  250.0 19.7 %collective-permute-start.32 = (bf16[512,768]{1,0:T(8,128)(2,1)S(1)}, bf16[512,768]{1,0:T(8,128)(2,1)S(1)}, u32[]{:S(2)}, u32[]{:S(2)}) collective-permute-start(bf16[512,768]{1,0:T(8,128)(2,1)S(1)} %get-tuple-element.118), channel_id=1, source_target_pairs={{0,4},{4,0},{8,12},{12,8},{16,20},{20,16},{24,28},{28,24},{1,5},{5... | collective-permute-start | bytes 2359304 | tf_op jit(solution)/shard_map/ppermute | solution.py:58
  283.1 16.4 %collective-permute-start.42 = (bf16[4,128,512]{2,1,0:T(8,128)(2,1)}, bf16[4,128,512]{2,1,0:T(8,128)(2,1)}, u32[]{:S(2)}, u32[]{:S(2)}) collective-permute-start(bf16[4,128,512]{2,1,0:T(8,128)(2,1)} %get-tuple-element.188), channel_id=1, source_target_pairs={{0,4},{4,0},{8,12},{12,8},{16,20},{20,16},{24,28},{28,24},{1,5},{5... | collective-permute-start | bytes 1572872 | tf_op jit(solution)/shard_map/ppermute | solution.py:58
  292.6 18.7 %collective-permute-start.41 = (bf16[128,768]{1,0:T(8,128)(2,1)S(1)}, bf16[128,768]{1,0:T(8,128)(2,1)}, u32[]{:S(2)}, u32[]{:S(2)}) collective-permute-start(bf16[128,768]{1,0:T(8,128)(2,1)S(1)} %slice.303), channel_id=1, source_target_pairs={{0,16},{4,20},{8,24},{12,28},{16,0},{20,4},{24,8},{28,12},{1,17},{... | collective-permute-start | bytes 589832 | tf_op jit(solution)/shard_map/ppermute | solution.py:58
  (80 other events, 610.6 us)

commit v8 on v7

--- a/solution.py
+++ b/solution.py
@@ -678,7 +678,7 @@
     both_this, both_other = weight_grad(hidden_pieces, kept_both, after(sent_both, sent_out), True)
     grad_near = to_neighbour(both_this, both_other)
     down_line = along(down_grad.reshape(pairs, 2 * part, wide))
-    sent = after(sent, down_line, both_other)
+    sent = after(sent, down_line)
     for k in range(2, steps_back - 1):
         kept, sent = scatter_stage(kept, sent, k)
     grad_kept, grad_got = scatter_stage(kept, after(sent, out_sent), steps_back - 1)

time: 323 us -> 323 us (level)
  no operation moved by 1% of the time
where the time goes in v8:
time: 323 us; the launch traced here: 322 us
  waiting for transfers between devices  126 us (39%)
  starting transfers between devices  65.7 us (20%)
  Pallas kernels  65 us (20%)
  other arithmetic  34.9 us (11%)
  local copies, waits for them, and re-layouts  29.2 us (9%)
    ppermute x19, waiting for transfers between devices, swap_by_parity(): return lax.ppermute(field, ('expert', 'tensor'), pairs)  68.8 us
    pallas_call x17, Pallas kernels, call(): pl.pallas_call(body, out_shape=list(outs), in_specs=[pl.BlockSpec(memory_...  65 us
    ppermute x24, waiting for transfers between devices, swap(): return lax.ppermute(field, axis, [(i, i ^ mask) for i in range(count)])  36.2 us
    ppermute x24, starting transfers between devices, swap(): return lax.ppermute(field, axis, [(i, i ^ mask) for i in range(count)])  29.4 us
    unnamed x115, local copies, waits for them, and re-layouts  21.2 us
    all_to_all x4, waiting for transfers between devices, along(): lax.all_to_all(blocks, 'expert', 0, 0, tiled=True, axis_index_groups=lines)  19.8 us
    all_to_all x4, starting transfers between devices, along(): lax.all_to_all(blocks, 'expert', 0, 0, tiled=True, axis_index_groups=lines)  17.1 us
    ppermute x19, starting transfers between devices, swap_by_parity(): return lax.ppermute(field, ('expert', 'tensor'), pairs)  15 us
  transfers between devices with their start and end apart: 48, of which 26 were waited for; matrix products, arithmetic and copies ran while one was open for 11% of the time, Pallas kernels for 17%

profile of v8, /device:TPU:1, one launch (start us, length us, event | category | flops | bytes accessed | tf_op | source)
XLA Modules:
  0.0 321.9 jit_solution(12870098231196056349)
XLA Ops:
  19.5 14.9 %collective-permute-done.1 = bf16[288,768]{1,0:T(8,128)(2,1)S(1)} collective-permute-done((bf16[288,768]{1,0:T(8,128)(2,1)S(1)}, bf16[288,768]{1,0:T(8,128)(2,1)S(1)}, u32[]{:S(2)}, u32[]{:S(2)}) %collective-permute-start.1) | collective-permute-done | bytes 442400 | tf_op jit(solution)/shard_map/ppermute | solution.py:73
  38.3 12.9 %collective-permute-done.3.refs_1_ = bf16[576,768]{1,0:T(8,128)(2,1)S(1)} collective-permute-done((bf16[576,768]{1,0:T(8,128)(2,1)S(1)}, bf16[576,768]{1,0:T(8,128)(2,1)S(1)}, u32[]{:S(2)}, u32[]{:S(2)}) %collective-permute-start.3) | collective-permute-done | bytes 884768 | tf_op jit(solution)/shard_map/ppermute | solution.py:73
  51.1 4.3 %all-to-all-start = ((bf16[4,256,512]{2,1,0:T(8,128)(2,1)}), bf16[4,256,512]{2,1,0:T(8,128)(2,1)}, u32[]{:S(2)}, u32[]{:S(2)}) async-start(bf16[4,256,512]{2,1,0:T(8,128)(2,1)} %bitcast.7), calls=%async_computation | async-start | bytes 2097152 | tf_op jit(solution)/shard_map/all_to_all | solution.py:441
  69.6 9.0 %all-to-all-done = bf16[4,256,512]{2,1,0:T(8,128)(2,1)} async-done(((bf16[4,256,512]{2,1,0:T(8,128)(2,1)}), bf16[4,256,512]{2,1,0:T(8,128)(2,1)}, u32[]{:S(2)}, u32[]{:S(2)}) %all-to-all-start) | async-done | bytes 1048608 | tf_op jit(solution)/shard_map/all_to_all | solution.py:441
  91.0 4.5 %collective-permute-done.10 = bf16[128,1024]{1,0:T(8,128)(2,1)S(1)} collective-permute-done((bf16[128,1024]{1,0:T(8,128)(2,1)S(1)}, bf16[128,1024]{1,0:T(8,128)(2,1)S(1)}, u32[]{:S(2)}, u32[]{:S(2)}) %collective-permute-start.10) | collective-permute-done | bytes 262176 | tf_op jit(solution)/shard_map/ppermute | solution.py:73
  96.2 4.7 %all-to-all-start.1 = ((bf16[4,256,1024]{2,1,0:T(8,128)(2,1)}), bf16[4,256,1024]{2,1,0:T(8,128)(2,1)}, u32[]{:S(2)}, u32[]{:S(2)}) async-start(bf16[4,256,1024]{2,1,0:T(8,128)(2,1)} %shard_map.224), calls=%async_computation.1 | async-start | bytes 4194304 | tf_op jit(solution)/shard_map/all_to_all | solution.py:441
  101.9 6.8 %collective-permute-done.11.refs_5_ = bf16[4,128,512]{2,1,0:T(8,128)(2,1)} collective-permute-done((bf16[4,128,512]{2,1,0:T(8,128)(2,1)}, bf16[4,128,512]{2,1,0:T(8,128)(2,1)}, u32[]{:S(2)}, u32[]{:S(2)}) %collective-permute-start.11) | collective-permute-done | bytes 524320 | tf_op jit(solution)/shard_map/ppermute | solution.py:58
  108.7 8.4 %collective-permute-done.13 = bf16[256,1024]{1,0:T(8,128)(2,1)S(1)} collective-permute-done((bf16[256,1024]{1,0:T(8,128)(2,1)S(1)}, bf16[256,1024]{1,0:T(8,128)(2,1)S(1)}, u32[]{:S(2)}, u32[]{:S(2)}) %collective-permute-start.13) | collective-permute-done | bytes 524320 | tf_op jit(solution)/shard_map/ppermute | solution.py:73
  120.3 10.8 %collective-permute-done.14.refs_1_ = bf16[512,1024]{1,0:T(8,128)(2,1)S(1)} collective-permute-done((bf16[512,1024]{1,0:T(8,128)(2,1)S(1)}, bf16[512,1024]{1,0:T(8,128)(2,1)S(1)}, u32[]{:S(2)}, u32[]{:S(2)}) %collective-permute-start.14) | collective-permute-done | bytes 1048608 | tf_op jit(solution)/shard_map/ppermute | solution.py:73
  136.6 7.2 %shard_map.225 = (f32[2048,128]{1,0:T(8,128)}, f32[2048,512]{1,0:T(8,128)}, bf16[1024,512]{1,0:T(8,128)(2,1)}) custom-call(s32[2]{0:T(128)} %copy-done.33, bf16[512,1152]{1,0:T(8,128)(2,1)} %copy-done.12, bf16[512,1152]{1,0:T(8,128)(2,1)} %collective-permute-done.12.refs_1_, bf16[512,1152]{1,0:T(8,128)(2,1)} %copy-done.36, bf16[512,1152]{1,0:T(8,128)(2,1)} %copy-done.38, ...), custom_call_target="tpu_custom_call" | custom-call | flops 2147483648 | bytes 12058632 | tf_op jit(solution)/shard_map/pallas_call | solution.py:44
  143.9 4.5 %all-to-all-done.1 = bf16[4,256,1024]{2,1,0:T(8,128)(2,1)} async-done(((bf16[4,256,1024]{2,1,0:T(8,128)(2,1)}), bf16[4,256,1024]{2,1,0:T(8,128)(2,1)}, u32[]{:S(2)}, u32[]{:S(2)}) %all-to-all-start.1) | async-done | bytes 2097184 | tf_op jit(solution)/shard_map/all_to_all | solution.py:441
  148.4 9.4 %shard_map.227 = (bf16[1024,1024]{1,0:T(8,128)(2,1)}, bf16[1024,512]{1,0:T(8,128)(2,1)}, bf16[1024,1024]{1,0:T(8,128)(2,1)}) custom-call(s32[2]{0:T(128)} %copy-done.33, bf16[512,1024]{1,0:T(8,128)(2,1)} %collective-permute-done.17.refs_0_.refs_2_, bf16[512,1024]{1,0:T(8,128)(2,1)} %collective-permute-done.18.refs_1_.refs_3_, ...), custom_call_target="tpu_custom_call" | custom-call | flops 4294967296 | bytes 14680072 | tf_op jit(solution)/shard_map/pallas_call | solution.py:44
  159.3 9.8 %shard_map.226 = (f32[1024,1024]{1,0:T(8,128)}, bf16[1024,512]{1,0:T(8,128)(2,1)}, bf16[1024,1024]{1,0:T(8,128)(2,1)}) custom-call(s32[2]{0:T(128)} %copy-done.33, bf16[512,1024]{1,0:T(8,128)(2,1)} %copy-done.25, bf16[512,1024]{1,0:T(8,128)(2,1)} %copy-done.41, bf16[1024,1024]{1,0:T(8,128)(2,1)} %bitcast.11.refs_2_, f32[2048,128]{1,0:T(8,128)} %get-tuple-element.91.refs_3_, ...), custom_call_target="tpu_custom_call" | custom-call | flops 4294967296 | bytes 16777224 | tf_op jit(solution)/shard_map/pallas_call | solution.py:44
  169.2 5.0 %convert_add_fusion = (f32[512,1024]{1,0:T(8,128)}, bf16[512,1024]{1,0:T(8,128)(2,1)}) fusion(f32[1024,1024]{1,0:T(8,128)} %get-tuple-element.95, bf16[1024,1024]{1,0:T(8,128)(2,1)S(1)} %collective-permute-done.19), kind=kLoop, calls=%fused_computation.3 | loop fusion | flops 2621440 | bytes 9437184 | tf_op jit(solution)/shard_map/add | solution.py:511
  174.9 4.5 %shard_map.228 = bf16[4,2,128,512]{3,2,1,0:T(8,128)(2,1)S(1)} custom-call(s32[2]{0:T(128)S(1)} %copy-done.34, bf16[512,1152]{1,0:T(8,128)(2,1)S(1)} %copy-done.13, bf16[512,1152]{1,0:T(8,128)(2,1)} %collective-permute-done.12.refs_1_, bf16[512,1152]{1,0:T(8,128)(2,1)S(1)} %copy-done.37, bf16[512,1152]{1,0:T(8,128)(2,1)S(1)} %copy-done.39, ...), custom_call_target="tpu_custom_call" | custom-call | flops 2147483648 | bytes 7864328 | tf_op jit(solution)/shard_map/pallas_call | solution.py:44
  182.8 4.5 %all-to-all-start.2 = ((bf16[4,256,512]{2,1,0:T(8,128)(2,1)}), bf16[4,256,512]{2,1,0:T(8,128)(2,1)}, u32[]{:S(2)}, u32[]{:S(2)}) async-start(bf16[4,256,512]{2,1,0:T(8,128)(2,1)} %bitcast.39), calls=%async_computation.2 | async-start | bytes 2097152 | tf_op jit(solution)/shard_map/all_to_all | solution.py:441
  193.2 7.4 %shard_map.231 = (bf16[4,128,1024]{2,1,0:T(8,128)(2,1)S(1)}, bf16[4,128,1024]{2,1,0:T(8,128)(2,1)}) custom-call(s32[2]{0:T(128)S(1)} %copy-done.34, bf16[512,1024]{1,0:T(8,128)(2,1)S(1)} %copy-done.26, bf16[512,1024]{1,0:T(8,128)(2,1)S(1)} %copy-done.42, bf16[512,1024]{1,0:T(8,128)(2,1)} %collective-permute-done.17.refs_0_.refs_2_, ...), custom_call_target="tpu_custom_call" | custom-call | flops 4294967296 | bytes 10485768 | tf_op jit(solution)/shard_map/pallas_call | solution.py:44
  206.5 6.4 %all-to-all-done.2 = bf16[4,256,512]{2,1,0:T(8,128)(2,1)} async-done(((bf16[4,256,512]{2,1,0:T(8,128)(2,1)}), bf16[4,256,512]{2,1,0:T(8,128)(2,1)}, u32[]{:S(2)}, u32[]{:S(2)}) %all-to-all-start.2) | async-done | bytes 1048608 | tf_op jit(solution)/shard_map/all_to_all | solution.py:441
  212.9 5.5 %fusion = (bf16[512,1024]{1,0:T(8,128)(2,1)}, f32[512,1024]{1,0:T(8,128)}) fusion(f32[1024,1024]{1,0:T(8,128)} %copy-done.2, bf16[1024,1024]{1,0:T(8,128)(2,1)} %collective-permute-done.20), kind=kLoop, calls=%fused_computation.1 | loop fusion | flops 2621440 | bytes 9437184 | tf_op jit(solution)/shard_map/convert_element_type | solution.py:513
  245.8 4.2 %shard_map.234 = (f32[512,768]{1,0:T(8,128)S(1)}, bf16[512,768]{1,0:T(8,128)(2,1)S(1)}, f32[128,1024]{1,0:T(8,128)S(1)}, bf16[128,1024]{1,0:T(8,128)(2,1)S(1)}) custom-call(s32[2]{0:T(128)S(1)} %copy-done.34, bf16[64,1024]{1,0:T(8,128)(2,1)S(1)} %get-tuple-element.111.refs_0_, bf16[64,1024]{1,0:T(8,128)(2,1)S(1)} %collective-permute-done.29.refs_1_, ...), custom_call_target="tpu_custom_call" | custom-call | flops 805306368 | bytes 6424584 | tf_op jit(solution)/shard_map/pallas_call | solution.py:44
  257.1 12.7 %collective-permute-done.32 = bf16[512,768]{1,0:T(8,128)(2,1)S(1)} collective-permute-done((bf16[512,768]{1,0:T(8,128)(2,1)S(1)}, bf16[512,768]{1,0:T(8,128)(2,1)S(1)}, u32[]{:S(2)}, u32[]{:S(2)}) %collective-permute-start.32) | collective-permute-done | bytes 786464 | tf_op jit(solution)/shard_map/ppermute | solution.py:58
  270.9 4.4 %collective-permute-done.39 = bf16[80,1024]{1,0:T(8,128)(2,1)S(1)} collective-permute-done((bf16[80,1024]{1,0:T(8,128)(2,1)S(1)}, bf16[80,1024]{1,0:T(8,128)(2,1)S(1)}, u32[]{:S(2)}, u32[]{:S(2)}) %collective-permute-start.39) | collective-permute-done | bytes 163872 | tf_op jit(solution)/shard_map/ppermute | solution.py:58
  284.6 4.3 %all-to-all-start.4 = ((f32[8,2,128]{2,1,0:T(2,128)}), f32[8,2,128]{2,1,0:T(2,128)S(1)}, u32[]{:S(2)}, u32[]{:S(2)}) async-start(f32[8,2,128]{2,1,0:T(2,128)} %bitcast.19), calls=%async_computation.4 | async-start | bytes 16384 | tf_op jit(solution)/shard_map/all_to_all | solution.py:738
  303.8 5.7 %collective-permute-done.34 = bf16[64,1024]{1,0:T(8,128)(2,1)S(1)} collective-permute-done((bf16[64,1024]{1,0:T(8,128)(2,1)S(1)}, bf16[64,1024]{1,0:T(8,128)(2,1)S(1)}, u32[]{:S(2)}, u32[]{:S(2)}) %collective-permute-start.34) | collective-permute-done | bytes 131104 | tf_op jit(solution)/shard_map/ppermute | solution.py:73
  (270 shorter events, 149.0 us)
Async XLA Ops:
  16.9 17.6 %collective-permute-start.1 = (bf16[288,768]{1,0:T(8,128)(2,1)S(1)}, bf16[288,768]{1,0:T(8,128)(2,1)S(1)}, u32[]{:S(2)}, u32[]{:S(2)}) collective-permute-start(bf16[288,768]{1,0:T(8,128)(2,1)S(1)} %pad_maximum_fusion.8), channel_id=1, source_target_pairs={{0,8},{1,17},{2,10},{3,19},{4,12},{5,21},{6,14},{7,23},{8,0},{9,25... | collective-permute-start | bytes 1327112 | tf_op jit(solution)/shard_map/ppermute | solution.py:73
  19.4 16.6 %collective-permute-start.2 = (bf16[64,1152]{1,0:T(8,128)(2,1)S(1)}, bf16[64,1152]{1,0:T(8,128)(2,1)S(1)}, u32[]{:S(2)}, u32[]{:S(2)}) collective-permute-start(bf16[64,1152]{1,0:T(8,128)(2,1)S(1)} %pad_maximum_fusion.14), channel_id=1, source_target_pairs={{0,16},{1,17},{2,18},{3,19},{4,20},{5,21},{6,22},{7,23},{8,24},{9,... | collective-permute-start | bytes 442376 | tf_op jit(solution)/shard_map/ppermute | solution.py:73
  36.1 15.1 %collective-permute-start.3 = (bf16[576,768]{1,0:T(8,128)(2,1)S(1)}, bf16[576,768]{1,0:T(8,128)(2,1)S(1)}, u32[]{:S(2)}, u32[]{:S(2)}) collective-permute-start(bf16[576,768]{1,0:T(8,128)(2,1)S(1)} %pad_maximum_fusion.1.refs_0_), channel_id=1, source_target_pairs={{0,4},{1,9},{2,6},{3,11},{4,0},{5,13},{6,2},{7,15},{8,12},{9,1},{1... | collective-permute-start | bytes 2654216 | tf_op jit(solution)/shard_map/ppermute | solution.py:73
  37.5 17.9 %collective-permute-start.4 = (bf16[128,1152]{1,0:T(8,128)(2,1)}, bf16[128,1152]{1,0:T(8,128)(2,1)}, u32[]{:S(2)}, u32[]{:S(2)}) collective-permute-start(bf16[128,1152]{1,0:T(8,128)(2,1)} %pad_maximum_fusion.10), channel_id=1, source_target_pairs={{0,8},{1,9},{2,10},{3,11},{4,12},{5,13},{6,14},{7,15},{8,0},{9,1},... | collective-permute-start | bytes 884744 | tf_op jit(solution)/shard_map/ppermute | solution.py:73
  51.1 27.4 %all-to-all-start = ((bf16[4,256,512]{2,1,0:T(8,128)(2,1)}), bf16[4,256,512]{2,1,0:T(8,128)(2,1)}, u32[]{:S(2)}, u32[]{:S(2)}) async-start(bf16[4,256,512]{2,1,0:T(8,128)(2,1)} %bitcast.7), calls=%async_computation | async-start | bytes 2097152 | tf_op jit(solution)/shard_map/all_to_all | solution.py:441
  58.2 25.6 %collective-permute-start.9 = (bf16[4,128,1024]{2,1,0:T(8,128)(2,1)}, bf16[4,128,1024]{2,1,0:T(8,128)(2,1)}, u32[]{:S(2)}, u32[]{:S(2)}) collective-permute-start(bf16[4,128,1024]{2,1,0:T(8,128)(2,1)} %copy-done.40), channel_id=1, source_target_pairs={{0,4},{4,0},{8,12},{12,8},{16,20},{20,16},{24,28},{28,24},{1,5},{5... | collective-permute-start | bytes 3145736 | tf_op jit(solution)/shard_map/ppermute | solution.py:58
  67.8 34.1 %collective-permute-start.12 = (bf16[512,1152]{1,0:T(8,128)(2,1)S(1)}, bf16[512,1152]{1,0:T(8,128)(2,1)}, u32[]{:S(2)}, u32[]{:S(2)}) collective-permute-start(bf16[512,1152]{1,0:T(8,128)(2,1)S(1)} %pad_maximum_fusion.refs_0_), channel_id=1, source_target_pairs={{0,2},{1,5},{2,0},{3,7},{4,6},{5,1},{6,4},{7,3},{8,10},{9,13},{10,... | collective-permute-start | bytes 3538952 | tf_op jit(solution)/shard_map/ppermute | solution.py:73
  90.9 17.8 %collective-permute-start.11 = (bf16[4,128,512]{2,1,0:T(8,128)(2,1)}, bf16[4,128,512]{2,1,0:T(8,128)(2,1)}, u32[]{:S(2)}, u32[]{:S(2)}) collective-permute-start(bf16[4,128,512]{2,1,0:T(8,128)(2,1)} %get-tuple-element.189), channel_id=1, source_target_pairs={{0,4},{4,0},{8,12},{12,8},{16,20},{20,16},{24,28},{28,24},{1,5},{5... | collective-permute-start | bytes 1572872 | tf_op jit(solution)/shard_map/ppermute | solution.py:58
  96.2 52.2 %all-to-all-start.1 = ((bf16[4,256,1024]{2,1,0:T(8,128)(2,1)}), bf16[4,256,1024]{2,1,0:T(8,128)(2,1)}, u32[]{:S(2)}, u32[]{:S(2)}) async-start(bf16[4,256,1024]{2,1,0:T(8,128)(2,1)} %shard_map.224), calls=%async_computation.1 | async-start | bytes 4194304 | tf_op jit(solution)/shard_map/all_to_all | solution.py:441
  117.2 14.0 %collective-permute-start.14 = (bf16[512,1024]{1,0:T(8,128)(2,1)S(1)}, bf16[512,1024]{1,0:T(8,128)(2,1)S(1)}, u32[]{:S(2)}, u32[]{:S(2)}) collective-permute-start(bf16[512,1024]{1,0:T(8,128)(2,1)S(1)} %constant_dynamic-update-slice_fusion.refs_0_), channel_id=1, source_target_pairs={{0,2},{1,5},{2,0},{3,7},{4,6},{5,1},{6,4},{7,3},{8,10},{9,13},{10,... | collective-permute-start | bytes 3145736 | tf_op jit(solution)/shard_map/ppermute | solution.py:73
  117.2 17.3 %collective-permute-start.15 = (bf16[512,1152]{1,0:T(8,128)(2,1)S(1)}, bf16[512,1152]{1,0:T(8,128)(2,1)S(1)}, u32[]{:S(2)}, u32[]{:S(2)}) collective-permute-start(bf16[512,1152]{1,0:T(8,128)(2,1)S(1)} %pad_maximum_fusion.refs_0_), channel_id=1, source_target_pairs={{0,1},{1,0},{2,3},{3,2},{4,5},{5,4},{6,7},{7,6},{8,9},{9,8},{10,11... | collective-permute-start | bytes 3538952 | tf_op jit(solution)/shard_map/ppermute | solution.py:58
  119.8 14.7 %collective-permute-start.16 = (bf16[512,1152]{1,0:T(8,128)(2,1)}, bf16[512,1152]{1,0:T(8,128)(2,1)S(1)}, u32[]{:S(2)}, u32[]{:S(2)}) collective-permute-start(bf16[512,1152]{1,0:T(8,128)(2,1)} %collective-permute-done.12.refs_1_), channel_id=1, source_target_pairs={{0,1},{1,0},{2,3},{3,2},{4,5},{5,4},{6,7},{7,6},{8,9},{9,8},{10,11... | collective-permute-start | bytes 3538952 | tf_op jit(solution)/shard_map/ppermute | solution.py:58
  119.9 24.0 %collective-permute-start.17 = (bf16[512,1024]{1,0:T(8,128)(2,1)S(1)}, bf16[512,1024]{1,0:T(8,128)(2,1)}, u32[]{:S(2)}, u32[]{:S(2)}) collective-permute-start(bf16[512,1024]{1,0:T(8,128)(2,1)S(1)} %constant_dynamic-update-slice_fusion.refs_0_), channel_id=1, source_target_pairs={{0,1},{1,0},{2,3},{3,2},{4,5},{5,4},{6,7},{7,6},{8,9},{9,8},{10,11... | collective-permute-start | bytes 3145736 | tf_op jit(solution)/shard_map/ppermute | solution.py:58
  131.2 12.7 %collective-permute-start.18 = (bf16[512,1024]{1,0:T(8,128)(2,1)S(1)}, bf16[512,1024]{1,0:T(8,128)(2,1)}, u32[]{:S(2)}, u32[]{:S(2)}) collective-permute-start(bf16[512,1024]{1,0:T(8,128)(2,1)S(1)} %collective-permute-done.14.refs_1_), channel_id=1, source_target_pairs={{0,1},{1,0},{2,3},{3,2},{4,5},{5,4},{6,7},{7,6},{8,9},{9,8},{10,11... | collective-permute-start | bytes 3145736 | tf_op jit(solution)/shard_map/ppermute | solution.py:58
  174.2 14.3 %collective-permute-start.24 = (bf16[512,1024]{1,0:T(8,128)(2,1)}, bf16[512,1024]{1,0:T(8,128)(2,1)}, u32[]{:S(2)}, u32[]{:S(2)}) collective-permute-start(bf16[512,1024]{1,0:T(8,128)(2,1)} %get-tuple-element.176), channel_id=1, source_target_pairs={{0,2},{1,5},{2,0},{3,7},{4,6},{5,1},{6,4},{7,3},{8,10},{9,13},{10,... | collective-permute-start | bytes 3145736 | tf_op jit(solution)/shard_map/ppermute | solution.py:73
  182.5 30.4 %collective-permute-start.20 = (bf16[1024,1024]{1,0:T(8,128)(2,1)}, bf16[1024,1024]{1,0:T(8,128)(2,1)}, u32[]{:S(2)}, u32[]{:S(2)}) collective-permute-start(bf16[1024,1024]{1,0:T(8,128)(2,1)} %shard_map.230), channel_id=1, source_target_pairs={{0,1},{1,0},{2,3},{3,2},{4,5},{5,4},{6,7},{7,6},{8,9},{9,8},{10,11... | collective-permute-start | bytes 6291464 | tf_op jit(solution)/shard_map/ppermute | solution.py:58
  182.8 30.1 %all-to-all-start.2 = ((bf16[4,256,512]{2,1,0:T(8,128)(2,1)}), bf16[4,256,512]{2,1,0:T(8,128)(2,1)}, u32[]{:S(2)}, u32[]{:S(2)}) async-start(bf16[4,256,512]{2,1,0:T(8,128)(2,1)} %bitcast.39), calls=%async_computation.2 | async-start | bytes 2097152 | tf_op jit(solution)/shard_map/all_to_all | solution.py:441
  190.8 14.7 %collective-permute-start.25 = (bf16[256,1024]{1,0:T(8,128)(2,1)S(1)}, bf16[256,1024]{1,0:T(8,128)(2,1)S(1)}, u32[]{:S(2)}, u32[]{:S(2)}) collective-permute-start(bf16[256,1024]{1,0:T(8,128)(2,1)S(1)} %get-tuple-element.106), channel_id=1, source_target_pairs={{0,4},{1,3},{2,6},{3,1},{4,0},{5,7},{6,2},{7,5},{8,12},{9,11},{10,... | collective-permute-start | bytes 1572872 | tf_op jit(solution)/shard_map/ppermute | solution.py:73
  200.7 23.8 %collective-permute-start.23 = (bf16[4,128,1024]{2,1,0:T(8,128)(2,1)}, bf16[4,128,1024]{2,1,0:T(8,128)(2,1)S(1)}, u32[]{:S(2)}, u32[]{:S(2)}) collective-permute-start(bf16[4,128,1024]{2,1,0:T(8,128)(2,1)} %get-tuple-element.105), channel_id=1, source_target_pairs={{0,4},{4,0},{8,12},{12,8},{16,20},{20,16},{24,28},{28,24},{1,5},{5... | collective-permute-start | bytes 3145736 | tf_op jit(solution)/shard_map/ppermute | solution.py:58
  218.3 23.9 %collective-permute-start.21 = (bf16[512,1024]{1,0:T(8,128)(2,1)}, bf16[512,1024]{1,0:T(8,128)(2,1)}, u32[]{:S(2)}, u32[]{:S(2)}) collective-permute-start(bf16[512,1024]{1,0:T(8,128)(2,1)} %get-tuple-element.177), channel_id=1, source_target_pairs={{0,2},{1,5},{2,0},{3,7},{4,6},{5,1},{6,4},{7,3},{8,10},{9,13},{10,... | collective-permute-start | bytes 3145736 | tf_op jit(solution)/shard_map/ppermute | solution.py:73
  229.6 54.9 %all-to-all-start.3 = ((bf16[4,256,1024]{2,1,0:T(8,128)(2,1)}), bf16[4,256,1024]{2,1,0:T(8,128)(2,1)S(1)}, u32[]{:S(2)}, u32[]{:S(2)}) async-start(bf16[4,256,1024]{2,1,0:T(8,128)(2,1)} %copy-done.3), calls=%async_computation.3 | async-start | bytes 4194304 | tf_op jit(solution)/shard_map/all_to_all | solution.py:441
  250.0 19.7 %collective-permute-start.32 = (bf16[512,768]{1,0:T(8,128)(2,1)S(1)}, bf16[512,768]{1,0:T(8,128)(2,1)S(1)}, u32[]{:S(2)}, u32[]{:S(2)}) collective-permute-start(bf16[512,768]{1,0:T(8,128)(2,1)S(1)} %get-tuple-element.118), channel_id=1, source_target_pairs={{0,4},{4,0},{8,12},{12,8},{16,20},{20,16},{24,28},{28,24},{1,5},{5... | collective-permute-start | bytes 2359304 | tf_op jit(solution)/shard_map/ppermute | solution.py:58
  283.1 16.4 %collective-permute-start.42 = (bf16[4,128,512]{2,1,0:T(8,128)(2,1)}, bf16[4,128,512]{2,1,0:T(8,128)(2,1)}, u32[]{:S(2)}, u32[]{:S(2)}) collective-permute-start(bf16[4,128,512]{2,1,0:T(8,128)(2,1)} %get-tuple-element.188), channel_id=1, source_target_pairs={{0,4},{4,0},{8,12},{12,8},{16,20},{20,16},{24,28},{28,24},{1,5},{5... | collective-permute-start | bytes 1572872 | tf_op jit(solution)/shard_map/ppermute | solution.py:58
  292.6 18.7 %collective-permute-start.41 = (bf16[128,768]{1,0:T(8,128)(2,1)S(1)}, bf16[128,768]{1,0:T(8,128)(2,1)}, u32[]{:S(2)}, u32[]{:S(2)}) collective-permute-start(bf16[128,768]{1,0:T(8,128)(2,1)S(1)} %slice.303), channel_id=1, source_target_pairs={{0,16},{4,20},{8,24},{12,28},{16,0},{20,4},{24,8},{28,12},{1,17},{... | collective-permute-start | bytes 589832 | tf_op jit(solution)/shard_map/ppermute | solution.py:58
  (80 other events, 610.6 us)
